TPU v7x, 32 devices: a whole 2x2x4 slice. The times are simulated.
32 devices in a mesh: feeder: 8 (over z, x), node: 4 (over y, core).
Axes of the slice: x: 2, y: 2, z: 4, core: 2. Of those that a mesh axis runs over, the one named last changes fastest.
Arguments:
- factors: bfloat16 [2048, 256], P('node'), may hold values from -6 to 6
- loadings: bfloat16 [4096, 256], P(('feeder', 'node')), may hold values from -0.35355339 to 0.5
- parents: int32 [4096], P(('feeder', 'node')), may hold values from -1 to 126, as said below
- load_base: float32 [2, 4096], P(None, ('feeder', 'node')), may hold values from 1.953125e-05 to 0.00390625, as said below
- lateral_z: float32 [2, 4096], P(None, ('feeder', 'node')), may hold values from 0.000875 to 0.021875, as said below
- trunk_z: float32 [2, 8, 4], P(None, 'feeder', 'node'), may hold values from 0.00275 to 0.04875, as said below
Outputs:
- volt_real: float32 [2048, 4096], P(None, ('feeder', 'node'))
- volt_imag: float32 [2048, 4096], P(None, ('feeder', 'node'))
Inputs may be any that keep to these rules, and one draw needn't show every extreme that they name: `parents`: within each aligned run of 128 nodes (one lateral), a node's entry is the position of its parent in the same lateral, which comes before it, or -1 for a branch from the section's head node; the first node of every lateral has -1 and the last node's parent is the node just before it. `load_base`: with unit = 1 / 1024, row 0 lies between 1 and 4 units and row 1 between 0.02 and 0.08 units. `lateral_z`: with unit = 128 * 8 / 128^2, row 0 lies between 0.014 and 0.056 units and row 1 between 0.087 and 0.35 units. `trunk_z`: with unit = 1 / 8, row 0 lies between 0.022 and 0.066 units and row 1 between 0.13 and 0.39 units.
All inputs are finite; a program needn't handle non-finite values.
Results may differ from a plain program's by a relative error of at most 0.0003.
Values may be sent and summed in bfloat16 or wider, within the bound.
No kernel may reach another device: no remote copies, remote signals or barrier semaphores. Data moves between devices by JAX's collectives and lax.ppermute only.
A program may use at most 64 MiB of HBM per device.

v0:
```python
import jax
import jax.numpy as jnp
from jax import lax
from jax.sharding import PartitionSpec as P

LAT_NODES = 128
SWEEPS = 3


HIGHEST = lax.Precision.HIGHEST


def path_matrix(parent_rows):
    laterals, width = parent_rows.shape
    column = jnp.arange(width, dtype=jnp.int32)
    adjacency = (parent_rows[:, :, None] == column[None, None, :]).astype(jnp.float32)
    identity = jnp.eye(width, dtype=jnp.float32)
    paths = identity[None] + adjacency
    power = adjacency
    for turn in range((width - 1).bit_length() - 1):
        power = jnp.einsum("alm,amn->aln", power, power, precision=HIGHEST)
        paths = paths + jnp.einsum("alm,amn->aln", paths, power, precision=HIGHEST)
    return paths


def node_currents(active, reactive, real_part, imag_part):
    magnitude = real_part * real_part + imag_part * imag_part
    return (
        (active * real_part + reactive * imag_part) / magnitude,
        (active * imag_part - reactive * real_part) / magnitude,
    )


def lateral_products(stacked, tables):
    blocks = jnp.dot(stacked, tables[0], precision=HIGHEST, preferred_element_type=jnp.float32)
    return blocks


def trunk_heads(inject, trunk_z, scen):
    every, every_z = (
        lax.all_gather(inject[None], "feeder", axis=0, tiled=True),
        lax.all_gather(trunk_z[:, 0, 0][None], "feeder", axis=0, tiled=True),
    )
    trunk = jnp.flip(jnp.cumsum(jnp.flip(every, 0), 0), 0)
    trunk_real = trunk[:, :scen]
    trunk_imag = trunk[:, scen:]
    drop_real = every_z[:, 0:1] * trunk_real - every_z[:, 1:2] * trunk_imag
    drop_imag = every_z[:, 0:1] * trunk_imag + every_z[:, 1:2] * trunk_real
    section_ids = jnp.arange(every.shape[0], dtype=jnp.int32)
    upto = (section_ids <= lax.axis_index("feeder")).astype(jnp.float32)[:, None]
    return (1.0 - jnp.sum(upto * drop_real, axis=0), -jnp.sum(upto * drop_imag, axis=0))


def local(factors, loadings, parents, load_base, lateral_z, trunk_z):
    levels = jnp.einsum(
        "sr,nr->sn",
        lax.all_gather(factors, "node", axis=0, tiled=True),
        loadings,
        preferred_element_type=jnp.float32,
    ).astype(jnp.bfloat16)
    scen = levels.shape[0]
    nodes_here = levels.shape[1]
    lat_count = nodes_here // LAT_NODES
    swing = 1.0 + 0.5 * jnp.tanh(levels.astype(jnp.float32))
    active = load_base[0][None, :] * swing
    reactive = load_base[1][None, :] * swing
    paths = path_matrix(parents.reshape(lat_count, LAT_NODES))
    paths_back = jnp.swapaxes(paths, 1, 2)
    resist = lateral_z[0][None, :]
    react = lateral_z[1][None, :]
    volts = jnp.concatenate(
        [jnp.ones((scen, nodes_here), jnp.float32), jnp.zeros((scen, nodes_here), jnp.float32)]
    )
    for sweep_index in range(SWEEPS):
        current_real, current_imag = node_currents(active, reactive, volts[:scen], volts[scen:])
        current = jnp.concatenate([current_real, current_imag])
        inject = jnp.sum(current, axis=1)
        branch = lateral_products(current, paths)
        branch_real = branch[:scen]
        branch_imag = branch[scen:]
        weighted = jnp.concatenate(
            [resist * branch_real - react * branch_imag, resist * branch_imag + react * branch_real]
        )
        drops = lateral_products(weighted, paths_back)
        head_real, head_imag = trunk_heads(inject, trunk_z, scen)
        volts = jnp.concatenate(
            [head_real[:, None] - drops[:scen], head_imag[:, None] - drops[scen:]]
        )
    return (volts[:scen], volts[scen:])


def solution(mesh):
    return jax.shard_map(
        local,
        mesh=mesh,
        in_specs=(
            P("node", None),
            P(("feeder", "node"), None),
            P(("feeder", "node")),
            P(None, ("feeder", "node")),
            P(None, ("feeder", "node")),
            P(None, "feeder", "node"),
        ),
        out_specs=(P(None, ("feeder", "node")), P(None, ("feeder", "node"))),
        check_vma=False,
    )
```

profile of v0, /device:TPU:0, one launch (start us, length us, event | category | flops | bytes accessed | tf_op | source)
XLA Modules:
  0.0 184.0 jit_solution(3400660566168212576)
XLA Ops:
  7.9 0.9 fusion.31
  9.1 0.9 convolution_add_fusion.5
  10.0 1.2 dynamic-slice
  13.3 23.1 %all-reduce = f32[16]{0:T(128)S(1)} all-reduce(f32[16]{0:T(128)S(1)} %bitcast_dynamic-update-slice_fusion), channel_id=2, replica_groups=mesh['feeder'=8,'node'=4] {'feeder'}, use_global_device_ids=true, to_apply=%add | all-reduce | flops 16 | bytes 128
  38.0 1.3 slice_bitcast_fusion.1
  40.6 1.8 multiply_add_fusion.5
  43.0 1.8 fusion.20
  44.7 30.5 %all-gather.1 = f32[32768]{0:T(1024)S(1)} all-gather(f32[4096]{0:T(1024)S(1)} %fusion.21), channel_id=3, replica_groups=mesh['feeder'=8,'node'=4] {'feeder'}, dimensions={0}, use_global_device_ids=true | all-gather | bytes 147456 | tf_op jit(solution)/shard_map/all_gather | solution.py:41
  75.3 9.5 %rev.13 = f32[8,4096]{1,0:T(8,128)} reverse(f32[8,4096]{1,0:T(8,128)S(1)} %reshape.190), dimensions={0} | reverse | bytes 262144 | tf_op jit(solution)/shard_map/jit(_flip)/rev | solution.py:44
  84.8 1.0 reduce_window_sum.20
  86.4 0.8 multiply_reduce_fusion.5
  87.3 0.9 multiply_subtract_fusion.2
  88.1 1.9 %fusion.4 = f32[4096,128]{1,0:T(8,128)S(1)} fusion(f32[2048,128]{1,0:T(8,128)S(1)} %get-tuple-element.19, f32[2048,128]{1,0:T(8,128)S(1)} %get-tuple-element.18, f32[128,128]{1,0:T(8,128)S(1)} %convolution_add_fusion), kind=kOutput, calls=%fused_computation.6 | convolution fusion | flops 805830656 | bytes 4259840 | tf_op jit(solution)/shard_map/dot_general | solution.py:35
  91.4 1.9 %fusion.18 = f32[4096,128]{1,0:T(8,128)S(1)} fusion(f32[128,128]{1,0:T(8,128)S(1)} %convolution_add_fusion, f32[2048,128]{1,0:T(8,128)S(1)} %get-tuple-element.13, f32[2048,128]{1,0:T(8,128)S(1)} %get-tuple-element.12), kind=kOutput, calls=%fused_computation.22 | convolution fusion | flops 805830656 | bytes 4259840 | tf_op jit(solution)/shard_map/dot_general | solution.py:35
  93.5 30.7 %all-gather.2 = f32[32768]{0:T(1024)S(1)} all-gather(f32[4096]{0:T(1024)S(1)} %fusion.19), channel_id=4, replica_groups=mesh['feeder'=8,'node'=4] {'feeder'}, dimensions={0}, use_global_device_ids=true | all-gather | bytes 147456 | tf_op jit(solution)/shard_map/all_gather | solution.py:41
  124.3 9.5 %rev.14 = f32[8,4096]{1,0:T(8,128)} reverse(f32[8,4096]{1,0:T(8,128)S(1)} %reshape.191), dimensions={0} | reverse | bytes 262144 | tf_op jit(solution)/shard_map/jit(_flip)/rev | solution.py:44
  133.8 1.0 reduce_window_sum.24
  135.4 0.8 multiply_reduce_fusion.3
  136.2 1.9 %fusion.8 = f32[4096,128]{1,0:T(8,128)S(1)} fusion(f32[2048,128]{1,0:T(8,128)S(1)} %get-tuple-element.17, f32[2048,128]{1,0:T(8,128)S(1)} %get-tuple-element.16, f32[128,128]{1,0:T(8,128)S(1)} %convolution_add_fusion), kind=kOutput, calls=%fused_computation.11 | convolution fusion | flops 805830656 | bytes 4259840 | tf_op jit(solution)/shard_map/dot_general | solution.py:35
  138.1 0.8 fusion.22
  139.5 1.8 %fusion.16 = f32[4096,128]{1,0:T(8,128)S(1)} fusion(f32[128,128]{1,0:T(8,128)S(1)} %convolution_add_fusion, f32[2048,128]{1,0:T(8,128)S(1)} %get-tuple-element.11, f32[2048,128]{1,0:T(8,128)S(1)} %get-tuple-element.10), kind=kOutput, calls=%fused_computation.20 | convolution fusion | flops 805830656 | bytes 4259840 | tf_op jit(solution)/shard_map/dot_general | solution.py:35
  141.7 30.5 %all-gather.3 = f32[32768]{0:T(1024)S(1)} all-gather(f32[4096]{0:T(1024)S(1)} %fusion.17), channel_id=5, replica_groups=mesh['feeder'=8,'node'=4] {'feeder'}, dimensions={0}, use_global_device_ids=true | all-gather | bytes 147456 | tf_op jit(solution)/shard_map/all_gather | solution.py:41
  173.6 1.9 %fusion.12 = f32[4096,128]{1,0:T(8,128)S(1)} fusion(f32[2048,128]{1,0:T(8,128)S(1)} %get-tuple-element.15, f32[2048,128]{1,0:T(8,128)S(1)} %get-tuple-element.14, f32[128,128]{1,0:T(8,128)S(1)} %convolution_add_fusion), kind=kOutput, calls=%fused_computation.16 | convolution fusion | flops 805830656 | bytes 4259840 | tf_op jit(solution)/shard_map/dot_general | solution.py:35
  175.5 1.7 slice_subtract_fusion
  (58 shorter events, 10.7 us)
Async XLA Ops:
  7.2 33.4 %copy-start = (bf16[128,256]{1,0:T(8,128)(2,1)S(1)}, bf16[128,256]{1,0:T(8,128)(2,1)}, u32[]{:S(2)}) copy-start(bf16[128,256]{1,0:T(8,128)(2,1)} %param.7) | copy-start | bytes 196612
  7.2 33.4 %all-gather.6.cloned.1.call-start = ((), (), s32[]{:S(2)}) async-start(), calls=%async_computation | async-start | bytes 1310720 | tf_op jit(solution)/shard_map/all_gather | solution.py:57
  91.4 1.9 %copy-start.1 = (f32[128]{0:T(128)S(1)}, f32[128]{0:T(128)}, u32[]{:S(2)}) copy-start(f32[128]{0:T(128)} %get-tuple-element.30) | copy-start | bytes 1540
  91.4 1.9 %copy-start.3 = (f32[128]{0:T(128)S(1)}, f32[128]{0:T(128)}, u32[]{:S(2)}) copy-start(f32[128]{0:T(128)} %get-tuple-element.31) | copy-start | bytes 1540
  139.5 1.9 %copy-start.2 = (f32[128]{0:T(128)S(1)}, f32[128]{0:T(128)}, u32[]{:S(2)}) copy-start(f32[128]{0:T(128)} %get-tuple-element.30) | copy-start | bytes 1540
  139.5 1.9 %copy-start.4 = (f32[128]{0:T(128)S(1)}, f32[128]{0:T(128)}, u32[]{:S(2)}) copy-start(f32[128]{0:T(128)} %get-tuple-element.31) | copy-start | bytes 1540
  141.4 32.0 %copy-start.5 = (f32[8]{0:T(128)S(1)}, f32[8]{0:T(128)}, u32[]{:S(2)}) copy-start(f32[8]{0:T(128)} %compare_convert_fusion) | copy-start | bytes 100
Sparse Core Ops, SparseCore 0:
  9.6 19.4 all-gather.5
where the time goes:
time: 184 us
  blocking collectives  115 us (62%)
  local copies, waits for them, and re-layouts  25.6 us (14%)
  matrix products  16.8 us (9%)
  between operations  15.2 us (8%)
  other arithmetic  10.9 us (6%)
    all_gather x3, blocking collectives, trunk_heads(): lax.all_gather(inject[None], 'feeder', axis=0, tiled=True)  91.7 us
    unnamed x1, blocking collectives  23.1 us
    rev x3, local copies, waits for them, and re-layouts, trunk_heads(): trunk = jnp.flip(jnp.cumsum(jnp.flip(every, 0), 0), 0)  19.6 us
    dot_general x6, matrix products, lateral_products(): jnp.dot(stacked, tables[0], precision=HIGHEST, preferred_element_type=jnp...  11.2 us
  transfers between devices with their start and end apart: 1, of which 0 were waited for; matrix products, arithmetic and copies ran while one was open for 5% of the time, Pallas kernels for 0%

commit v1 on v0

v1 whole, which is shorter than its diff:
```python
import jax
import jax.numpy as jnp
from jax import lax
from jax.sharding import PartitionSpec as P

LAT_NODES = 128
SWEEPS = 3


HIGHEST = lax.Precision.HIGHEST


def path_matrix(parent_rows):
    laterals, width = parent_rows.shape
    column = jnp.arange(width, dtype=jnp.int32)
    adjacency = (parent_rows[:, :, None] == column[None, None, :]).astype(jnp.bfloat16)
    identity = jnp.eye(width, dtype=jnp.bfloat16)
    paths = identity[None] + adjacency
    power = adjacency
    for turn in range((width - 1).bit_length() - 1):
        power = jnp.einsum("alm,amn->aln", power, power)
        paths = paths + jnp.einsum("alm,amn->aln", paths, power)
    return paths


def node_currents(active, reactive, real_part, imag_part):
    magnitude = real_part * real_part + imag_part * imag_part
    return (
        (active * real_part + reactive * imag_part) / magnitude,
        (active * imag_part - reactive * real_part) / magnitude,
    )


def lateral_products(stacked, table):
    high = stacked.astype(jnp.bfloat16)
    low = (stacked - high.astype(jnp.float32)).astype(jnp.bfloat16)
    both = jnp.concatenate([high, low], axis=1)
    return jnp.dot(both, jnp.concatenate([table, table]), preferred_element_type=jnp.float32)


def xor_gather(block, axis, size):
    held = block[None]
    step = 1
    while step < size:
        other = lax.ppermute(held, axis, [(i, i ^ step) for i in range(size)])
        held = jnp.concatenate([held, other])
        step *= 2
    return held


def trunk_table(z_all, index):
    size = z_all.shape[0]
    section = index ^ jnp.arange(size, dtype=jnp.int32)
    shared = (section[None, :] <= jnp.minimum(index, section)[:, None]).astype(jnp.float32)
    return jnp.sum(shared[:, :, None] * z_all[None], axis=1)


def local(feeders, nodes, factors, loadings, parents, load_base, lateral_z, trunk_z):
    node = lax.axis_index("node")
    feeder = lax.axis_index("feeder")
    rows = factors.shape[0]
    scen = rows * nodes
    held = factors[None]
    order = [0]
    step = nodes // 2
    while step >= 1:
        other = lax.ppermute(held, "node", [(i, i ^ step) for i in range(nodes)])
        held = jnp.concatenate([held, other])
        order = order + [o ^ step for o in order]
        step //= 2
    whole = jnp.zeros((scen, factors.shape[1]), factors.dtype)
    for place, offset in enumerate(order):
        whole = lax.dynamic_update_slice(whole, held[place], ((node ^ offset) * rows, 0))
    levels = jnp.einsum("sr,nr->sn", whole, loadings, preferred_element_type=jnp.float32).astype(jnp.bfloat16)
    nodes_here = levels.shape[1]
    swing = 1.0 + 0.5 * jnp.tanh(levels.astype(jnp.float32))
    active = load_base[0][None, :] * swing
    reactive = load_base[1][None, :] * swing
    paths = path_matrix(parents.reshape(1, LAT_NODES))[0]
    resist = lateral_z[0][None, :]
    react = lateral_z[1][None, :]
    volts = None
    table = None
    for sweep_index in range(SWEEPS):
        if volts is None:
            current_real, current_imag = active, -reactive
        else:
            current_real, current_imag = node_currents(active, reactive, volts[:scen], volts[scen:])
        current = jnp.concatenate([current_real, current_imag])
        inject = jnp.sum(current, axis=1).reshape(2, scen // 128, 128)
        if table is None:
            extra = jnp.broadcast_to(trunk_z.reshape(2, 1, 1), (2, 8, 128))
            every = xor_gather(jnp.concatenate([inject, extra], axis=1), "feeder", feeders)
            table = trunk_table(every[:, :, scen // 128, 0], feeder)
            every = every[:, :, : scen // 128]
        else:
            every = xor_gather(inject, "feeder", feeders)
        branch = lateral_products(current, paths)
        branch_real = branch[:scen]
        branch_imag = branch[scen:]
        weighted = jnp.concatenate(
            [resist * branch_real - react * branch_imag, resist * branch_imag + react * branch_real]
        )
        drops = lateral_products(weighted, paths.T)
        r = table[:, 0, None, None]
        x = table[:, 1, None, None]
        head_real = 1.0 - jnp.sum(r * every[:, 0] - x * every[:, 1], axis=0).reshape(scen)
        head_imag = -jnp.sum(r * every[:, 1] + x * every[:, 0], axis=0).reshape(scen)
        volts = jnp.concatenate(
            [head_real[:, None] - drops[:scen], head_imag[:, None] - drops[scen:]]
        )
    return (volts[:scen], volts[scen:])


def solution(mesh):
    feeders = mesh.shape["feeder"]
    nodes = mesh.shape["node"]

    def part(*args):
        return local(feeders, nodes, *args)

    return jax.shard_map(
        part,
        mesh=mesh,
        in_specs=(
            P("node", None),
            P(("feeder", "node"), None),
            P(("feeder", "node")),
            P(None, ("feeder", "node")),
            P(None, ("feeder", "node")),
            P(None, "feeder", "node"),
        ),
        out_specs=(P(None, ("feeder", "node")), P(None, ("feeder", "node"))),
        check_vma=False,
    )
```

time: 184 us -> 59.9 us (0.33)
  blocking collectives: 115 us -> 0 us
  local copies, waits for them, and re-layouts: 25.6 us -> 1.92 us
  starting transfers between devices: 0.04 us -> 23.1 us
  waiting for transfers between devices: 0.7 us -> 16 us
  between operations: 15.2 us -> 1.07 us
  matrix products: 16.8 us -> 9.25 us
  other arithmetic: 10.9 us -> 8.3 us
    all_gather x3 -> x0, blocking collectives: 91.7 us -> none  [trunk_heads(): lax.all_gather(inject[None], 'feeder', axis=0, tiled=True)]
    ppermute x0 -> x11, starting transfers between devices: none -> 23.1 us  [the longest x9 20 us: xor_gather(): other = lax.ppermute(held, axis, [(i, i ^ step) for i in range(size)])]
    unnamed x1 -> x0, blocking collectives: 23.1 us -> none
    rev x3 -> x0, local copies, waits for them, and re-layouts: 19.6 us -> none  [trunk_heads(): trunk = jnp.flip(jnp.cumsum(jnp.flip(every, 0), 0), 0)]
    ppermute x0 -> x11, waiting for transfers between devices: none -> 16 us  [the longest x9 14.2 us: xor_gather(): other = lax.ppermute(held, axis, [(i, i ^ step) for i in range(size)])]
    dot_general x19 -> x18, matrix products: 16.8 us -> 9.25 us  [the longest x6 4.15 us: lateral_products(): jnp.dot(both, jnp.concatenate([table, table]), preferred_element_type=jnp...]
    another operation x3 -> x0, other arithmetic: 2.18 us -> none  [trunk_heads(): trunk = jnp.flip(jnp.cumsum(jnp.flip(every, 0), 0), 0)]
    unnamed x15 -> x8, local copies, waits for them, and re-layouts: 2.03 us -> 0.05 us
  transfers between devices with their start and end apart: 1 -> 11, of which waited for: 0 -> 11; matrix products, arithmetic and copies ran while one was open for 5% -> 20% of each run, Pallas kernels for 0% -> 0%
where the time goes in v1:
time: 59.9 us; the launch traced here: 59.7 us
  starting transfers between devices  23.1 us (39%)
  waiting for transfers between devices  16 us (27%)
  matrix products  9.25 us (15%)
  other arithmetic  8.3 us (14%)
  local copies, waits for them, and re-layouts  1.92 us (3%)
  between operations  1.07 us (2%)
    ppermute x9, starting transfers between devices, xor_gather(): other = lax.ppermute(held, axis, [(i, i ^ step) for i in range(size)])  20 us
    ppermute x9, waiting for transfers between devices, xor_gather(): other = lax.ppermute(held, axis, [(i, i ^ step) for i in range(size)])  14.2 us
    dot_general x6, matrix products, lateral_products(): jnp.dot(both, jnp.concatenate([table, table]), preferred_element_type=jnp...  4.15 us
    dot_general x6, matrix products, path_matrix(): paths = paths + jnp.einsum('alm,amn->aln', paths, power)  3.2 us
    ppermute x2, starting transfers between devices, local(): other = lax.ppermute(held, 'node', [(i, i ^ step) for i in range(nodes)])  3.1 us
    reduce_sum x3, other arithmetic, local(): inject = jnp.sum(current, axis=1).reshape(2, scen // 128, 128)  1.84 us
    ppermute x2, waiting for transfers between devices, local(): other = lax.ppermute(held, 'node', [(i, i ^ step) for i in range(nodes)])  1.79 us
    sub x1, other arithmetic, local(): head_imag[:, None] - drops[scen:]  1.67 us
  transfers between devices with their start and end apart: 11, of which 11 were waited for; matrix products, arithmetic and copies ran while one was open for 20% of the time, Pallas kernels for 0%

profile of v1, /device:TPU:0, one launch (start us, length us, event | category | flops | bytes accessed | tf_op | source)
XLA Modules:
  0.0 59.7 jit_solution(3905364371408692926)
XLA Ops:
  0.7 3.0 %collective-permute-start = (bf16[1,512,256]{2,1,0:T(8,128)(2,1)}, bf16[1,512,256]{2,1,0:T(8,128)(2,1)S(1)}, u32[]{:S(2)}, u32[]{:S(2)}) collective-permute-start(bf16[1,512,256]{2,1,0:T(8,128)(2,1)} %bitcast.125), channel_id=1, source_target_pairs={{0,2},{1,3},{2,0},{3,1},{4,6},{5,7},{6,4},{7,5},{8,10},{9,11},{10,... | collective-permute-start | bytes 786440 | tf_op jit(solution)/shard_map/ppermute | solution.py:67
  3.7 0.9 %fusion.48 = bf16[128,128]{1,0:T(8,128)(2,1)S(1)} fusion(s32[128]{0:T(128)} %param.8), kind=kOutput, calls=%fused_computation.108 | convolution fusion | flops 4210688 | bytes 33280 | tf_op jit(solution)/shard_map/alm,amn->aln/dot_general | solution.py:21
  7.7 0.9 %fusion.74 = (bf16[128,128]{1,0:T(8,128)(2,1)S(1)}, bf16[128,128]{1,0:T(8,128)(2,1)S(1)}) fusion(bf16[128,128]{1,0:T(8,128)(2,1)S(1)} %fusion.66, bf16[128,128]{1,0:T(8,128)(2,1)S(1)} %fusion.61, s32[128]{0:T(128)} %param.8, bf16[128,128]{1,0:T(8,128)(2,1)S(1)} %fusion.81), kind=kOutput, calls=%fused_computation.153 | convolution fusion | flops 4620288 | bytes 164352 | tf_op jit(solution)/shard_map/alm,amn->aln/dot_general | solution.py:22
  10.2 1.0 %pad_maximum_fusion.6 = bf16[2,512,256]{2,1,0:T(8,128)(2,1)S(1)} fusion(bf16[1,512,256]{2,1,0:T(8,128)(2,1)S(1)} %collective-permute-done, bf16[1,512,256]{2,1,0:T(8,128)(2,1)} %bitcast.126), kind=kLoop, calls=%fused_computation.71 | loop fusion | flops 262144 | bytes 1048576 | tf_op jit(solution)/shard_map/concatenate | solution.py:68
  11.6 1.6 %collective-permute-done.1 = bf16[2,512,256]{2,1,0:T(8,128)(2,1)S(1)} collective-permute-done((bf16[2,512,256]{2,1,0:T(8,128)(2,1)S(1)}, bf16[2,512,256]{2,1,0:T(8,128)(2,1)S(1)}, u32[]{:S(2)}, u32[]{:S(2)}) %collective-permute-start.1) | collective-permute-done | bytes 524320 | tf_op jit(solution)/shard_map/ppermute | solution.py:67
  14.6 1.7 %collective-permute-start.2 = (f32[1,2,24,128]{3,2,1,0:T(8,128)S(1)}, f32[1,2,24,128]{3,2,1,0:T(8,128)S(1)}, u32[]{:S(2)}, u32[]{:S(2)}) collective-permute-start(f32[1,2,24,128]{3,2,1,0:T(8,128)S(1)} %maximum_bitcast_fusion.1), channel_id=1, source_target_pairs={{0,4},{4,0},{8,12},{12,8},{16,20},{20,16},{24,28},{28,24},{1,5},{5... | collective-permute-start | bytes 73736 | tf_op jit(solution)/shard_map/ppermute | solution.py:45
  17.3 1.1 %collective-permute-done.2 = f32[1,2,24,128]{3,2,1,0:T(8,128)S(1)} collective-permute-done((f32[1,2,24,128]{3,2,1,0:T(8,128)S(1)}, f32[1,2,24,128]{3,2,1,0:T(8,128)S(1)}, u32[]{:S(2)}, u32[]{:S(2)}) %collective-permute-start.2) | collective-permute-done | bytes 24608 | tf_op jit(solution)/shard_map/ppermute | solution.py:45
  18.4 1.8 %collective-permute-start.3 = (f32[2,2,24,128]{3,2,1,0:T(8,128)S(1)}, f32[2,2,24,128]{3,2,1,0:T(8,128)S(1)}, u32[]{:S(2)}, u32[]{:S(2)}) collective-permute-start(f32[2,2,24,128]{3,2,1,0:T(8,128)S(1)} %pad_maximum_fusion.23), channel_id=1, source_target_pairs={{0,8},{4,12},{8,0},{12,4},{16,24},{20,28},{24,16},{28,20},{1,9},{5... | collective-permute-start | bytes 147464 | tf_op jit(solution)/shard_map/ppermute | solution.py:45
  20.3 2.2 %collective-permute-done.3 = f32[2,2,24,128]{3,2,1,0:T(8,128)S(1)} collective-permute-done((f32[2,2,24,128]{3,2,1,0:T(8,128)S(1)}, f32[2,2,24,128]{3,2,1,0:T(8,128)S(1)}, u32[]{:S(2)}, u32[]{:S(2)}) %collective-permute-start.3) | collective-permute-done | bytes 49184 | tf_op jit(solution)/shard_map/ppermute | solution.py:45
  22.5 2.9 %collective-permute-start.4 = (f32[4,2,24,128]{3,2,1,0:T(8,128)S(1)}, f32[4,2,24,128]{3,2,1,0:T(8,128)S(1)}, u32[]{:S(2)}, u32[]{:S(2)}) collective-permute-start(f32[4,2,24,128]{3,2,1,0:T(8,128)S(1)} %pad_maximum_fusion.9), channel_id=1, source_target_pairs={{0,16},{4,20},{8,24},{12,28},{16,0},{20,4},{24,8},{28,12},{1,17},{... | collective-permute-start | bytes 294920 | tf_op jit(solution)/shard_map/ppermute | solution.py:45
  26.1 2.0 %collective-permute-done.4 = f32[4,2,24,128]{3,2,1,0:T(8,128)S(1)} collective-permute-done((f32[4,2,24,128]{3,2,1,0:T(8,128)S(1)}, f32[4,2,24,128]{3,2,1,0:T(8,128)S(1)}, u32[]{:S(2)}, u32[]{:S(2)}) %collective-permute-start.4) | collective-permute-done | bytes 98336 | tf_op jit(solution)/shard_map/ppermute | solution.py:45
  29.9 1.8 %collective-permute-start.5 = (f32[1,2,16,128]{3,2,0,1:T(8,128)S(1)}, f32[1,2,16,128]{3,2,0,1:T(8,128)S(1)}, u32[]{:S(2)}, u32[]{:S(2)}) collective-permute-start(f32[1,2,16,128]{3,2,0,1:T(8,128)S(1)} %bitcast.131), channel_id=1, source_target_pairs={{0,4},{4,0},{8,12},{12,8},{16,20},{20,16},{24,28},{28,24},{1,5},{5... | collective-permute-start | bytes 49160 | tf_op jit(solution)/shard_map/ppermute | solution.py:45
  32.7 1.0 %collective-permute-done.5 = f32[1,2,16,128]{3,2,0,1:T(8,128)S(1)} collective-permute-done((f32[1,2,16,128]{3,2,0,1:T(8,128)S(1)}, f32[1,2,16,128]{3,2,0,1:T(8,128)S(1)}, u32[]{:S(2)}, u32[]{:S(2)}) %collective-permute-start.5) | collective-permute-done | bytes 16416 | tf_op jit(solution)/shard_map/ppermute | solution.py:45
  33.7 1.9 %collective-permute-start.6 = (f32[2,2,16,128]{3,2,0,1:T(8,128)S(1)}, f32[2,2,16,128]{3,2,0,1:T(8,128)S(1)}, u32[]{:S(2)}, u32[]{:S(2)}) collective-permute-start(f32[2,2,16,128]{3,2,0,1:T(8,128)S(1)} %pad_maximum_fusion.24), channel_id=1, source_target_pairs={{0,8},{4,12},{8,0},{12,4},{16,24},{20,28},{24,16},{28,20},{1,9},{5... | collective-permute-start | bytes 98312 | tf_op jit(solution)/shard_map/ppermute | solution.py:45
  35.8 1.9 %collective-permute-done.6 = f32[2,2,16,128]{3,2,0,1:T(8,128)S(1)} collective-permute-done((f32[2,2,16,128]{3,2,0,1:T(8,128)S(1)}, f32[2,2,16,128]{3,2,0,1:T(8,128)S(1)}, u32[]{:S(2)}, u32[]{:S(2)}) %collective-permute-start.6) | collective-permute-done | bytes 32800 | tf_op jit(solution)/shard_map/ppermute | solution.py:45
  37.6 3.3 %collective-permute-start.7 = (f32[4,2,16,128]{3,2,0,1:T(8,128)S(1)}, f32[4,2,16,128]{3,2,0,1:T(8,128)S(1)}, u32[]{:S(2)}, u32[]{:S(2)}) collective-permute-start(f32[4,2,16,128]{3,2,0,1:T(8,128)S(1)} %pad_maximum_fusion.15), channel_id=1, source_target_pairs={{0,16},{4,20},{8,24},{12,28},{16,0},{20,4},{24,8},{28,12},{1,17},{... | collective-permute-start | bytes 196616 | tf_op jit(solution)/shard_map/ppermute | solution.py:45
  41.6 1.5 %collective-permute-done.7 = f32[4,2,16,128]{3,2,0,1:T(8,128)S(1)} collective-permute-done((f32[4,2,16,128]{3,2,0,1:T(8,128)S(1)}, f32[4,2,16,128]{3,2,0,1:T(8,128)S(1)}, u32[]{:S(2)}, u32[]{:S(2)}) %collective-permute-start.7) | collective-permute-done | bytes 65568 | tf_op jit(solution)/shard_map/ppermute | solution.py:45
  44.8 1.6 %collective-permute-start.8 = (f32[1,2,16,128]{3,2,0,1:T(8,128)S(1)}, f32[1,2,16,128]{3,2,0,1:T(8,128)S(1)}, u32[]{:S(2)}, u32[]{:S(2)}) collective-permute-start(f32[1,2,16,128]{3,2,0,1:T(8,128)S(1)} %bitcast.127), channel_id=1, source_target_pairs={{0,4},{4,0},{8,12},{12,8},{16,20},{20,16},{24,28},{28,24},{1,5},{5... | collective-permute-start | bytes 49160 | tf_op jit(solution)/shard_map/ppermute | solution.py:45
  47.4 1.2 %collective-permute-done.8 = f32[1,2,16,128]{3,2,0,1:T(8,128)S(1)} collective-permute-done((f32[1,2,16,128]{3,2,0,1:T(8,128)S(1)}, f32[1,2,16,128]{3,2,0,1:T(8,128)S(1)}, u32[]{:S(2)}, u32[]{:S(2)}) %collective-permute-start.8) | collective-permute-done | bytes 16416 | tf_op jit(solution)/shard_map/ppermute | solution.py:45
  48.6 2.0 %collective-permute-start.9 = (f32[2,2,16,128]{3,2,0,1:T(8,128)S(1)}, f32[2,2,16,128]{3,2,0,1:T(8,128)S(1)}, u32[]{:S(2)}, u32[]{:S(2)}) collective-permute-start(f32[2,2,16,128]{3,2,0,1:T(8,128)S(1)} %pad_maximum_fusion.25), channel_id=1, source_target_pairs={{0,8},{4,12},{8,0},{12,4},{16,24},{20,28},{24,16},{28,20},{1,9},{5... | collective-permute-start | bytes 98312 | tf_op jit(solution)/shard_map/ppermute | solution.py:45
  50.8 1.8 %collective-permute-done.9 = f32[2,2,16,128]{3,2,0,1:T(8,128)S(1)} collective-permute-done((f32[2,2,16,128]{3,2,0,1:T(8,128)S(1)}, f32[2,2,16,128]{3,2,0,1:T(8,128)S(1)}, u32[]{:S(2)}, u32[]{:S(2)}) %collective-permute-start.9) | collective-permute-done | bytes 32800 | tf_op jit(solution)/shard_map/ppermute | solution.py:45
  52.5 3.1 %collective-permute-start.10 = (f32[4,2,16,128]{3,2,0,1:T(8,128)S(1)}, f32[4,2,16,128]{3,2,0,1:T(8,128)S(1)}, u32[]{:S(2)}, u32[]{:S(2)}) collective-permute-start(f32[4,2,16,128]{3,2,0,1:T(8,128)S(1)} %pad_maximum_fusion.16), channel_id=1, source_target_pairs={{0,16},{4,20},{8,24},{12,28},{16,0},{20,4},{24,8},{28,12},{1,17},{... | collective-permute-start | bytes 196616 | tf_op jit(solution)/shard_map/ppermute | solution.py:45
  56.3 1.5 %collective-permute-done.10 = f32[4,2,16,128]{3,2,0,1:T(8,128)S(1)} collective-permute-done((f32[4,2,16,128]{3,2,0,1:T(8,128)S(1)}, f32[4,2,16,128]{3,2,0,1:T(8,128)S(1)}, u32[]{:S(2)}, u32[]{:S(2)}) %collective-permute-start.10) | collective-permute-done | bytes 65568 | tf_op jit(solution)/shard_map/ppermute | solution.py:45
  58.0 1.7 %slice_subtract_fusion = (f32[2048,128]{1,0:T(8,128)}, f32[2048,128]{1,0:T(8,128)}) fusion(f32[4096,128]{1,0:T(8,128)S(1)} %fusion.24, f32[2048]{0:T(1024)S(1)} %negate_bitcast_fusion, f32[2048]{0:T(1024)S(1)} %subtract_bitcast_fusion), kind=kLoop, calls=%fused_computation.52 | loop fusion | flops 524288 | bytes 4210688 | tf_op jit(solution)/shard_map/sub | solution.py:110
  (76 shorter events, 15.2 us)
Async XLA Ops:
  0.6 12.6 %copy-start = (bf16[128,256]{1,0:T(8,128)(2,1)S(1)}, bf16[128,256]{1,0:T(8,128)(2,1)}, u32[]{:S(2)}) copy-start(bf16[128,256]{1,0:T(8,128)(2,1)} %param.7) | copy-start | bytes 196612
  0.6 10.7 %copy-start.1 = (bf16[512,256]{1,0:T(8,128)(2,1)S(1)}, bf16[512,256]{1,0:T(8,128)(2,1)}, u32[]{:S(2)}) copy-start(bf16[512,256]{1,0:T(8,128)(2,1)} %param.6) | copy-start | bytes 786436
  0.7 10.8 %copy-start.2 = (s32[128]{0:T(128)S(1)}, s32[128]{0:T(128)}, u32[]{:S(2)}) copy-start(s32[128]{0:T(128)} %param.8) | copy-start | bytes 1540
  0.7 9.6 %collective-permute-start = (bf16[1,512,256]{2,1,0:T(8,128)(2,1)}, bf16[1,512,256]{2,1,0:T(8,128)(2,1)S(1)}, u32[]{:S(2)}, u32[]{:S(2)}) collective-permute-start(bf16[1,512,256]{2,1,0:T(8,128)(2,1)} %bitcast.125), channel_id=1, source_target_pairs={{0,2},{1,3},{2,0},{3,1},{4,6},{5,7},{6,4},{7,5},{8,10},{9,11},{10,... | collective-permute-start | bytes 786440 | tf_op jit(solution)/shard_map/ppermute | solution.py:67
  11.2 2.0 %collective-permute-start.1 = (bf16[2,512,256]{2,1,0:T(8,128)(2,1)S(1)}, bf16[2,512,256]{2,1,0:T(8,128)(2,1)S(1)}, u32[]{:S(2)}, u32[]{:S(2)}) collective-permute-start(bf16[2,512,256]{2,1,0:T(8,128)(2,1)S(1)} %pad_maximum_fusion.6), channel_id=1, source_target_pairs={{0,1},{1,0},{2,3},{3,2},{4,5},{5,4},{6,7},{7,6},{8,9},{9,8},{10,11... | collective-permute-start | bytes 1572872 | tf_op jit(solution)/shard_map/ppermute | solution.py:67
  13.8 0.7 %copy-start.3 = (f32[2,1,1]{0,2,1:T(1,128)S(1)}, f32[2,1,1]{0,2,1:T(1,128)}, u32[]{:S(2)}) copy-start(f32[2,1,1]{0,2,1:T(1,128)} %param.11) | copy-start | bytes 28
  14.6 3.8 %collective-permute-start.2 = (f32[1,2,24,128]{3,2,1,0:T(8,128)S(1)}, f32[1,2,24,128]{3,2,1,0:T(8,128)S(1)}, u32[]{:S(2)}, u32[]{:S(2)}) collective-permute-start(f32[1,2,24,128]{3,2,1,0:T(8,128)S(1)} %maximum_bitcast_fusion.1), channel_id=1, source_target_pairs={{0,4},{4,0},{8,12},{12,8},{16,20},{20,16},{24,28},{28,24},{1,5},{5... | collective-permute-start | bytes 73736 | tf_op jit(solution)/shard_map/ppermute | solution.py:45
  18.4 4.1 %collective-permute-start.3 = (f32[2,2,24,128]{3,2,1,0:T(8,128)S(1)}, f32[2,2,24,128]{3,2,1,0:T(8,128)S(1)}, u32[]{:S(2)}, u32[]{:S(2)}) collective-permute-start(f32[2,2,24,128]{3,2,1,0:T(8,128)S(1)} %pad_maximum_fusion.23), channel_id=1, source_target_pairs={{0,8},{4,12},{8,0},{12,4},{16,24},{20,28},{24,16},{28,20},{1,9},{5... | collective-permute-start | bytes 147464 | tf_op jit(solution)/shard_map/ppermute | solution.py:45
  22.5 5.6 %collective-permute-start.4 = (f32[4,2,24,128]{3,2,1,0:T(8,128)S(1)}, f32[4,2,24,128]{3,2,1,0:T(8,128)S(1)}, u32[]{:S(2)}, u32[]{:S(2)}) collective-permute-start(f32[4,2,24,128]{3,2,1,0:T(8,128)S(1)} %pad_maximum_fusion.9), channel_id=1, source_target_pairs={{0,16},{4,20},{8,24},{12,28},{16,0},{20,4},{24,8},{28,12},{1,17},{... | collective-permute-start | bytes 294920 | tf_op jit(solution)/shard_map/ppermute | solution.py:45
  29.9 3.8 %collective-permute-start.5 = (f32[1,2,16,128]{3,2,0,1:T(8,128)S(1)}, f32[1,2,16,128]{3,2,0,1:T(8,128)S(1)}, u32[]{:S(2)}, u32[]{:S(2)}) collective-permute-start(f32[1,2,16,128]{3,2,0,1:T(8,128)S(1)} %bitcast.131), channel_id=1, source_target_pairs={{0,4},{4,0},{8,12},{12,8},{16,20},{20,16},{24,28},{28,24},{1,5},{5... | collective-permute-start | bytes 49160 | tf_op jit(solution)/shard_map/ppermute | solution.py:45
  33.7 3.9 %collective-permute-start.6 = (f32[2,2,16,128]{3,2,0,1:T(8,128)S(1)}, f32[2,2,16,128]{3,2,0,1:T(8,128)S(1)}, u32[]{:S(2)}, u32[]{:S(2)}) collective-permute-start(f32[2,2,16,128]{3,2,0,1:T(8,128)S(1)} %pad_maximum_fusion.24), channel_id=1, source_target_pairs={{0,8},{4,12},{8,0},{12,4},{16,24},{20,28},{24,16},{28,20},{1,9},{5... | collective-permute-start | bytes 98312 | tf_op jit(solution)/shard_map/ppermute | solution.py:45
  37.6 5.5 %collective-permute-start.7 = (f32[4,2,16,128]{3,2,0,1:T(8,128)S(1)}, f32[4,2,16,128]{3,2,0,1:T(8,128)S(1)}, u32[]{:S(2)}, u32[]{:S(2)}) collective-permute-start(f32[4,2,16,128]{3,2,0,1:T(8,128)S(1)} %pad_maximum_fusion.15), channel_id=1, source_target_pairs={{0,16},{4,20},{8,24},{12,28},{16,0},{20,4},{24,8},{28,12},{1,17},{... | collective-permute-start | bytes 196616 | tf_op jit(solution)/shard_map/ppermute | solution.py:45
  44.8 3.8 %collective-permute-start.8 = (f32[1,2,16,128]{3,2,0,1:T(8,128)S(1)}, f32[1,2,16,128]{3,2,0,1:T(8,128)S(1)}, u32[]{:S(2)}, u32[]{:S(2)}) collective-permute-start(f32[1,2,16,128]{3,2,0,1:T(8,128)S(1)} %bitcast.127), channel_id=1, source_target_pairs={{0,4},{4,0},{8,12},{12,8},{16,20},{20,16},{24,28},{28,24},{1,5},{5... | collective-permute-start | bytes 49160 | tf_op jit(solution)/shard_map/ppermute | solution.py:45
  48.6 3.9 %collective-permute-start.9 = (f32[2,2,16,128]{3,2,0,1:T(8,128)S(1)}, f32[2,2,16,128]{3,2,0,1:T(8,128)S(1)}, u32[]{:S(2)}, u32[]{:S(2)}) collective-permute-start(f32[2,2,16,128]{3,2,0,1:T(8,128)S(1)} %pad_maximum_fusion.25), channel_id=1, source_target_pairs={{0,8},{4,12},{8,0},{12,4},{16,24},{20,28},{24,16},{28,20},{1,9},{5... | collective-permute-start | bytes 98312 | tf_op jit(solution)/shard_map/ppermute | solution.py:45
  52.5 5.3 %collective-permute-start.10 = (f32[4,2,16,128]{3,2,0,1:T(8,128)S(1)}, f32[4,2,16,128]{3,2,0,1:T(8,128)S(1)}, u32[]{:S(2)}, u32[]{:S(2)}) collective-permute-start(f32[4,2,16,128]{3,2,0,1:T(8,128)S(1)} %pad_maximum_fusion.16), channel_id=1, source_target_pairs={{0,16},{4,20},{8,24},{12,28},{16,0},{20,4},{24,8},{28,12},{1,17},{... | collective-permute-start | bytes 196616 | tf_op jit(solution)/shard_map/ppermute | solution.py:45

commit v2 on v1

--- a/solution.py
+++ b/solution.py
@@ -38,19 +38,13 @@
     return jnp.dot(both, jnp.concatenate([table, table]), preferred_element_type=jnp.float32)
 
 
-def xor_gather(block, axis, size):
-    held = block[None]
-    step = 1
-    while step < size:
-        other = lax.ppermute(held, axis, [(i, i ^ step) for i in range(size)])
-        held = jnp.concatenate([held, other])
-        step *= 2
-    return held
+def spread_gather(block, axis, size):
+    return lax.all_to_all(jnp.broadcast_to(block[None], (size, *block.shape)), axis, 0, 0, tiled=True)
 
 
 def trunk_table(z_all, index):
     size = z_all.shape[0]
-    section = index ^ jnp.arange(size, dtype=jnp.int32)
+    section = jnp.arange(size, dtype=jnp.int32)
     shared = (section[None, :] <= jnp.minimum(index, section)[:, None]).astype(jnp.float32)
     return jnp.sum(shared[:, :, None] * z_all[None], axis=1)
 
@@ -90,11 +84,11 @@
         inject = jnp.sum(current, axis=1).reshape(2, scen // 128, 128)
         if table is None:
             extra = jnp.broadcast_to(trunk_z.reshape(2, 1, 1), (2, 8, 128))
-            every = xor_gather(jnp.concatenate([inject, extra], axis=1), "feeder", feeders)
+            every = spread_gather(jnp.concatenate([inject, extra], axis=1), "feeder", feeders)
             table = trunk_table(every[:, :, scen // 128, 0], feeder)
             every = every[:, :, : scen // 128]
         else:
-            every = xor_gather(inject, "feeder", feeders)
+            every = spread_gather(inject, "feeder", feeders)
         branch = lateral_products(current, paths)
         branch_real = branch[:scen]
         branch_imag = branch[scen:]

time: 59.9 us -> 57.9 us (0.967)
  starting transfers between devices: 23.1 us -> 15.9 us
  waiting for transfers between devices: 16 us -> 19 us
  local copies, waits for them, and re-layouts: 1.92 us -> 3.95 us
    ppermute x9 -> x0, starting transfers between devices: 20 us -> none  [xor_gather(): other = lax.ppermute(held, axis, [(i, i ^ step) for i in range(size)])]
    all_to_all x0 -> x3, waiting for transfers between devices: none -> 17.2 us  [spread_gather(): lax.all_to_all(jnp.broadcast_to(block[None], (size, *block.shape)), axis,...]
    ppermute x9 -> x0, waiting for transfers between devices: 14.2 us -> none  [xor_gather(): other = lax.ppermute(held, axis, [(i, i ^ step) for i in range(size)])]
    all_to_all x0 -> x3, starting transfers between devices: none -> 12.8 us  [spread_gather(): lax.all_to_all(jnp.broadcast_to(block[None], (size, *block.shape)), axis,...]
    broadcast_in_dim x0 -> x3, local copies, waits for them, and re-layouts: none -> 2.02 us  [spread_gather(): jnp.broadcast_to(block[None], (size, *block.shape))]
  transfers between devices with their start and end apart: 11 -> 5, of which waited for: 11 -> 5; matrix products, arithmetic and copies ran while one was open for 20% -> 21% of each run, Pallas kernels for 0% -> 0%
where the time goes in v2:
time: 57.9 us; the launch traced here: 57.4 us
  waiting for transfers between devices  19 us (33%)
  starting transfers between devices  15.9 us (27%)
  matrix products  9.27 us (16%)
  other arithmetic  8.24 us (14%)
  local copies, waits for them, and re-layouts  3.95 us (7%)
  between operations  1.08 us (2%)
    all_to_all x3, waiting for transfers between devices, spread_gather(): lax.all_to_all(jnp.broadcast_to(block[None], (size, *block.shape)), axis,...  17.2 us
    all_to_all x3, starting transfers between devices, spread_gather(): lax.all_to_all(jnp.broadcast_to(block[None], (size, *block.shape)), axis,...  12.8 us
    dot_general x6, matrix products, lateral_products(): jnp.dot(both, jnp.concatenate([table, table]), preferred_element_type=jnp...  4.16 us
    dot_general x6, matrix products, path_matrix(): paths = paths + jnp.einsum('alm,amn->aln', paths, power)  3.21 us
    ppermute x2, starting transfers between devices, local(): other = lax.ppermute(held, 'node', [(i, i ^ step) for i in range(nodes)])  3.1 us
    broadcast_in_dim x3, local copies, waits for them, and re-layouts, spread_gather(): jnp.broadcast_to(block[None], (size, *block.shape))  2.02 us
    reduce_sum x3, other arithmetic, local(): inject = jnp.sum(current, axis=1).reshape(2, scen // 128, 128)  1.84 us
    ppermute x2, waiting for transfers between devices, local(): other = lax.ppermute(held, 'node', [(i, i ^ step) for i in range(nodes)])  1.79 us
  transfers between devices with their start and end apart: 5, of which 5 were waited for; matrix products, arithmetic and copies ran while one was open for 21% of the time, Pallas kernels for 0%

profile of v2, /device:TPU:0, one launch (start us, length us, event | category | flops | bytes accessed | tf_op | source)
XLA Modules:
  0.0 57.4 jit_solution(13537835352145123958)
XLA Ops:
  0.7 3.0 %collective-permute-start = (bf16[1,512,256]{2,1,0:T(8,128)(2,1)}, bf16[1,512,256]{2,1,0:T(8,128)(2,1)S(1)}, u32[]{:S(2)}, u32[]{:S(2)}) collective-permute-start(bf16[1,512,256]{2,1,0:T(8,128)(2,1)} %bitcast.121), channel_id=1, source_target_pairs={{0,2},{1,3},{2,0},{3,1},{4,6},{5,7},{6,4},{7,5},{8,10},{9,11},{10,... | collective-permute-start | bytes 786440 | tf_op jit(solution)/shard_map/ppermute | solution.py:61
  3.7 0.9 %fusion.47 = bf16[128,128]{1,0:T(8,128)(2,1)S(1)} fusion(s32[128]{0:T(128)} %param.8), kind=kOutput, calls=%fused_computation.100 | convolution fusion | flops 4210688 | bytes 33280 | tf_op jit(solution)/shard_map/alm,amn->aln/dot_general | solution.py:21
  4.6 0.9 %fusion.60 = bf16[128,128]{1,0:T(8,128)(2,1)S(1)} fusion(bf16[128,128]{1,0:T(8,128)(2,1)S(1)} %fusion.47, s32[128]{0:T(128)} %param.8), kind=kOutput, calls=%fused_computation.112 | convolution fusion | flops 4325376 | bytes 66048 | tf_op jit(solution)/shard_map/alm,amn->aln/dot_general | solution.py:22
  5.7 0.8 %slice_bitcast_fusion.13 = (f32[128]{0:T(128)S(1)}, f32[128]{0:T(128)S(1)}) fusion(f32[2,128]{1,0:T(2,128)} %param.9), kind=kLoop, calls=%fused_computation.133 | loop fusion | bytes 2048 | tf_op jit(solution)/shard_map/mul | solution.py:71
  6.6 0.9 %fusion.66 = bf16[128,128]{1,0:T(8,128)(2,1)S(1)} fusion(bf16[128,128]{1,0:T(8,128)(2,1)S(1)} %fusion.80, bf16[128,128]{1,0:T(8,128)(2,1)S(1)} %fusion.60, s32[128]{0:T(128)} %param.8), kind=kOutput, calls=%fused_computation.126 | convolution fusion | flops 4358144 | bytes 98816 | tf_op jit(solution)/shard_map/alm,amn->aln/dot_general | solution.py:22
  7.7 0.9 %fusion.74 = (bf16[128,128]{1,0:T(8,128)(2,1)S(1)}, bf16[128,128]{1,0:T(8,128)(2,1)S(1)}) fusion(bf16[128,128]{1,0:T(8,128)(2,1)S(1)} %fusion.66, bf16[128,128]{1,0:T(8,128)(2,1)S(1)} %fusion.60, s32[128]{0:T(128)} %param.8, bf16[128,128]{1,0:T(8,128)(2,1)S(1)} %fusion.81), kind=kOutput, calls=%fused_computation.141 | convolution fusion | flops 4620288 | bytes 164352 | tf_op jit(solution)/shard_map/alm,amn->aln/dot_general | solution.py:22
  9.0 0.8 %slice_bitcast_fusion.9 = (f32[128]{0:T(128)S(1)}, f32[128]{0:T(128)S(1)}) fusion(f32[2,128]{1,0:T(2,128)} %param.10), kind=kLoop, calls=%fused_computation.129 | loop fusion | bytes 2048 | tf_op jit(solution)/shard_map/mul | solution.py:96
  10.2 1.0 %pad_maximum_fusion.6 = bf16[2,512,256]{2,1,0:T(8,128)(2,1)S(1)} fusion(bf16[1,512,256]{2,1,0:T(8,128)(2,1)S(1)} %collective-permute-done, bf16[1,512,256]{2,1,0:T(8,128)(2,1)} %bitcast.122), kind=kLoop, calls=%fused_computation.71 | loop fusion | flops 262144 | bytes 1048576 | tf_op jit(solution)/shard_map/concatenate | solution.py:62
  11.6 1.6 %collective-permute-done.1 = bf16[2,512,256]{2,1,0:T(8,128)(2,1)S(1)} collective-permute-done((bf16[2,512,256]{2,1,0:T(8,128)(2,1)S(1)}, bf16[2,512,256]{2,1,0:T(8,128)(2,1)S(1)}, u32[]{:S(2)}, u32[]{:S(2)}) %collective-permute-start.1) | collective-permute-done | bytes 524320 | tf_op jit(solution)/shard_map/ppermute | solution.py:61
  14.6 0.7 %broadcast_in_dim.22 = f32[8,2,24,128]{3,2,1,0:T(8,128)} broadcast(f32[2,24,128]{2,1,0:T(8,128)S(1)} %pad_maximum_fusion.15), dimensions={1,2,3} | broadcast | bytes 221184 | tf_op jit(solution)/shard_map/broadcast_in_dim | solution.py:42
  15.3 6.0 %all-to-all-start = ((f32[8,2,24,128]{3,2,1,0:T(8,128)}), f32[8,2,24,128]{3,2,1,0:T(8,128)S(1)}, u32[]{:S(2)}, u32[]{:S(2)}) async-start(f32[8,2,24,128]{3,2,1,0:T(8,128)} %broadcast_in_dim.22), calls=%async_computation | async-start | bytes 393216 | tf_op jit(solution)/shard_map/all_to_all | solution.py:42
  22.4 0.7 %fusion.8 = f32[4096,128]{1,0:T(8,128)S(1)} fusion(bf16[4096,128]{1,0:T(8,128)(2,1)S(1)} %subtract_convert_fusion.4, bf16[4096,128]{1,0:T(8,128)(2,1)S(1)} %fusion.30, bf16[128,128]{0,1:T(8,128)(2,1)S(1)} %fusion.57), kind=kOutput, calls=%fused_computation.11 | convolution fusion | flops 272760832 | bytes 4227072 | tf_op jit(solution)/shard_map/dot_general | solution.py:38
  23.1 6.4 %all-to-all-done = f32[8,2,24,128]{3,2,1,0:T(8,128)S(1)} async-done(((f32[8,2,24,128]{3,2,1,0:T(8,128)}), f32[8,2,24,128]{3,2,1,0:T(8,128)S(1)}, u32[]{:S(2)}, u32[]{:S(2)}) %all-to-all-start) | async-done | bytes 196640 | tf_op jit(solution)/shard_map/all_to_all | solution.py:42
  29.8 0.8 %fusion.41 = (f32[2048,128]{1,0:T(8,128)S(1)}, f32[2048,128]{1,0:T(8,128)S(1)}) fusion(f32[4096,128]{1,0:T(8,128)S(1)} %fusion.8, f32[2048,128]{1,0:T(8,128)S(1)} %get-tuple-element.34, f32[2048]{0:T(1024)S(1)} %get-tuple-element.43, f32[2048]{0:T(1024)S(1)} %get-tuple-element.44, f32[128]{0:T(128)S(1)} %get-tuple-element.33, f32[128]{0:T(128)S(1)} %get-tuple-element.32), kind=kLoop, calls=%fused_computation.67 | loop fusion | flops 3932160 | bytes 5260288 | tf_op jit(solution)/shard_map/div | solution.py:29
  32.0 3.4 %all-to-all-start.1 = ((f32[8,2,16,128]{3,2,1,0:T(8,128)}), f32[8,2,16,128]{3,2,1,0:T(8,128)S(1)}, u32[]{:S(2)}, u32[]{:S(2)}) async-start(f32[8,2,16,128]{3,2,1,0:T(8,128)} %broadcast_in_dim.24), calls=%async_computation.1 | async-start | bytes 262144 | tf_op jit(solution)/shard_map/all_to_all | solution.py:42
  35.4 0.7 %fusion.12 = f32[4096,128]{1,0:T(8,128)S(1)} fusion(bf16[4096,128]{1,0:T(8,128)(2,1)S(1)} %get-tuple-element.23, bf16[4096,128]{1,0:T(8,128)(2,1)S(1)} %fusion.33, bf16[128,128]{1,0:T(8,128)(2,1)S(1)} %get-tuple-element.41), kind=kOutput, calls=%fused_computation.16 | convolution fusion | flops 272760832 | bytes 4227072 | tf_op jit(solution)/shard_map/dot_general | solution.py:38
  36.6 0.7 %fusion.16 = f32[4096,128]{1,0:T(8,128)S(1)} fusion(bf16[4096,128]{1,0:T(8,128)(2,1)S(1)} %subtract_convert_fusion.2, bf16[4096,128]{1,0:T(8,128)(2,1)S(1)} %fusion.29, bf16[128,128]{0,1:T(8,128)(2,1)S(1)} %fusion.57), kind=kOutput, calls=%fused_computation.21 | convolution fusion | flops 272760832 | bytes 4227072 | tf_op jit(solution)/shard_map/dot_general | solution.py:38
  37.3 5.4 %all-to-all-done.1 = f32[8,2,16,128]{3,2,1,0:T(8,128)S(1)} async-done(((f32[8,2,16,128]{3,2,1,0:T(8,128)}), f32[8,2,16,128]{3,2,1,0:T(8,128)S(1)}, u32[]{:S(2)}, u32[]{:S(2)}) %all-to-all-start.1) | async-done | bytes 131104 | tf_op jit(solution)/shard_map/all_to_all | solution.py:42
  42.8 0.8 %fusion.40 = (f32[2048,128]{1,0:T(8,128)S(1)}, f32[2048,128]{1,0:T(8,128)S(1)}) fusion(f32[4096,128]{1,0:T(8,128)S(1)} %fusion.16, f32[2048,128]{1,0:T(8,128)S(1)} %get-tuple-element.34, f32[2048]{0:T(1024)S(1)} %negate_bitcast_fusion.1, f32[2048]{0:T(1024)S(1)} %subtract_bitcast_fusion.1, f32[128]{0:T(128)S(1)} %get-tuple-element.33, ...), kind=kLoop, calls=%fused_computation.62 | loop fusion | flops 3932160 | bytes 5260288 | tf_op jit(solution)/shard_map/div | solution.py:29
  45.0 3.4 %all-to-all-start.2 = ((f32[8,2,16,128]{3,2,1,0:T(8,128)}), f32[8,2,16,128]{3,2,1,0:T(8,128)S(1)}, u32[]{:S(2)}, u32[]{:S(2)}) async-start(f32[8,2,16,128]{3,2,1,0:T(8,128)} %broadcast_in_dim.52), calls=%async_computation.2 | async-start | bytes 262144 | tf_op jit(solution)/shard_map/all_to_all | solution.py:42
  48.3 0.7 %fusion.20 = f32[4096,128]{1,0:T(8,128)S(1)} fusion(bf16[4096,128]{1,0:T(8,128)(2,1)S(1)} %get-tuple-element.21, bf16[4096,128]{1,0:T(8,128)(2,1)S(1)} %fusion.31, bf16[128,128]{1,0:T(8,128)(2,1)S(1)} %get-tuple-element.41), kind=kOutput, calls=%fused_computation.26 | convolution fusion | flops 272760832 | bytes 4227072 | tf_op jit(solution)/shard_map/dot_general | solution.py:38
  49.5 0.7 %fusion.24 = f32[4096,128]{1,0:T(8,128)S(1)} fusion(bf16[4096,128]{1,0:T(8,128)(2,1)S(1)} %subtract_convert_fusion, bf16[4096,128]{1,0:T(8,128)(2,1)S(1)} %fusion.28, bf16[128,128]{0,1:T(8,128)(2,1)S(1)} %fusion.57), kind=kOutput, calls=%fused_computation.31 | convolution fusion | flops 272760832 | bytes 4227072 | tf_op jit(solution)/shard_map/dot_general | solution.py:38
  50.2 5.4 %all-to-all-done.2 = f32[8,2,16,128]{3,2,1,0:T(8,128)S(1)} async-done(((f32[8,2,16,128]{3,2,1,0:T(8,128)}), f32[8,2,16,128]{3,2,1,0:T(8,128)S(1)}, u32[]{:S(2)}, u32[]{:S(2)}) %all-to-all-start.2) | async-done | bytes 131104 | tf_op jit(solution)/shard_map/all_to_all | solution.py:42
  55.7 1.7 %slice_subtract_fusion = (f32[2048,128]{1,0:T(8,128)}, f32[2048,128]{1,0:T(8,128)}) fusion(f32[4096,128]{1,0:T(8,128)S(1)} %fusion.24, f32[2048]{0:T(1024)S(1)} %negate_bitcast_fusion, f32[2048]{0:T(1024)S(1)} %subtract_bitcast_fusion), kind=kLoop, calls=%fused_computation.52 | loop fusion | flops 524288 | bytes 4210688 | tf_op jit(solution)/shard_map/sub | solution.py:104
  (58 shorter events, 8.2 us)
Async XLA Ops:
  0.6 12.6 %copy-start = (bf16[128,256]{1,0:T(8,128)(2,1)S(1)}, bf16[128,256]{1,0:T(8,128)(2,1)}, u32[]{:S(2)}) copy-start(bf16[128,256]{1,0:T(8,128)(2,1)} %param.7) | copy-start | bytes 196612
  0.6 10.7 %copy-start.1 = (bf16[512,256]{1,0:T(8,128)(2,1)S(1)}, bf16[512,256]{1,0:T(8,128)(2,1)}, u32[]{:S(2)}) copy-start(bf16[512,256]{1,0:T(8,128)(2,1)} %param.6) | copy-start | bytes 786436
  0.7 10.8 %copy-start.2 = (s32[128]{0:T(128)S(1)}, s32[128]{0:T(128)}, u32[]{:S(2)}) copy-start(s32[128]{0:T(128)} %param.8) | copy-start | bytes 1540
  0.7 9.6 %collective-permute-start = (bf16[1,512,256]{2,1,0:T(8,128)(2,1)}, bf16[1,512,256]{2,1,0:T(8,128)(2,1)S(1)}, u32[]{:S(2)}, u32[]{:S(2)}) collective-permute-start(bf16[1,512,256]{2,1,0:T(8,128)(2,1)} %bitcast.121), channel_id=1, source_target_pairs={{0,2},{1,3},{2,0},{3,1},{4,6},{5,7},{6,4},{7,5},{8,10},{9,11},{10,... | collective-permute-start | bytes 786440 | tf_op jit(solution)/shard_map/ppermute | solution.py:61
  11.2 2.0 %collective-permute-start.1 = (bf16[2,512,256]{2,1,0:T(8,128)(2,1)S(1)}, bf16[2,512,256]{2,1,0:T(8,128)(2,1)S(1)}, u32[]{:S(2)}, u32[]{:S(2)}) collective-permute-start(bf16[2,512,256]{2,1,0:T(8,128)(2,1)S(1)} %pad_maximum_fusion.6), channel_id=1, source_target_pairs={{0,1},{1,0},{2,3},{3,2},{4,5},{5,4},{6,7},{7,6},{8,9},{9,8},{10,11... | collective-permute-start | bytes 1572872 | tf_op jit(solution)/shard_map/ppermute | solution.py:61
  13.8 0.7 %copy-start.3 = (f32[2,1,1]{0,2,1:T(1,128)S(1)}, f32[2,1,1]{0,2,1:T(1,128)}, u32[]{:S(2)}) copy-start(f32[2,1,1]{0,2,1:T(1,128)} %param.11) | copy-start | bytes 28
  15.3 14.3 %all-to-all-start = ((f32[8,2,24,128]{3,2,1,0:T(8,128)}), f32[8,2,24,128]{3,2,1,0:T(8,128)S(1)}, u32[]{:S(2)}, u32[]{:S(2)}) async-start(f32[8,2,24,128]{3,2,1,0:T(8,128)} %broadcast_in_dim.22), calls=%async_computation | async-start | bytes 393216 | tf_op jit(solution)/shard_map/all_to_all | solution.py:42
  32.0 10.7 %all-to-all-start.1 = ((f32[8,2,16,128]{3,2,1,0:T(8,128)}), f32[8,2,16,128]{3,2,1,0:T(8,128)S(1)}, u32[]{:S(2)}, u32[]{:S(2)}) async-start(f32[8,2,16,128]{3,2,1,0:T(8,128)} %broadcast_in_dim.24), calls=%async_computation.1 | async-start | bytes 262144 | tf_op jit(solution)/shard_map/all_to_all | solution.py:42
  45.0 10.7 %all-to-all-start.2 = ((f32[8,2,16,128]{3,2,1,0:T(8,128)}), f32[8,2,16,128]{3,2,1,0:T(8,128)S(1)}, u32[]{:S(2)}, u32[]{:S(2)}) async-start(f32[8,2,16,128]{3,2,1,0:T(8,128)} %broadcast_in_dim.52), calls=%async_computation.2 | async-start | bytes 262144 | tf_op jit(solution)/shard_map/all_to_all | solution.py:42

commit v3 on v0

v3 whole, which is shorter than its diff:
```python
import functools

import jax
import jax.numpy as jnp
from jax import lax
from jax.experimental import pallas as pl
from jax.experimental.pallas import tpu as pltpu
from jax.sharding import PartitionSpec as P

SWEEPS = 3
EXTRA = 16
LANES = 128

VMEM = pl.BlockSpec(memory_space=pltpu.VMEM)
SMEM = pl.BlockSpec(memory_space=pltpu.SMEM)


def split(x):
    high = x.astype(jnp.bfloat16)
    low = (x - high.astype(jnp.float32)).astype(jnp.bfloat16)
    return high, low


def product(left, right):
    return jnp.dot(left, right, preferred_element_type=jnp.float32)


def product_nt(left, right):
    return lax.dot_general(left, right, (((1,), (1,)), ((), ())), preferred_element_type=jnp.float32)


def wide(row, width):
    n = row.shape[1]
    if width <= n:
        return row[:, :width]
    return jnp.concatenate([row] * (width // n), axis=1)


def pack_kernel(feeders, trunk_ref, loadings_ref, parents_ref, base_ref, z_ref, out_ref, rows_ref, meta_ref):
    n = loadings_ref.shape[0]
    rows_ref[0:2, :] = base_ref[...]
    rows_ref[2:4, :] = z_ref[...]
    rows_ref[4:5, :] = jnp.full((1, n), trunk_ref[0], jnp.float32)
    rows_ref[5:6, :] = jnp.full((1, n), trunk_ref[1], jnp.float32)
    rows_ref[6:7, :] = parents_ref[...].astype(jnp.float32)
    rows_ref[7:8, :] = jnp.zeros((1, n), jnp.float32)
    rows = rows_ref[...]
    high = rows.astype(jnp.bfloat16).astype(jnp.float32)
    middle = (rows - high).astype(jnp.bfloat16).astype(jnp.float32)
    low = rows - high - middle
    meta_ref[0:8, 0:n] = high
    meta_ref[0:8, n : 2 * n] = middle
    meta_ref[8:16, 0:n] = low
    meta_ref[8:16, n : 2 * n] = jnp.zeros_like(low)
    meta = meta_ref[...].astype(jnp.bfloat16)
    loadings = loadings_ref[...]
    for to in range(feeders):
        out_ref[to, 0:n, :] = loadings
        out_ref[to, n : n + EXTRA, :] = meta


def section_matrix(parts, n):
    high, middle, low = parts[0:8, 0:n], parts[0:8, n : 2 * n], parts[8:16, 0:n]
    rows = high + middle + low
    row_ids = lax.broadcasted_iota(jnp.int32, (n, n), 0)
    lane_ids = lax.broadcasted_iota(jnp.int32, (n, n), 1)
    children = (jnp.broadcast_to(rows[6:7], (n, n)) == row_ids.astype(jnp.float32)).astype(jnp.bfloat16)
    identity = (row_ids == lane_ids).astype(jnp.bfloat16)
    power = product_nt(identity, children).astype(jnp.bfloat16)
    paths = identity + power
    reach = 2
    power = product(power, power).astype(jnp.bfloat16)
    while reach < n:
        if 2 * reach < n:
            both = product(power, jnp.concatenate([power, paths], axis=1))
            paths = paths + both[:, n:].astype(jnp.bfloat16)
            power = both[:, :n].astype(jnp.bfloat16)
        else:
            paths = paths + product(power, paths).astype(jnp.bfloat16)
        reach *= 2
    paths32 = paths.astype(jnp.float32)

    def scaled(index):
        return jnp.concatenate([paths32 * high[index : index + 1], paths32 * middle[index : index + 1]], axis=1)

    left = jnp.concatenate([scaled(2), scaled(3)], axis=0).astype(jnp.bfloat16)
    shared = product_nt(left, jnp.concatenate([paths, paths], axis=1))
    resist, react = shared[:n], shared[n:]
    base_active, base_reactive = rows[0:1], rows[1:2]
    real = resist * base_active + react * base_reactive
    imag = react * base_active - resist * base_reactive
    real_high, real_low = split(real)
    imag_high, imag_low = split(imag)
    pad_ids = lax.broadcasted_iota(jnp.int32, (EXTRA, 2 * n), 0)
    row_real = jnp.concatenate([base_active, base_reactive], axis=1)
    row_imag = jnp.concatenate([-base_reactive, base_active], axis=1)
    sums = jnp.where(pad_ids == 0, row_real, jnp.where(pad_ids == 1, row_imag, 0.0))
    sums_high, sums_low = split(sums)

    def whole(real_part, imag_part, sums_part):
        top = jnp.concatenate([real_part, -imag_part], axis=1)
        bottom = jnp.concatenate([imag_part, real_part], axis=1)
        return jnp.concatenate([top, bottom, sums_part], axis=0)

    return jnp.concatenate(
        [whole(real_high, imag_high, sums_high), whole(real_low, imag_low, sums_low)], axis=0
    )


def swing_of(loadings, factors):
    level = product_nt(loadings, factors).astype(jnp.bfloat16).astype(jnp.float32)
    return 1.0 + 0.5 * jnp.tanh(level)


def apply(matrix, high, low):
    half = matrix.shape[0] // 2
    first = product(matrix, high)
    return first[:half] + first[half:] + product(matrix[:half], low)


def scaled_volts(swing, real, imag):
    inverse = swing / (real * real + imag * imag)
    return jnp.concatenate([real * inverse, imag * inverse], axis=0)


def heads_kernel(
    feeders, pieces, place_ref, every_ref, *refs
):
    piece_refs, (head_ref, own_ref, factors_ref, matrix_ref, swing_ref, drop_ref, inject_ref) = refs[:pieces], refs[pieces:]
    rows = piece_refs[0].shape[0]
    width = factors_ref.shape[0]
    n = swing_ref.shape[1]
    span = 2 * n
    piece, offset = place_ref[0], place_ref[1]
    for index, piece_ref in enumerate(piece_refs):
        @pl.when(piece == index)
        def _(piece_ref=piece_ref):
            factors_ref[...] = piece_ref[pl.ds(pl.multiple_of(offset, width), width), :]
    group = min(feeders, 8)

    def sections(body):
        if group == feeders:
            for g in range(feeders):
                body(g)
        else:
            @pl.loop(0, feeders // group)
            def _(outer):
                for inner in range(group):
                    body(outer * group + inner)

    def first(g):
        matrix_ref[g] = section_matrix(every_ref[g, n : n + EXTRA, :].astype(jnp.float32), n)
        swing = swing_of(every_ref[g, 0:n, :], factors_ref[...])
        swing_ref[g] = swing
        high, low = split(swing)
        out = apply(matrix_ref[g][:, :n], high, low)
        drop_ref[g] = out[:span]
        inject_ref[g] = out[span:]

    sections(first)

    def trunk_row(g, index):
        parts = every_ref[g, n : n + EXTRA, :].astype(jnp.float32)
        row = parts[index : index + 1, 0:n] + parts[index : index + 1, n : 2 * n] + parts[index + 8 : index + 9, 0:n]
        return wide(row, width)

    trunk = [(trunk_row(g, 4), trunk_row(g, 5)) for g in range(feeders)]

    def heads(sweep):
        flows = [None] * feeders
        real = jnp.zeros((1, width), jnp.float32)
        imag = real
        for g in reversed(range(feeders)):
            real = real + inject_ref[g, 0:1, :]
            imag = imag + inject_ref[g, 1:2, :]
            flows[g] = (real, imag)
        head_real = jnp.ones((1, width), jnp.float32)
        head_imag = jnp.zeros((1, width), jnp.float32)
        for g in range(feeders):
            r, x = trunk[g]
            real, imag = flows[g]
            head_real = head_real - (r * real - x * imag)
            head_imag = head_imag - (r * imag + x * real)
            head_ref[g, 2 * sweep : 2 * sweep + 1, :] = head_real
            head_ref[g, 2 * sweep + 1 : 2 * sweep + 2, :] = head_imag

    heads(0)
    for sweep in range(1, SWEEPS):
        last = sweep == SWEEPS - 1

        def again(g, sweep=sweep, last=last):
            real = head_ref[g, 2 * sweep - 2 : 2 * sweep - 1, :] - drop_ref[g, 0:n, :]
            imag = head_ref[g, 2 * sweep - 1 : 2 * sweep, :] - drop_ref[g, n:span, :]
            high, low = split(scaled_volts(swing_ref[g], real, imag))
            if last:
                half = span + EXTRA
                row_high = matrix_ref[g, span:half, :]
                row_low = matrix_ref[g, half + span :, :]
                inject_ref[g] = product(row_high, high) + product(row_low, high) + product(row_high, low)
            else:
                out = apply(matrix_ref[g], high, low)
                drop_ref[g] = out[:span]
                inject_ref[g] = out[span:]

        sections(again)
        heads(sweep)
    for g in range(feeders):
        head_ref[g, 2 * SWEEPS :, :] = jnp.zeros((head_ref.shape[1] - 2 * SWEEPS, width), jnp.float32)
    own_ref[...] = matrix_ref[place_ref[2]]


def first_kernel(pieces, node_ref, matrix_ref, loadings_ref, *refs):
    piece_refs, (swing_ref, drop_ref) = refs[:pieces], refs[pieces:]
    n = loadings_ref.shape[0]
    width = swing_ref.shape[2]
    chunks = piece_refs[0].shape[0] // width
    loadings = loadings_ref[...]
    half = matrix_ref.shape[0] // 2
    matrix = jnp.concatenate([matrix_ref[0 : 2 * n, 0:n], matrix_ref[half : half + 2 * n, 0:n]], axis=0)
    for index, piece_ref in enumerate(piece_refs):
        for part in range(chunks):
            chunk = jnp.bitwise_xor(node_ref[0], index) * chunks + part
            swing = swing_of(loadings, piece_ref[part * width : (part + 1) * width, :])
            swing_ref[chunk] = swing
            high, low = split(swing)
            drop_ref[chunk] = apply(matrix, high, low)


def volts_kernel(matrix_ref, swing_ref, drop_ref, head_ref, real_ref, imag_ref):
    n = swing_ref.shape[1]
    width = swing_ref.shape[2]
    half = matrix_ref.shape[0] // 2
    matrix = jnp.concatenate([matrix_ref[0 : 2 * n, :], matrix_ref[half : half + 2 * n, :]], axis=0)
    for chunk in range(swing_ref.shape[0]):
        drop = drop_ref[chunk]
        for sweep in range(SWEEPS):
            real = head_ref[chunk, 2 * sweep : 2 * sweep + 1, :] - drop[:n]
            imag = head_ref[chunk, 2 * sweep + 1 : 2 * sweep + 2, :] - drop[n:]
            if sweep < SWEEPS - 1:
                high, low = split(scaled_volts(swing_ref[chunk], real, imag))
                drop = apply(matrix, high, low)
        real_ref[chunk * width : (chunk + 1) * width, :] = real.T
        imag_ref[chunk * width : (chunk + 1) * width, :] = imag.T


def limit(nbytes):
    return pltpu.CompilerParams(vmem_limit_bytes=min(60 << 20, int(nbytes) + (16 << 20)))


def local(feeders, nodes, factors, loadings, parents, load_base, lateral_z, trunk_z):
    node = lax.axis_index("node").astype(jnp.int32)
    feeder = lax.axis_index("feeder").astype(jnp.int32)
    rows, rank = factors.shape
    scen = rows * nodes
    n = loadings.shape[0]
    width = max(scen // feeders, LANES)
    share = feeders * width // scen
    f32, bf16 = jnp.float32, jnp.bfloat16
    matrix_rows = 2 * (2 * n + EXTRA)

    packed = pl.pallas_call(
        functools.partial(pack_kernel, feeders),
        out_shape=jax.ShapeDtypeStruct((feeders, n + EXTRA, rank), bf16),
        in_specs=[SMEM, VMEM, VMEM, VMEM, VMEM],
        out_specs=VMEM,
        scratch_shapes=[pltpu.VMEM((8, n), f32), pltpu.VMEM((EXTRA, rank), f32)],
        compiler_params=limit(feeders * (n + EXTRA) * rank * 2),
        name="pack",
    )(trunk_z.reshape(2), loadings, parents.reshape(1, n), load_base, lateral_z)
    every = lax.all_to_all(packed, "feeder", 0, 0, tiled=True)

    held = {0: factors}
    step = nodes // 2
    while step >= 1:
        pairs = [(i, i ^ step) for i in range(nodes)]
        for offset in list(held):
            held[offset ^ step] = lax.ppermute(held[offset], "node", pairs)
        step //= 2
    pieces = [held[offset] for offset in range(nodes)]

    start = (feeder // share) * width
    place = jnp.stack([(start // rows) ^ node, start % rows, feeder])
    heads, matrix = pl.pallas_call(
        functools.partial(heads_kernel, feeders, nodes),
        out_shape=(
            jax.ShapeDtypeStruct((feeders, 8, width), f32),
            jax.ShapeDtypeStruct((matrix_rows, 2 * n), bf16),
        ),
        in_specs=[SMEM] + [VMEM] * (1 + nodes),
        out_specs=(VMEM, VMEM),
        scratch_shapes=[
            pltpu.VMEM((width, rank), bf16),
            pltpu.VMEM((feeders, matrix_rows, 2 * n), bf16),
            pltpu.VMEM((feeders, n, width), f32),
            pltpu.VMEM((feeders, 2 * n, width), f32),
            pltpu.VMEM((feeders, EXTRA, width), f32),
        ],
        compiler_params=limit(feeders * (matrix_rows * 4 * n + 3 * n * width * 4 + EXTRA * width * 4 + (n + EXTRA) * rank * 2)),
        name="heads",
    )(place, every, *pieces)
    given = lax.all_to_all(heads, "feeder", 0, 0, tiled=True)
    given = given[::share]

    chunks = scen // width
    swing, drop = pl.pallas_call(
        functools.partial(first_kernel, nodes),
        out_shape=(
            jax.ShapeDtypeStruct((chunks, n, width), f32),
            jax.ShapeDtypeStruct((chunks, 2 * n, width), f32),
        ),
        in_specs=[SMEM] + [VMEM] * (2 + nodes),
        out_specs=(VMEM, VMEM),
        compiler_params=limit(3 * n * scen * 4 + scen * rank * 2),
        cost_estimate=pl.CostEstimate(flops=2 * scen * n * rank * 4, bytes_accessed=3 * n * scen * 4, transcendentals=scen * n),
        name="first",
    )(node.reshape(1), matrix, loadings, *pieces)
    return pl.pallas_call(
        volts_kernel,
        out_shape=(
            jax.ShapeDtypeStruct((scen, n), f32),
            jax.ShapeDtypeStruct((scen, n), f32),
        ),
        in_specs=[VMEM] * 4,
        out_specs=(VMEM, VMEM),
        compiler_params=limit(5 * n * scen * 4),
        name="volts",
    )(matrix, swing, drop, given)


def solution(mesh):
    feeders = mesh.shape["feeder"]
    nodes = mesh.shape["node"]
    return jax.shard_map(
        functools.partial(local, feeders, nodes),
        mesh=mesh,
        in_specs=(
            P("node", None),
            P(("feeder", "node"), None),
            P(("feeder", "node")),
            P(None, ("feeder", "node")),
            P(None, ("feeder", "node")),
            P(None, "feeder", "node"),
        ),
        out_specs=(P(None, ("feeder", "node")), P(None, ("feeder", "node"))),
        check_vma=False,
    )
```

time: 184 us -> 57.2 us (0.31)
  blocking collectives: 115 us -> 0 us
  Pallas kernels: 0 us -> 19.6 us
  local copies, waits for them, and re-layouts: 25.6 us -> 8.26 us
  matrix products: 16.8 us -> 0 us
  waiting for transfers between devices: 0.7 us -> 15.6 us
  between operations: 15.2 us -> 0.7 us
  starting transfers between devices: 0.04 us -> 12.4 us
  other arithmetic: 10.9 us -> 0.08 us
    all_gather x3 -> x0, blocking collectives: 91.7 us -> none  [trunk_heads(): lax.all_gather(inject[None], 'feeder', axis=0, tiled=True)]
    unnamed x1 -> x0, blocking collectives: 23.1 us -> none
    pallas_call x0 -> x4, Pallas kernels: none -> 19.6 us  [the longest x1 12.9 us: local(): pl.pallas_call(functools.partial(heads_kernel, feeders, nodes), out_shape...]
    rev x3 -> x0, local copies, waits for them, and re-layouts: 19.6 us -> none  [trunk_heads(): trunk = jnp.flip(jnp.cumsum(jnp.flip(every, 0), 0), 0)]
    dot_general x19 -> x0, matrix products: 16.8 us -> none  [the longest x6 11.2 us: lateral_products(): jnp.dot(stacked, tables[0], precision=HIGHEST, preferred_element_type=jnp...]
    all_to_all x0 -> x2, starting transfers between devices: none -> 10.9 us  [the longest x1 7.25 us: local(): every = lax.all_to_all(packed, 'feeder', 0, 0, tiled=True)]
    ppermute x0 -> x3, waiting for transfers between devices: none -> 7.91 us  [local(): held[offset ^ step] = lax.ppermute(held[offset], 'node', pairs)]
    all_to_all x0 -> x2, waiting for transfers between devices: none -> 7.72 us  [the longest x1 6.37 us: local(): every = lax.all_to_all(packed, 'feeder', 0, 0, tiled=True)]
  transfers between devices with their start and end apart: 1 -> 5, of which waited for: 0 -> 4; matrix products, arithmetic and copies ran while one was open for 5% -> 0% of each run, Pallas kernels for 0% -> 3%
where the time goes in v3:
time: 57.2 us; the launch traced here: 56.7 us
  Pallas kernels  19.6 us (34%)
  waiting for transfers between devices  15.6 us (27%)
  starting transfers between devices  12.4 us (22%)
  local copies, waits for them, and re-layouts  8.26 us (14%)
  between operations  0.7 us (1%)
    pallas_call x1, Pallas kernels, local(): pl.pallas_call(functools.partial(heads_kernel, feeders, nodes), out_shape...  12.9 us
    unnamed x28, local copies, waits for them, and re-layouts  8.26 us
    ppermute x3, waiting for transfers between devices, local(): held[offset ^ step] = lax.ppermute(held[offset], 'node', pairs)  7.91 us
    all_to_all x1, starting transfers between devices, local(): every = lax.all_to_all(packed, 'feeder', 0, 0, tiled=True)  7.25 us
    all_to_all x1, waiting for transfers between devices, local(): every = lax.all_to_all(packed, 'feeder', 0, 0, tiled=True)  6.37 us
    all_to_all x1, starting transfers between devices, local(): given = lax.all_to_all(heads, 'feeder', 0, 0, tiled=True)  3.63 us
    pallas_call x1, Pallas kernels, local(): pl.pallas_call(volts_kernel, out_shape=(jax.ShapeDtypeStruct((scen, n), f...  3.56 us
    pallas_call x1, Pallas kernels, local(): pl.pallas_call(functools.partial(first_kernel, nodes), out_shape=(jax.Sha...  1.72 us
  transfers between devices with their start and end apart: 5, of which 4 were waited for; matrix products, arithmetic and copies ran while one was open for 0% of the time, Pallas kernels for 3%

profile of v3, /device:TPU:0, one launch (start us, length us, event | category | flops | bytes accessed | tf_op | source)
XLA Modules:
  0.0 56.7 jit_solution(1222336173553710542)
XLA Ops:
  0.6 0.8 %copy-done.8 = bf16[128,256]{1,0:T(8,128)(2,1)S(1)} copy-done((bf16[128,256]{1,0:T(8,128)(2,1)S(1)}, bf16[128,256]{1,0:T(8,128)(2,1)}, u32[]{:S(2)}) %copy-start.8) | copy-done | bytes 65560
  1.5 0.7 %copy-done.10 = f32[2,128]{1,0:T(2,128)S(1)} copy-done((f32[2,128]{1,0:T(2,128)S(1)}, f32[2,128]{1,0:T(2,128)}, u32[]{:S(2)}) %copy-start.10) | copy-done | bytes 1048
  2.2 0.7 %copy-done.11 = f32[2,128]{1,0:T(2,128)S(1)} copy-done((f32[2,128]{1,0:T(2,128)S(1)}, f32[2,128]{1,0:T(2,128)}, u32[]{:S(2)}) %copy-start.11) | copy-done | bytes 1048
  2.8 0.7 %copy-done.12 = f32[2,1,1]{0,2,1:T(1,128)S(1)} copy-done((f32[2,1,1]{0,2,1:T(1,128)S(1)}, f32[2,1,1]{0,2,1:T(1,128)}, u32[]{:S(2)}) %copy-start.12) | copy-done | bytes 32
  3.5 0.7 %copy-done.13 = s32[128]{0:T(128)S(1)} copy-done((s32[128]{0:T(128)S(1)}, s32[128]{0:T(128)}, u32[]{:S(2)}) %copy-start.13) | copy-done | bytes 536
  4.1 1.4 %pack.1 = bf16[8,144,256]{2,1,0:T(8,128)(2,1)} custom-call(f32[2]{0:T(128)S(1)} %bitcast.6, bf16[128,256]{1,0:T(8,128)(2,1)S(1)} %copy-done.8, s32[1,128]{1,0:T(1,128)S(1)} %bitcast.7, f32[2,128]{1,0:T(2,128)S(1)} %copy-done.10, f32[2,128]{1,0:T(2,128)S(1)} %copy-done.11), custom_call_target="tpu_custom_call" | custom-call | tf_op jit(solution)/shard_map/pack/pallas_call | solution.py:261
  5.6 7.3 %all-to-all-start = ((bf16[8,144,256]{2,1,0:T(8,128)(2,1)}), bf16[8,144,256]{2,1,0:T(8,128)(2,1)S(1)}, u32[]{:S(2)}, u32[]{:S(2)}) async-start(bf16[8,144,256]{2,1,0:T(8,128)(2,1)} %pack.1), calls=%async_computation | async-start | bytes 1179648 | tf_op jit(solution)/shard_map/all_to_all | solution.py:270
  12.8 1.5 %collective-permute-start.1 = (bf16[512,256]{1,0:T(8,128)(2,1)}, bf16[512,256]{1,0:T(8,128)(2,1)S(1)}, u32[]{:S(2)}, u32[]{:S(2)}) collective-permute-start(bf16[512,256]{1,0:T(8,128)(2,1)} %refs_0_.3), channel_id=1, source_target_pairs={{0,2},{1,3},{2,0},{3,1},{4,6},{5,7},{6,4},{7,5},{8,10},{9,11},{10,... | collective-permute-start | bytes 786440 | tf_op jit(solution)/shard_map/ppermute | solution.py:277
  14.3 6.5 %collective-permute-done.1.refs_2_ = bf16[512,256]{1,0:T(8,128)(2,1)S(1)} collective-permute-done((bf16[512,256]{1,0:T(8,128)(2,1)}, bf16[512,256]{1,0:T(8,128)(2,1)S(1)}, u32[]{:S(2)}, u32[]{:S(2)}) %collective-permute-start.1) | collective-permute-done | bytes 262176 | tf_op jit(solution)/shard_map/ppermute | solution.py:277
  20.8 0.0 collective-permute-start.2
  20.8 0.1 pad_add_fusion.place_ref
  20.9 1.5 %collective-permute-done.2.refs_3_ = bf16[512,256]{1,0:T(8,128)(2,1)S(1)} collective-permute-done((bf16[512,256]{1,0:T(8,128)(2,1)S(1)}, bf16[512,256]{1,0:T(8,128)(2,1)S(1)}, u32[]{:S(2)}, u32[]{:S(2)}) %collective-permute-start.2) | collective-permute-done | bytes 262176 | tf_op jit(solution)/shard_map/ppermute | solution.py:277
  22.3 6.4 %all-to-all-done.every_ref = bf16[8,144,256]{2,1,0:T(8,128)(2,1)S(1)} async-done(((bf16[8,144,256]{2,1,0:T(8,128)(2,1)}), bf16[8,144,256]{2,1,0:T(8,128)(2,1)S(1)}, u32[]{:S(2)}, u32[]{:S(2)}) %all-to-all-start) | async-done | bytes 589856 | tf_op jit(solution)/shard_map/all_to_all | solution.py:270
  28.7 0.9 %copy-done = bf16[512,256]{1,0:T(8,128)(2,1)S(1)} copy-done((bf16[512,256]{1,0:T(8,128)(2,1)S(1)}, bf16[512,256]{1,0:T(8,128)(2,1)}, u32[]{:S(2)}) %copy-start) | copy-done | bytes 262168
  29.6 12.9 %heads.1 = (f32[8,8,256]{2,1,0:T(8,128)}, bf16[544,256]{1,0:T(8,128)(2,1)S(1)}) custom-call(s32[3]{0:T(128)S(1)} %pad_add_fusion.place_ref, bf16[8,144,256]{2,1,0:T(8,128)(2,1)S(1)} %all-to-all-done.every_ref, bf16[512,256]{1,0:T(8,128)(2,1)S(1)} %copy-done, bf16[512,256]{1,0:T(8,128)(2,1)S(1)} %collective-permute-done.refs_1_, ...), custom_call_target="tpu_custom_call" | custom-call | tf_op jit(solution)/shard_map/heads/pallas_call | solution.py:283
  42.6 3.6 %all-to-all-start.1 = ((f32[8,8,256]{2,1,0:T(8,128)}), f32[8,8,256]{2,1,0:T(8,128)S(1)}, u32[]{:S(2)}, u32[]{:S(2)}) async-start(f32[8,8,256]{2,1,0:T(8,128)} %get-tuple-element.9), calls=%async_computation.1 | async-start | bytes 131072 | tf_op jit(solution)/shard_map/all_to_all | solution.py:301
  46.2 0.0 copy-start.1
  46.2 0.9 %copy-done.1 = bf16[512,256]{1,0:T(8,128)(2,1)S(1)} copy-done((bf16[512,256]{1,0:T(8,128)(2,1)S(1)}, bf16[512,256]{1,0:T(8,128)(2,1)}, u32[]{:S(2)}) %copy-start.1) | copy-done | bytes 262168
  47.2 0.9 %copy-done.3 = bf16[512,256]{1,0:T(8,128)(2,1)S(1)} copy-done((bf16[512,256]{1,0:T(8,128)(2,1)S(1)}, bf16[512,256]{1,0:T(8,128)(2,1)}, u32[]{:S(2)}) %copy-start.3) | copy-done | bytes 262168
  48.1 0.9 %copy-done.5 = bf16[512,256]{1,0:T(8,128)(2,1)S(1)} copy-done((bf16[512,256]{1,0:T(8,128)(2,1)S(1)}, bf16[512,256]{1,0:T(8,128)(2,1)}, u32[]{:S(2)}) %copy-start.5) | copy-done | bytes 262168
  49.1 0.9 %copy-done.7 = bf16[512,256]{1,0:T(8,128)(2,1)S(1)} copy-done((bf16[512,256]{1,0:T(8,128)(2,1)S(1)}, bf16[512,256]{1,0:T(8,128)(2,1)}, u32[]{:S(2)}) %copy-start.7) | copy-done | bytes 262168
  50.0 1.7 %first.1 = (f32[8,128,256]{2,1,0:T(8,128)S(1)}, f32[8,256,256]{2,1,0:T(8,128)S(1)}) custom-call(s32[1]{0:T(128)} %bitcast.5.node_ref, bf16[544,256]{1,0:T(8,128)(2,1)S(1)} %get-tuple-element.6.matrix_ref, bf16[128,256]{1,0:T(8,128)(2,1)S(1)} %copy-done.9, bf16[512,256]{1,0:T(8,128)(2,1)S(1)} %copy-done.1, bf16[512,256]{1,0:T(8,128)(2,1)S(1)} %copy-done.5, ...), custom_call_target="tpu_custom_call" | custom-call | flops 536870912 | bytes 3145728 | tf_op jit(solution)/shard_map/first/pallas_call | solution.py:305
  51.8 1.3 %all-to-all-done.1.head_ref = f32[8,8,256]{2,1,0:T(8,128)S(1)} async-done(((f32[8,8,256]{2,1,0:T(8,128)}), f32[8,8,256]{2,1,0:T(8,128)S(1)}, u32[]{:S(2)}, u32[]{:S(2)}) %all-to-all-start.1) | async-done | bytes 65568 | tf_op jit(solution)/shard_map/all_to_all | solution.py:301
  53.1 3.6 %volts.1 = (f32[2048,128]{1,0:T(8,128)}, f32[2048,128]{1,0:T(8,128)}) custom-call(bf16[544,256]{1,0:T(8,128)(2,1)S(1)} %get-tuple-element.6.matrix_ref, f32[8,128,256]{2,1,0:T(8,128)S(1)} %get-tuple-element.7.swing_ref, f32[8,256,256]{2,1,0:T(8,128)S(1)} %get-tuple-element.8.drop_ref, f32[8,8,256]{2,1,0:T(8,128)S(1)} %all-to-all-done.1.head_ref), custom_call_target="tpu_custom_call" | custom-call | tf_op jit(solution)/shard_map/volts/pallas_call | solution.py:317
  (19 shorter events, 0.0 us)
Async XLA Ops:
  0.6 0.8 %copy-start.8 = (bf16[128,256]{1,0:T(8,128)(2,1)S(1)}, bf16[128,256]{1,0:T(8,128)(2,1)}, u32[]{:S(2)}) copy-start(bf16[128,256]{1,0:T(8,128)(2,1)} %loadings_ref.3) | copy-start | bytes 196612
  1.5 0.7 %copy-start.10 = (f32[2,128]{1,0:T(2,128)S(1)}, f32[2,128]{1,0:T(2,128)}, u32[]{:S(2)}) copy-start(f32[2,128]{1,0:T(2,128)} %base_ref.1) | copy-start | bytes 3076
  2.2 0.7 %copy-start.11 = (f32[2,128]{1,0:T(2,128)S(1)}, f32[2,128]{1,0:T(2,128)}, u32[]{:S(2)}) copy-start(f32[2,128]{1,0:T(2,128)} %z_ref.1) | copy-start | bytes 3076
  2.8 0.7 %copy-start.12 = (f32[2,1,1]{0,2,1:T(1,128)S(1)}, f32[2,1,1]{0,2,1:T(1,128)}, u32[]{:S(2)}) copy-start(f32[2,1,1]{0,2,1:T(1,128)} %param.11) | copy-start | bytes 28
  3.5 0.7 %copy-start.13 = (s32[128]{0:T(128)S(1)}, s32[128]{0:T(128)}, u32[]{:S(2)}) copy-start(s32[128]{0:T(128)} %param.8) | copy-start | bytes 1540
  4.1 42.1 %copy-start.9 = (bf16[128,256]{1,0:T(8,128)(2,1)S(1)}, bf16[128,256]{1,0:T(8,128)(2,1)}, u32[]{:S(2)}) copy-start(bf16[128,256]{1,0:T(8,128)(2,1)} %loadings_ref.3) | copy-start | bytes 196612
  5.6 23.1 %all-to-all-start = ((bf16[8,144,256]{2,1,0:T(8,128)(2,1)}), bf16[8,144,256]{2,1,0:T(8,128)(2,1)S(1)}, u32[]{:S(2)}, u32[]{:S(2)}) async-start(bf16[8,144,256]{2,1,0:T(8,128)(2,1)} %pack.1), calls=%async_computation | async-start | bytes 1179648 | tf_op jit(solution)/shard_map/all_to_all | solution.py:270
  12.8 8.0 %collective-permute-start.1 = (bf16[512,256]{1,0:T(8,128)(2,1)}, bf16[512,256]{1,0:T(8,128)(2,1)S(1)}, u32[]{:S(2)}, u32[]{:S(2)}) collective-permute-start(bf16[512,256]{1,0:T(8,128)(2,1)} %refs_0_.3), channel_id=1, source_target_pairs={{0,2},{1,3},{2,0},{3,1},{4,6},{5,7},{6,4},{7,5},{8,10},{9,11},{10,... | collective-permute-start | bytes 786440 | tf_op jit(solution)/shard_map/ppermute | solution.py:277
  14.3 6.5 %collective-permute-start = (bf16[512,256]{1,0:T(8,128)(2,1)}, bf16[512,256]{1,0:T(8,128)(2,1)S(1)}, u32[]{:S(2)}, u32[]{:S(2)}) collective-permute-start(bf16[512,256]{1,0:T(8,128)(2,1)} %refs_0_.3), channel_id=1, source_target_pairs={{0,1},{1,0},{2,3},{3,2},{4,5},{5,4},{6,7},{7,6},{8,9},{9,8},{10,11... | collective-permute-start | bytes 786440 | tf_op jit(solution)/shard_map/ppermute | solution.py:277
  20.8 25.4 %copy-start.2 = (bf16[512,256]{1,0:T(8,128)(2,1)}, bf16[512,256]{1,0:T(8,128)(2,1)S(1)}, u32[]{:S(2)}) copy-start(bf16[512,256]{1,0:T(8,128)(2,1)S(1)} %collective-permute-done.1.refs_2_) | copy-start | bytes 786436
  20.8 1.5 %collective-permute-start.2 = (bf16[512,256]{1,0:T(8,128)(2,1)S(1)}, bf16[512,256]{1,0:T(8,128)(2,1)S(1)}, u32[]{:S(2)}, u32[]{:S(2)}) collective-permute-start(bf16[512,256]{1,0:T(8,128)(2,1)S(1)} %collective-permute-done.1.refs_2_), channel_id=1, source_target_pairs={{0,1},{1,0},{2,3},{3,2},{4,5},{5,4},{6,7},{7,6},{8,9},{9,8},{10,11... | collective-permute-start | bytes 786440 | tf_op jit(solution)/shard_map/ppermute | solution.py:277
  20.9 25.3 %copy-start.4 = (bf16[512,256]{1,0:T(8,128)(2,1)}, bf16[512,256]{1,0:T(8,128)(2,1)S(1)}, u32[]{:S(2)}) copy-start(bf16[512,256]{1,0:T(8,128)(2,1)S(1)} %collective-permute-done.refs_1_) | copy-start | bytes 786436
  22.3 23.9 %copy-start.6 = (bf16[512,256]{1,0:T(8,128)(2,1)}, bf16[512,256]{1,0:T(8,128)(2,1)S(1)}, u32[]{:S(2)}) copy-start(bf16[512,256]{1,0:T(8,128)(2,1)S(1)} %collective-permute-done.2.refs_3_) | copy-start | bytes 786436
  28.7 1.0 %copy-start = (bf16[512,256]{1,0:T(8,128)(2,1)S(1)}, bf16[512,256]{1,0:T(8,128)(2,1)}, u32[]{:S(2)}) copy-start(bf16[512,256]{1,0:T(8,128)(2,1)} %refs_0_.3) | copy-start | bytes 786436
  42.6 10.5 %all-to-all-start.1 = ((f32[8,8,256]{2,1,0:T(8,128)}), f32[8,8,256]{2,1,0:T(8,128)S(1)}, u32[]{:S(2)}, u32[]{:S(2)}) async-start(f32[8,8,256]{2,1,0:T(8,128)} %get-tuple-element.9), calls=%async_computation.1 | async-start | bytes 131072 | tf_op jit(solution)/shard_map/all_to_all | solution.py:301
  46.2 1.0 %copy-start.1 = (bf16[512,256]{1,0:T(8,128)(2,1)S(1)}, bf16[512,256]{1,0:T(8,128)(2,1)}, u32[]{:S(2)}) copy-start(bf16[512,256]{1,0:T(8,128)(2,1)} %refs_0_.3) | copy-start | bytes 786436
  47.2 0.9 %copy-start.3 = (bf16[512,256]{1,0:T(8,128)(2,1)S(1)}, bf16[512,256]{1,0:T(8,128)(2,1)}, u32[]{:S(2)}) copy-start(bf16[512,256]{1,0:T(8,128)(2,1)} %copy-done.2) | copy-start | bytes 786436
  48.1 0.9 %copy-start.5 = (bf16[512,256]{1,0:T(8,128)(2,1)S(1)}, bf16[512,256]{1,0:T(8,128)(2,1)}, u32[]{:S(2)}) copy-start(bf16[512,256]{1,0:T(8,128)(2,1)} %copy-done.4) | copy-start | bytes 786436
  49.1 0.9 %copy-start.7 = (bf16[512,256]{1,0:T(8,128)(2,1)S(1)}, bf16[512,256]{1,0:T(8,128)(2,1)}, u32[]{:S(2)}) copy-start(bf16[512,256]{1,0:T(8,128)(2,1)} %copy-done.6) | copy-start | bytes 786436

commit v4 on v3

v4 whole, which is shorter than its diff:
```python
import functools

import jax
import jax.numpy as jnp
from jax import lax
from jax.experimental import pallas as pl
from jax.experimental.pallas import tpu as pltpu
from jax.sharding import PartitionSpec as P

SWEEPS = 3
EXTRA = 16
LANES = 128

VMEM = pl.BlockSpec(memory_space=pltpu.VMEM)
SMEM = pl.BlockSpec(memory_space=pltpu.SMEM)
HBM = pl.BlockSpec(memory_space=pltpu.HBM)


def split(x):
    high = x.astype(jnp.bfloat16)
    low = (x - high.astype(jnp.float32)).astype(jnp.bfloat16)
    return high, low


def product(left, right):
    return jnp.dot(left, right, preferred_element_type=jnp.float32)


def product_nt(left, right):
    return lax.dot_general(left, right, (((1,), (1,)), ((), ())), preferred_element_type=jnp.float32)


def wide(row, width):
    n = row.shape[1]
    if width <= n:
        return row[:, :width]
    return jnp.concatenate([row] * (width // n), axis=1)


def pack_kernel(
    feeders, trunk_ref, loadings_ref, parents_ref, base_ref, z_ref, out_ref, trunk, loads, owners, rows_ref, meta_ref, sems
):
    n = loadings_ref.shape[0]
    copies = [
        pltpu.make_async_copy(loadings_ref, loads, sems.at[0]),
        pltpu.make_async_copy(parents_ref, owners, sems.at[1]),
        pltpu.make_async_copy(base_ref, rows_ref.at[0], sems.at[2]),
        pltpu.make_async_copy(z_ref, rows_ref.at[1], sems.at[3]),
        pltpu.make_async_copy(trunk_ref, trunk, sems.at[4]),
    ]
    for copy in copies:
        copy.start()
    for copy in copies[1:]:
        copy.wait()
    pair_ids = lax.broadcasted_iota(jnp.int32, (2, n), 0)
    trunk_rows = jnp.where(pair_ids == 0, trunk[0], trunk[1])
    for index, rows in enumerate((rows_ref[0], rows_ref[1], trunk_rows)):
        high = rows.astype(jnp.bfloat16).astype(jnp.float32)
        middle = (rows - high).astype(jnp.bfloat16).astype(jnp.float32)
        meta_ref[2 * index : 2 * index + 2, 0:n] = high
        meta_ref[2 * index : 2 * index + 2, n : 2 * n] = middle
        meta_ref[8 + 2 * index : 10 + 2 * index, 0:n] = rows - high - middle
    meta_ref[6:8, 0:n] = jnp.broadcast_to(owners[...].astype(jnp.float32), (2, n))
    meta_ref[6:8, n : 2 * n] = jnp.zeros((2, n), jnp.float32)
    meta_ref[14:16, 0:n] = jnp.zeros((2, n), jnp.float32)
    meta_ref[8:16, n : 2 * n] = jnp.zeros((8, n), jnp.float32)
    meta = meta_ref[...].astype(jnp.bfloat16)
    copies[0].wait()
    loadings = loads[...]
    for to in range(feeders):
        out_ref[to, 0:n, :] = loadings
        out_ref[to, n : n + EXTRA, :] = meta


def section_matrices(metas, n):
    row_ids = lax.broadcasted_iota(jnp.int32, (n, n), 0).astype(jnp.float32)
    lane_ids = lax.broadcasted_iota(jnp.int32, (n, n), 1).astype(jnp.float32)
    identity = (row_ids == lane_ids).astype(jnp.bfloat16)
    pad_ids = lax.broadcasted_iota(jnp.int32, (EXTRA, 2 * n), 0)
    highs = [meta[0:8, 0:n] for meta in metas]
    middles = [meta[0:8, n : 2 * n] for meta in metas]
    rows = [high + middle + meta[8:16, 0:n] for high, middle, meta in zip(highs, middles, metas)]
    powers = [(jnp.broadcast_to(high[6:7], (n, n)) == row_ids).astype(jnp.bfloat16) for high in highs]
    powers = [product_nt(identity, power).astype(jnp.bfloat16) for power in powers]
    paths = [identity + power for power in powers]
    powers = [product(power, power).astype(jnp.bfloat16) for power in powers]
    reach = 2
    while reach < n:
        if 2 * reach < n:
            both = [product(x, jnp.concatenate([x, p], axis=1)) for x, p in zip(powers, paths)]
            paths = [p + b[:, n:].astype(jnp.bfloat16) for p, b in zip(paths, both)]
            powers = [b[:, :n].astype(jnp.bfloat16) for b in both]
        else:
            paths = [p + product(x, p).astype(jnp.bfloat16) for x, p in zip(powers, paths)]
        reach *= 2
    shared = []
    for path, high, middle in zip(paths, highs, middles):
        wide_path = path.astype(jnp.float32)

        def scaled(index):
            return jnp.concatenate([wide_path * high[index : index + 1], wide_path * middle[index : index + 1]], axis=1)

        left = jnp.concatenate([scaled(2), scaled(3)], axis=0).astype(jnp.bfloat16)
        shared.append(product_nt(left, jnp.concatenate([path, path], axis=1)))
    out = []
    for both, row in zip(shared, rows):
        resist, react = both[:n], both[n:]
        base_active, base_reactive = row[0:1], row[1:2]
        real_high, real_low = split(resist * base_active + react * base_reactive)
        imag_high, imag_low = split(react * base_active - resist * base_reactive)
        row_real = jnp.concatenate([base_active, base_reactive], axis=1)
        row_imag = jnp.concatenate([-base_reactive, base_active], axis=1)
        sums_high, sums_low = split(jnp.where(pad_ids == 0, row_real, jnp.where(pad_ids == 1, row_imag, 0.0)))

        def whole(real_part, imag_part, sums_part):
            top = jnp.concatenate([real_part, -imag_part], axis=1)
            bottom = jnp.concatenate([imag_part, real_part], axis=1)
            return jnp.concatenate([top, bottom, sums_part], axis=0)

        out.append(
            jnp.concatenate(
                [whole(real_high, imag_high, sums_high), whole(real_low, imag_low, sums_low)], axis=0
            )
        )
    return out


def swing_of(loadings, factors):
    level = product_nt(loadings, factors).astype(jnp.bfloat16).astype(jnp.float32)
    return 1.0 + 0.5 * jnp.tanh(level)


def apply(matrix, high, low):
    half = matrix.shape[0] // 2
    first = product(matrix, high)
    return first[:half] + first[half:] + product(matrix[:half], low)


def scaled_volts(swing, real, imag):
    inverse = swing / (real * real + imag * imag)
    return jnp.concatenate([real * inverse, imag * inverse], axis=0)


def heads_kernel(feeders, pieces, place_ref, every_ref, *refs):
    piece_refs = refs[:pieces]
    head_ref, own_ref, factors_ref, matrix_ref, swing_ref, drop_ref, inject_ref, sem = refs[pieces:]
    width = factors_ref.shape[0]
    n = swing_ref.shape[1]
    span = 2 * n
    piece, offset = place_ref[0], place_ref[1]
    for index, piece_ref in enumerate(piece_refs):
        @pl.when(piece == index)
        def _(piece_ref=piece_ref):
            rows = piece_ref.at[pl.ds(pl.multiple_of(offset, width), width), :]
            copy = pltpu.make_async_copy(rows, factors_ref, sem)
            copy.start()
            copy.wait()
    group = min(feeders, 8)

    def sections(body):
        if group == feeders:
            body(list(range(feeders)))
        else:
            @pl.loop(0, feeders // group)
            def _(outer):
                body([outer * group + inner for inner in range(group)])

    def keep(g, out):
        drop_ref[g] = out[:span]
        inject_ref[g] = out[span:]

    def first(gs):
        for g, matrix in zip(gs, section_matrices([every_ref[g, n : n + EXTRA, :].astype(jnp.float32) for g in gs], n)):
            matrix_ref[g] = matrix
        factors = factors_ref[...]
        for g in gs:
            swing = swing_of(every_ref[g, 0:n, :], factors)
            swing_ref[g] = swing
            high, low = split(swing)
            keep(g, apply(matrix_ref[g][:, :n], high, low))

    sections(first)

    def trunk_row(g, index):
        parts = every_ref[g, n : n + EXTRA, :].astype(jnp.float32)
        row = parts[index : index + 1, 0:n] + parts[index : index + 1, n : 2 * n] + parts[index + 8 : index + 9, 0:n]
        return wide(row, width)

    trunk = [(trunk_row(g, 4), trunk_row(g, 5)) for g in range(feeders)]

    def heads(sweep):
        flows = [None] * feeders
        real = jnp.zeros((1, width), jnp.float32)
        imag = real
        for g in reversed(range(feeders)):
            real = real + inject_ref[g, 0:1, :]
            imag = imag + inject_ref[g, 1:2, :]
            flows[g] = (real, imag)
        head_real = jnp.ones((1, width), jnp.float32)
        head_imag = jnp.zeros((1, width), jnp.float32)
        for g in range(feeders):
            r, x = trunk[g]
            real, imag = flows[g]
            head_real = head_real - (r * real - x * imag)
            head_imag = head_imag - (r * imag + x * real)
            head_ref[g, 2 * sweep : 2 * sweep + 1, :] = head_real
            head_ref[g, 2 * sweep + 1 : 2 * sweep + 2, :] = head_imag

    heads(0)
    for sweep in range(1, SWEEPS):
        def again(gs, sweep=sweep):
            for g in gs:
                real = head_ref[g, 2 * sweep - 2 : 2 * sweep - 1, :] - drop_ref[g, 0:n, :]
                imag = head_ref[g, 2 * sweep - 1 : 2 * sweep, :] - drop_ref[g, n:span, :]
                high, low = split(scaled_volts(swing_ref[g], real, imag))
                if sweep == SWEEPS - 1:
                    half = span + EXTRA
                    row_high = matrix_ref[g, span:half, :]
                    row_low = matrix_ref[g, half + span :, :]
                    inject_ref[g] = product(row_high, high) + product(row_low, high) + product(row_high, low)
                else:
                    keep(g, apply(matrix_ref[g], high, low))

        sections(again)
        heads(sweep)
    for g in range(feeders):
        head_ref[g, 2 * SWEEPS :, :] = jnp.zeros((head_ref.shape[1] - 2 * SWEEPS, width), jnp.float32)
    own_ref[...] = matrix_ref[place_ref[2]]


def drop_rows(matrix_ref, n):
    half = matrix_ref.shape[0] // 2
    return jnp.concatenate([matrix_ref[0 : 2 * n, :], matrix_ref[half : half + 2 * n, :]], axis=0)


def first_kernel(pieces, node_ref, matrix_ref, loadings_ref, *refs):
    piece_refs, (swing_ref, drop_ref, loads, factors_ref, sems) = refs[:pieces], refs[pieces:]
    n = loadings_ref.shape[0]
    width = swing_ref.shape[2]
    chunks = piece_refs[0].shape[0] // width
    copies = [
        pltpu.make_async_copy(loadings_ref, loads, sems.at[0]),
        pltpu.make_async_copy(piece_refs[0], factors_ref, sems.at[1]),
    ]
    for copy in copies:
        copy.start()
    matrix = drop_rows(matrix_ref, n)[:, 0:n]
    copies[0].wait()
    loadings = loads[...]
    for index in reversed(range(pieces)):
        piece_ref = piece_refs[index]
        if index == 0:
            copies[1].wait()
            piece_ref = factors_ref
        for part in range(chunks):
            chunk = jnp.bitwise_xor(node_ref[0], index) * chunks + part
            swing = swing_of(loadings, piece_ref[part * width : (part + 1) * width, :])
            swing_ref[chunk] = swing
            high, low = split(swing)
            drop_ref[chunk] = apply(matrix, high, low)


def volts_kernel(matrix_ref, swing_ref, drop_ref, head_ref, real_ref, imag_ref, out_ref, sems):
    n = swing_ref.shape[1]
    chunks, width = swing_ref.shape[0], swing_ref.shape[2]
    matrix = drop_rows(matrix_ref, n)
    drops = [None] * chunks
    copies = []
    for sweep in range(SWEEPS):
        for chunk in range(chunks):
            drop = drop_ref[chunk] if sweep == 0 else drops[chunk]
            real = head_ref[chunk, 2 * sweep : 2 * sweep + 1, :] - drop[:n]
            imag = head_ref[chunk, 2 * sweep + 1 : 2 * sweep + 2, :] - drop[n:]
            if sweep < SWEEPS - 1:
                high, low = split(scaled_volts(swing_ref[chunk], real, imag))
                drops[chunk] = apply(matrix, high, low)
            else:
                rows = slice(chunk * width, (chunk + 1) * width)
                for index, (part, to_ref) in enumerate(((real, real_ref), (imag, imag_ref))):
                    out_ref[index, rows, :] = part.T
                    copy = pltpu.make_async_copy(out_ref.at[index, rows, :], to_ref.at[rows, :], sems.at[index, chunk])
                    copy.start()
                    copies.append(copy)
    for copy in copies:
        copy.wait()


def in_hbm(*arrays):
    return [pltpu.with_memory_space_constraint(array, pltpu.HBM) for array in arrays]


def limit(nbytes):
    return pltpu.CompilerParams(vmem_limit_bytes=min(60 << 20, int(nbytes) + (16 << 20)))


def local(feeders, nodes, factors, loadings, parents, load_base, lateral_z, trunk_z):
    node = lax.axis_index("node").astype(jnp.int32)
    feeder = lax.axis_index("feeder").astype(jnp.int32)
    rows, rank = factors.shape
    scen = rows * nodes
    n = loadings.shape[0]
    width = max(scen // feeders, LANES)
    share = feeders * width // scen
    f32, bf16 = jnp.float32, jnp.bfloat16
    matrix_rows = 2 * (2 * n + EXTRA)

    packed = pl.pallas_call(
        functools.partial(pack_kernel, feeders),
        out_shape=jax.ShapeDtypeStruct((feeders, n + EXTRA, rank), bf16),
        in_specs=[HBM] * 5,
        out_specs=VMEM,
        scratch_shapes=[
            pltpu.SMEM((2,), f32),
            pltpu.VMEM((n, rank), bf16),
            pltpu.VMEM((1, n), jnp.int32),
            pltpu.VMEM((2, 2, n), f32),
            pltpu.VMEM((EXTRA, rank), f32),
            pltpu.SemaphoreType.DMA((5,)),
        ],
        compiler_params=limit(feeders * (n + EXTRA) * rank * 2),
        name="pack",
    )(*in_hbm(trunk_z.reshape(2), loadings, parents.reshape(1, n), load_base, lateral_z))
    every = lax.all_to_all(packed, "feeder", 0, 0, tiled=True)

    held = {0: factors}
    step = nodes // 2
    while step >= 1:
        pairs = [(i, i ^ step) for i in range(nodes)]
        for offset in list(held):
            held[offset ^ step] = lax.ppermute(held[offset], "node", pairs)
        step //= 2
    pieces = [held[offset] for offset in range(nodes)]

    start = (feeder // share) * width
    place = jnp.stack([(start // rows) ^ node, start % rows, feeder])
    heads, matrix = pl.pallas_call(
        functools.partial(heads_kernel, feeders, nodes),
        out_shape=(
            jax.ShapeDtypeStruct((feeders, 8, width), f32),
            jax.ShapeDtypeStruct((matrix_rows, 2 * n), bf16),
        ),
        in_specs=[SMEM, VMEM, HBM] + [VMEM] * (nodes - 1),
        out_specs=(VMEM, VMEM),
        scratch_shapes=[
            pltpu.VMEM((width, rank), bf16),
            pltpu.VMEM((feeders, matrix_rows, 2 * n), bf16),
            pltpu.VMEM((feeders, n, width), f32),
            pltpu.VMEM((feeders, 2 * n, width), f32),
            pltpu.VMEM((feeders, EXTRA, width), f32),
            pltpu.SemaphoreType.DMA,
        ],
        compiler_params=limit(feeders * (matrix_rows * 4 * n + 3 * n * width * 4 + EXTRA * width * 4 + (n + EXTRA) * rank * 2)),
        name="heads",
    )(place, every, *in_hbm(pieces[0]), *pieces[1:])
    given = lax.all_to_all(heads, "feeder", 0, 0, tiled=True)
    given = given[::share]

    chunks = scen // width
    swing, drop = pl.pallas_call(
        functools.partial(first_kernel, nodes),
        out_shape=(
            jax.ShapeDtypeStruct((chunks, n, width), f32),
            jax.ShapeDtypeStruct((chunks, 2 * n, width), f32),
        ),
        in_specs=[SMEM, VMEM, HBM, HBM] + [VMEM] * (nodes - 1),
        out_specs=(VMEM, VMEM),
        scratch_shapes=[
            pltpu.VMEM((n, rank), bf16),
            pltpu.VMEM((rows, rank), bf16),
            pltpu.SemaphoreType.DMA((2,)),
        ],
        compiler_params=limit(3 * n * scen * 4 + scen * rank * 2),
        cost_estimate=pl.CostEstimate(flops=2 * scen * n * rank * 4, bytes_accessed=3 * n * scen * 4, transcendentals=scen * n),
        name="first",
    )(node.reshape(1), matrix, *in_hbm(loadings, pieces[0]), *pieces[1:])
    return pl.pallas_call(
        volts_kernel,
        out_shape=(
            jax.ShapeDtypeStruct((scen, n), f32),
            jax.ShapeDtypeStruct((scen, n), f32),
        ),
        in_specs=[VMEM] * 4,
        out_specs=(HBM, HBM),
        scratch_shapes=[pltpu.VMEM((2, scen, n), f32), pltpu.SemaphoreType.DMA((2, chunks))],
        compiler_params=limit(5 * n * scen * 4),
        name="volts",
    )(matrix, swing, drop, given)


def solution(mesh):
    feeders = mesh.shape["feeder"]
    nodes = mesh.shape["node"]
    return jax.shard_map(
        functools.partial(local, feeders, nodes),
        mesh=mesh,
        in_specs=(
            P("node", None),
            P(("feeder", "node"), None),
            P(("feeder", "node")),
            P(None, ("feeder", "node")),
            P(None, ("feeder", "node")),
            P(None, "feeder", "node"),
        ),
        out_specs=(P(None, ("feeder", "node")), P(None, ("feeder", "node"))),
        check_vma=False,
    )
```

time: 57.2 us -> 47.1 us (0.82)
  local copies, waits for them, and re-layouts: 8.26 us -> 2.85 us
  Pallas kernels: 19.6 us -> 15.4 us
    unnamed x28 -> x12, local copies, waits for them, and re-layouts: 8.26 us -> 2.85 us
    pallas_call x1, Pallas kernels: 12.9 us -> 7.75 us  [local(): pl.pallas_call(functools.partial(heads_kernel, feeders, nodes), out_shape...]
    pallas_call x1, Pallas kernels: 1.72 us -> 2.79 us  [local(): pl.pallas_call(functools.partial(first_kernel, nodes), out_shape=(jax.Sha...]
  transfers between devices with their start and end apart: 5 -> 5, of which waited for: 4 -> 4; matrix products, arithmetic and copies ran while one was open for 0% -> 0% of each run, Pallas kernels for 3% -> 6%
where the time goes in v4:
time: 47.1 us; the launch traced here: 46.6 us
  Pallas kernels  15.4 us (33%)
  waiting for transfers between devices  15.4 us (33%)
  starting transfers between devices  12.2 us (26%)
  local copies, waits for them, and re-layouts  2.85 us (6%)
  between operations  0.7 us (1%)
    ppermute x3, waiting for transfers between devices, local(): held[offset ^ step] = lax.ppermute(held[offset], 'node', pairs)  7.91 us
    pallas_call x1, Pallas kernels, local(): pl.pallas_call(functools.partial(heads_kernel, feeders, nodes), out_shape...  7.75 us
    all_to_all x1, starting transfers between devices, local(): every = lax.all_to_all(packed, 'feeder', 0, 0, tiled=True)  7.26 us
    all_to_all x1, waiting for transfers between devices, local(): every = lax.all_to_all(packed, 'feeder', 0, 0, tiled=True)  6.37 us
    all_to_all x1, starting transfers between devices, local(): given = lax.all_to_all(heads, 'feeder', 0, 0, tiled=True)  3.36 us
    pallas_call x1, Pallas kernels, local(): pl.pallas_call(volts_kernel, out_shape=(jax.ShapeDtypeStruct((scen, n), f...  3.13 us
    unnamed x12, local copies, waits for them, and re-layouts  2.85 us
    pallas_call x1, Pallas kernels, local(): pl.pallas_call(functools.partial(first_kernel, nodes), out_shape=(jax.Sha...  2.79 us
  transfers between devices with their start and end apart: 5, of which 4 were waited for; matrix products, arithmetic and copies ran while one was open for 0% of the time, Pallas kernels for 6%

profile of v4, /device:TPU:0, one launch (start us, length us, event | category | flops | bytes accessed | tf_op | source)
XLA Modules:
  0.0 46.6 jit_solution(13858147859054549542)
XLA Ops:
  0.6 1.7 %pack.1 = bf16[8,144,256]{2,1,0:T(8,128)(2,1)} custom-call(f32[2]{0:T(128)} %bitcast.6, bf16[128,256]{1,0:T(8,128)(2,1)} %loadings_ref.3, s32[1,128]{1,0:T(1,128)} %bitcast.7, f32[2,128]{1,0:T(2,128)} %base_ref.1, f32[2,128]{1,0:T(2,128)} %z_ref.1), custom_call_target="tpu_custom_call" | custom-call | tf_op jit(solution)/shard_map/pack/pallas_call | solution.py:307
  2.4 7.3 %all-to-all-start = ((bf16[8,144,256]{2,1,0:T(8,128)(2,1)}), bf16[8,144,256]{2,1,0:T(8,128)(2,1)S(1)}, u32[]{:S(2)}, u32[]{:S(2)}) async-start(bf16[8,144,256]{2,1,0:T(8,128)(2,1)} %pack.1), calls=%async_computation | async-start | bytes 1179648 | tf_op jit(solution)/shard_map/all_to_all | solution.py:323
  9.6 1.5 %collective-permute-start.1 = (bf16[512,256]{1,0:T(8,128)(2,1)}, bf16[512,256]{1,0:T(8,128)(2,1)S(1)}, u32[]{:S(2)}, u32[]{:S(2)}) collective-permute-start(bf16[512,256]{1,0:T(8,128)(2,1)} %refs_0_.3), channel_id=1, source_target_pairs={{0,2},{1,3},{2,0},{3,1},{4,6},{5,7},{6,4},{7,5},{8,10},{9,11},{10,... | collective-permute-start | bytes 786440 | tf_op jit(solution)/shard_map/ppermute | solution.py:330
  11.2 0.0 collective-permute-start
  11.2 6.5 %collective-permute-done.1.refs_2_ = bf16[512,256]{1,0:T(8,128)(2,1)S(1)} collective-permute-done((bf16[512,256]{1,0:T(8,128)(2,1)}, bf16[512,256]{1,0:T(8,128)(2,1)S(1)}, u32[]{:S(2)}, u32[]{:S(2)}) %collective-permute-start.1) | collective-permute-done | bytes 262176 | tf_op jit(solution)/shard_map/ppermute | solution.py:330
  17.6 0.0 copy-start
  17.6 0.0 collective-permute-start.2
  17.6 0.1 pad_add_fusion.place_ref
  17.7 0.0 collective-permute-done.refs_1_
  17.7 1.5 %collective-permute-done.2.refs_3_ = bf16[512,256]{1,0:T(8,128)(2,1)S(1)} collective-permute-done((bf16[512,256]{1,0:T(8,128)(2,1)S(1)}, bf16[512,256]{1,0:T(8,128)(2,1)S(1)}, u32[]{:S(2)}, u32[]{:S(2)}) %collective-permute-start.2) | collective-permute-done | bytes 262176 | tf_op jit(solution)/shard_map/ppermute | solution.py:330
  19.2 0.0 copy-start.4
  19.2 6.4 %all-to-all-done.every_ref = bf16[8,144,256]{2,1,0:T(8,128)(2,1)S(1)} async-done(((bf16[8,144,256]{2,1,0:T(8,128)(2,1)}), bf16[8,144,256]{2,1,0:T(8,128)(2,1)S(1)}, u32[]{:S(2)}, u32[]{:S(2)}) %all-to-all-start) | async-done | bytes 589856 | tf_op jit(solution)/shard_map/all_to_all | solution.py:323
  25.5 7.7 %heads.1 = (f32[8,8,256]{2,1,0:T(8,128)}, bf16[544,256]{1,0:T(8,128)(2,1)S(1)}) custom-call(s32[3]{0:T(128)S(1)} %pad_add_fusion.place_ref, bf16[8,144,256]{2,1,0:T(8,128)(2,1)S(1)} %all-to-all-done.every_ref, bf16[512,256]{1,0:T(8,128)(2,1)} %refs_0_.3, bf16[512,256]{1,0:T(8,128)(2,1)S(1)} %collective-permute-done.refs_1_, ...), custom_call_target="tpu_custom_call" | custom-call | tf_op jit(solution)/shard_map/heads/pallas_call | solution.py:336
  33.3 3.4 %all-to-all-start.1 = ((f32[8,8,256]{2,1,0:T(8,128)}), f32[8,8,256]{2,1,0:T(8,128)S(1)}, u32[]{:S(2)}, u32[]{:S(2)}) async-start(f32[8,8,256]{2,1,0:T(8,128)} %get-tuple-element.9), calls=%async_computation.1 | async-start | bytes 131072 | tf_op jit(solution)/shard_map/all_to_all | solution.py:355
  36.7 0.0 copy-done
  36.7 0.0 copy-done.2
  36.7 0.0 copy-done.4
  36.7 0.0 copy-start.1
  36.7 0.9 %copy-done.1 = bf16[512,256]{1,0:T(8,128)(2,1)S(1)} copy-done((bf16[512,256]{1,0:T(8,128)(2,1)S(1)}, bf16[512,256]{1,0:T(8,128)(2,1)}, u32[]{:S(2)}) %copy-start.1) | copy-done | bytes 262168
  37.6 0.9 %copy-done.3 = bf16[512,256]{1,0:T(8,128)(2,1)S(1)} copy-done((bf16[512,256]{1,0:T(8,128)(2,1)S(1)}, bf16[512,256]{1,0:T(8,128)(2,1)}, u32[]{:S(2)}) %copy-start.3) | copy-done | bytes 262168
  38.6 0.9 %copy-done.5 = bf16[512,256]{1,0:T(8,128)(2,1)S(1)} copy-done((bf16[512,256]{1,0:T(8,128)(2,1)S(1)}, bf16[512,256]{1,0:T(8,128)(2,1)}, u32[]{:S(2)}) %copy-start.5) | copy-done | bytes 262168
  39.5 2.8 %first.1 = (f32[8,128,256]{2,1,0:T(8,128)S(1)}, f32[8,256,256]{2,1,0:T(8,128)S(1)}) custom-call(s32[1]{0:T(128)} %bitcast.5.node_ref, bf16[544,256]{1,0:T(8,128)(2,1)S(1)} %get-tuple-element.6.matrix_ref, bf16[128,256]{1,0:T(8,128)(2,1)} %loadings_ref.3, bf16[512,256]{1,0:T(8,128)(2,1)} %refs_0_.3, bf16[512,256]{1,0:T(8,128)(2,1)S(1)} %copy-done.3, ...), custom_call_target="tpu_custom_call" | custom-call | flops 536870912 | bytes 3145728 | tf_op jit(solution)/shard_map/first/pallas_call | solution.py:359
  42.3 1.2 %all-to-all-done.1.head_ref = f32[8,8,256]{2,1,0:T(8,128)S(1)} async-done(((f32[8,8,256]{2,1,0:T(8,128)}), f32[8,8,256]{2,1,0:T(8,128)S(1)}, u32[]{:S(2)}, u32[]{:S(2)}) %all-to-all-start.1) | async-done | bytes 65568 | tf_op jit(solution)/shard_map/all_to_all | solution.py:355
  43.5 3.1 %volts.1 = (f32[2048,128]{1,0:T(8,128)}, f32[2048,128]{1,0:T(8,128)}) custom-call(bf16[544,256]{1,0:T(8,128)(2,1)S(1)} %get-tuple-element.6.matrix_ref, f32[8,128,256]{2,1,0:T(8,128)S(1)} %get-tuple-element.7.swing_ref, f32[8,256,256]{2,1,0:T(8,128)S(1)} %get-tuple-element.8.drop_ref, f32[8,8,256]{2,1,0:T(8,128)S(1)} %all-to-all-done.1.head_ref), custom_call_target="tpu_custom_call" | custom-call | tf_op jit(solution)/shard_map/volts/pallas_call | solution.py:376
  (3 shorter events, 0.0 us)
Async XLA Ops:
  2.4 23.2 %all-to-all-start = ((bf16[8,144,256]{2,1,0:T(8,128)(2,1)}), bf16[8,144,256]{2,1,0:T(8,128)(2,1)S(1)}, u32[]{:S(2)}, u32[]{:S(2)}) async-start(bf16[8,144,256]{2,1,0:T(8,128)(2,1)} %pack.1), calls=%async_computation | async-start | bytes 1179648 | tf_op jit(solution)/shard_map/all_to_all | solution.py:323
  9.6 8.0 %collective-permute-start.1 = (bf16[512,256]{1,0:T(8,128)(2,1)}, bf16[512,256]{1,0:T(8,128)(2,1)S(1)}, u32[]{:S(2)}, u32[]{:S(2)}) collective-permute-start(bf16[512,256]{1,0:T(8,128)(2,1)} %refs_0_.3), channel_id=1, source_target_pairs={{0,2},{1,3},{2,0},{3,1},{4,6},{5,7},{6,4},{7,5},{8,10},{9,11},{10,... | collective-permute-start | bytes 786440 | tf_op jit(solution)/shard_map/ppermute | solution.py:330
  11.2 6.5 %collective-permute-start = (bf16[512,256]{1,0:T(8,128)(2,1)}, bf16[512,256]{1,0:T(8,128)(2,1)S(1)}, u32[]{:S(2)}, u32[]{:S(2)}) collective-permute-start(bf16[512,256]{1,0:T(8,128)(2,1)} %refs_0_.3), channel_id=1, source_target_pairs={{0,1},{1,0},{2,3},{3,2},{4,5},{5,4},{6,7},{7,6},{8,9},{9,8},{10,11... | collective-permute-start | bytes 786440 | tf_op jit(solution)/shard_map/ppermute | solution.py:330
  17.6 19.0 %copy-start = (bf16[512,256]{1,0:T(8,128)(2,1)}, bf16[512,256]{1,0:T(8,128)(2,1)S(1)}, u32[]{:S(2)}) copy-start(bf16[512,256]{1,0:T(8,128)(2,1)S(1)} %collective-permute-done.1.refs_2_) | copy-start | bytes 786436
  17.6 1.5 %collective-permute-start.2 = (bf16[512,256]{1,0:T(8,128)(2,1)S(1)}, bf16[512,256]{1,0:T(8,128)(2,1)S(1)}, u32[]{:S(2)}, u32[]{:S(2)}) collective-permute-start(bf16[512,256]{1,0:T(8,128)(2,1)S(1)} %collective-permute-done.1.refs_2_), channel_id=1, source_target_pairs={{0,1},{1,0},{2,3},{3,2},{4,5},{5,4},{6,7},{7,6},{8,9},{9,8},{10,11... | collective-permute-start | bytes 786440 | tf_op jit(solution)/shard_map/ppermute | solution.py:330
  17.7 19.0 %copy-start.2 = (bf16[512,256]{1,0:T(8,128)(2,1)}, bf16[512,256]{1,0:T(8,128)(2,1)S(1)}, u32[]{:S(2)}) copy-start(bf16[512,256]{1,0:T(8,128)(2,1)S(1)} %collective-permute-done.refs_1_) | copy-start | bytes 786436
  19.2 17.5 %copy-start.4 = (bf16[512,256]{1,0:T(8,128)(2,1)}, bf16[512,256]{1,0:T(8,128)(2,1)S(1)}, u32[]{:S(2)}) copy-start(bf16[512,256]{1,0:T(8,128)(2,1)S(1)} %collective-permute-done.2.refs_3_) | copy-start | bytes 786436
  33.3 10.2 %all-to-all-start.1 = ((f32[8,8,256]{2,1,0:T(8,128)}), f32[8,8,256]{2,1,0:T(8,128)S(1)}, u32[]{:S(2)}, u32[]{:S(2)}) async-start(f32[8,8,256]{2,1,0:T(8,128)} %get-tuple-element.9), calls=%async_computation.1 | async-start | bytes 131072 | tf_op jit(solution)/shard_map/all_to_all | solution.py:355
  36.7 1.0 %copy-start.1 = (bf16[512,256]{1,0:T(8,128)(2,1)S(1)}, bf16[512,256]{1,0:T(8,128)(2,1)}, u32[]{:S(2)}) copy-start(bf16[512,256]{1,0:T(8,128)(2,1)} %copy-done) | copy-start | bytes 786436
  37.6 0.9 %copy-start.3 = (bf16[512,256]{1,0:T(8,128)(2,1)S(1)}, bf16[512,256]{1,0:T(8,128)(2,1)}, u32[]{:S(2)}) copy-start(bf16[512,256]{1,0:T(8,128)(2,1)} %copy-done.2) | copy-start | bytes 786436
  38.6 0.9 %copy-start.5 = (bf16[512,256]{1,0:T(8,128)(2,1)S(1)}, bf16[512,256]{1,0:T(8,128)(2,1)}, u32[]{:S(2)}) copy-start(bf16[512,256]{1,0:T(8,128)(2,1)} %copy-done.4) | copy-start | bytes 786436

commit v5 on v4

--- a/solution.py
+++ b/solution.py
@@ -14,6 +14,7 @@
 VMEM = pl.BlockSpec(memory_space=pltpu.VMEM)
 SMEM = pl.BlockSpec(memory_space=pltpu.SMEM)
 HBM = pl.BlockSpec(memory_space=pltpu.HBM)
+ANY = pl.BlockSpec(memory_space=pl.ANY)
 
 
 def split(x):
@@ -38,7 +39,7 @@
 
 
 def pack_kernel(
-    feeders, trunk_ref, loadings_ref, parents_ref, base_ref, z_ref, out_ref, trunk, loads, owners, rows_ref, meta_ref, sems
+    trunk_ref, loadings_ref, parents_ref, base_ref, z_ref, out_ref, trunk, loads, owners, rows_ref, meta_ref, sems
 ):
     n = loadings_ref.shape[0]
     copies = [
@@ -66,22 +67,23 @@
     meta_ref[8:16, n : 2 * n] = jnp.zeros((8, n), jnp.float32)
     meta = meta_ref[...].astype(jnp.bfloat16)
     copies[0].wait()
-    loadings = loads[...]
-    for to in range(feeders):
-        out_ref[to, 0:n, :] = loadings
-        out_ref[to, n : n + EXTRA, :] = meta
-
-
-def section_matrices(metas, n):
+    out_ref[0:n, :] = loads[...]
+    out_ref[n : n + EXTRA, :] = meta
+
+
+def constants(section_ref, n):
+    meta = section_ref[n : n + EXTRA, :].astype(jnp.float32)
+    high, middle = meta[0:8, 0:n], meta[0:8, n : 2 * n]
+    return high, middle, high + middle + meta[8:16, 0:n]
+
+
+def section_matrices(sections, n):
     row_ids = lax.broadcasted_iota(jnp.int32, (n, n), 0).astype(jnp.float32)
     lane_ids = lax.broadcasted_iota(jnp.int32, (n, n), 1).astype(jnp.float32)
     identity = (row_ids == lane_ids).astype(jnp.bfloat16)
     pad_ids = lax.broadcasted_iota(jnp.int32, (EXTRA, 2 * n), 0)
-    highs = [meta[0:8, 0:n] for meta in metas]
-    middles = [meta[0:8, n : 2 * n] for meta in metas]
-    rows = [high + middle + meta[8:16, 0:n] for high, middle, meta in zip(highs, middles, metas)]
-    powers = [(jnp.broadcast_to(high[6:7], (n, n)) == row_ids).astype(jnp.bfloat16) for high in highs]
-    powers = [product_nt(identity, power).astype(jnp.bfloat16) for power in powers]
+    highs, middles, rows = zip(*(constants(section, n) for section in sections))
+    powers = [(jnp.broadcast_to(row.T[:, 6:7], (n, n)) == lane_ids).astype(jnp.bfloat16) for row in rows]
     paths = [identity + power for power in powers]
     powers = [product(power, power).astype(jnp.bfloat16) for power in powers]
     reach = 2
@@ -136,18 +138,54 @@
     return first[:half] + first[half:] + product(matrix[:half], low)
 
 
+def apply_real(matrix, real):
+    half, n = matrix.shape[0] // 2, matrix.shape[1] // 2
+    high_part, low_part = matrix[:half, :n], matrix[half:, :n]
+    left = jnp.concatenate(
+        [
+            jnp.concatenate([high_part, high_part], axis=1),
+            jnp.concatenate([low_part, jnp.zeros_like(low_part)], axis=1),
+        ],
+        axis=0,
+    )
+    out = product(left, jnp.concatenate(split(real), axis=0))
+    return out[:half] + out[half:]
+
+
+def inverse_of(swing, real, imag):
+    return swing / (real * real + imag * imag)
+
+
 def scaled_volts(swing, real, imag):
-    inverse = swing / (real * real + imag * imag)
+    inverse = inverse_of(swing, real, imag)
     return jnp.concatenate([real * inverse, imag * inverse], axis=0)
 
 
-def heads_kernel(feeders, pieces, place_ref, every_ref, *refs):
-    piece_refs = refs[:pieces]
-    head_ref, own_ref, factors_ref, matrix_ref, swing_ref, drop_ref, inject_ref, sem = refs[pieces:]
+def first_sweep(sections, factors, matrix_ref, swing_ref, drop_ref, inject_ref):
+    n = swing_ref.shape[1]
+    for start in range(0, len(sections), 8):
+        group = sections[start : start + 8]
+        for slot, matrix in enumerate(section_matrices(group, n), start):
+            matrix_ref[slot] = matrix
+        for slot, section in enumerate(group, start):
+            swing = swing_of(section[0:n, :], factors)
+            swing_ref[slot] = swing
+            out = apply_real(matrix_ref[slot], swing)
+            drop_ref[slot] = out[: 2 * n]
+            inject_ref[slot] = out[2 * n :]
+
+
+def early_kernel(pieces, place_ref, *refs):
+    piece_refs, sections = refs[:pieces], refs[pieces:-9]
+    factors_ref, own_ref, kept_ref, matrix_ref, swing_ref, drop_ref, inject_ref, sem, keep_sems = refs[-9:]
     width = factors_ref.shape[0]
-    n = swing_ref.shape[1]
-    span = 2 * n
     piece, offset = place_ref[0], place_ref[1]
+    keeps = [
+        pltpu.make_async_copy(piece_ref, kept_ref.at[index], keep_sems.at[index])
+        for index, piece_ref in enumerate(piece_refs[1:])
+    ]
+    for copy in keeps:
+        copy.start()
     for index, piece_ref in enumerate(piece_refs):
         @pl.when(piece == index)
         def _(piece_ref=piece_ref):
@@ -155,51 +193,43 @@
             copy = pltpu.make_async_copy(rows, factors_ref, sem)
             copy.start()
             copy.wait()
-    group = min(feeders, 8)
-
-    def sections(body):
-        if group == feeders:
-            body(list(range(feeders)))
-        else:
-            @pl.loop(0, feeders // group)
-            def _(outer):
-                body([outer * group + inner for inner in range(group)])
-
-    def keep(g, out):
-        drop_ref[g] = out[:span]
-        inject_ref[g] = out[span:]
-
-    def first(gs):
-        for g, matrix in zip(gs, section_matrices([every_ref[g, n : n + EXTRA, :].astype(jnp.float32) for g in gs], n)):
-            matrix_ref[g] = matrix
-        factors = factors_ref[...]
-        for g in gs:
-            swing = swing_of(every_ref[g, 0:n, :], factors)
-            swing_ref[g] = swing
-            high, low = split(swing)
-            keep(g, apply(matrix_ref[g][:, :n], high, low))
-
-    sections(first)
-
-    def trunk_row(g, index):
-        parts = every_ref[g, n : n + EXTRA, :].astype(jnp.float32)
-        row = parts[index : index + 1, 0:n] + parts[index : index + 1, n : 2 * n] + parts[index + 8 : index + 9, 0:n]
-        return wide(row, width)
-
-    trunk = [(trunk_row(g, 4), trunk_row(g, 5)) for g in range(feeders)]
+    first_sweep(sections, factors_ref[...], matrix_ref, swing_ref, drop_ref, inject_ref)
+    own_ref[...] = matrix_ref[0]
+    for copy in keeps:
+        copy.wait()
+
+
+def heads_kernel(slots, early, place_ref, factors_ref, *refs):
+    feeders = len(slots)
+    sections = refs[:feeders]
+    early_refs = refs[feeders : feeders + 4]
+    head_ref, matrix_ref, swing_ref, drop_ref, inject_ref, again_ref, flow_ref, trunk_ref = refs[feeders + 4 :]
+    width = factors_ref.shape[0]
+    n = swing_ref.shape[1]
+    first_sweep(sections[early:], factors_ref[...], matrix_ref, swing_ref, drop_ref, inject_ref)
+    late_refs = (matrix_ref, swing_ref, drop_ref, inject_ref)
+    place = [jnp.bitwise_xor(place_ref[2], slot) for slot in slots]
+
+    def of(index, which):
+        return early_refs[which].at[index] if index < early else late_refs[which].at[index - early]
+
+    for index in range(feeders):
+        row = constants(sections[index], n)[2]
+        trunk_ref[place[index], 0:2, :] = wide(row[4:6], width)
+        flow_ref[place[index]] = of(index, 3)[0:8, :]
 
     def heads(sweep):
         flows = [None] * feeders
         real = jnp.zeros((1, width), jnp.float32)
         imag = real
         for g in reversed(range(feeders)):
-            real = real + inject_ref[g, 0:1, :]
-            imag = imag + inject_ref[g, 1:2, :]
+            real = real + flow_ref[g, 0:1, :]
+            imag = imag + flow_ref[g, 1:2, :]
             flows[g] = (real, imag)
         head_real = jnp.ones((1, width), jnp.float32)
         head_imag = jnp.zeros((1, width), jnp.float32)
         for g in range(feeders):
-            r, x = trunk[g]
+            r, x = trunk_ref[g, 0:1, :], trunk_ref[g, 1:2, :]
             real, imag = flows[g]
             head_real = head_real - (r * real - x * imag)
             head_imag = head_imag - (r * imag + x * real)
@@ -208,24 +238,24 @@
 
     heads(0)
     for sweep in range(1, SWEEPS):
-        def again(gs, sweep=sweep):
-            for g in gs:
-                real = head_ref[g, 2 * sweep - 2 : 2 * sweep - 1, :] - drop_ref[g, 0:n, :]
-                imag = head_ref[g, 2 * sweep - 1 : 2 * sweep, :] - drop_ref[g, n:span, :]
-                high, low = split(scaled_volts(swing_ref[g], real, imag))
-                if sweep == SWEEPS - 1:
-                    half = span + EXTRA
-                    row_high = matrix_ref[g, span:half, :]
-                    row_low = matrix_ref[g, half + span :, :]
-                    inject_ref[g] = product(row_high, high) + product(row_low, high) + product(row_high, low)
-                else:
-                    keep(g, apply(matrix_ref[g], high, low))
-
-        sections(again)
+        for index in range(feeders):
+            drop = of(index, 2) if sweep == 1 else again_ref.at[index]
+            real = head_ref[place[index], 2 * sweep - 2 : 2 * sweep - 1, :] - drop[0:n, :]
+            imag = head_ref[place[index], 2 * sweep - 1 : 2 * sweep, :] - drop[n : 2 * n, :]
+            swing = of(index, 1)[...]
+            if sweep < SWEEPS - 1:
+                out = apply(of(index, 0)[...], *split(scaled_volts(swing, real, imag)))
+                again_ref[index] = out[: 2 * n]
+                flow_ref[place[index]] = out[2 * n : 2 * n + 8]
+            else:
+                base = constants(sections[index], n)[2].T
+                active, reactive = base[:, 0:1], base[:, 1:2]
+                inverse = inverse_of(swing, real, imag)
+                flow_ref[place[index], 0:1, :] = jnp.sum(inverse * (active * real + reactive * imag), axis=0, keepdims=True)
+                flow_ref[place[index], 1:2, :] = jnp.sum(inverse * (active * imag - reactive * real), axis=0, keepdims=True)
         heads(sweep)
     for g in range(feeders):
         head_ref[g, 2 * SWEEPS :, :] = jnp.zeros((head_ref.shape[1] - 2 * SWEEPS, width), jnp.float32)
-    own_ref[...] = matrix_ref[place_ref[2]]
 
 
 def drop_rows(matrix_ref, n):
@@ -233,31 +263,29 @@
     return jnp.concatenate([matrix_ref[0 : 2 * n, :], matrix_ref[half : half + 2 * n, :]], axis=0)
 
 
-def first_kernel(pieces, node_ref, matrix_ref, loadings_ref, *refs):
-    piece_refs, (swing_ref, drop_ref, loads, factors_ref, sems) = refs[:pieces], refs[pieces:]
+def first_kernel(
+    node_ref, matrix_ref, loadings_ref, rows_ref, kept_ref, swing_ref, drop_ref, loads, factors_ref, sems
+):
     n = loadings_ref.shape[0]
     width = swing_ref.shape[2]
-    chunks = piece_refs[0].shape[0] // width
-    copies = [
-        pltpu.make_async_copy(loadings_ref, loads, sems.at[0]),
-        pltpu.make_async_copy(piece_refs[0], factors_ref, sems.at[1]),
-    ]
+    pieces = 1 + kept_ref.shape[0]
+    chunks = rows_ref.shape[0] // width
+    copies = [pltpu.make_async_copy(loadings_ref, loads, sems.at[pieces])]
+    for index in range(pieces):
+        piece_ref = kept_ref.at[index - 1] if index else rows_ref
+        copies.append(pltpu.make_async_copy(piece_ref, factors_ref.at[index], sems.at[index]))
     for copy in copies:
         copy.start()
-    matrix = drop_rows(matrix_ref, n)[:, 0:n]
+    matrix = drop_rows(matrix_ref, n)
     copies[0].wait()
     loadings = loads[...]
-    for index in reversed(range(pieces)):
-        piece_ref = piece_refs[index]
-        if index == 0:
-            copies[1].wait()
-            piece_ref = factors_ref
+    for index in range(pieces):
+        copies[1 + index].wait()
         for part in range(chunks):
             chunk = jnp.bitwise_xor(node_ref[0], index) * chunks + part
-            swing = swing_of(loadings, piece_ref[part * width : (part + 1) * width, :])
+            swing = swing_of(loadings, factors_ref[index, part * width : (part + 1) * width, :])
             swing_ref[chunk] = swing
-            high, low = split(swing)
-            drop_ref[chunk] = apply(matrix, high, low)
+            drop_ref[chunk] = apply_real(matrix, swing)
 
 
 def volts_kernel(matrix_ref, swing_ref, drop_ref, head_ref, real_ref, imag_ref, out_ref, sems):
@@ -304,9 +332,18 @@
     f32, bf16 = jnp.float32, jnp.bfloat16
     matrix_rows = 2 * (2 * n + EXTRA)
 
+    held = {0: factors}
+    step = nodes // 2
+    while step >= 1:
+        pairs = [(i, i ^ step) for i in range(nodes)]
+        for offset in list(held):
+            held[offset ^ step] = lax.ppermute(held[offset], "node", pairs)
+        step //= 2
+    pieces = [held[offset] for offset in range(nodes)]
+
     packed = pl.pallas_call(
-        functools.partial(pack_kernel, feeders),
-        out_shape=jax.ShapeDtypeStruct((feeders, n + EXTRA, rank), bf16),
+        pack_kernel,
+        out_shape=jax.ShapeDtypeStruct((n + EXTRA, rank), bf16),
         in_specs=[HBM] * 5,
         out_specs=VMEM,
         scratch_shapes=[
@@ -317,62 +354,85 @@
             pltpu.VMEM((EXTRA, rank), f32),
             pltpu.SemaphoreType.DMA((5,)),
         ],
-        compiler_params=limit(feeders * (n + EXTRA) * rank * 2),
+        compiler_params=limit(2 * (n + EXTRA) * rank * 2),
         name="pack",
     )(*in_hbm(trunk_z.reshape(2), loadings, parents.reshape(1, n), load_base, lateral_z))
-    every = lax.all_to_all(packed, "feeder", 0, 0, tiled=True)
-
-    held = {0: factors}
-    step = nodes // 2
-    while step >= 1:
-        pairs = [(i, i ^ step) for i in range(nodes)]
-        for offset in list(held):
-            held[offset ^ step] = lax.ppermute(held[offset], "node", pairs)
-        step //= 2
-    pieces = [held[offset] for offset in range(nodes)]
+
+    def swap(block, offset):
+        return lax.ppermute(block, "feeder", [(i, i ^ offset) for i in range(feeders)])
+
+    every = {0: packed}
+    for offset in sorted(range(2, feeders, 2), key=lambda o: -(o & -o)):
+        every[offset] = swap(packed, offset)
+    every[1] = swap(packed, 1)
+    slots = list(every)
+    early = len(slots)
+    for offset in slots[1:-1]:
+        every[offset + 1] = swap(every[offset], 1)
+    slots = list(every)
 
     start = (feeder // share) * width
     place = jnp.stack([(start // rows) ^ node, start % rows, feeder])
-    heads, matrix = pl.pallas_call(
-        functools.partial(heads_kernel, feeders, nodes),
-        out_shape=(
-            jax.ShapeDtypeStruct((feeders, 8, width), f32),
+
+    def states(count):
+        return [
+            ((count, matrix_rows, 2 * n), bf16),
+            ((count, n, width), f32),
+            ((count, 2 * n, width), f32),
+            ((count, EXTRA, width), f32),
+        ]
+
+    state_bytes = matrix_rows * 4 * n + (3 * n + EXTRA) * width * 4 + (n + EXTRA) * rank * 2
+    block, own, kept, *started = pl.pallas_call(
+        functools.partial(early_kernel, nodes),
+        out_shape=[
+            jax.ShapeDtypeStruct((width, rank), bf16),
             jax.ShapeDtypeStruct((matrix_rows, 2 * n), bf16),
-        ),
-        in_specs=[SMEM, VMEM, HBM] + [VMEM] * (nodes - 1),
-        out_specs=(VMEM, VMEM),
-        scratch_shapes=[
-            pltpu.VMEM((width, rank), bf16),
-            pltpu.VMEM((feeders, matrix_rows, 2 * n), bf16),
-            pltpu.VMEM((feeders, n, width), f32),
+            pltpu.HBM((nodes - 1, rows, rank), bf16),
+        ]
+        + [jax.ShapeDtypeStruct(*state) for state in states(early)],
+        in_specs=[SMEM, HBM] + [ANY] * (nodes - 1) + [VMEM] * early,
+        out_specs=[VMEM, VMEM, HBM] + [VMEM] * 4,
+        scratch_shapes=[pltpu.SemaphoreType.DMA, pltpu.SemaphoreType.DMA((nodes - 1,))],
+        compiler_params=limit(early * state_bytes),
+        cost_estimate=pl.CostEstimate(flops=early * (1 << 29), bytes_accessed=early * state_bytes, transcendentals=early * n * width),
+        name="early",
+    )(place, *in_hbm(pieces[0]), *pieces[1:], *(every[slot] for slot in slots[:early]))
+    heads = pl.pallas_call(
+        functools.partial(heads_kernel, slots, early),
+        out_shape=jax.ShapeDtypeStruct((feeders, 8, width), f32),
+        in_specs=[SMEM] + [VMEM] * (1 + feeders + 4),
+        out_specs=VMEM,
+        scratch_shapes=[pltpu.VMEM(*state) for state in states(max(feeders - early, 1))]
+        + [
             pltpu.VMEM((feeders, 2 * n, width), f32),
-            pltpu.VMEM((feeders, EXTRA, width), f32),
-            pltpu.SemaphoreType.DMA,
+            pltpu.VMEM((feeders, 8, width), f32),
+            pltpu.VMEM((feeders, 8, width), f32),
         ],
-        compiler_params=limit(feeders * (matrix_rows * 4 * n + 3 * n * width * 4 + EXTRA * width * 4 + (n + EXTRA) * rank * 2)),
+        compiler_params=limit((feeders - early) * state_bytes + feeders * (2 * n + 16) * width * 4),
         name="heads",
-    )(place, every, *in_hbm(pieces[0]), *pieces[1:])
+    )(place, block, *(every[slot] for slot in slots), *started)
     given = lax.all_to_all(heads, "feeder", 0, 0, tiled=True)
     given = given[::share]
 
     chunks = scen // width
     swing, drop = pl.pallas_call(
-        functools.partial(first_kernel, nodes),
+        first_kernel,
         out_shape=(
             jax.ShapeDtypeStruct((chunks, n, width), f32),
             jax.ShapeDtypeStruct((chunks, 2 * n, width), f32),
         ),
-        in_specs=[SMEM, VMEM, HBM, HBM] + [VMEM] * (nodes - 1),
+        in_specs=[SMEM, VMEM, HBM, HBM, HBM],
         out_specs=(VMEM, VMEM),
         scratch_shapes=[
             pltpu.VMEM((n, rank), bf16),
-            pltpu.VMEM((rows, rank), bf16),
-            pltpu.SemaphoreType.DMA((2,)),
+            pltpu.VMEM((nodes, rows, rank), bf16),
+            pltpu.SemaphoreType.DMA((nodes + 1,)),
         ],
         compiler_params=limit(3 * n * scen * 4 + scen * rank * 2),
         cost_estimate=pl.CostEstimate(flops=2 * scen * n * rank * 4, bytes_accessed=3 * n * scen * 4, transcendentals=scen * n),
         name="first",
-    )(node.reshape(1), matrix, *in_hbm(loadings, pieces[0]), *pieces[1:])
+    )(node.reshape(1), own, *in_hbm(loadings, factors, kept))
     return pl.pallas_call(
         volts_kernel,
         out_shape=(
@@ -384,7 +444,7 @@
         scratch_shapes=[pltpu.VMEM((2, scen, n), f32), pltpu.SemaphoreType.DMA((2, chunks))],
         compiler_params=limit(5 * n * scen * 4),
         name="volts",
-    )(matrix, swing, drop, given)
+    )(own, swing, drop, given)
 
 
 def solution(mesh):

time: 47.1 us -> 50.1 us (1.064)
  starting transfers between devices: 12.2 us -> 17.1 us
  local copies, waits for them, and re-layouts: 2.85 us -> 0 us
  Pallas kernels: 15.4 us -> 17.1 us
    ppermute x0 -> x7, starting transfers between devices: none -> 8.87 us  [swap(): lax.ppermute(block, 'feeder', [(i, i ^ offset) for i in range(feeders)])]
    all_to_all x1 -> x0, starting transfers between devices: 7.26 us -> none  [local(): every = lax.all_to_all(packed, 'feeder', 0, 0, tiled=True)]
    all_to_all x1 -> x0, waiting for transfers between devices: 6.37 us -> none  [local(): every = lax.all_to_all(packed, 'feeder', 0, 0, tiled=True)]
    ppermute x0 -> x7, waiting for transfers between devices: none -> 4.63 us  [swap(): lax.ppermute(block, 'feeder', [(i, i ^ offset) for i in range(feeders)])]
    unnamed x12 -> x0, local copies, waits for them, and re-layouts: 2.85 us -> none
    all_to_all x1, waiting for transfers between devices: 1.16 us -> 3.78 us  [local(): given = lax.all_to_all(heads, 'feeder', 0, 0, tiled=True)]
    all_to_all x1, starting transfers between devices: 3.36 us -> 5.18 us  [local(): given = lax.all_to_all(heads, 'feeder', 0, 0, tiled=True)]
    pallas_call x3 -> x4, Pallas kernels: 12.3 us -> 13.9 us  [the longest x1 5.66 us: local(): pl.pallas_call(functools.partial(heads_kernel, slots, early), out_shape=j...]
  transfers between devices with their start and end apart: 5 -> 11, of which waited for: 4 -> 5; matrix products, arithmetic and copies ran while one was open for 0% -> 0% of each run, Pallas kernels for 6% -> 17%
where the time goes in v5:
time: 50.1 us; the launch traced here: 49.9 us
  starting transfers between devices  17.1 us (34%)
  Pallas kernels  17.1 us (34%)
  waiting for transfers between devices  14.9 us (30%)
  between operations  0.69 us (1%)
    ppermute x7, starting transfers between devices, swap(): lax.ppermute(block, 'feeder', [(i, i ^ offset) for i in range(feeders)])  8.87 us
    ppermute x3, waiting for transfers between devices, local(): held[offset ^ step] = lax.ppermute(held[offset], 'node', pairs)  6.52 us
    pallas_call x1, Pallas kernels, local(): pl.pallas_call(functools.partial(heads_kernel, slots, early), out_shape=j...  5.66 us
    all_to_all x1, starting transfers between devices, local(): given = lax.all_to_all(heads, 'feeder', 0, 0, tiled=True)  5.18 us
    ppermute x7, waiting for transfers between devices, swap(): lax.ppermute(block, 'feeder', [(i, i ^ offset) for i in range(feeders)])  4.63 us
    pallas_call x1, Pallas kernels, local(): pl.pallas_call(functools.partial(early_kernel, nodes), out_shape=[jax.Sha...  4.28 us
    all_to_all x1, waiting for transfers between devices, local(): given = lax.all_to_all(heads, 'feeder', 0, 0, tiled=True)  3.78 us
    pallas_call x1, Pallas kernels, local(): pl.pallas_call(volts_kernel, out_shape=(jax.ShapeDtypeStruct((scen, n), f...  3.14 us
  transfers between devices with their start and end apart: 11, of which 5 were waited for; matrix products, arithmetic and copies ran while one was open for 0% of the time, Pallas kernels for 17%

profile of v5, /device:TPU:0, one launch (start us, length us, event | category | flops | bytes accessed | tf_op | source)
XLA Modules:
  0.0 49.9 jit_solution(14449849612998805235)
XLA Ops:
  0.6 3.0 %collective-permute-start.1 = (bf16[512,256]{1,0:T(8,128)(2,1)}, bf16[512,256]{1,0:T(8,128)(2,1)S(1)}, u32[]{:S(2)}, u32[]{:S(2)}) collective-permute-start(bf16[512,256]{1,0:T(8,128)(2,1)} %rows_ref.1), channel_id=1, source_target_pairs={{0,2},{1,3},{2,0},{3,1},{4,6},{5,7},{6,4},{7,5},{8,10},{9,11},{10,... | collective-permute-start | bytes 786440 | tf_op jit(solution)/shard_map/ppermute | solution.py:340
  3.7 6.5 %collective-permute-done.1.refs_2_ = bf16[512,256]{1,0:T(8,128)(2,1)S(1)} collective-permute-done((bf16[512,256]{1,0:T(8,128)(2,1)}, bf16[512,256]{1,0:T(8,128)(2,1)S(1)}, u32[]{:S(2)}, u32[]{:S(2)}) %collective-permute-start.1) | collective-permute-done | bytes 262176 | tf_op jit(solution)/shard_map/ppermute | solution.py:340
  10.2 0.9 %pack.1.refs_4_.refs_0_ = bf16[144,256]{1,0:T(8,128)(2,1)S(1)} custom-call(f32[2]{0:T(128)} %bitcast.6, bf16[128,256]{1,0:T(8,128)(2,1)} %loadings_ref.3, s32[1,128]{1,0:T(1,128)} %bitcast.7, f32[2,128]{1,0:T(2,128)} %base_ref.1, f32[2,128]{1,0:T(2,128)} %z_ref.1), custom_call_target="tpu_custom_call" | custom-call | tf_op jit(solution)/shard_map/pack/pallas_call | solution.py:344
  11.1 2.9 %collective-permute-start.3 = (bf16[144,256]{1,0:T(8,128)(2,1)S(1)}, bf16[144,256]{1,0:T(8,128)(2,1)S(1)}, u32[]{:S(2)}, u32[]{:S(2)}) collective-permute-start(bf16[144,256]{1,0:T(8,128)(2,1)S(1)} %pack.1.refs_4_.refs_0_), channel_id=1, source_target_pairs={{0,16},{4,20},{8,24},{12,28},{16,0},{20,4},{24,8},{28,12},{1,17},{... | collective-permute-start | bytes 221192 | tf_op jit(solution)/shard_map/ppermute | solution.py:362
  14.0 1.6 %collective-permute-start.4 = (bf16[144,256]{1,0:T(8,128)(2,1)S(1)}, bf16[144,256]{1,0:T(8,128)(2,1)S(1)}, u32[]{:S(2)}, u32[]{:S(2)}) collective-permute-start(bf16[144,256]{1,0:T(8,128)(2,1)S(1)} %pack.1.refs_4_.refs_0_), channel_id=1, source_target_pairs={{0,8},{4,12},{8,0},{12,4},{16,24},{20,28},{24,16},{28,20},{1,9},{5... | collective-permute-start | bytes 221192 | tf_op jit(solution)/shard_map/ppermute | solution.py:362
  15.5 0.0 collective-permute-start.5
  15.5 3.2 %collective-permute-done.3.refs_5_.refs_1_ = bf16[144,256]{1,0:T(8,128)(2,1)S(1)} collective-permute-done((bf16[144,256]{1,0:T(8,128)(2,1)S(1)}, bf16[144,256]{1,0:T(8,128)(2,1)S(1)}, u32[]{:S(2)}, u32[]{:S(2)}) %collective-permute-start.3) | collective-permute-done | bytes 73760 | tf_op jit(solution)/shard_map/ppermute | solution.py:362
  18.8 1.5 %collective-permute-start.6 = (bf16[144,256]{1,0:T(8,128)(2,1)S(1)}, bf16[144,256]{1,0:T(8,128)(2,1)S(1)}, u32[]{:S(2)}, u32[]{:S(2)}) collective-permute-start(bf16[144,256]{1,0:T(8,128)(2,1)S(1)} %pack.1.refs_4_.refs_0_), channel_id=1, source_target_pairs={{0,4},{4,0},{8,12},{12,8},{16,20},{20,16},{24,28},{28,24},{1,5},{5... | collective-permute-start | bytes 221192 | tf_op jit(solution)/shard_map/ppermute | solution.py:362
  20.3 0.1 pad_add_fusion.place_ref
  20.4 0.0 collective-permute-done.4.refs_6_.refs_2_
  20.4 0.5 %collective-permute-start.7 = (bf16[144,256]{1,0:T(8,128)(2,1)S(1)}, bf16[144,256]{1,0:T(8,128)(2,1)S(1)}, u32[]{:S(2)}, u32[]{:S(2)}) collective-permute-start(bf16[144,256]{1,0:T(8,128)(2,1)S(1)} %collective-permute-done.3.refs_5_.refs_1_), channel_id=1, source_target_pairs={{0,4},{4,0},{8,12},{12,8},{16,20},{20,16},{24,28},{28,24},{1,5},{5... | collective-permute-start | bytes 221192 | tf_op jit(solution)/shard_map/ppermute | solution.py:362
  20.9 0.8 %collective-permute-done.5.refs_7_.refs_3_ = bf16[144,256]{1,0:T(8,128)(2,1)S(1)} collective-permute-done((bf16[144,256]{1,0:T(8,128)(2,1)S(1)}, bf16[144,256]{1,0:T(8,128)(2,1)S(1)}, u32[]{:S(2)}, u32[]{:S(2)}) %collective-permute-start.5) | collective-permute-done | bytes 73760 | tf_op jit(solution)/shard_map/ppermute | solution.py:362
  21.7 1.5 %collective-permute-start.8 = (bf16[144,256]{1,0:T(8,128)(2,1)S(1)}, bf16[144,256]{1,0:T(8,128)(2,1)S(1)}, u32[]{:S(2)}, u32[]{:S(2)}) collective-permute-start(bf16[144,256]{1,0:T(8,128)(2,1)S(1)} %collective-permute-done.4.refs_6_.refs_2_), channel_id=1, source_target_pairs={{0,4},{4,0},{8,12},{12,8},{16,20},{20,16},{24,28},{28,24},{1,5},{5... | collective-permute-start | bytes 221192 | tf_op jit(solution)/shard_map/ppermute | solution.py:362
  23.2 0.6 %collective-permute-done.6.refs_8_.refs_4_ = bf16[144,256]{1,0:T(8,128)(2,1)S(1)} collective-permute-done((bf16[144,256]{1,0:T(8,128)(2,1)S(1)}, bf16[144,256]{1,0:T(8,128)(2,1)S(1)}, u32[]{:S(2)}, u32[]{:S(2)}) %collective-permute-start.6) | collective-permute-done | bytes 73760 | tf_op jit(solution)/shard_map/ppermute | solution.py:362
  23.8 0.9 %collective-permute-start.9 = (bf16[144,256]{1,0:T(8,128)(2,1)S(1)}, bf16[144,256]{1,0:T(8,128)(2,1)S(1)}, u32[]{:S(2)}, u32[]{:S(2)}) collective-permute-start(bf16[144,256]{1,0:T(8,128)(2,1)S(1)} %collective-permute-done.5.refs_7_.refs_3_), channel_id=1, source_target_pairs={{0,4},{4,0},{8,12},{12,8},{16,20},{20,16},{24,28},{28,24},{1,5},{5... | collective-permute-start | bytes 221192 | tf_op jit(solution)/shard_map/ppermute | solution.py:362
  24.7 0.0 collective-permute-done.refs_1_
  24.7 0.0 collective-permute-done.2.refs_3_
  24.7 4.3 %early.1 = (bf16[256,256]{1,0:T(8,128)(2,1)S(1)}, bf16[544,256]{1,0:T(8,128)(2,1)S(1)}, bf16[3,512,256]{2,1,0:T(8,128)(2,1)}, bf16[5,544,256]{2,1,0:T(8,128)(2,1...) custom-call(s32[3]{0:T(128)S(1)} %pad_add_fusion.place_ref, ...), custom_call_target="tpu_custom_call" | custom-call | flops 2684354560 | bytes 3809280 | tf_op jit(solution)/shard_map/early/pallas_call | solution.py:386
  29.0 0.0 collective-permute-done.7.refs_5_
  29.0 5.7 %heads.1 = f32[8,8,256]{2,1,0:T(8,128)} custom-call(s32[3]{0:T(128)S(1)} %pad_add_fusion.place_ref, bf16[256,256]{1,0:T(8,128)(2,1)S(1)} %get-tuple-element.15.factors_ref, bf16[144,256]{1,0:T(8,128)(2,1)S(1)} %pack.1.refs_4_.refs_0_, bf16[144,256]{1,0:T(8,128)(2,1)S(1)} %collective-permute-done.3.refs_5_.refs_1_, ...), custom_call_target="tpu_custom_call" | custom-call | tf_op jit(solution)/shard_map/heads/pallas_call | solution.py:401
  34.6 5.2 %all-to-all-start = ((f32[8,8,256]{2,1,0:T(8,128)}), f32[8,8,256]{2,1,0:T(8,128)S(1)}, u32[]{:S(2)}, u32[]{:S(2)}) async-start(f32[8,8,256]{2,1,0:T(8,128)} %heads.1), calls=%async_computation | async-start | bytes 131072 | tf_op jit(solution)/shard_map/all_to_all | solution.py:415
  39.8 3.1 %first.1 = (f32[8,128,256]{2,1,0:T(8,128)S(1)}, f32[8,256,256]{2,1,0:T(8,128)S(1)}) custom-call(s32[1]{0:T(128)} %bitcast.5.node_ref, bf16[544,256]{1,0:T(8,128)(2,1)S(1)} %get-tuple-element.11.matrix_ref, bf16[128,256]{1,0:T(8,128)(2,1)} %loadings_ref.3, bf16[512,256]{1,0:T(8,128)(2,1)} %rows_ref.1, bf16[3,512,256]{2,1,0:T(8,128)(2,1)} %get-tuple-element.12.kept_ref), custom_call_target="tpu_custom_call" | custom-call | flops 536870912 | bytes 3145728 | tf_op jit(solution)/shard_map/first/pallas_call | solution.py:419
  42.9 3.8 %all-to-all-done.head_ref = f32[8,8,256]{2,1,0:T(8,128)S(1)} async-done(((f32[8,8,256]{2,1,0:T(8,128)}), f32[8,8,256]{2,1,0:T(8,128)S(1)}, u32[]{:S(2)}, u32[]{:S(2)}) %all-to-all-start) | async-done | bytes 65568 | tf_op jit(solution)/shard_map/all_to_all | solution.py:415
  46.7 3.1 %volts.1 = (f32[2048,128]{1,0:T(8,128)}, f32[2048,128]{1,0:T(8,128)}) custom-call(bf16[544,256]{1,0:T(8,128)(2,1)S(1)} %get-tuple-element.11.matrix_ref, f32[8,128,256]{2,1,0:T(8,128)S(1)} %get-tuple-element.13.swing_ref, f32[8,256,256]{2,1,0:T(8,128)S(1)} %get-tuple-element.14.drop_ref, f32[8,8,256]{2,1,0:T(8,128)S(1)} %all-to-all-done.head_ref), custom_call_target="tpu_custom_call" | custom-call | tf_op jit(solution)/shard_map/volts/pallas_call | solution.py:436
  (4 shorter events, 0.0 us)
Async XLA Ops:
  0.6 9.6 %collective-permute-start.1 = (bf16[512,256]{1,0:T(8,128)(2,1)}, bf16[512,256]{1,0:T(8,128)(2,1)S(1)}, u32[]{:S(2)}, u32[]{:S(2)}) collective-permute-start(bf16[512,256]{1,0:T(8,128)(2,1)} %rows_ref.1), channel_id=1, source_target_pairs={{0,2},{1,3},{2,0},{3,1},{4,6},{5,7},{6,4},{7,5},{8,10},{9,11},{10,... | collective-permute-start | bytes 786440 | tf_op jit(solution)/shard_map/ppermute | solution.py:340
  3.7 21.0 %collective-permute-start = (bf16[512,256]{1,0:T(8,128)(2,1)}, bf16[512,256]{1,0:T(8,128)(2,1)S(1)}, u32[]{:S(2)}, u32[]{:S(2)}) collective-permute-start(bf16[512,256]{1,0:T(8,128)(2,1)} %rows_ref.1), channel_id=1, source_target_pairs={{0,1},{1,0},{2,3},{3,2},{4,5},{5,4},{6,7},{7,6},{8,9},{9,8},{10,11... | collective-permute-start | bytes 786440 | tf_op jit(solution)/shard_map/ppermute | solution.py:340
  10.2 14.5 %collective-permute-start.2 = (bf16[512,256]{1,0:T(8,128)(2,1)S(1)}, bf16[512,256]{1,0:T(8,128)(2,1)S(1)}, u32[]{:S(2)}, u32[]{:S(2)}) collective-permute-start(bf16[512,256]{1,0:T(8,128)(2,1)S(1)} %collective-permute-done.1.refs_2_), channel_id=1, source_target_pairs={{0,1},{1,0},{2,3},{3,2},{4,5},{5,4},{6,7},{7,6},{8,9},{9,8},{10,11... | collective-permute-start | bytes 786440 | tf_op jit(solution)/shard_map/ppermute | solution.py:340
  11.1 7.7 %collective-permute-start.3 = (bf16[144,256]{1,0:T(8,128)(2,1)S(1)}, bf16[144,256]{1,0:T(8,128)(2,1)S(1)}, u32[]{:S(2)}, u32[]{:S(2)}) collective-permute-start(bf16[144,256]{1,0:T(8,128)(2,1)S(1)} %pack.1.refs_4_.refs_0_), channel_id=1, source_target_pairs={{0,16},{4,20},{8,24},{12,28},{16,0},{20,4},{24,8},{28,12},{1,17},{... | collective-permute-start | bytes 221192 | tf_op jit(solution)/shard_map/ppermute | solution.py:362
  14.0 6.4 %collective-permute-start.4 = (bf16[144,256]{1,0:T(8,128)(2,1)S(1)}, bf16[144,256]{1,0:T(8,128)(2,1)S(1)}, u32[]{:S(2)}, u32[]{:S(2)}) collective-permute-start(bf16[144,256]{1,0:T(8,128)(2,1)S(1)} %pack.1.refs_4_.refs_0_), channel_id=1, source_target_pairs={{0,8},{4,12},{8,0},{12,4},{16,24},{20,28},{24,16},{28,20},{1,9},{5... | collective-permute-start | bytes 221192 | tf_op jit(solution)/shard_map/ppermute | solution.py:362
  15.5 6.2 %collective-permute-start.5 = (bf16[144,256]{1,0:T(8,128)(2,1)S(1)}, bf16[144,256]{1,0:T(8,128)(2,1)S(1)}, u32[]{:S(2)}, u32[]{:S(2)}) collective-permute-start(bf16[144,256]{1,0:T(8,128)(2,1)S(1)} %pack.1.refs_4_.refs_0_), channel_id=1, source_target_pairs={{0,24},{4,28},{8,16},{12,20},{16,8},{20,12},{24,0},{28,4},{1,25},{... | collective-permute-start | bytes 221192 | tf_op jit(solution)/shard_map/ppermute | solution.py:362
  18.8 5.0 %collective-permute-start.6 = (bf16[144,256]{1,0:T(8,128)(2,1)S(1)}, bf16[144,256]{1,0:T(8,128)(2,1)S(1)}, u32[]{:S(2)}, u32[]{:S(2)}) collective-permute-start(bf16[144,256]{1,0:T(8,128)(2,1)S(1)} %pack.1.refs_4_.refs_0_), channel_id=1, source_target_pairs={{0,4},{4,0},{8,12},{12,8},{16,20},{20,16},{24,28},{28,24},{1,5},{5... | collective-permute-start | bytes 221192 | tf_op jit(solution)/shard_map/ppermute | solution.py:362
  20.4 8.6 %collective-permute-start.7 = (bf16[144,256]{1,0:T(8,128)(2,1)S(1)}, bf16[144,256]{1,0:T(8,128)(2,1)S(1)}, u32[]{:S(2)}, u32[]{:S(2)}) collective-permute-start(bf16[144,256]{1,0:T(8,128)(2,1)S(1)} %collective-permute-done.3.refs_5_.refs_1_), channel_id=1, source_target_pairs={{0,4},{4,0},{8,12},{12,8},{16,20},{20,16},{24,28},{28,24},{1,5},{5... | collective-permute-start | bytes 221192 | tf_op jit(solution)/shard_map/ppermute | solution.py:362
  21.7 7.3 %collective-permute-start.8 = (bf16[144,256]{1,0:T(8,128)(2,1)S(1)}, bf16[144,256]{1,0:T(8,128)(2,1)S(1)}, u32[]{:S(2)}, u32[]{:S(2)}) collective-permute-start(bf16[144,256]{1,0:T(8,128)(2,1)S(1)} %collective-permute-done.4.refs_6_.refs_2_), channel_id=1, source_target_pairs={{0,4},{4,0},{8,12},{12,8},{16,20},{20,16},{24,28},{28,24},{1,5},{5... | collective-permute-start | bytes 221192 | tf_op jit(solution)/shard_map/ppermute | solution.py:362
  23.8 5.2 %collective-permute-start.9 = (bf16[144,256]{1,0:T(8,128)(2,1)S(1)}, bf16[144,256]{1,0:T(8,128)(2,1)S(1)}, u32[]{:S(2)}, u32[]{:S(2)}) collective-permute-start(bf16[144,256]{1,0:T(8,128)(2,1)S(1)} %collective-permute-done.5.refs_7_.refs_3_), channel_id=1, source_target_pairs={{0,4},{4,0},{8,12},{12,8},{16,20},{20,16},{24,28},{28,24},{1,5},{5... | collective-permute-start | bytes 221192 | tf_op jit(solution)/shard_map/ppermute | solution.py:362
  34.6 12.1 %all-to-all-start = ((f32[8,8,256]{2,1,0:T(8,128)}), f32[8,8,256]{2,1,0:T(8,128)S(1)}, u32[]{:S(2)}, u32[]{:S(2)}) async-start(f32[8,8,256]{2,1,0:T(8,128)} %heads.1), calls=%async_computation | async-start | bytes 131072 | tf_op jit(solution)/shard_map/all_to_all | solution.py:415

commit v6 on v5

--- a/solution.py
+++ b/solution.py
@@ -121,7 +121,7 @@
 
         out.append(
             jnp.concatenate(
-                [whole(real_high, imag_high, sums_high), whole(real_low, imag_low, sums_low)], axis=0
+                [whole(real_high, imag_high, sums_high), whole(real_low, imag_low, sums_low)], axis=1
             )
         )
     return out
@@ -132,28 +132,25 @@
     return 1.0 + 0.5 * jnp.tanh(level)
 
 
-def apply(matrix, high, low):
-    half = matrix.shape[0] // 2
-    first = product(matrix, high)
-    return first[:half] + first[half:] + product(matrix[:half], low)
+def apply(matrix, u):
+    span = matrix.shape[1] // 2
+    high, low = split(u)
+    left = jnp.concatenate([matrix, matrix[:, :span]], axis=1)
+    return product(left, jnp.concatenate([high, high, low], axis=0))
 
 
 def apply_real(matrix, real):
-    half, n = matrix.shape[0] // 2, matrix.shape[1] // 2
-    high_part, low_part = matrix[:half, :n], matrix[half:, :n]
-    left = jnp.concatenate(
-        [
-            jnp.concatenate([high_part, high_part], axis=1),
-            jnp.concatenate([low_part, jnp.zeros_like(low_part)], axis=1),
-        ],
-        axis=0,
-    )
-    out = product(left, jnp.concatenate(split(real), axis=0))
-    return out[:half] + out[half:]
+    n = matrix.shape[1] // 4
+    high, low = split(real)
+    high_part, low_part = matrix[:, :n], matrix[:, 2 * n : 3 * n]
+    left = jnp.concatenate([high_part, low_part, high_part], axis=1)
+    return product(left, jnp.concatenate([high, high, low], axis=0))
 
 
 def inverse_of(swing, real, imag):
-    return swing / (real * real + imag * imag)
+    square = real * real + imag * imag
+    guess = pl.reciprocal(square, approx=True)
+    return swing * (guess * (2.0 - square * guess))
 
 
 def scaled_volts(swing, real, imag):
@@ -161,12 +158,13 @@
     return jnp.concatenate([real * inverse, imag * inverse], axis=0)
 
 
-def first_sweep(sections, factors, matrix_ref, swing_ref, drop_ref, inject_ref):
+def first_sweep(sections, factors_of, matrix_ref, swing_ref, drop_ref, inject_ref):
     n = swing_ref.shape[1]
     for start in range(0, len(sections), 8):
         group = sections[start : start + 8]
         for slot, matrix in enumerate(section_matrices(group, n), start):
             matrix_ref[slot] = matrix
+        factors = factors_of(start)
         for slot, section in enumerate(group, start):
             swing = swing_of(section[0:n, :], factors)
             swing_ref[slot] = swing
@@ -190,10 +188,14 @@
         @pl.when(piece == index)
         def _(piece_ref=piece_ref):
             rows = piece_ref.at[pl.ds(pl.multiple_of(offset, width), width), :]
-            copy = pltpu.make_async_copy(rows, factors_ref, sem)
-            copy.start()
-            copy.wait()
-    first_sweep(sections, factors_ref[...], matrix_ref, swing_ref, drop_ref, inject_ref)
+            pltpu.make_async_copy(rows, factors_ref, sem).start()
+
+    def factors_of(start):
+        if start == 0:
+            pltpu.make_async_copy(piece_refs[0].at[0:width, :], factors_ref, sem).wait()
+        return factors_ref[...]
+
+    first_sweep(sections, factors_of, matrix_ref, swing_ref, drop_ref, inject_ref)
     own_ref[...] = matrix_ref[0]
     for copy in keeps:
         copy.wait()
@@ -206,7 +208,7 @@
     head_ref, matrix_ref, swing_ref, drop_ref, inject_ref, again_ref, flow_ref, trunk_ref = refs[feeders + 4 :]
     width = factors_ref.shape[0]
     n = swing_ref.shape[1]
-    first_sweep(sections[early:], factors_ref[...], matrix_ref, swing_ref, drop_ref, inject_ref)
+    first_sweep(sections[early:], lambda start: factors_ref[...], matrix_ref, swing_ref, drop_ref, inject_ref)
     late_refs = (matrix_ref, swing_ref, drop_ref, inject_ref)
     place = [jnp.bitwise_xor(place_ref[2], slot) for slot in slots]
 
@@ -244,7 +246,7 @@
             imag = head_ref[place[index], 2 * sweep - 1 : 2 * sweep, :] - drop[n : 2 * n, :]
             swing = of(index, 1)[...]
             if sweep < SWEEPS - 1:
-                out = apply(of(index, 0)[...], *split(scaled_volts(swing, real, imag)))
+                out = apply(of(index, 0)[...], scaled_volts(swing, real, imag))
                 again_ref[index] = out[: 2 * n]
                 flow_ref[place[index]] = out[2 * n : 2 * n + 8]
             else:
@@ -256,11 +258,6 @@
         heads(sweep)
     for g in range(feeders):
         head_ref[g, 2 * SWEEPS :, :] = jnp.zeros((head_ref.shape[1] - 2 * SWEEPS, width), jnp.float32)
-
-
-def drop_rows(matrix_ref, n):
-    half = matrix_ref.shape[0] // 2
-    return jnp.concatenate([matrix_ref[0 : 2 * n, :], matrix_ref[half : half + 2 * n, :]], axis=0)
 
 
 def first_kernel(
@@ -276,7 +273,7 @@
         copies.append(pltpu.make_async_copy(piece_ref, factors_ref.at[index], sems.at[index]))
     for copy in copies:
         copy.start()
-    matrix = drop_rows(matrix_ref, n)
+    matrix = matrix_ref[0 : 2 * n, :]
     copies[0].wait()
     loadings = loads[...]
     for index in range(pieces):
@@ -291,7 +288,7 @@
 def volts_kernel(matrix_ref, swing_ref, drop_ref, head_ref, real_ref, imag_ref, out_ref, sems):
     n = swing_ref.shape[1]
     chunks, width = swing_ref.shape[0], swing_ref.shape[2]
-    matrix = drop_rows(matrix_ref, n)
+    matrix = matrix_ref[0 : 2 * n, :]
     drops = [None] * chunks
     copies = []
     for sweep in range(SWEEPS):
@@ -300,8 +297,7 @@
             real = head_ref[chunk, 2 * sweep : 2 * sweep + 1, :] - drop[:n]
             imag = head_ref[chunk, 2 * sweep + 1 : 2 * sweep + 2, :] - drop[n:]
             if sweep < SWEEPS - 1:
-                high, low = split(scaled_volts(swing_ref[chunk], real, imag))
-                drops[chunk] = apply(matrix, high, low)
+                drops[chunk] = apply(matrix, scaled_volts(swing_ref[chunk], real, imag))
             else:
                 rows = slice(chunk * width, (chunk + 1) * width)
                 for index, (part, to_ref) in enumerate(((real, real_ref), (imag, imag_ref))):
@@ -313,6 +309,21 @@
         copy.wait()
 
 
+def after_kernel(*refs):
+    del refs
+
+
+def after(array, *others):
+    return pl.pallas_call(
+        after_kernel,
+        out_shape=jax.ShapeDtypeStruct(array.shape, array.dtype),
+        in_specs=[ANY] * (1 + len(others)),
+        out_specs=ANY,
+        input_output_aliases={0: 0},
+        name="after",
+    )(array, *others)
+
+
 def in_hbm(*arrays):
     return [pltpu.with_memory_space_constraint(array, pltpu.HBM) for array in arrays]
 
@@ -330,16 +341,15 @@
     width = max(scen // feeders, LANES)
     share = feeders * width // scen
     f32, bf16 = jnp.float32, jnp.bfloat16
-    matrix_rows = 2 * (2 * n + EXTRA)
+    matrix_shape = (2 * n + EXTRA, 4 * n)
+
+    def trade(block, offset):
+        return lax.ppermute(block, "node", [(i, i ^ offset) for i in range(nodes)])
 
     held = {0: factors}
-    step = nodes // 2
-    while step >= 1:
-        pairs = [(i, i ^ step) for i in range(nodes)]
-        for offset in list(held):
-            held[offset ^ step] = lax.ppermute(held[offset], "node", pairs)
-        step //= 2
-    pieces = [held[offset] for offset in range(nodes)]
+    far = nodes // 2
+    if far:
+        held[far] = trade(factors, far)
 
     packed = pl.pallas_call(
         pack_kernel,
@@ -371,23 +381,32 @@
         every[offset + 1] = swap(every[offset], 1)
     slots = list(every)
 
+    if far:
+        held[far] = after(held[far], *(every[slot] for slot in slots[:early]))
+    step = far // 2
+    while step >= 1:
+        for offset in list(held):
+            held[offset ^ step] = trade(held[offset], step)
+        step //= 2
+    pieces = [held[offset] for offset in range(nodes)]
+
     start = (feeder // share) * width
     place = jnp.stack([(start // rows) ^ node, start % rows, feeder])
 
     def states(count):
         return [
-            ((count, matrix_rows, 2 * n), bf16),
+            ((count, *matrix_shape), bf16),
             ((count, n, width), f32),
             ((count, 2 * n, width), f32),
             ((count, EXTRA, width), f32),
         ]
 
-    state_bytes = matrix_rows * 4 * n + (3 * n + EXTRA) * width * 4 + (n + EXTRA) * rank * 2
+    state_bytes = (2 * n + EXTRA) * 8 * n + (3 * n + EXTRA) * width * 4 + (n + EXTRA) * rank * 2
     block, own, kept, *started = pl.pallas_call(
         functools.partial(early_kernel, nodes),
         out_shape=[
             jax.ShapeDtypeStruct((width, rank), bf16),
-            jax.ShapeDtypeStruct((matrix_rows, 2 * n), bf16),
+            jax.ShapeDtypeStruct(matrix_shape, bf16),
             pltpu.HBM((nodes - 1, rows, rank), bf16),
         ]
         + [jax.ShapeDtypeStruct(*state) for state in states(early)],

time: 50.1 us -> 49.1 us (0.980)
  local copies, waits for them, and re-layouts: 0 us -> 6.71 us
  waiting for transfers between devices: 14.9 us -> 8.2 us
  starting transfers between devices: 17.1 us -> 16.2 us
    unnamed x0 -> x34, local copies, waits for them, and re-layouts: none -> 6.71 us
    ppermute x3, waiting for transfers between devices: 6.52 us -> 0.01 us  [trade(): return lax.ppermute(block, 'node', [(i, i ^ offset) for i in range(nodes)])]
    all_to_all x1, starting transfers between devices: 5.18 us -> 3.67 us  [local(): given = lax.all_to_all(heads, 'feeder', 0, 0, tiled=True)]
    pallas_call x1, Pallas kernels: 4.28 us -> 3.54 us  [local(): pl.pallas_call(functools.partial(early_kernel, nodes), out_shape=[jax.Sha...]
    ppermute x7, starting transfers between devices: 8.87 us -> 9.46 us  [swap(): lax.ppermute(block, 'feeder', [(i, i ^ offset) for i in range(feeders)])]
  transfers between devices with their start and end apart: 11 -> 11, of which waited for: 5 -> 3; matrix products, arithmetic and copies ran while one was open for 0% -> 0% of each run, Pallas kernels for 17% -> 16%
where the time goes in v6:
time: 49.1 us; the launch traced here: 48.6 us
  Pallas kernels  16.6 us (34%)
  starting transfers between devices  16.2 us (33%)
  waiting for transfers between devices  8.2 us (17%)
  local copies, waits for them, and re-layouts  6.71 us (14%)
  between operations  0.79 us (2%)
    ppermute x7, starting transfers between devices, swap(): lax.ppermute(block, 'feeder', [(i, i ^ offset) for i in range(feeders)])  9.46 us
    unnamed x34, local copies, waits for them, and re-layouts  6.71 us
    pallas_call x1, Pallas kernels, local(): pl.pallas_call(functools.partial(heads_kernel, slots, early), out_shape=j...  5.72 us
    ppermute x7, waiting for transfers between devices, swap(): lax.ppermute(block, 'feeder', [(i, i ^ offset) for i in range(feeders)])  4.44 us
    all_to_all x1, waiting for transfers between devices, local(): given = lax.all_to_all(heads, 'feeder', 0, 0, tiled=True)  3.76 us
    all_to_all x1, starting transfers between devices, local(): given = lax.all_to_all(heads, 'feeder', 0, 0, tiled=True)  3.67 us
    pallas_call x1, Pallas kernels, local(): pl.pallas_call(functools.partial(early_kernel, nodes), out_shape=[jax.Sha...  3.54 us
    pallas_call x1, Pallas kernels, local(): pl.pallas_call(volts_kernel, out_shape=(jax.ShapeDtypeStruct((scen, n), f...  3.32 us
  transfers between devices with their start and end apart: 11, of which 3 were waited for; matrix products, arithmetic and copies ran while one was open for 0% of the time, Pallas kernels for 16%

profile of v6, /device:TPU:0, one launch (start us, length us, event | category | flops | bytes accessed | tf_op | source)
XLA Modules:
  0.0 48.6 jit_solution(761180483206743604)
XLA Ops:
  0.6 3.0 %collective-permute-start.1 = (bf16[512,256]{1,0:T(8,128)(2,1)}, bf16[512,256]{1,0:T(8,128)(2,1)S(1)}, u32[]{:S(2)}, u32[]{:S(2)}) collective-permute-start(bf16[512,256]{1,0:T(8,128)(2,1)} %rows_ref.1), channel_id=1, source_target_pairs={{0,2},{1,3},{2,0},{3,1},{4,6},{5,7},{6,4},{7,5},{8,10},{9,11},{10,... | collective-permute-start | bytes 786440 | tf_op jit(solution)/shard_map/ppermute | solution.py:347
  3.7 0.9 %pack.1.refs_1_.refs_4_.refs_0_ = bf16[144,256]{1,0:T(8,128)(2,1)S(1)} custom-call(f32[2]{0:T(128)} %bitcast.6, bf16[128,256]{1,0:T(8,128)(2,1)} %loadings_ref.3, s32[1,128]{1,0:T(1,128)} %bitcast.7, f32[2,128]{1,0:T(2,128)} %base_ref.1, f32[2,128]{1,0:T(2,128)} %z_ref.1), custom_call_target="tpu_custom_call" | custom-call | tf_op jit(solution)/shard_map/pack/pallas_call | solution.py:354
  4.6 2.7 %collective-permute-start.2 = (bf16[144,256]{1,0:T(8,128)(2,1)S(1)}, bf16[144,256]{1,0:T(8,128)(2,1)S(1)}, u32[]{:S(2)}, u32[]{:S(2)}) collective-permute-start(bf16[144,256]{1,0:T(8,128)(2,1)S(1)} %pack.1.refs_1_.refs_4_.refs_0_), channel_id=1, source_target_pairs={{0,16},{4,20},{8,24},{12,28},{16,0},{20,4},{24,8},{28,12},{1,17},{... | collective-permute-start | bytes 221192 | tf_op jit(solution)/shard_map/ppermute | solution.py:372
  7.2 1.6 %collective-permute-start.3 = (bf16[144,256]{1,0:T(8,128)(2,1)S(1)}, bf16[144,256]{1,0:T(8,128)(2,1)S(1)}, u32[]{:S(2)}, u32[]{:S(2)}) collective-permute-start(bf16[144,256]{1,0:T(8,128)(2,1)S(1)} %pack.1.refs_1_.refs_4_.refs_0_), channel_id=1, source_target_pairs={{0,8},{4,12},{8,0},{12,4},{16,24},{20,28},{24,16},{28,20},{1,9},{5... | collective-permute-start | bytes 221192 | tf_op jit(solution)/shard_map/ppermute | solution.py:372
  9.0 1.5 %collective-permute-start.5 = (bf16[144,256]{1,0:T(8,128)(2,1)S(1)}, bf16[144,256]{1,0:T(8,128)(2,1)S(1)}, u32[]{:S(2)}, u32[]{:S(2)}) collective-permute-start(bf16[144,256]{1,0:T(8,128)(2,1)S(1)} %pack.1.refs_1_.refs_4_.refs_0_), channel_id=1, source_target_pairs={{0,4},{4,0},{8,12},{12,8},{16,20},{20,16},{24,28},{28,24},{1,5},{5... | collective-permute-start | bytes 221192 | tf_op jit(solution)/shard_map/ppermute | solution.py:372
  10.5 1.1 %collective-permute-done.3.refs_3_.refs_6_.refs_2_ = bf16[144,256]{1,0:T(8,128)(2,1)S(1)} collective-permute-done((bf16[144,256]{1,0:T(8,128)(2,1)S(1)}, bf16[144,256]{1,0:T(8,128)(2,1)S(1)}, u32[]{:S(2)}, u32[]{:S(2)}) %collective-permute-start.3) | collective-permute-done | bytes 73760 | tf_op jit(solution)/shard_map/ppermute | solution.py:372
  11.6 3.4 %collective-permute-done.4.refs_4_.refs_7_.refs_3_ = bf16[144,256]{1,0:T(8,128)(2,1)S(1)} collective-permute-done((bf16[144,256]{1,0:T(8,128)(2,1)S(1)}, bf16[144,256]{1,0:T(8,128)(2,1)S(1)}, u32[]{:S(2)}, u32[]{:S(2)}) %collective-permute-start.4) | collective-permute-done | bytes 73760 | tf_op jit(solution)/shard_map/ppermute | solution.py:372
  15.0 0.6 %copy-done.9 = bf16[144,256]{1,0:T(8,128)(2,1)} copy-done((bf16[144,256]{1,0:T(8,128)(2,1)}, bf16[144,256]{1,0:T(8,128)(2,1)S(1)}, u32[]{:S(2)}) %copy-start.9) | copy-done | bytes 73752
  15.6 0.7 %copy-done.15 = bf16[512,256]{1,0:T(8,128)(2,1)} copy-done((bf16[512,256]{1,0:T(8,128)(2,1)}, bf16[512,256]{1,0:T(8,128)(2,1)S(1)}, u32[]{:S(2)}) %copy-start.15) | copy-done | bytes 262168
  16.4 1.5 %collective-permute-start.7 = (bf16[144,256]{1,0:T(8,128)(2,1)}, bf16[144,256]{1,0:T(8,128)(2,1)S(1)}, u32[]{:S(2)}, u32[]{:S(2)}) collective-permute-start(bf16[144,256]{1,0:T(8,128)(2,1)} %copy-done.3), channel_id=1, source_target_pairs={{0,4},{4,0},{8,12},{12,8},{16,20},{20,16},{24,28},{28,24},{1,5},{5... | collective-permute-start | bytes 221192 | tf_op jit(solution)/shard_map/ppermute | solution.py:372
  17.9 0.5 %collective-permute-start.8 = (bf16[144,256]{1,0:T(8,128)(2,1)}, bf16[144,256]{1,0:T(8,128)(2,1)S(1)}, u32[]{:S(2)}, u32[]{:S(2)}) collective-permute-start(bf16[144,256]{1,0:T(8,128)(2,1)} %copy-done.6), channel_id=1, source_target_pairs={{0,4},{4,0},{8,12},{12,8},{16,20},{20,16},{24,28},{28,24},{1,5},{5... | collective-permute-start | bytes 221192 | tf_op jit(solution)/shard_map/ppermute | solution.py:372
  18.4 1.5 %collective-permute-start.9 = (bf16[144,256]{1,0:T(8,128)(2,1)}, bf16[144,256]{1,0:T(8,128)(2,1)S(1)}, u32[]{:S(2)}, u32[]{:S(2)}) collective-permute-start(bf16[144,256]{1,0:T(8,128)(2,1)} %copy-done.9), channel_id=1, source_target_pairs={{0,4},{4,0},{8,12},{12,8},{16,20},{20,16},{24,28},{28,24},{1,5},{5... | collective-permute-start | bytes 221192 | tf_op jit(solution)/shard_map/ppermute | solution.py:372
  19.9 0.9 %copy-done.1 = bf16[144,256]{1,0:T(8,128)(2,1)S(1)} copy-done((bf16[144,256]{1,0:T(8,128)(2,1)S(1)}, bf16[144,256]{1,0:T(8,128)(2,1)}, u32[]{:S(2)}) %copy-start.1) | copy-done | bytes 73752
  20.8 0.9 %copy-done.4 = bf16[144,256]{1,0:T(8,128)(2,1)S(1)} copy-done((bf16[144,256]{1,0:T(8,128)(2,1)S(1)}, bf16[144,256]{1,0:T(8,128)(2,1)}, u32[]{:S(2)}) %copy-start.4) | copy-done | bytes 73752
  21.7 0.9 %copy-done.7 = bf16[144,256]{1,0:T(8,128)(2,1)S(1)} copy-done((bf16[144,256]{1,0:T(8,128)(2,1)S(1)}, bf16[144,256]{1,0:T(8,128)(2,1)}, u32[]{:S(2)}) %copy-start.7) | copy-done | bytes 73752
  22.6 0.9 %copy-done.10 = bf16[144,256]{1,0:T(8,128)(2,1)S(1)} copy-done((bf16[144,256]{1,0:T(8,128)(2,1)S(1)}, bf16[144,256]{1,0:T(8,128)(2,1)}, u32[]{:S(2)}) %copy-start.10) | copy-done | bytes 73752
  23.5 0.9 %copy-done.13 = bf16[144,256]{1,0:T(8,128)(2,1)S(1)} copy-done((bf16[144,256]{1,0:T(8,128)(2,1)S(1)}, bf16[144,256]{1,0:T(8,128)(2,1)}, u32[]{:S(2)}) %copy-start.13) | copy-done | bytes 73752
  24.3 0.9 %copy-done.16 = bf16[512,256]{1,0:T(8,128)(2,1)S(1)} copy-done((bf16[512,256]{1,0:T(8,128)(2,1)S(1)}, bf16[512,256]{1,0:T(8,128)(2,1)}, u32[]{:S(2)}) %copy-start.16) | copy-done | bytes 262168
  25.3 3.5 %early.1 = (bf16[256,256]{1,0:T(8,128)(2,1)S(1)}, bf16[272,512]{1,0:T(8,128)(2,1)S(1)}, bf16[3,512,256]{2,1,0:T(8,128)(2,1)}, bf16[5,272,512]{2,1,0:T(8,128)(2,1...) custom-call(s32[3]{0:T(128)S(1)} %pad_add_fusion.place_ref, ...), custom_call_target="tpu_custom_call" | custom-call | flops 2684354560 | bytes 3809280 | tf_op jit(solution)/shard_map/early/pallas_call | solution.py:405
  28.9 5.7 %heads.1 = f32[8,8,256]{2,1,0:T(8,128)} custom-call(s32[3]{0:T(128)S(1)} %pad_add_fusion.place_ref, bf16[256,256]{1,0:T(8,128)(2,1)S(1)} %get-tuple-element.15.factors_ref, bf16[144,256]{1,0:T(8,128)(2,1)S(1)} %copy-done.2, bf16[144,256]{1,0:T(8,128)(2,1)S(1)} %copy-done.5, bf16[144,256]{1,0:T(8,128)(2,1)S(1)} %copy-done.8, bf16[144,256]{1,0:T(8,128)(2,1)S(1)} %copy-done.11, ...), custom_call_target="tpu_custom_call" | custom-call | tf_op jit(solution)/shard_map/heads/pallas_call | solution.py:420
  34.7 3.7 %all-to-all-start = ((f32[8,8,256]{2,1,0:T(8,128)}), f32[8,8,256]{2,1,0:T(8,128)S(1)}, u32[]{:S(2)}, u32[]{:S(2)}) async-start(f32[8,8,256]{2,1,0:T(8,128)} %heads.1), calls=%async_computation | async-start | bytes 131072 | tf_op jit(solution)/shard_map/all_to_all | solution.py:434
  38.3 3.1 %first.1 = (f32[8,128,256]{2,1,0:T(8,128)S(1)}, f32[8,256,256]{2,1,0:T(8,128)S(1)}) custom-call(s32[1]{0:T(128)} %bitcast.5.node_ref, bf16[272,512]{1,0:T(8,128)(2,1)S(1)} %get-tuple-element.11.matrix_ref, bf16[128,256]{1,0:T(8,128)(2,1)} %loadings_ref.3, bf16[512,256]{1,0:T(8,128)(2,1)} %rows_ref.1, bf16[3,512,256]{2,1,0:T(8,128)(2,1)} %get-tuple-element.12.kept_ref), custom_call_target="tpu_custom_call" | custom-call | flops 536870912 | bytes 3145728 | tf_op jit(solution)/shard_map/first/pallas_call | solution.py:438
  41.5 3.8 %all-to-all-done.head_ref = f32[8,8,256]{2,1,0:T(8,128)S(1)} async-done(((f32[8,8,256]{2,1,0:T(8,128)}), f32[8,8,256]{2,1,0:T(8,128)S(1)}, u32[]{:S(2)}, u32[]{:S(2)}) %all-to-all-start) | async-done | bytes 65568 | tf_op jit(solution)/shard_map/all_to_all | solution.py:434
  45.2 3.3 %volts.1 = (f32[2048,128]{1,0:T(8,128)}, f32[2048,128]{1,0:T(8,128)}) custom-call(bf16[272,512]{1,0:T(8,128)(2,1)S(1)} %get-tuple-element.11.matrix_ref, f32[8,128,256]{2,1,0:T(8,128)S(1)} %get-tuple-element.13.swing_ref, f32[8,256,256]{2,1,0:T(8,128)S(1)} %get-tuple-element.14.drop_ref, f32[8,8,256]{2,1,0:T(8,128)S(1)} %all-to-all-done.head_ref), custom_call_target="tpu_custom_call" | custom-call | tf_op jit(solution)/shard_map/volts/pallas_call | solution.py:455
  (39 shorter events, 0.4 us)
Async XLA Ops:
  0.6 14.3 %collective-permute-start.1 = (bf16[512,256]{1,0:T(8,128)(2,1)}, bf16[512,256]{1,0:T(8,128)(2,1)S(1)}, u32[]{:S(2)}, u32[]{:S(2)}) collective-permute-start(bf16[512,256]{1,0:T(8,128)(2,1)} %rows_ref.1), channel_id=1, source_target_pairs={{0,2},{1,3},{2,0},{3,1},{4,6},{5,7},{6,4},{7,5},{8,10},{9,11},{10,... | collective-permute-start | bytes 786440 | tf_op jit(solution)/shard_map/ppermute | solution.py:347
  4.6 10.4 %copy-start = (bf16[144,256]{1,0:T(8,128)(2,1)}, bf16[144,256]{1,0:T(8,128)(2,1)S(1)}, u32[]{:S(2)}) copy-start(bf16[144,256]{1,0:T(8,128)(2,1)S(1)} %pack.1.refs_1_.refs_4_.refs_0_) | copy-start | bytes 221188
  4.6 5.9 %collective-permute-start.2 = (bf16[144,256]{1,0:T(8,128)(2,1)S(1)}, bf16[144,256]{1,0:T(8,128)(2,1)S(1)}, u32[]{:S(2)}, u32[]{:S(2)}) collective-permute-start(bf16[144,256]{1,0:T(8,128)(2,1)S(1)} %pack.1.refs_1_.refs_4_.refs_0_), channel_id=1, source_target_pairs={{0,16},{4,20},{8,24},{12,28},{16,0},{20,4},{24,8},{28,12},{1,17},{... | collective-permute-start | bytes 221192 | tf_op jit(solution)/shard_map/ppermute | solution.py:372
  7.2 4.4 %collective-permute-start.3 = (bf16[144,256]{1,0:T(8,128)(2,1)S(1)}, bf16[144,256]{1,0:T(8,128)(2,1)S(1)}, u32[]{:S(2)}, u32[]{:S(2)}) collective-permute-start(bf16[144,256]{1,0:T(8,128)(2,1)S(1)} %pack.1.refs_1_.refs_4_.refs_0_), channel_id=1, source_target_pairs={{0,8},{4,12},{8,0},{12,4},{16,24},{20,28},{24,16},{28,20},{1,9},{5... | collective-permute-start | bytes 221192 | tf_op jit(solution)/shard_map/ppermute | solution.py:372
  8.8 6.2 %collective-permute-start.4 = (bf16[144,256]{1,0:T(8,128)(2,1)S(1)}, bf16[144,256]{1,0:T(8,128)(2,1)S(1)}, u32[]{:S(2)}, u32[]{:S(2)}) collective-permute-start(bf16[144,256]{1,0:T(8,128)(2,1)S(1)} %pack.1.refs_1_.refs_4_.refs_0_), channel_id=1, source_target_pairs={{0,24},{4,28},{8,16},{12,20},{16,8},{20,12},{24,0},{28,4},{1,25},{... | collective-permute-start | bytes 221192 | tf_op jit(solution)/shard_map/ppermute | solution.py:372
  9.0 5.9 %collective-permute-start.5 = (bf16[144,256]{1,0:T(8,128)(2,1)S(1)}, bf16[144,256]{1,0:T(8,128)(2,1)S(1)}, u32[]{:S(2)}, u32[]{:S(2)}) collective-permute-start(bf16[144,256]{1,0:T(8,128)(2,1)S(1)} %pack.1.refs_1_.refs_4_.refs_0_), channel_id=1, source_target_pairs={{0,4},{4,0},{8,12},{12,8},{16,20},{20,16},{24,28},{28,24},{1,5},{5... | collective-permute-start | bytes 221192 | tf_op jit(solution)/shard_map/ppermute | solution.py:372
  10.5 4.5 %copy-start.3 = (bf16[144,256]{1,0:T(8,128)(2,1)}, bf16[144,256]{1,0:T(8,128)(2,1)S(1)}, u32[]{:S(2)}) copy-start(bf16[144,256]{1,0:T(8,128)(2,1)S(1)} %collective-permute-done.2.refs_2_.refs_5_.refs_1_) | copy-start | bytes 221188
  10.5 9.4 %collective-permute-start = (bf16[512,256]{1,0:T(8,128)(2,1)}, bf16[512,256]{1,0:T(8,128)(2,1)S(1)}, u32[]{:S(2)}, u32[]{:S(2)}) collective-permute-start(bf16[512,256]{1,0:T(8,128)(2,1)} %rows_ref.1), channel_id=1, source_target_pairs={{0,1},{1,0},{2,3},{3,2},{4,5},{5,4},{6,7},{7,6},{8,9},{9,8},{10,11... | collective-permute-start | bytes 786440 | tf_op jit(solution)/shard_map/ppermute | solution.py:347
  11.6 3.4 %copy-start.6 = (bf16[144,256]{1,0:T(8,128)(2,1)}, bf16[144,256]{1,0:T(8,128)(2,1)S(1)}, u32[]{:S(2)}) copy-start(bf16[144,256]{1,0:T(8,128)(2,1)S(1)} %collective-permute-done.3.refs_3_.refs_6_.refs_2_) | copy-start | bytes 221188
  16.3 3.6 %collective-permute-start.6 = (bf16[512,256]{1,0:T(8,128)(2,1)}, bf16[512,256]{1,0:T(8,128)(2,1)S(1)}, u32[]{:S(2)}, u32[]{:S(2)}) collective-permute-start(bf16[512,256]{1,0:T(8,128)(2,1)} %after.1.refs_2_), channel_id=1, source_target_pairs={{0,1},{1,0},{2,3},{3,2},{4,5},{5,4},{6,7},{7,6},{8,9},{9,8},{10,11... | collective-permute-start | bytes 786440 | tf_op jit(solution)/shard_map/ppermute | solution.py:347
  16.4 12.5 %collective-permute-start.7 = (bf16[144,256]{1,0:T(8,128)(2,1)}, bf16[144,256]{1,0:T(8,128)(2,1)S(1)}, u32[]{:S(2)}, u32[]{:S(2)}) collective-permute-start(bf16[144,256]{1,0:T(8,128)(2,1)} %copy-done.3), channel_id=1, source_target_pairs={{0,4},{4,0},{8,12},{12,8},{16,20},{20,16},{24,28},{28,24},{1,5},{5... | collective-permute-start | bytes 221192 | tf_op jit(solution)/shard_map/ppermute | solution.py:372
  17.9 11.0 %collective-permute-start.8 = (bf16[144,256]{1,0:T(8,128)(2,1)}, bf16[144,256]{1,0:T(8,128)(2,1)S(1)}, u32[]{:S(2)}, u32[]{:S(2)}) collective-permute-start(bf16[144,256]{1,0:T(8,128)(2,1)} %copy-done.6), channel_id=1, source_target_pairs={{0,4},{4,0},{8,12},{12,8},{16,20},{20,16},{24,28},{28,24},{1,5},{5... | collective-permute-start | bytes 221192 | tf_op jit(solution)/shard_map/ppermute | solution.py:372
  18.4 10.5 %collective-permute-start.9 = (bf16[144,256]{1,0:T(8,128)(2,1)}, bf16[144,256]{1,0:T(8,128)(2,1)S(1)}, u32[]{:S(2)}, u32[]{:S(2)}) collective-permute-start(bf16[144,256]{1,0:T(8,128)(2,1)} %copy-done.9), channel_id=1, source_target_pairs={{0,4},{4,0},{8,12},{12,8},{16,20},{20,16},{24,28},{28,24},{1,5},{5... | collective-permute-start | bytes 221192 | tf_op jit(solution)/shard_map/ppermute | solution.py:372
  19.9 0.9 %copy-start.1 = (bf16[144,256]{1,0:T(8,128)(2,1)S(1)}, bf16[144,256]{1,0:T(8,128)(2,1)}, u32[]{:S(2)}) copy-start(bf16[144,256]{1,0:T(8,128)(2,1)} %copy-done) | copy-start | bytes 221188
  20.8 0.9 %copy-start.4 = (bf16[144,256]{1,0:T(8,128)(2,1)S(1)}, bf16[144,256]{1,0:T(8,128)(2,1)}, u32[]{:S(2)}) copy-start(bf16[144,256]{1,0:T(8,128)(2,1)} %copy-done.3) | copy-start | bytes 221188
  22.6 0.9 %copy-start.10 = (bf16[144,256]{1,0:T(8,128)(2,1)S(1)}, bf16[144,256]{1,0:T(8,128)(2,1)}, u32[]{:S(2)}) copy-start(bf16[144,256]{1,0:T(8,128)(2,1)} %copy-done.9) | copy-start | bytes 221188
  23.5 0.9 %copy-start.13 = (bf16[144,256]{1,0:T(8,128)(2,1)S(1)}, bf16[144,256]{1,0:T(8,128)(2,1)}, u32[]{:S(2)}) copy-start(bf16[144,256]{1,0:T(8,128)(2,1)} %copy-done.12) | copy-start | bytes 221188
  24.3 0.9 %copy-start.16 = (bf16[512,256]{1,0:T(8,128)(2,1)S(1)}, bf16[512,256]{1,0:T(8,128)(2,1)}, u32[]{:S(2)}) copy-start(bf16[512,256]{1,0:T(8,128)(2,1)} %after.1.refs_2_) | copy-start | bytes 786436
  25.3 3.6 %copy-start.2 = (bf16[144,256]{1,0:T(8,128)(2,1)S(1)}, bf16[144,256]{1,0:T(8,128)(2,1)}, u32[]{:S(2)}) copy-start(bf16[144,256]{1,0:T(8,128)(2,1)} %copy-done) | copy-start | bytes 221188
  25.3 3.6 %copy-start.5 = (bf16[144,256]{1,0:T(8,128)(2,1)S(1)}, bf16[144,256]{1,0:T(8,128)(2,1)}, u32[]{:S(2)}) copy-start(bf16[144,256]{1,0:T(8,128)(2,1)} %copy-done.3) | copy-start | bytes 221188
  25.3 3.6 %copy-start.8 = (bf16[144,256]{1,0:T(8,128)(2,1)S(1)}, bf16[144,256]{1,0:T(8,128)(2,1)}, u32[]{:S(2)}) copy-start(bf16[144,256]{1,0:T(8,128)(2,1)} %copy-done.6) | copy-start | bytes 221188
  25.3 3.6 %copy-start.11 = (bf16[144,256]{1,0:T(8,128)(2,1)S(1)}, bf16[144,256]{1,0:T(8,128)(2,1)}, u32[]{:S(2)}) copy-start(bf16[144,256]{1,0:T(8,128)(2,1)} %copy-done.9) | copy-start | bytes 221188
  25.3 3.6 %copy-start.14 = (bf16[144,256]{1,0:T(8,128)(2,1)S(1)}, bf16[144,256]{1,0:T(8,128)(2,1)}, u32[]{:S(2)}) copy-start(bf16[144,256]{1,0:T(8,128)(2,1)} %copy-done.12) | copy-start | bytes 221188
  34.7 10.6 %all-to-all-start = ((f32[8,8,256]{2,1,0:T(8,128)}), f32[8,8,256]{2,1,0:T(8,128)S(1)}, u32[]{:S(2)}, u32[]{:S(2)}) async-start(f32[8,8,256]{2,1,0:T(8,128)} %heads.1), calls=%async_computation | async-start | bytes 131072 | tf_op jit(solution)/shard_map/all_to_all | solution.py:434
  (4 other events, 2.9 us)

commit v7 on v6

--- a/solution.py
+++ b/solution.py
@@ -77,24 +77,51 @@
     return high, middle, high + middle + meta[8:16, 0:n]
 
 
+def section_paths(parents, n):
+    rows = max(8, len(parents))
+    row_ids = lax.broadcasted_iota(jnp.int32, (n, n), 0)
+    lane_ids = lax.broadcasted_iota(jnp.int32, (n, n), 1)
+    section_ids = lax.broadcasted_iota(jnp.int32, (rows, n), 0)
+    stacked = jnp.full((rows, n), -1, jnp.int32)
+    for index, row in enumerate(parents):
+        stacked = jnp.where(section_ids == index, row.astype(jnp.int32), stacked)
+    known = {1: stacked}
+
+    def ancestor(distance):
+        if distance not in known:
+            step = 1 << (distance.bit_length() - 1)
+            if step == distance:
+                step //= 2
+            far, near = ancestor(step), ancestor(distance - step)
+            known[distance] = jnp.where(near < 0, -1, jnp.take_along_axis(far, jnp.maximum(near, 0), axis=1))
+        return known[distance]
+
+    digits = []
+    unit = 1
+    while unit < n:
+        digits.append([ancestor(unit * digit) for digit in range(1, 8) if unit * digit < n])
+        unit *= 8
+    last = [found.astype(jnp.float32).T.astype(jnp.int32) for found in digits.pop()]
+    out = []
+    for index in range(len(parents)):
+        product_t = None
+        for digit in digits:
+            mask = row_ids == lane_ids
+            for found in digit:
+                mask = mask | (row_ids == found[index : index + 1, :])
+            factor = mask.astype(jnp.bfloat16)
+            product_t = factor if product_t is None else product(product_t, factor).astype(jnp.bfloat16)
+        mask = row_ids == lane_ids
+        for found in last:
+            mask = mask | (lane_ids == found[:, index : index + 1])
+        out.append((mask.astype(jnp.bfloat16), product_t))
+    return [product_nt(left, right).astype(jnp.bfloat16) for left, right in out]
+
+
 def section_matrices(sections, n):
-    row_ids = lax.broadcasted_iota(jnp.int32, (n, n), 0).astype(jnp.float32)
-    lane_ids = lax.broadcasted_iota(jnp.int32, (n, n), 1).astype(jnp.float32)
-    identity = (row_ids == lane_ids).astype(jnp.bfloat16)
     pad_ids = lax.broadcasted_iota(jnp.int32, (EXTRA, 2 * n), 0)
     highs, middles, rows = zip(*(constants(section, n) for section in sections))
-    powers = [(jnp.broadcast_to(row.T[:, 6:7], (n, n)) == lane_ids).astype(jnp.bfloat16) for row in rows]
-    paths = [identity + power for power in powers]
-    powers = [product(power, power).astype(jnp.bfloat16) for power in powers]
-    reach = 2
-    while reach < n:
-        if 2 * reach < n:
-            both = [product(x, jnp.concatenate([x, p], axis=1)) for x, p in zip(powers, paths)]
-            paths = [p + b[:, n:].astype(jnp.bfloat16) for p, b in zip(paths, both)]
-            powers = [b[:, :n].astype(jnp.bfloat16) for b in both]
-        else:
-            paths = [p + product(x, p).astype(jnp.bfloat16) for x, p in zip(powers, paths)]
-        reach *= 2
+    paths = section_paths([row[6:7] for row in rows], n)
     shared = []
     for path, high, middle in zip(paths, highs, middles):
         wide_path = path.astype(jnp.float32)
@@ -139,12 +166,16 @@
     return product(left, jnp.concatenate([high, high, low], axis=0))
 
 
-def apply_real(matrix, real):
+def apply_first(matrix, swing):
     n = matrix.shape[1] // 4
-    high, low = split(real)
-    high_part, low_part = matrix[:, :n], matrix[:, 2 * n : 3 * n]
-    left = jnp.concatenate([high_part, low_part, high_part], axis=1)
-    return product(left, jnp.concatenate([high, high, low], axis=0))
+    high = swing.astype(jnp.bfloat16)
+    return product(
+        jnp.concatenate([matrix[:, :n], matrix[:, 2 * n : 3 * n]], axis=1), jnp.concatenate([high, high], axis=0)
+    )
+
+
+def apply_change(matrix, change):
+    return product(matrix[:, : matrix.shape[1] // 2], change.astype(jnp.bfloat16))
 
 
 def inverse_of(swing, real, imag):
@@ -153,9 +184,12 @@
     return swing * (guess * (2.0 - square * guess))
 
 
-def scaled_volts(swing, real, imag):
+def scaled_volts(swing, real, imag, change=False):
     inverse = inverse_of(swing, real, imag)
-    return jnp.concatenate([real * inverse, imag * inverse], axis=0)
+    scaled = real * inverse
+    if change:
+        scaled = scaled - swing.astype(jnp.bfloat16).astype(jnp.float32)
+    return jnp.concatenate([scaled, imag * inverse], axis=0)
 
 
 def first_sweep(sections, factors_of, matrix_ref, swing_ref, drop_ref, inject_ref):
@@ -168,7 +202,7 @@
         for slot, section in enumerate(group, start):
             swing = swing_of(section[0:n, :], factors)
             swing_ref[slot] = swing
-            out = apply_real(matrix_ref[slot], swing)
+            out = apply_first(matrix_ref[slot], swing)
             drop_ref[slot] = out[: 2 * n]
             inject_ref[slot] = out[2 * n :]
 
@@ -246,9 +280,9 @@
             imag = head_ref[place[index], 2 * sweep - 1 : 2 * sweep, :] - drop[n : 2 * n, :]
             swing = of(index, 1)[...]
             if sweep < SWEEPS - 1:
-                out = apply(of(index, 0)[...], scaled_volts(swing, real, imag))
-                again_ref[index] = out[: 2 * n]
-                flow_ref[place[index]] = out[2 * n : 2 * n + 8]
+                out = apply_change(of(index, 0)[...], scaled_volts(swing, real, imag, change=True))
+                again_ref[index] = of(index, 2)[...] + out[: 2 * n]
+                flow_ref[place[index]] = of(index, 3)[0:8, :] + out[2 * n : 2 * n + 8]
             else:
                 base = constants(sections[index], n)[2].T
                 active, reactive = base[:, 0:1], base[:, 1:2]
@@ -282,7 +316,7 @@
             chunk = jnp.bitwise_xor(node_ref[0], index) * chunks + part
             swing = swing_of(loadings, factors_ref[index, part * width : (part + 1) * width, :])
             swing_ref[chunk] = swing
-            drop_ref[chunk] = apply_real(matrix, swing)
+            drop_ref[chunk] = apply_first(matrix, swing)
 
 
 def volts_kernel(matrix_ref, swing_ref, drop_ref, head_ref, real_ref, imag_ref, out_ref, sems):
@@ -296,8 +330,11 @@
             drop = drop_ref[chunk] if sweep == 0 else drops[chunk]
             real = head_ref[chunk, 2 * sweep : 2 * sweep + 1, :] - drop[:n]
             imag = head_ref[chunk, 2 * sweep + 1 : 2 * sweep + 2, :] - drop[n:]
-            if sweep < SWEEPS - 1:
-                drops[chunk] = apply(matrix, scaled_volts(swing_ref[chunk], real, imag))
+            swing = swing_ref[chunk]
+            if sweep < SWEEPS - 2:
+                drops[chunk] = drop_ref[chunk] + apply_change(matrix, scaled_volts(swing, real, imag, change=True))
+            elif sweep < SWEEPS - 1:
+                drops[chunk] = apply(matrix, scaled_volts(swing, real, imag))
             else:
                 rows = slice(chunk * width, (chunk + 1) * width)
                 for index, (part, to_ref) in enumerate(((real, real_ref), (imag, imag_ref))):
@@ -320,6 +357,7 @@
         in_specs=[ANY] * (1 + len(others)),
         out_specs=ANY,
         input_output_aliases={0: 0},
+        compiler_params=limit(0),
         name="after",
     )(array, *others)
 

time: 49.1 us -> 42.8 us (0.87)
  local copies, waits for them, and re-layouts: 6.71 us -> 0 us
  waiting for transfers between devices: 8.2 us -> 8.84 us
  starting transfers between devices: 16.2 us -> 16.7 us
    unnamed x34 -> x0, local copies, waits for them, and re-layouts: 6.71 us -> none
    ppermute x7, waiting for transfers between devices: 4.44 us -> 5.65 us  [swap(): lax.ppermute(block, 'feeder', [(i, i ^ offset) for i in range(feeders)])]
    all_to_all x1, waiting for transfers between devices: 3.76 us -> 3.18 us  [local(): given = lax.all_to_all(heads, 'feeder', 0, 0, tiled=True)]
    pallas_call x1, Pallas kernels: 3.14 us -> 3.72 us  [local(): pl.pallas_call(first_kernel, out_shape=(jax.ShapeDtypeStruct((chunks, n,...]
    all_to_all x1, starting transfers between devices: 3.67 us -> 4.17 us  [local(): given = lax.all_to_all(heads, 'feeder', 0, 0, tiled=True)]
  transfers between devices with their start and end apart: 11 -> 11, of which waited for: 3 -> 4; matrix products, arithmetic and copies ran while one was open for 0% -> 0% of each run, Pallas kernels for 16% -> 18%
where the time goes in v7:
time: 42.8 us; the launch traced here: 42.5 us
  starting transfers between devices  16.7 us (39%)
  Pallas kernels  16.2 us (38%)
  waiting for transfers between devices  8.84 us (21%)
  between operations  0.71 us (2%)
    ppermute x7, starting transfers between devices, swap(): lax.ppermute(block, 'feeder', [(i, i ^ offset) for i in range(feeders)])  9.47 us
    ppermute x7, waiting for transfers between devices, swap(): lax.ppermute(block, 'feeder', [(i, i ^ offset) for i in range(feeders)])  5.65 us
    pallas_call x1, Pallas kernels, local(): pl.pallas_call(functools.partial(heads_kernel, slots, early), out_shape=j...  5.44 us
    all_to_all x1, starting transfers between devices, local(): given = lax.all_to_all(heads, 'feeder', 0, 0, tiled=True)  4.17 us
    pallas_call x1, Pallas kernels, local(): pl.pallas_call(first_kernel, out_shape=(jax.ShapeDtypeStruct((chunks, n,...  3.72 us
    all_to_all x1, waiting for transfers between devices, local(): given = lax.all_to_all(heads, 'feeder', 0, 0, tiled=True)  3.18 us
    ppermute x3, starting transfers between devices, trade(): return lax.ppermute(block, 'node', [(i, i ^ offset) for i in range(nodes)])  3.1 us
    pallas_call x1, Pallas kernels, local(): pl.pallas_call(volts_kernel, out_shape=(jax.ShapeDtypeStruct((scen, n), f...  3.1 us
  transfers between devices with their start and end apart: 11, of which 4 were waited for; matrix products, arithmetic and copies ran while one was open for 0% of the time, Pallas kernels for 18%

profile of v7, /device:TPU:0, one launch (start us, length us, event | category | flops | bytes accessed | tf_op | source)
XLA Modules:
  0.0 42.5 jit_solution(12523808341503747826)
XLA Ops:
  0.6 3.0 %collective-permute-start.1 = (bf16[512,256]{1,0:T(8,128)(2,1)}, bf16[512,256]{1,0:T(8,128)(2,1)S(1)}, u32[]{:S(2)}, u32[]{:S(2)}) collective-permute-start(bf16[512,256]{1,0:T(8,128)(2,1)} %rows_ref.1), channel_id=1, source_target_pairs={{0,2},{1,3},{2,0},{3,1},{4,6},{5,7},{6,4},{7,5},{8,10},{9,11},{10,... | collective-permute-start | bytes 786440 | tf_op jit(solution)/shard_map/ppermute | solution.py:385
  3.7 0.9 %pack.1.refs_1_.refs_4_.refs_0_ = bf16[144,256]{1,0:T(8,128)(2,1)S(1)} custom-call(f32[2]{0:T(128)} %bitcast.6, bf16[128,256]{1,0:T(8,128)(2,1)} %loadings_ref.3, s32[1,128]{1,0:T(1,128)} %bitcast.7, f32[2,128]{1,0:T(2,128)} %base_ref.1, f32[2,128]{1,0:T(2,128)} %z_ref.1), custom_call_target="tpu_custom_call" | custom-call | tf_op jit(solution)/shard_map/pack/pallas_call | solution.py:392
  4.6 2.7 %collective-permute-start.2 = (bf16[144,256]{1,0:T(8,128)(2,1)S(1)}, bf16[144,256]{1,0:T(8,128)(2,1)S(1)}, u32[]{:S(2)}, u32[]{:S(2)}) collective-permute-start(bf16[144,256]{1,0:T(8,128)(2,1)S(1)} %pack.1.refs_1_.refs_4_.refs_0_), channel_id=1, source_target_pairs={{0,16},{4,20},{8,24},{12,28},{16,0},{20,4},{24,8},{28,12},{1,17},{... | collective-permute-start | bytes 221192 | tf_op jit(solution)/shard_map/ppermute | solution.py:410
  7.2 1.6 %collective-permute-start.3 = (bf16[144,256]{1,0:T(8,128)(2,1)S(1)}, bf16[144,256]{1,0:T(8,128)(2,1)S(1)}, u32[]{:S(2)}, u32[]{:S(2)}) collective-permute-start(bf16[144,256]{1,0:T(8,128)(2,1)S(1)} %pack.1.refs_1_.refs_4_.refs_0_), channel_id=1, source_target_pairs={{0,8},{4,12},{8,0},{12,4},{16,24},{20,28},{24,16},{28,20},{1,9},{5... | collective-permute-start | bytes 221192 | tf_op jit(solution)/shard_map/ppermute | solution.py:410
  8.8 0.2 collective-permute-start.4
  9.0 1.5 %collective-permute-start.5 = (bf16[144,256]{1,0:T(8,128)(2,1)S(1)}, bf16[144,256]{1,0:T(8,128)(2,1)S(1)}, u32[]{:S(2)}, u32[]{:S(2)}) collective-permute-start(bf16[144,256]{1,0:T(8,128)(2,1)S(1)} %pack.1.refs_1_.refs_4_.refs_0_), channel_id=1, source_target_pairs={{0,4},{4,0},{8,12},{12,8},{16,20},{20,16},{24,28},{28,24},{1,5},{5... | collective-permute-start | bytes 221192 | tf_op jit(solution)/shard_map/ppermute | solution.py:410
  10.5 0.0 collective-permute-done.2.refs_2_.refs_5_.refs_1_
  10.5 0.0 collective-permute-start
  10.5 1.1 %collective-permute-done.3.refs_3_.refs_6_.refs_2_ = bf16[144,256]{1,0:T(8,128)(2,1)S(1)} collective-permute-done((bf16[144,256]{1,0:T(8,128)(2,1)S(1)}, bf16[144,256]{1,0:T(8,128)(2,1)S(1)}, u32[]{:S(2)}, u32[]{:S(2)}) %collective-permute-start.3) | collective-permute-done | bytes 73760 | tf_op jit(solution)/shard_map/ppermute | solution.py:410
  11.6 3.4 %collective-permute-done.4.refs_4_.refs_7_.refs_3_ = bf16[144,256]{1,0:T(8,128)(2,1)S(1)} collective-permute-done((bf16[144,256]{1,0:T(8,128)(2,1)S(1)}, bf16[144,256]{1,0:T(8,128)(2,1)S(1)}, u32[]{:S(2)}, u32[]{:S(2)}) %collective-permute-start.4) | collective-permute-done | bytes 73760 | tf_op jit(solution)/shard_map/ppermute | solution.py:410
  14.9 0.1 collective-permute-start.6
  15.0 0.1 pad_add_fusion.place_ref
  15.1 1.5 %collective-permute-start.7 = (bf16[144,256]{1,0:T(8,128)(2,1)S(1)}, bf16[144,256]{1,0:T(8,128)(2,1)S(1)}, u32[]{:S(2)}, u32[]{:S(2)}) collective-permute-start(bf16[144,256]{1,0:T(8,128)(2,1)S(1)} %collective-permute-done.2.refs_2_.refs_5_.refs_1_), channel_id=1, source_target_pairs={{0,4},{4,0},{8,12},{12,8},{16,20},{20,16},{24,28},{28,24},{1,5},{5... | collective-permute-start | bytes 221192 | tf_op jit(solution)/shard_map/ppermute | solution.py:410
  16.6 0.5 %collective-permute-start.8 = (bf16[144,256]{1,0:T(8,128)(2,1)S(1)}, bf16[144,256]{1,0:T(8,128)(2,1)S(1)}, u32[]{:S(2)}, u32[]{:S(2)}) collective-permute-start(bf16[144,256]{1,0:T(8,128)(2,1)S(1)} %collective-permute-done.3.refs_3_.refs_6_.refs_2_), channel_id=1, source_target_pairs={{0,4},{4,0},{8,12},{12,8},{16,20},{20,16},{24,28},{28,24},{1,5},{5... | collective-permute-start | bytes 221192 | tf_op jit(solution)/shard_map/ppermute | solution.py:410
  17.2 1.5 %collective-permute-start.9 = (bf16[144,256]{1,0:T(8,128)(2,1)S(1)}, bf16[144,256]{1,0:T(8,128)(2,1)S(1)}, u32[]{:S(2)}, u32[]{:S(2)}) collective-permute-start(bf16[144,256]{1,0:T(8,128)(2,1)S(1)} %collective-permute-done.4.refs_4_.refs_7_.refs_3_), channel_id=1, source_target_pairs={{0,4},{4,0},{8,12},{12,8},{16,20},{20,16},{24,28},{28,24},{1,5},{5... | collective-permute-start | bytes 221192 | tf_op jit(solution)/shard_map/ppermute | solution.py:410
  18.6 0.0 collective-permute-done.refs_1_
  18.7 3.0 %early.1 = (bf16[256,256]{1,0:T(8,128)(2,1)S(1)}, bf16[272,512]{1,0:T(8,128)(2,1)S(1)}, bf16[3,512,256]{2,1,0:T(8,128)(2,1)}, bf16[5,272,512]{2,1,0:T(8,128)(2,1...) custom-call(s32[3]{0:T(128)S(1)} %pad_add_fusion.place_ref, ...), custom_call_target="tpu_custom_call" | custom-call | flops 2684354560 | bytes 3809280 | tf_op jit(solution)/shard_map/early/pallas_call | solution.py:443
  21.7 0.0 collective-permute-done.8.refs_6_
  21.7 1.2 %collective-permute-done.9.refs_7_ = bf16[144,256]{1,0:T(8,128)(2,1)S(1)} collective-permute-done((bf16[144,256]{1,0:T(8,128)(2,1)S(1)}, bf16[144,256]{1,0:T(8,128)(2,1)S(1)}, u32[]{:S(2)}, u32[]{:S(2)}) %collective-permute-start.9) | collective-permute-done | bytes 73760 | tf_op jit(solution)/shard_map/ppermute | solution.py:410
  22.9 5.4 %heads.1 = f32[8,8,256]{2,1,0:T(8,128)} custom-call(s32[3]{0:T(128)S(1)} %pad_add_fusion.place_ref, bf16[256,256]{1,0:T(8,128)(2,1)S(1)} %get-tuple-element.15.factors_ref, bf16[144,256]{1,0:T(8,128)(2,1)S(1)} %pack.1.refs_1_.refs_4_.refs_0_, bf16[144,256]{1,0:T(8,128)(2,1)S(1)} %collective-permute-done.2.refs_2_.refs_5_.refs_1_, ...), custom_call_target="tpu_custom_call" | custom-call | tf_op jit(solution)/shard_map/heads/pallas_call | solution.py:458
  28.4 4.2 %all-to-all-start = ((f32[8,8,256]{2,1,0:T(8,128)}), f32[8,8,256]{2,1,0:T(8,128)S(1)}, u32[]{:S(2)}, u32[]{:S(2)}) async-start(f32[8,8,256]{2,1,0:T(8,128)} %heads.1), calls=%async_computation | async-start | bytes 131072 | tf_op jit(solution)/shard_map/all_to_all | solution.py:472
  32.5 3.7 %first.1 = (f32[8,128,256]{2,1,0:T(8,128)S(1)}, f32[8,256,256]{2,1,0:T(8,128)S(1)}) custom-call(s32[1]{0:T(128)} %bitcast.5.node_ref, bf16[272,512]{1,0:T(8,128)(2,1)S(1)} %get-tuple-element.11.matrix_ref, bf16[128,256]{1,0:T(8,128)(2,1)} %loadings_ref.3, bf16[512,256]{1,0:T(8,128)(2,1)} %rows_ref.1, bf16[3,512,256]{2,1,0:T(8,128)(2,1)} %get-tuple-element.12.kept_ref), custom_call_target="tpu_custom_call" | custom-call | flops 536870912 | bytes 3145728 | tf_op jit(solution)/shard_map/first/pallas_call | solution.py:476
  36.3 3.2 %all-to-all-done.head_ref = f32[8,8,256]{2,1,0:T(8,128)S(1)} async-done(((f32[8,8,256]{2,1,0:T(8,128)}), f32[8,8,256]{2,1,0:T(8,128)S(1)}, u32[]{:S(2)}, u32[]{:S(2)}) %all-to-all-start) | async-done | bytes 65568 | tf_op jit(solution)/shard_map/all_to_all | solution.py:472
  39.4 3.1 %volts.1 = (f32[2048,128]{1,0:T(8,128)}, f32[2048,128]{1,0:T(8,128)}) custom-call(bf16[272,512]{1,0:T(8,128)(2,1)S(1)} %get-tuple-element.11.matrix_ref, f32[8,128,256]{2,1,0:T(8,128)S(1)} %get-tuple-element.13.swing_ref, f32[8,256,256]{2,1,0:T(8,128)S(1)} %get-tuple-element.14.drop_ref, f32[8,8,256]{2,1,0:T(8,128)S(1)} %all-to-all-done.head_ref), custom_call_target="tpu_custom_call" | custom-call | tf_op jit(solution)/shard_map/volts/pallas_call | solution.py:493
  (5 shorter events, 0.0 us)
Async XLA Ops:
  0.6 14.3 %collective-permute-start.1 = (bf16[512,256]{1,0:T(8,128)(2,1)}, bf16[512,256]{1,0:T(8,128)(2,1)S(1)}, u32[]{:S(2)}, u32[]{:S(2)}) collective-permute-start(bf16[512,256]{1,0:T(8,128)(2,1)} %rows_ref.1), channel_id=1, source_target_pairs={{0,2},{1,3},{2,0},{3,1},{4,6},{5,7},{6,4},{7,5},{8,10},{9,11},{10,... | collective-permute-start | bytes 786440 | tf_op jit(solution)/shard_map/ppermute | solution.py:385
  4.6 5.9 %collective-permute-start.2 = (bf16[144,256]{1,0:T(8,128)(2,1)S(1)}, bf16[144,256]{1,0:T(8,128)(2,1)S(1)}, u32[]{:S(2)}, u32[]{:S(2)}) collective-permute-start(bf16[144,256]{1,0:T(8,128)(2,1)S(1)} %pack.1.refs_1_.refs_4_.refs_0_), channel_id=1, source_target_pairs={{0,16},{4,20},{8,24},{12,28},{16,0},{20,4},{24,8},{28,12},{1,17},{... | collective-permute-start | bytes 221192 | tf_op jit(solution)/shard_map/ppermute | solution.py:410
  7.2 4.4 %collective-permute-start.3 = (bf16[144,256]{1,0:T(8,128)(2,1)S(1)}, bf16[144,256]{1,0:T(8,128)(2,1)S(1)}, u32[]{:S(2)}, u32[]{:S(2)}) collective-permute-start(bf16[144,256]{1,0:T(8,128)(2,1)S(1)} %pack.1.refs_1_.refs_4_.refs_0_), channel_id=1, source_target_pairs={{0,8},{4,12},{8,0},{12,4},{16,24},{20,28},{24,16},{28,20},{1,9},{5... | collective-permute-start | bytes 221192 | tf_op jit(solution)/shard_map/ppermute | solution.py:410
  8.8 6.2 %collective-permute-start.4 = (bf16[144,256]{1,0:T(8,128)(2,1)S(1)}, bf16[144,256]{1,0:T(8,128)(2,1)S(1)}, u32[]{:S(2)}, u32[]{:S(2)}) collective-permute-start(bf16[144,256]{1,0:T(8,128)(2,1)S(1)} %pack.1.refs_1_.refs_4_.refs_0_), channel_id=1, source_target_pairs={{0,24},{4,28},{8,16},{12,20},{16,8},{20,12},{24,0},{28,4},{1,25},{... | collective-permute-start | bytes 221192 | tf_op jit(solution)/shard_map/ppermute | solution.py:410
  9.0 5.9 %collective-permute-start.5 = (bf16[144,256]{1,0:T(8,128)(2,1)S(1)}, bf16[144,256]{1,0:T(8,128)(2,1)S(1)}, u32[]{:S(2)}, u32[]{:S(2)}) collective-permute-start(bf16[144,256]{1,0:T(8,128)(2,1)S(1)} %pack.1.refs_1_.refs_4_.refs_0_), channel_id=1, source_target_pairs={{0,4},{4,0},{8,12},{12,8},{16,20},{20,16},{24,28},{28,24},{1,5},{5... | collective-permute-start | bytes 221192 | tf_op jit(solution)/shard_map/ppermute | solution.py:410
  10.5 8.1 %collective-permute-start = (bf16[512,256]{1,0:T(8,128)(2,1)}, bf16[512,256]{1,0:T(8,128)(2,1)S(1)}, u32[]{:S(2)}, u32[]{:S(2)}) collective-permute-start(bf16[512,256]{1,0:T(8,128)(2,1)} %rows_ref.1), channel_id=1, source_target_pairs={{0,1},{1,0},{2,3},{3,2},{4,5},{5,4},{6,7},{7,6},{8,9},{9,8},{10,11... | collective-permute-start | bytes 786440 | tf_op jit(solution)/shard_map/ppermute | solution.py:385
  14.9 3.7 %collective-permute-start.6 = (bf16[512,256]{1,0:T(8,128)(2,1)S(1)}, bf16[512,256]{1,0:T(8,128)(2,1)S(1)}, u32[]{:S(2)}, u32[]{:S(2)}) collective-permute-start(bf16[512,256]{1,0:T(8,128)(2,1)S(1)} %after.1.refs_2_), channel_id=1, source_target_pairs={{0,1},{1,0},{2,3},{3,2},{4,5},{5,4},{6,7},{7,6},{8,9},{9,8},{10,11... | collective-permute-start | bytes 786440 | tf_op jit(solution)/shard_map/ppermute | solution.py:385
  15.1 6.6 %collective-permute-start.7 = (bf16[144,256]{1,0:T(8,128)(2,1)S(1)}, bf16[144,256]{1,0:T(8,128)(2,1)S(1)}, u32[]{:S(2)}, u32[]{:S(2)}) collective-permute-start(bf16[144,256]{1,0:T(8,128)(2,1)S(1)} %collective-permute-done.2.refs_2_.refs_5_.refs_1_), channel_id=1, source_target_pairs={{0,4},{4,0},{8,12},{12,8},{16,20},{20,16},{24,28},{28,24},{1,5},{5... | collective-permute-start | bytes 221192 | tf_op jit(solution)/shard_map/ppermute | solution.py:410
  16.6 5.1 %collective-permute-start.8 = (bf16[144,256]{1,0:T(8,128)(2,1)S(1)}, bf16[144,256]{1,0:T(8,128)(2,1)S(1)}, u32[]{:S(2)}, u32[]{:S(2)}) collective-permute-start(bf16[144,256]{1,0:T(8,128)(2,1)S(1)} %collective-permute-done.3.refs_3_.refs_6_.refs_2_), channel_id=1, source_target_pairs={{0,4},{4,0},{8,12},{12,8},{16,20},{20,16},{24,28},{28,24},{1,5},{5... | collective-permute-start | bytes 221192 | tf_op jit(solution)/shard_map/ppermute | solution.py:410
  17.2 5.8 %collective-permute-start.9 = (bf16[144,256]{1,0:T(8,128)(2,1)S(1)}, bf16[144,256]{1,0:T(8,128)(2,1)S(1)}, u32[]{:S(2)}, u32[]{:S(2)}) collective-permute-start(bf16[144,256]{1,0:T(8,128)(2,1)S(1)} %collective-permute-done.4.refs_4_.refs_7_.refs_3_), channel_id=1, source_target_pairs={{0,4},{4,0},{8,12},{12,8},{16,20},{20,16},{24,28},{28,24},{1,5},{5... | collective-permute-start | bytes 221192 | tf_op jit(solution)/shard_map/ppermute | solution.py:410
  28.4 11.1 %all-to-all-start = ((f32[8,8,256]{2,1,0:T(8,128)}), f32[8,8,256]{2,1,0:T(8,128)S(1)}, u32[]{:S(2)}, u32[]{:S(2)}) async-start(f32[8,8,256]{2,1,0:T(8,128)} %heads.1), calls=%async_computation | async-start | bytes 131072 | tf_op jit(solution)/shard_map/all_to_all | solution.py:472

commit v8 on v7

--- a/solution.py
+++ b/solution.py
@@ -99,22 +99,26 @@
     digits = []
     unit = 1
     while unit < n:
-        digits.append([ancestor(unit * digit) for digit in range(1, 8) if unit * digit < n])
+        digits.append([ancestor(unit * digit).astype(jnp.float32) for digit in range(1, 8) if unit * digit < n])
         unit *= 8
-    last = [found.astype(jnp.float32).T.astype(jnp.int32) for found in digits.pop()]
+    last = [found.T for found in digits.pop()]
+    rows_b, lanes_b = (ids.astype(jnp.float32).astype(jnp.bfloat16) for ids in (row_ids, lane_ids))
+    one, zero = jnp.ones((n, n), jnp.bfloat16), jnp.zeros((n, n), jnp.bfloat16)
+    identity = jnp.where(rows_b == lanes_b, one, zero)
     out = []
     for index in range(len(parents)):
         product_t = None
         for digit in digits:
-            mask = row_ids == lane_ids
+            factor = identity
             for found in digit:
-                mask = mask | (row_ids == found[index : index + 1, :])
-            factor = mask.astype(jnp.bfloat16)
+                row = jnp.broadcast_to(found[index : index + 1, :].astype(jnp.bfloat16), (n, n))
+                factor = jnp.where(rows_b == row, one, factor)
             product_t = factor if product_t is None else product(product_t, factor).astype(jnp.bfloat16)
-        mask = row_ids == lane_ids
+        factor = identity
         for found in last:
-            mask = mask | (lane_ids == found[:, index : index + 1])
-        out.append((mask.astype(jnp.bfloat16), product_t))
+            column = jnp.broadcast_to(found[:, index : index + 1], (n, n)).astype(jnp.bfloat16)
+            factor = jnp.where(lanes_b == column, one, factor)
+        out.append((factor, product_t))
     return [product_nt(left, right).astype(jnp.bfloat16) for left, right in out]
 
 
@@ -168,28 +172,20 @@
 
 def apply_first(matrix, swing):
     n = matrix.shape[1] // 4
-    high = swing.astype(jnp.bfloat16)
+    high, low = split(swing)
+    high_part, low_part = matrix[:, :n], matrix[:, 2 * n : 3 * n]
     return product(
-        jnp.concatenate([matrix[:, :n], matrix[:, 2 * n : 3 * n]], axis=1), jnp.concatenate([high, high], axis=0)
+        jnp.concatenate([high_part, low_part, high_part], axis=1), jnp.concatenate([high, high, low], axis=0)
     )
 
 
-def apply_change(matrix, change):
-    return product(matrix[:, : matrix.shape[1] // 2], change.astype(jnp.bfloat16))
-
-
 def inverse_of(swing, real, imag):
-    square = real * real + imag * imag
-    guess = pl.reciprocal(square, approx=True)
-    return swing * (guess * (2.0 - square * guess))
-
-
-def scaled_volts(swing, real, imag, change=False):
+    return swing * pltpu.reciprocal(real * real + imag * imag, approx=True)
+
+
+def scaled_volts(swing, real, imag):
     inverse = inverse_of(swing, real, imag)
-    scaled = real * inverse
-    if change:
-        scaled = scaled - swing.astype(jnp.bfloat16).astype(jnp.float32)
-    return jnp.concatenate([scaled, imag * inverse], axis=0)
+    return jnp.concatenate([real * inverse, imag * inverse], axis=0)
 
 
 def first_sweep(sections, factors_of, matrix_ref, swing_ref, drop_ref, inject_ref):
@@ -280,9 +276,9 @@
             imag = head_ref[place[index], 2 * sweep - 1 : 2 * sweep, :] - drop[n : 2 * n, :]
             swing = of(index, 1)[...]
             if sweep < SWEEPS - 1:
-                out = apply_change(of(index, 0)[...], scaled_volts(swing, real, imag, change=True))
-                again_ref[index] = of(index, 2)[...] + out[: 2 * n]
-                flow_ref[place[index]] = of(index, 3)[0:8, :] + out[2 * n : 2 * n + 8]
+                out = apply(of(index, 0)[...], scaled_volts(swing, real, imag))
+                again_ref[index] = out[: 2 * n]
+                flow_ref[place[index]] = out[2 * n : 2 * n + 8]
             else:
                 base = constants(sections[index], n)[2].T
                 active, reactive = base[:, 0:1], base[:, 1:2]
@@ -308,42 +304,57 @@
     for copy in copies:
         copy.start()
     matrix = matrix_ref[0 : 2 * n, :]
-    copies[0].wait()
+    for copy in copies:
+        copy.wait()
     loadings = loads[...]
-    for index in range(pieces):
-        copies[1 + index].wait()
-        for part in range(chunks):
-            chunk = jnp.bitwise_xor(node_ref[0], index) * chunks + part
-            swing = swing_of(loadings, factors_ref[index, part * width : (part + 1) * width, :])
-            swing_ref[chunk] = swing
-            drop_ref[chunk] = apply_first(matrix, swing)
+    together = 4 // chunks if chunks < 4 else 1
+
+    @pl.loop(0, pieces // together)
+    def _(outer):
+        for inner in range(together):
+            index = outer * together + inner
+            for part in range(chunks):
+                chunk = jnp.bitwise_xor(node_ref[0], index) * chunks + part
+                swing = swing_of(loadings, factors_ref[index, part * width : (part + 1) * width, :])
+                swing_ref[chunk] = swing
+                drop_ref[chunk] = apply_first(matrix, swing)
 
 
 def volts_kernel(matrix_ref, swing_ref, drop_ref, head_ref, real_ref, imag_ref, out_ref, sems):
     n = swing_ref.shape[1]
     chunks, width = swing_ref.shape[0], swing_ref.shape[2]
     matrix = matrix_ref[0 : 2 * n, :]
-    drops = [None] * chunks
-    copies = []
-    for sweep in range(SWEEPS):
-        for chunk in range(chunks):
-            drop = drop_ref[chunk] if sweep == 0 else drops[chunk]
-            real = head_ref[chunk, 2 * sweep : 2 * sweep + 1, :] - drop[:n]
-            imag = head_ref[chunk, 2 * sweep + 1 : 2 * sweep + 2, :] - drop[n:]
-            swing = swing_ref[chunk]
-            if sweep < SWEEPS - 2:
-                drops[chunk] = drop_ref[chunk] + apply_change(matrix, scaled_volts(swing, real, imag, change=True))
-            elif sweep < SWEEPS - 1:
-                drops[chunk] = apply(matrix, scaled_volts(swing, real, imag))
-            else:
-                rows = slice(chunk * width, (chunk + 1) * width)
-                for index, (part, to_ref) in enumerate(((real, real_ref), (imag, imag_ref))):
-                    out_ref[index, rows, :] = part.T
-                    copy = pltpu.make_async_copy(out_ref.at[index, rows, :], to_ref.at[rows, :], sems.at[index, chunk])
-                    copy.start()
-                    copies.append(copy)
-    for copy in copies:
-        copy.wait()
+    together = 4
+    rounds = chunks // together
+
+    def copies(outer):
+        rows = pl.ds(pl.multiple_of(outer * together * width, together * width), together * width)
+        return [
+            pltpu.make_async_copy(out_ref.at[index, rows, :], to_ref.at[rows, :], sems.at[index, outer])
+            for index, to_ref in enumerate((real_ref, imag_ref))
+        ]
+
+    @pl.loop(0, rounds)
+    def _(outer):
+        drops = [None] * together
+        for sweep in range(SWEEPS):
+            for inner in range(together):
+                chunk = outer * together + inner
+                drop = drop_ref[chunk] if sweep == 0 else drops[inner]
+                real = head_ref[chunk, 2 * sweep : 2 * sweep + 1, :] - drop[:n]
+                imag = head_ref[chunk, 2 * sweep + 1 : 2 * sweep + 2, :] - drop[n:]
+                if sweep < SWEEPS - 1:
+                    drops[inner] = apply(matrix, scaled_volts(swing_ref[chunk], real, imag))
+                else:
+                    rows = pl.ds(pl.multiple_of(chunk * width, width), width)
+                    out_ref[0, rows, :] = real.T
+                    out_ref[1, rows, :] = imag.T
+        for copy in copies(outer):
+            copy.start()
+
+    for outer in range(rounds):
+        for copy in copies(outer):
+            copy.wait()
 
 
 def after_kernel(*refs):

time: 42.8 us -> 43.6 us (1.019)
  waiting for transfers between devices: 8.84 us -> 9.71 us
    all_to_all x1, waiting for transfers between devices: 3.18 us -> 3.88 us  [local(): given = lax.all_to_all(heads, 'feeder', 0, 0, tiled=True)]
    pallas_call x1, Pallas kernels: 3.72 us -> 3.02 us  [local(): pl.pallas_call(first_kernel, out_shape=(jax.ShapeDtypeStruct((chunks, n,...]
    pallas_call x1, Pallas kernels: 3.1 us -> 3.69 us  [local(): pl.pallas_call(volts_kernel, out_shape=(jax.ShapeDtypeStruct((scen, n), f...]
  transfers between devices with their start and end apart: 11 -> 11, of which waited for: 4 -> 5; matrix products, arithmetic and copies ran while one was open for 0% -> 0% of each run, Pallas kernels for 18% -> 16%
where the time goes in v8:
time: 43.6 us; the launch traced here: 43.3 us
  starting transfers between devices  16.7 us (38%)
  Pallas kernels  16.1 us (37%)
  waiting for transfers between devices  9.71 us (22%)
  between operations  0.71 us (2%)
    ppermute x7, starting transfers between devices, swap(): lax.ppermute(block, 'feeder', [(i, i ^ offset) for i in range(feeders)])  9.47 us
    ppermute x7, waiting for transfers between devices, swap(): lax.ppermute(block, 'feeder', [(i, i ^ offset) for i in range(feeders)])  5.82 us
    pallas_call x1, Pallas kernels, local(): pl.pallas_call(functools.partial(heads_kernel, slots, early), out_shape=j...  5.62 us
    all_to_all x1, starting transfers between devices, local(): given = lax.all_to_all(heads, 'feeder', 0, 0, tiled=True)  4.15 us
    all_to_all x1, waiting for transfers between devices, local(): given = lax.all_to_all(heads, 'feeder', 0, 0, tiled=True)  3.88 us
    pallas_call x1, Pallas kernels, local(): pl.pallas_call(volts_kernel, out_shape=(jax.ShapeDtypeStruct((scen, n), f...  3.69 us
    ppermute x3, starting transfers between devices, trade(): return lax.ppermute(block, 'node', [(i, i ^ offset) for i in range(nodes)])  3.1 us
    pallas_call x1, Pallas kernels, local(): pl.pallas_call(first_kernel, out_shape=(jax.ShapeDtypeStruct((chunks, n,...  3.02 us
  transfers between devices with their start and end apart: 11, of which 5 were waited for; matrix products, arithmetic and copies ran while one was open for 0% of the time, Pallas kernels for 16%

profile of v8, /device:TPU:0, one launch (start us, length us, event | category | flops | bytes accessed | tf_op | source)
XLA Modules:
  0.0 43.3 jit_solution(12330046520386202035)
XLA Ops:
  0.6 3.0 %collective-permute-start.1 = (bf16[512,256]{1,0:T(8,128)(2,1)}, bf16[512,256]{1,0:T(8,128)(2,1)S(1)}, u32[]{:S(2)}, u32[]{:S(2)}) collective-permute-start(bf16[512,256]{1,0:T(8,128)(2,1)} %rows_ref.1), channel_id=1, source_target_pairs={{0,2},{1,3},{2,0},{3,1},{4,6},{5,7},{6,4},{7,5},{8,10},{9,11},{10,... | collective-permute-start | bytes 786440 | tf_op jit(solution)/shard_map/ppermute | solution.py:396
  3.7 0.9 %pack.1.refs_1_.refs_4_.refs_0_ = bf16[144,256]{1,0:T(8,128)(2,1)S(1)} custom-call(f32[2]{0:T(128)} %bitcast.6, bf16[128,256]{1,0:T(8,128)(2,1)} %loadings_ref.3, s32[1,128]{1,0:T(1,128)} %bitcast.7, f32[2,128]{1,0:T(2,128)} %base_ref.1, f32[2,128]{1,0:T(2,128)} %z_ref.1), custom_call_target="tpu_custom_call" | custom-call | tf_op jit(solution)/shard_map/pack/pallas_call | solution.py:403
  4.6 2.7 %collective-permute-start.2 = (bf16[144,256]{1,0:T(8,128)(2,1)S(1)}, bf16[144,256]{1,0:T(8,128)(2,1)S(1)}, u32[]{:S(2)}, u32[]{:S(2)}) collective-permute-start(bf16[144,256]{1,0:T(8,128)(2,1)S(1)} %pack.1.refs_1_.refs_4_.refs_0_), channel_id=1, source_target_pairs={{0,16},{4,20},{8,24},{12,28},{16,0},{20,4},{24,8},{28,12},{1,17},{... | collective-permute-start | bytes 221192 | tf_op jit(solution)/shard_map/ppermute | solution.py:421
  7.2 1.6 %collective-permute-start.3 = (bf16[144,256]{1,0:T(8,128)(2,1)S(1)}, bf16[144,256]{1,0:T(8,128)(2,1)S(1)}, u32[]{:S(2)}, u32[]{:S(2)}) collective-permute-start(bf16[144,256]{1,0:T(8,128)(2,1)S(1)} %pack.1.refs_1_.refs_4_.refs_0_), channel_id=1, source_target_pairs={{0,8},{4,12},{8,0},{12,4},{16,24},{20,28},{24,16},{28,20},{1,9},{5... | collective-permute-start | bytes 221192 | tf_op jit(solution)/shard_map/ppermute | solution.py:421
  8.8 0.2 collective-permute-start.4
  9.0 1.5 %collective-permute-start.5 = (bf16[144,256]{1,0:T(8,128)(2,1)S(1)}, bf16[144,256]{1,0:T(8,128)(2,1)S(1)}, u32[]{:S(2)}, u32[]{:S(2)}) collective-permute-start(bf16[144,256]{1,0:T(8,128)(2,1)S(1)} %pack.1.refs_1_.refs_4_.refs_0_), channel_id=1, source_target_pairs={{0,4},{4,0},{8,12},{12,8},{16,20},{20,16},{24,28},{28,24},{1,5},{5... | collective-permute-start | bytes 221192 | tf_op jit(solution)/shard_map/ppermute | solution.py:421
  10.5 0.0 collective-permute-done.2.refs_2_.refs_5_.refs_1_
  10.5 0.0 collective-permute-start
  10.5 1.1 %collective-permute-done.3.refs_3_.refs_6_.refs_2_ = bf16[144,256]{1,0:T(8,128)(2,1)S(1)} collective-permute-done((bf16[144,256]{1,0:T(8,128)(2,1)S(1)}, bf16[144,256]{1,0:T(8,128)(2,1)S(1)}, u32[]{:S(2)}, u32[]{:S(2)}) %collective-permute-start.3) | collective-permute-done | bytes 73760 | tf_op jit(solution)/shard_map/ppermute | solution.py:421
  11.6 3.4 %collective-permute-done.4.refs_4_.refs_7_.refs_3_ = bf16[144,256]{1,0:T(8,128)(2,1)S(1)} collective-permute-done((bf16[144,256]{1,0:T(8,128)(2,1)S(1)}, bf16[144,256]{1,0:T(8,128)(2,1)S(1)}, u32[]{:S(2)}, u32[]{:S(2)}) %collective-permute-start.4) | collective-permute-done | bytes 73760 | tf_op jit(solution)/shard_map/ppermute | solution.py:421
  14.9 0.1 collective-permute-start.6
  15.0 0.1 pad_add_fusion.place_ref
  15.1 1.5 %collective-permute-start.7 = (bf16[144,256]{1,0:T(8,128)(2,1)S(1)}, bf16[144,256]{1,0:T(8,128)(2,1)S(1)}, u32[]{:S(2)}, u32[]{:S(2)}) collective-permute-start(bf16[144,256]{1,0:T(8,128)(2,1)S(1)} %collective-permute-done.2.refs_2_.refs_5_.refs_1_), channel_id=1, source_target_pairs={{0,4},{4,0},{8,12},{12,8},{16,20},{20,16},{24,28},{28,24},{1,5},{5... | collective-permute-start | bytes 221192 | tf_op jit(solution)/shard_map/ppermute | solution.py:421
  16.6 0.5 %collective-permute-start.8 = (bf16[144,256]{1,0:T(8,128)(2,1)S(1)}, bf16[144,256]{1,0:T(8,128)(2,1)S(1)}, u32[]{:S(2)}, u32[]{:S(2)}) collective-permute-start(bf16[144,256]{1,0:T(8,128)(2,1)S(1)} %collective-permute-done.3.refs_3_.refs_6_.refs_2_), channel_id=1, source_target_pairs={{0,4},{4,0},{8,12},{12,8},{16,20},{20,16},{24,28},{28,24},{1,5},{5... | collective-permute-start | bytes 221192 | tf_op jit(solution)/shard_map/ppermute | solution.py:421
  17.2 1.5 %collective-permute-start.9 = (bf16[144,256]{1,0:T(8,128)(2,1)S(1)}, bf16[144,256]{1,0:T(8,128)(2,1)S(1)}, u32[]{:S(2)}, u32[]{:S(2)}) collective-permute-start(bf16[144,256]{1,0:T(8,128)(2,1)S(1)} %collective-permute-done.4.refs_4_.refs_7_.refs_3_), channel_id=1, source_target_pairs={{0,4},{4,0},{8,12},{12,8},{16,20},{20,16},{24,28},{28,24},{1,5},{5... | collective-permute-start | bytes 221192 | tf_op jit(solution)/shard_map/ppermute | solution.py:421
  18.6 0.0 collective-permute-done.refs_1_
  18.7 2.9 %early.1 = (bf16[256,256]{1,0:T(8,128)(2,1)S(1)}, bf16[272,512]{1,0:T(8,128)(2,1)S(1)}, bf16[3,512,256]{2,1,0:T(8,128)(2,1)}, bf16[5,272,512]{2,1,0:T(8,128)(2,1...) custom-call(s32[3]{0:T(128)S(1)} %pad_add_fusion.place_ref, ...), custom_call_target="tpu_custom_call" | custom-call | flops 2684354560 | bytes 3809280 | tf_op jit(solution)/shard_map/early/pallas_call | solution.py:454
  21.5 0.2 collective-permute-done.8.refs_6_
  21.7 1.2 %collective-permute-done.9.refs_7_ = bf16[144,256]{1,0:T(8,128)(2,1)S(1)} collective-permute-done((bf16[144,256]{1,0:T(8,128)(2,1)S(1)}, bf16[144,256]{1,0:T(8,128)(2,1)S(1)}, u32[]{:S(2)}, u32[]{:S(2)}) %collective-permute-start.9) | collective-permute-done | bytes 73760 | tf_op jit(solution)/shard_map/ppermute | solution.py:421
  22.9 5.6 %heads.1 = f32[8,8,256]{2,1,0:T(8,128)} custom-call(s32[3]{0:T(128)S(1)} %pad_add_fusion.place_ref, bf16[256,256]{1,0:T(8,128)(2,1)S(1)} %get-tuple-element.15.factors_ref, bf16[144,256]{1,0:T(8,128)(2,1)S(1)} %pack.1.refs_1_.refs_4_.refs_0_, bf16[144,256]{1,0:T(8,128)(2,1)S(1)} %collective-permute-done.2.refs_2_.refs_5_.refs_1_, ...), custom_call_target="tpu_custom_call" | custom-call | tf_op jit(solution)/shard_map/heads/pallas_call | solution.py:469
  28.6 4.2 %all-to-all-start = ((f32[8,8,256]{2,1,0:T(8,128)}), f32[8,8,256]{2,1,0:T(8,128)S(1)}, u32[]{:S(2)}, u32[]{:S(2)}) async-start(f32[8,8,256]{2,1,0:T(8,128)} %heads.1), calls=%async_computation | async-start | bytes 131072 | tf_op jit(solution)/shard_map/all_to_all | solution.py:483
  32.7 3.0 %first.1 = (f32[8,128,256]{2,1,0:T(8,128)S(1)}, f32[8,256,256]{2,1,0:T(8,128)S(1)}) custom-call(s32[1]{0:T(128)} %bitcast.5.node_ref, bf16[272,512]{1,0:T(8,128)(2,1)S(1)} %get-tuple-element.11.matrix_ref, bf16[128,256]{1,0:T(8,128)(2,1)} %loadings_ref.3, bf16[512,256]{1,0:T(8,128)(2,1)} %rows_ref.1, bf16[3,512,256]{2,1,0:T(8,128)(2,1)} %get-tuple-element.12.kept_ref), custom_call_target="tpu_custom_call" | custom-call | flops 536870912 | bytes 3145728 | tf_op jit(solution)/shard_map/first/pallas_call | solution.py:487
  35.7 3.9 %all-to-all-done.head_ref = f32[8,8,256]{2,1,0:T(8,128)S(1)} async-done(((f32[8,8,256]{2,1,0:T(8,128)}), f32[8,8,256]{2,1,0:T(8,128)S(1)}, u32[]{:S(2)}, u32[]{:S(2)}) %all-to-all-start) | async-done | bytes 65568 | tf_op jit(solution)/shard_map/all_to_all | solution.py:483
  39.6 3.7 %volts.1 = (f32[2048,128]{1,0:T(8,128)}, f32[2048,128]{1,0:T(8,128)}) custom-call(bf16[272,512]{1,0:T(8,128)(2,1)S(1)} %get-tuple-element.11.matrix_ref, f32[8,128,256]{2,1,0:T(8,128)S(1)} %get-tuple-element.13.swing_ref, f32[8,256,256]{2,1,0:T(8,128)S(1)} %get-tuple-element.14.drop_ref, f32[8,8,256]{2,1,0:T(8,128)S(1)} %all-to-all-done.head_ref), custom_call_target="tpu_custom_call" | custom-call | tf_op jit(solution)/shard_map/volts/pallas_call | solution.py:504
  (5 shorter events, 0.0 us)
Async XLA Ops:
  0.6 14.3 %collective-permute-start.1 = (bf16[512,256]{1,0:T(8,128)(2,1)}, bf16[512,256]{1,0:T(8,128)(2,1)S(1)}, u32[]{:S(2)}, u32[]{:S(2)}) collective-permute-start(bf16[512,256]{1,0:T(8,128)(2,1)} %rows_ref.1), channel_id=1, source_target_pairs={{0,2},{1,3},{2,0},{3,1},{4,6},{5,7},{6,4},{7,5},{8,10},{9,11},{10,... | collective-permute-start | bytes 786440 | tf_op jit(solution)/shard_map/ppermute | solution.py:396
  4.6 5.9 %collective-permute-start.2 = (bf16[144,256]{1,0:T(8,128)(2,1)S(1)}, bf16[144,256]{1,0:T(8,128)(2,1)S(1)}, u32[]{:S(2)}, u32[]{:S(2)}) collective-permute-start(bf16[144,256]{1,0:T(8,128)(2,1)S(1)} %pack.1.refs_1_.refs_4_.refs_0_), channel_id=1, source_target_pairs={{0,16},{4,20},{8,24},{12,28},{16,0},{20,4},{24,8},{28,12},{1,17},{... | collective-permute-start | bytes 221192 | tf_op jit(solution)/shard_map/ppermute | solution.py:421
  7.2 4.4 %collective-permute-start.3 = (bf16[144,256]{1,0:T(8,128)(2,1)S(1)}, bf16[144,256]{1,0:T(8,128)(2,1)S(1)}, u32[]{:S(2)}, u32[]{:S(2)}) collective-permute-start(bf16[144,256]{1,0:T(8,128)(2,1)S(1)} %pack.1.refs_1_.refs_4_.refs_0_), channel_id=1, source_target_pairs={{0,8},{4,12},{8,0},{12,4},{16,24},{20,28},{24,16},{28,20},{1,9},{5... | collective-permute-start | bytes 221192 | tf_op jit(solution)/shard_map/ppermute | solution.py:421
  8.8 6.2 %collective-permute-start.4 = (bf16[144,256]{1,0:T(8,128)(2,1)S(1)}, bf16[144,256]{1,0:T(8,128)(2,1)S(1)}, u32[]{:S(2)}, u32[]{:S(2)}) collective-permute-start(bf16[144,256]{1,0:T(8,128)(2,1)S(1)} %pack.1.refs_1_.refs_4_.refs_0_), channel_id=1, source_target_pairs={{0,24},{4,28},{8,16},{12,20},{16,8},{20,12},{24,0},{28,4},{1,25},{... | collective-permute-start | bytes 221192 | tf_op jit(solution)/shard_map/ppermute | solution.py:421
  9.0 5.9 %collective-permute-start.5 = (bf16[144,256]{1,0:T(8,128)(2,1)S(1)}, bf16[144,256]{1,0:T(8,128)(2,1)S(1)}, u32[]{:S(2)}, u32[]{:S(2)}) collective-permute-start(bf16[144,256]{1,0:T(8,128)(2,1)S(1)} %pack.1.refs_1_.refs_4_.refs_0_), channel_id=1, source_target_pairs={{0,4},{4,0},{8,12},{12,8},{16,20},{20,16},{24,28},{28,24},{1,5},{5... | collective-permute-start | bytes 221192 | tf_op jit(solution)/shard_map/ppermute | solution.py:421
  10.5 8.1 %collective-permute-start = (bf16[512,256]{1,0:T(8,128)(2,1)}, bf16[512,256]{1,0:T(8,128)(2,1)S(1)}, u32[]{:S(2)}, u32[]{:S(2)}) collective-permute-start(bf16[512,256]{1,0:T(8,128)(2,1)} %rows_ref.1), channel_id=1, source_target_pairs={{0,1},{1,0},{2,3},{3,2},{4,5},{5,4},{6,7},{7,6},{8,9},{9,8},{10,11... | collective-permute-start | bytes 786440 | tf_op jit(solution)/shard_map/ppermute | solution.py:396
  14.9 3.7 %collective-permute-start.6 = (bf16[512,256]{1,0:T(8,128)(2,1)S(1)}, bf16[512,256]{1,0:T(8,128)(2,1)S(1)}, u32[]{:S(2)}, u32[]{:S(2)}) collective-permute-start(bf16[512,256]{1,0:T(8,128)(2,1)S(1)} %after.1.refs_2_), channel_id=1, source_target_pairs={{0,1},{1,0},{2,3},{3,2},{4,5},{5,4},{6,7},{7,6},{8,9},{9,8},{10,11... | collective-permute-start | bytes 786440 | tf_op jit(solution)/shard_map/ppermute | solution.py:396
  15.1 6.4 %collective-permute-start.7 = (bf16[144,256]{1,0:T(8,128)(2,1)S(1)}, bf16[144,256]{1,0:T(8,128)(2,1)S(1)}, u32[]{:S(2)}, u32[]{:S(2)}) collective-permute-start(bf16[144,256]{1,0:T(8,128)(2,1)S(1)} %collective-permute-done.2.refs_2_.refs_5_.refs_1_), channel_id=1, source_target_pairs={{0,4},{4,0},{8,12},{12,8},{16,20},{20,16},{24,28},{28,24},{1,5},{5... | collective-permute-start | bytes 221192 | tf_op jit(solution)/shard_map/ppermute | solution.py:421
  16.6 5.1 %collective-permute-start.8 = (bf16[144,256]{1,0:T(8,128)(2,1)S(1)}, bf16[144,256]{1,0:T(8,128)(2,1)S(1)}, u32[]{:S(2)}, u32[]{:S(2)}) collective-permute-start(bf16[144,256]{1,0:T(8,128)(2,1)S(1)} %collective-permute-done.3.refs_3_.refs_6_.refs_2_), channel_id=1, source_target_pairs={{0,4},{4,0},{8,12},{12,8},{16,20},{20,16},{24,28},{28,24},{1,5},{5... | collective-permute-start | bytes 221192 | tf_op jit(solution)/shard_map/ppermute | solution.py:421
  17.2 5.8 %collective-permute-start.9 = (bf16[144,256]{1,0:T(8,128)(2,1)S(1)}, bf16[144,256]{1,0:T(8,128)(2,1)S(1)}, u32[]{:S(2)}, u32[]{:S(2)}) collective-permute-start(bf16[144,256]{1,0:T(8,128)(2,1)S(1)} %collective-permute-done.4.refs_4_.refs_7_.refs_3_), channel_id=1, source_target_pairs={{0,4},{4,0},{8,12},{12,8},{16,20},{20,16},{24,28},{28,24},{1,5},{5... | collective-permute-start | bytes 221192 | tf_op jit(solution)/shard_map/ppermute | solution.py:421
  28.6 11.1 %all-to-all-start = ((f32[8,8,256]{2,1,0:T(8,128)}), f32[8,8,256]{2,1,0:T(8,128)S(1)}, u32[]{:S(2)}, u32[]{:S(2)}) async-start(f32[8,8,256]{2,1,0:T(8,128)} %heads.1), calls=%async_computation | async-start | bytes 131072 | tf_op jit(solution)/shard_map/all_to_all | solution.py:483

commit v9 on v8

--- a/solution.py
+++ b/solution.py
@@ -77,14 +77,14 @@
     return high, middle, high + middle + meta[8:16, 0:n]
 
 
-def section_paths(parents, n):
-    rows = max(8, len(parents))
+def matrix_steps(sections, n):
+    highs, middles, rows = zip(*(constants(section, n) for section in sections))
     row_ids = lax.broadcasted_iota(jnp.int32, (n, n), 0)
     lane_ids = lax.broadcasted_iota(jnp.int32, (n, n), 1)
-    section_ids = lax.broadcasted_iota(jnp.int32, (rows, n), 0)
-    stacked = jnp.full((rows, n), -1, jnp.int32)
-    for index, row in enumerate(parents):
-        stacked = jnp.where(section_ids == index, row.astype(jnp.int32), stacked)
+    section_ids = lax.broadcasted_iota(jnp.int32, (max(8, len(sections)), n), 0)
+    stacked = jnp.full(section_ids.shape, -1, jnp.int32)
+    for index, row in enumerate(rows):
+        stacked = jnp.where(section_ids == index, row[6:7].astype(jnp.int32), stacked)
     known = {1: stacked}
 
     def ancestor(distance):
@@ -102,30 +102,31 @@
         digits.append([ancestor(unit * digit).astype(jnp.float32) for digit in range(1, 8) if unit * digit < n])
         unit *= 8
     last = [found.T for found in digits.pop()]
+    yield None
+
     rows_b, lanes_b = (ids.astype(jnp.float32).astype(jnp.bfloat16) for ids in (row_ids, lane_ids))
     one, zero = jnp.ones((n, n), jnp.bfloat16), jnp.zeros((n, n), jnp.bfloat16)
     identity = jnp.where(rows_b == lanes_b, one, zero)
-    out = []
-    for index in range(len(parents)):
-        product_t = None
+    products = [None] * len(sections)
+    for index in range(len(sections)):
         for digit in digits:
             factor = identity
             for found in digit:
                 row = jnp.broadcast_to(found[index : index + 1, :].astype(jnp.bfloat16), (n, n))
                 factor = jnp.where(rows_b == row, one, factor)
-            product_t = factor if product_t is None else product(product_t, factor).astype(jnp.bfloat16)
+            done = products[index]
+            products[index] = factor if done is None else product(done, factor).astype(jnp.bfloat16)
+    yield None
+
+    paths = []
+    for index in range(len(sections)):
         factor = identity
         for found in last:
             column = jnp.broadcast_to(found[:, index : index + 1], (n, n)).astype(jnp.bfloat16)
             factor = jnp.where(lanes_b == column, one, factor)
-        out.append((factor, product_t))
-    return [product_nt(left, right).astype(jnp.bfloat16) for left, right in out]
-
-
-def section_matrices(sections, n):
-    pad_ids = lax.broadcasted_iota(jnp.int32, (EXTRA, 2 * n), 0)
-    highs, middles, rows = zip(*(constants(section, n) for section in sections))
-    paths = section_paths([row[6:7] for row in rows], n)
+        paths.append(product_nt(factor, products[index]).astype(jnp.bfloat16))
+    yield None
+
     shared = []
     for path, high, middle in zip(paths, highs, middles):
         wide_path = path.astype(jnp.float32)
@@ -135,6 +136,9 @@
 
         left = jnp.concatenate([scaled(2), scaled(3)], axis=0).astype(jnp.bfloat16)
         shared.append(product_nt(left, jnp.concatenate([path, path], axis=1)))
+    yield None
+
+    pad_ids = lax.broadcasted_iota(jnp.int32, (EXTRA, 2 * n), 0)
     out = []
     for both, row in zip(shared, rows):
         resist, react = both[:n], both[n:]
@@ -155,7 +159,7 @@
                 [whole(real_high, imag_high, sums_high), whole(real_low, imag_low, sums_low)], axis=1
             )
         )
-    return out
+    yield out
 
 
 def swing_of(loadings, factors):
@@ -186,21 +190,6 @@
 def scaled_volts(swing, real, imag):
     inverse = inverse_of(swing, real, imag)
     return jnp.concatenate([real * inverse, imag * inverse], axis=0)
-
-
-def first_sweep(sections, factors_of, matrix_ref, swing_ref, drop_ref, inject_ref):
-    n = swing_ref.shape[1]
-    for start in range(0, len(sections), 8):
-        group = sections[start : start + 8]
-        for slot, matrix in enumerate(section_matrices(group, n), start):
-            matrix_ref[slot] = matrix
-        factors = factors_of(start)
-        for slot, section in enumerate(group, start):
-            swing = swing_of(section[0:n, :], factors)
-            swing_ref[slot] = swing
-            out = apply_first(matrix_ref[slot], swing)
-            drop_ref[slot] = out[: 2 * n]
-            inject_ref[slot] = out[2 * n :]
 
 
 def early_kernel(pieces, place_ref, *refs):
@@ -220,12 +209,21 @@
             rows = piece_ref.at[pl.ds(pl.multiple_of(offset, width), width), :]
             pltpu.make_async_copy(rows, factors_ref, sem).start()
 
-    def factors_of(start):
+    n = swing_ref.shape[1]
+    for start in range(0, len(sections), 8):
+        group = list(enumerate(sections))[start : start + 8]
+        steps = matrix_steps([section for _, section in group], n)
+        next(steps)
         if start == 0:
             pltpu.make_async_copy(piece_refs[0].at[0:width, :], factors_ref, sem).wait()
-        return factors_ref[...]
-
-    first_sweep(sections, factors_of, matrix_ref, swing_ref, drop_ref, inject_ref)
+        for slot, section in group:
+            swing_ref[slot] = swing_of(section[0:n, :], factors_ref[...])
+        *_, matrices = steps
+        for (slot, _), matrix in zip(group, matrices):
+            matrix_ref[slot] = matrix
+            out = apply_first(matrix_ref[slot], swing_ref[slot])
+            drop_ref[slot] = out[: 2 * n]
+            inject_ref[slot] = out[2 * n :]
     own_ref[...] = matrix_ref[0]
     for copy in keeps:
         copy.wait()
@@ -235,20 +233,38 @@
     feeders = len(slots)
     sections = refs[:feeders]
     early_refs = refs[feeders : feeders + 4]
-    head_ref, matrix_ref, swing_ref, drop_ref, inject_ref, again_ref, flow_ref, trunk_ref = refs[feeders + 4 :]
+    head_ref, matrix_ref, swing_ref, drop_ref, again_ref, flow_ref, trunk_ref = refs[feeders + 4 :]
     width = factors_ref.shape[0]
     n = swing_ref.shape[1]
-    first_sweep(sections[early:], lambda start: factors_ref[...], matrix_ref, swing_ref, drop_ref, inject_ref)
-    late_refs = (matrix_ref, swing_ref, drop_ref, inject_ref)
     place = [jnp.bitwise_xor(place_ref[2], slot) for slot in slots]
+    late_refs = (matrix_ref, swing_ref, drop_ref)
 
     def of(index, which):
         return early_refs[which].at[index] if index < early else late_refs[which].at[index - early]
 
+    def flow_of(index, real, imag):
+        base = constants(sections[index], n)[2].T
+        active, reactive = base[:, 0:1], base[:, 1:2]
+        if imag is None:
+            parts = (active * real, -reactive * real)
+        else:
+            parts = (active * real + reactive * imag, active * imag - reactive * real)
+        return [jnp.sum(part, axis=0, keepdims=True) for part in parts]
+
+    groups = [list(range(start, min(start + 8, feeders))) for start in range(early, feeders, 8)]
+    steps = [matrix_steps([sections[index] for index in group], n) for group in groups]
+    if steps:
+        next(steps[0])
     for index in range(feeders):
         row = constants(sections[index], n)[2]
         trunk_ref[place[index], 0:2, :] = wide(row[4:6], width)
-        flow_ref[place[index]] = of(index, 3)[0:8, :]
+        if index < early:
+            flow_ref[place[index]] = of(index, 3)[0:8, :]
+        else:
+            swing = swing_of(sections[index][0:n, :], factors_ref[...])
+            of(index, 1)[...] = swing
+            for part, total in enumerate(flow_of(index, swing, None)):
+                flow_ref[place[index], part : part + 1, :] = total
 
     def heads(sweep):
         flows = [None] * feeders
@@ -268,23 +284,38 @@
             head_ref[g, 2 * sweep : 2 * sweep + 1, :] = head_real
             head_ref[g, 2 * sweep + 1 : 2 * sweep + 2, :] = head_imag
 
+    def volts(index, sweep):
+        drop = of(index, 2) if sweep == 1 else again_ref.at[index]
+        real = head_ref[place[index], 2 * sweep - 2 : 2 * sweep - 1, :] - drop[0:n, :]
+        imag = head_ref[place[index], 2 * sweep - 1 : 2 * sweep, :] - drop[n : 2 * n, :]
+        return real, imag
+
+    def middle(index, sweep):
+        out = apply(of(index, 0)[...], scaled_volts(of(index, 1)[...], *volts(index, sweep)))
+        again_ref[index] = out[: 2 * n]
+        flow_ref[place[index]] = out[2 * n : 2 * n + 8]
+
     heads(0)
-    for sweep in range(1, SWEEPS):
+    ready = list(range(early))
+    for group, step in zip(groups, steps):
+        for matrices in step:
+            if ready:
+                middle(ready.pop(0), 1)
+        for index, matrix in zip(group, matrices):
+            of(index, 0)[...] = matrix
+            of(index, 2)[...] = apply_first(matrix, of(index, 1)[...])[: 2 * n]
+    for index in ready + list(range(early, feeders)):
+        middle(index, 1)
+    heads(1)
+    for sweep in range(2, SWEEPS):
         for index in range(feeders):
-            drop = of(index, 2) if sweep == 1 else again_ref.at[index]
-            real = head_ref[place[index], 2 * sweep - 2 : 2 * sweep - 1, :] - drop[0:n, :]
-            imag = head_ref[place[index], 2 * sweep - 1 : 2 * sweep, :] - drop[n : 2 * n, :]
-            swing = of(index, 1)[...]
             if sweep < SWEEPS - 1:
-                out = apply(of(index, 0)[...], scaled_volts(swing, real, imag))
-                again_ref[index] = out[: 2 * n]
-                flow_ref[place[index]] = out[2 * n : 2 * n + 8]
+                middle(index, sweep)
             else:
-                base = constants(sections[index], n)[2].T
-                active, reactive = base[:, 0:1], base[:, 1:2]
-                inverse = inverse_of(swing, real, imag)
-                flow_ref[place[index], 0:1, :] = jnp.sum(inverse * (active * real + reactive * imag), axis=0, keepdims=True)
-                flow_ref[place[index], 1:2, :] = jnp.sum(inverse * (active * imag - reactive * real), axis=0, keepdims=True)
+                real, imag = volts(index, sweep)
+                inverse = inverse_of(of(index, 1)[...], real, imag)
+                for part, total in enumerate(flow_of(index, real * inverse, imag * inverse)):
+                    flow_ref[place[index], part : part + 1, :] = total
         heads(sweep)
     for g in range(feeders):
         head_ref[g, 2 * SWEEPS :, :] = jnp.zeros((head_ref.shape[1] - 2 * SWEEPS, width), jnp.float32)
@@ -324,37 +355,28 @@
     n = swing_ref.shape[1]
     chunks, width = swing_ref.shape[0], swing_ref.shape[2]
     matrix = matrix_ref[0 : 2 * n, :]
-    together = 4
-    rounds = chunks // together
-
-    def copies(outer):
-        rows = pl.ds(pl.multiple_of(outer * together * width, together * width), together * width)
-        return [
-            pltpu.make_async_copy(out_ref.at[index, rows, :], to_ref.at[rows, :], sems.at[index, outer])
-            for index, to_ref in enumerate((real_ref, imag_ref))
-        ]
-
-    @pl.loop(0, rounds)
-    def _(outer):
-        drops = [None] * together
-        for sweep in range(SWEEPS):
-            for inner in range(together):
-                chunk = outer * together + inner
-                drop = drop_ref[chunk] if sweep == 0 else drops[inner]
-                real = head_ref[chunk, 2 * sweep : 2 * sweep + 1, :] - drop[:n]
-                imag = head_ref[chunk, 2 * sweep + 1 : 2 * sweep + 2, :] - drop[n:]
-                if sweep < SWEEPS - 1:
-                    drops[inner] = apply(matrix, scaled_volts(swing_ref[chunk], real, imag))
-                else:
-                    rows = pl.ds(pl.multiple_of(chunk * width, width), width)
-                    out_ref[0, rows, :] = real.T
-                    out_ref[1, rows, :] = imag.T
-        for copy in copies(outer):
-            copy.start()
-
-    for outer in range(rounds):
-        for copy in copies(outer):
-            copy.wait()
+    drops = [None] * chunks
+    copies = []
+
+    def advance(chunk, sweep):
+        drop = drop_ref[chunk] if sweep == 0 else drops[chunk]
+        real = head_ref[chunk, 2 * sweep : 2 * sweep + 1, :] - drop[:n]
+        imag = head_ref[chunk, 2 * sweep + 1 : 2 * sweep + 2, :] - drop[n:]
+        if sweep < SWEEPS - 1:
+            drops[chunk] = apply(matrix, scaled_volts(swing_ref[chunk], real, imag))
+            return
+        rows = slice(chunk * width, (chunk + 1) * width)
+        for index, (part, to_ref) in enumerate(((real, real_ref), (imag, imag_ref))):
+            out_ref[index, rows, :] = part.T
+            copies.append(pltpu.make_async_copy(out_ref.at[index, rows, :], to_ref.at[rows, :], sems.at[index, chunk]))
+            copies[-1].start()
+
+    for turn in range(chunks + SWEEPS - 1):
+        for sweep in reversed(range(SWEEPS)):
+            if 0 <= turn - sweep < chunks:
+                advance(turn - sweep, sweep)
+    for copy in copies:
+        copy.wait()
 
 
 def after_kernel(*refs):
@@ -471,7 +493,7 @@
         out_shape=jax.ShapeDtypeStruct((feeders, 8, width), f32),
         in_specs=[SMEM] + [VMEM] * (1 + feeders + 4),
         out_specs=VMEM,
-        scratch_shapes=[pltpu.VMEM(*state) for state in states(max(feeders - early, 1))]
+        scratch_shapes=[pltpu.VMEM(*state) for state in states(max(feeders - early, 1))[:3]]
         + [
             pltpu.VMEM((feeders, 2 * n, width), f32),
             pltpu.VMEM((feeders, 8, width), f32),

time: 43.6 us -> 41.9 us (0.961)
  Pallas kernels: 16.1 us -> 14.4 us
    pallas_call x1, Pallas kernels: 5.62 us -> 4.47 us  [local(): pl.pallas_call(functools.partial(heads_kernel, slots, early), out_shape=j...]
    pallas_call x1, Pallas kernels: 3.69 us -> 3.15 us  [local(): pl.pallas_call(volts_kernel, out_shape=(jax.ShapeDtypeStruct((scen, n), f...]
where the time goes in v9:
time: 41.9 us; the launch traced here: 41.6 us
  starting transfers between devices  16.7 us (40%)
  Pallas kernels  14.4 us (34%)
  waiting for transfers between devices  9.66 us (23%)
  between operations  0.71 us (2%)
    ppermute x7, starting transfers between devices, swap(): lax.ppermute(block, 'feeder', [(i, i ^ offset) for i in range(feeders)])  9.47 us
    ppermute x7, waiting for transfers between devices, swap(): lax.ppermute(block, 'feeder', [(i, i ^ offset) for i in range(feeders)])  5.77 us
    pallas_call x1, Pallas kernels, local(): pl.pallas_call(functools.partial(heads_kernel, slots, early), out_shape=j...  4.47 us
    all_to_all x1, starting transfers between devices, local(): given = lax.all_to_all(heads, 'feeder', 0, 0, tiled=True)  4.16 us
    all_to_all x1, waiting for transfers between devices, local(): given = lax.all_to_all(heads, 'feeder', 0, 0, tiled=True)  3.88 us
    pallas_call x1, Pallas kernels, local(): pl.pallas_call(volts_kernel, out_shape=(jax.ShapeDtypeStruct((scen, n), f...  3.15 us
    ppermute x3, starting transfers between devices, trade(): return lax.ppermute(block, 'node', [(i, i ^ offset) for i in range(nodes)])  3.1 us
    pallas_call x1, Pallas kernels, local(): pl.pallas_call(first_kernel, out_shape=(jax.ShapeDtypeStruct((chunks, n,...  3.01 us
  transfers between devices with their start and end apart: 11, of which 5 were waited for; matrix products, arithmetic and copies ran while one was open for 0% of the time, Pallas kernels for 16%

profile of v9, /device:TPU:0, one launch (start us, length us, event | category | flops | bytes accessed | tf_op | source)
XLA Modules:
  0.0 41.6 jit_solution(11224695087335447758)
XLA Ops:
  0.6 3.0 %collective-permute-start.1 = (bf16[512,256]{1,0:T(8,128)(2,1)}, bf16[512,256]{1,0:T(8,128)(2,1)S(1)}, u32[]{:S(2)}, u32[]{:S(2)}) collective-permute-start(bf16[512,256]{1,0:T(8,128)(2,1)} %rows_ref.1), channel_id=1, source_target_pairs={{0,2},{1,3},{2,0},{3,1},{4,6},{5,7},{6,4},{7,5},{8,10},{9,11},{10,... | collective-permute-start | bytes 786440 | tf_op jit(solution)/shard_map/ppermute | solution.py:418
  3.7 0.9 %pack.1.refs_1_.refs_4_.refs_0_ = bf16[144,256]{1,0:T(8,128)(2,1)S(1)} custom-call(f32[2]{0:T(128)} %bitcast.6, bf16[128,256]{1,0:T(8,128)(2,1)} %loadings_ref.3, s32[1,128]{1,0:T(1,128)} %bitcast.7, f32[2,128]{1,0:T(2,128)} %base_ref.1, f32[2,128]{1,0:T(2,128)} %z_ref.1), custom_call_target="tpu_custom_call" | custom-call | tf_op jit(solution)/shard_map/pack/pallas_call | solution.py:425
  4.6 2.7 %collective-permute-start.2 = (bf16[144,256]{1,0:T(8,128)(2,1)S(1)}, bf16[144,256]{1,0:T(8,128)(2,1)S(1)}, u32[]{:S(2)}, u32[]{:S(2)}) collective-permute-start(bf16[144,256]{1,0:T(8,128)(2,1)S(1)} %pack.1.refs_1_.refs_4_.refs_0_), channel_id=1, source_target_pairs={{0,16},{4,20},{8,24},{12,28},{16,0},{20,4},{24,8},{28,12},{1,17},{... | collective-permute-start | bytes 221192 | tf_op jit(solution)/shard_map/ppermute | solution.py:443
  7.2 1.6 %collective-permute-start.3 = (bf16[144,256]{1,0:T(8,128)(2,1)S(1)}, bf16[144,256]{1,0:T(8,128)(2,1)S(1)}, u32[]{:S(2)}, u32[]{:S(2)}) collective-permute-start(bf16[144,256]{1,0:T(8,128)(2,1)S(1)} %pack.1.refs_1_.refs_4_.refs_0_), channel_id=1, source_target_pairs={{0,8},{4,12},{8,0},{12,4},{16,24},{20,28},{24,16},{28,20},{1,9},{5... | collective-permute-start | bytes 221192 | tf_op jit(solution)/shard_map/ppermute | solution.py:443
  8.8 0.2 collective-permute-start.4
  9.0 1.5 %collective-permute-start.5 = (bf16[144,256]{1,0:T(8,128)(2,1)S(1)}, bf16[144,256]{1,0:T(8,128)(2,1)S(1)}, u32[]{:S(2)}, u32[]{:S(2)}) collective-permute-start(bf16[144,256]{1,0:T(8,128)(2,1)S(1)} %pack.1.refs_1_.refs_4_.refs_0_), channel_id=1, source_target_pairs={{0,4},{4,0},{8,12},{12,8},{16,20},{20,16},{24,28},{28,24},{1,5},{5... | collective-permute-start | bytes 221192 | tf_op jit(solution)/shard_map/ppermute | solution.py:443
  10.5 0.0 collective-permute-done.2.refs_2_.refs_5_.refs_1_
  10.5 0.0 collective-permute-start
  10.5 1.1 %collective-permute-done.3.refs_3_.refs_6_.refs_2_ = bf16[144,256]{1,0:T(8,128)(2,1)S(1)} collective-permute-done((bf16[144,256]{1,0:T(8,128)(2,1)S(1)}, bf16[144,256]{1,0:T(8,128)(2,1)S(1)}, u32[]{:S(2)}, u32[]{:S(2)}) %collective-permute-start.3) | collective-permute-done | bytes 73760 | tf_op jit(solution)/shard_map/ppermute | solution.py:443
  11.6 3.4 %collective-permute-done.4.refs_4_.refs_7_.refs_3_ = bf16[144,256]{1,0:T(8,128)(2,1)S(1)} collective-permute-done((bf16[144,256]{1,0:T(8,128)(2,1)S(1)}, bf16[144,256]{1,0:T(8,128)(2,1)S(1)}, u32[]{:S(2)}, u32[]{:S(2)}) %collective-permute-start.4) | collective-permute-done | bytes 73760 | tf_op jit(solution)/shard_map/ppermute | solution.py:443
  14.9 0.1 collective-permute-start.6
  15.0 0.1 pad_add_fusion.place_ref
  15.1 1.5 %collective-permute-start.7 = (bf16[144,256]{1,0:T(8,128)(2,1)S(1)}, bf16[144,256]{1,0:T(8,128)(2,1)S(1)}, u32[]{:S(2)}, u32[]{:S(2)}) collective-permute-start(bf16[144,256]{1,0:T(8,128)(2,1)S(1)} %collective-permute-done.2.refs_2_.refs_5_.refs_1_), channel_id=1, source_target_pairs={{0,4},{4,0},{8,12},{12,8},{16,20},{20,16},{24,28},{28,24},{1,5},{5... | collective-permute-start | bytes 221192 | tf_op jit(solution)/shard_map/ppermute | solution.py:443
  16.6 0.5 %collective-permute-start.8 = (bf16[144,256]{1,0:T(8,128)(2,1)S(1)}, bf16[144,256]{1,0:T(8,128)(2,1)S(1)}, u32[]{:S(2)}, u32[]{:S(2)}) collective-permute-start(bf16[144,256]{1,0:T(8,128)(2,1)S(1)} %collective-permute-done.3.refs_3_.refs_6_.refs_2_), channel_id=1, source_target_pairs={{0,4},{4,0},{8,12},{12,8},{16,20},{20,16},{24,28},{28,24},{1,5},{5... | collective-permute-start | bytes 221192 | tf_op jit(solution)/shard_map/ppermute | solution.py:443
  17.2 1.5 %collective-permute-start.9 = (bf16[144,256]{1,0:T(8,128)(2,1)S(1)}, bf16[144,256]{1,0:T(8,128)(2,1)S(1)}, u32[]{:S(2)}, u32[]{:S(2)}) collective-permute-start(bf16[144,256]{1,0:T(8,128)(2,1)S(1)} %collective-permute-done.4.refs_4_.refs_7_.refs_3_), channel_id=1, source_target_pairs={{0,4},{4,0},{8,12},{12,8},{16,20},{20,16},{24,28},{28,24},{1,5},{5... | collective-permute-start | bytes 221192 | tf_op jit(solution)/shard_map/ppermute | solution.py:443
  18.6 0.0 collective-permute-done.refs_1_
  18.7 2.9 %early.1 = (bf16[256,256]{1,0:T(8,128)(2,1)S(1)}, bf16[272,512]{1,0:T(8,128)(2,1)S(1)}, bf16[3,512,256]{2,1,0:T(8,128)(2,1)}, bf16[5,272,512]{2,1,0:T(8,128)(2,1...) custom-call(s32[3]{0:T(128)S(1)} %pad_add_fusion.place_ref, ...), custom_call_target="tpu_custom_call" | custom-call | flops 2684354560 | bytes 3809280 | tf_op jit(solution)/shard_map/early/pallas_call | solution.py:476
  21.6 0.1 collective-permute-done.8.refs_6_
  21.7 1.2 %collective-permute-done.9.refs_7_ = bf16[144,256]{1,0:T(8,128)(2,1)S(1)} collective-permute-done((bf16[144,256]{1,0:T(8,128)(2,1)S(1)}, bf16[144,256]{1,0:T(8,128)(2,1)S(1)}, u32[]{:S(2)}, u32[]{:S(2)}) %collective-permute-start.9) | collective-permute-done | bytes 73760 | tf_op jit(solution)/shard_map/ppermute | solution.py:443
  22.9 4.5 %heads.1 = f32[8,8,256]{2,1,0:T(8,128)} custom-call(s32[3]{0:T(128)S(1)} %pad_add_fusion.place_ref, bf16[256,256]{1,0:T(8,128)(2,1)S(1)} %get-tuple-element.15.factors_ref, bf16[144,256]{1,0:T(8,128)(2,1)S(1)} %pack.1.refs_1_.refs_4_.refs_0_, bf16[144,256]{1,0:T(8,128)(2,1)S(1)} %collective-permute-done.2.refs_2_.refs_5_.refs_1_, ...), custom_call_target="tpu_custom_call" | custom-call | tf_op jit(solution)/shard_map/heads/pallas_call | solution.py:491
  27.4 4.2 %all-to-all-start = ((f32[8,8,256]{2,1,0:T(8,128)}), f32[8,8,256]{2,1,0:T(8,128)S(1)}, u32[]{:S(2)}, u32[]{:S(2)}) async-start(f32[8,8,256]{2,1,0:T(8,128)} %heads.1), calls=%async_computation | async-start | bytes 131072 | tf_op jit(solution)/shard_map/all_to_all | solution.py:505
  31.6 3.0 %first.1 = (f32[8,128,256]{2,1,0:T(8,128)S(1)}, f32[8,256,256]{2,1,0:T(8,128)S(1)}) custom-call(s32[1]{0:T(128)} %bitcast.5.node_ref, bf16[272,512]{1,0:T(8,128)(2,1)S(1)} %get-tuple-element.11.matrix_ref, bf16[128,256]{1,0:T(8,128)(2,1)} %loadings_ref.3, bf16[512,256]{1,0:T(8,128)(2,1)} %rows_ref.1, bf16[3,512,256]{2,1,0:T(8,128)(2,1)} %get-tuple-element.12.kept_ref), custom_call_target="tpu_custom_call" | custom-call | flops 536870912 | bytes 3145728 | tf_op jit(solution)/shard_map/first/pallas_call | solution.py:509
  34.6 3.9 %all-to-all-done.head_ref = f32[8,8,256]{2,1,0:T(8,128)S(1)} async-done(((f32[8,8,256]{2,1,0:T(8,128)}), f32[8,8,256]{2,1,0:T(8,128)S(1)}, u32[]{:S(2)}, u32[]{:S(2)}) %all-to-all-start) | async-done | bytes 65568 | tf_op jit(solution)/shard_map/all_to_all | solution.py:505
  38.5 3.1 %volts.1 = (f32[2048,128]{1,0:T(8,128)}, f32[2048,128]{1,0:T(8,128)}) custom-call(bf16[272,512]{1,0:T(8,128)(2,1)S(1)} %get-tuple-element.11.matrix_ref, f32[8,128,256]{2,1,0:T(8,128)S(1)} %get-tuple-element.13.swing_ref, f32[8,256,256]{2,1,0:T(8,128)S(1)} %get-tuple-element.14.drop_ref, f32[8,8,256]{2,1,0:T(8,128)S(1)} %all-to-all-done.head_ref), custom_call_target="tpu_custom_call" | custom-call | tf_op jit(solution)/shard_map/volts/pallas_call | solution.py:526
  (5 shorter events, 0.0 us)
Async XLA Ops:
  0.6 14.3 %collective-permute-start.1 = (bf16[512,256]{1,0:T(8,128)(2,1)}, bf16[512,256]{1,0:T(8,128)(2,1)S(1)}, u32[]{:S(2)}, u32[]{:S(2)}) collective-permute-start(bf16[512,256]{1,0:T(8,128)(2,1)} %rows_ref.1), channel_id=1, source_target_pairs={{0,2},{1,3},{2,0},{3,1},{4,6},{5,7},{6,4},{7,5},{8,10},{9,11},{10,... | collective-permute-start | bytes 786440 | tf_op jit(solution)/shard_map/ppermute | solution.py:418
  4.6 5.9 %collective-permute-start.2 = (bf16[144,256]{1,0:T(8,128)(2,1)S(1)}, bf16[144,256]{1,0:T(8,128)(2,1)S(1)}, u32[]{:S(2)}, u32[]{:S(2)}) collective-permute-start(bf16[144,256]{1,0:T(8,128)(2,1)S(1)} %pack.1.refs_1_.refs_4_.refs_0_), channel_id=1, source_target_pairs={{0,16},{4,20},{8,24},{12,28},{16,0},{20,4},{24,8},{28,12},{1,17},{... | collective-permute-start | bytes 221192 | tf_op jit(solution)/shard_map/ppermute | solution.py:443
  7.2 4.4 %collective-permute-start.3 = (bf16[144,256]{1,0:T(8,128)(2,1)S(1)}, bf16[144,256]{1,0:T(8,128)(2,1)S(1)}, u32[]{:S(2)}, u32[]{:S(2)}) collective-permute-start(bf16[144,256]{1,0:T(8,128)(2,1)S(1)} %pack.1.refs_1_.refs_4_.refs_0_), channel_id=1, source_target_pairs={{0,8},{4,12},{8,0},{12,4},{16,24},{20,28},{24,16},{28,20},{1,9},{5... | collective-permute-start | bytes 221192 | tf_op jit(solution)/shard_map/ppermute | solution.py:443
  8.8 6.2 %collective-permute-start.4 = (bf16[144,256]{1,0:T(8,128)(2,1)S(1)}, bf16[144,256]{1,0:T(8,128)(2,1)S(1)}, u32[]{:S(2)}, u32[]{:S(2)}) collective-permute-start(bf16[144,256]{1,0:T(8,128)(2,1)S(1)} %pack.1.refs_1_.refs_4_.refs_0_), channel_id=1, source_target_pairs={{0,24},{4,28},{8,16},{12,20},{16,8},{20,12},{24,0},{28,4},{1,25},{... | collective-permute-start | bytes 221192 | tf_op jit(solution)/shard_map/ppermute | solution.py:443
  9.0 5.9 %collective-permute-start.5 = (bf16[144,256]{1,0:T(8,128)(2,1)S(1)}, bf16[144,256]{1,0:T(8,128)(2,1)S(1)}, u32[]{:S(2)}, u32[]{:S(2)}) collective-permute-start(bf16[144,256]{1,0:T(8,128)(2,1)S(1)} %pack.1.refs_1_.refs_4_.refs_0_), channel_id=1, source_target_pairs={{0,4},{4,0},{8,12},{12,8},{16,20},{20,16},{24,28},{28,24},{1,5},{5... | collective-permute-start | bytes 221192 | tf_op jit(solution)/shard_map/ppermute | solution.py:443
  10.5 8.1 %collective-permute-start = (bf16[512,256]{1,0:T(8,128)(2,1)}, bf16[512,256]{1,0:T(8,128)(2,1)S(1)}, u32[]{:S(2)}, u32[]{:S(2)}) collective-permute-start(bf16[512,256]{1,0:T(8,128)(2,1)} %rows_ref.1), channel_id=1, source_target_pairs={{0,1},{1,0},{2,3},{3,2},{4,5},{5,4},{6,7},{7,6},{8,9},{9,8},{10,11... | collective-permute-start | bytes 786440 | tf_op jit(solution)/shard_map/ppermute | solution.py:418
  14.9 3.7 %collective-permute-start.6 = (bf16[512,256]{1,0:T(8,128)(2,1)S(1)}, bf16[512,256]{1,0:T(8,128)(2,1)S(1)}, u32[]{:S(2)}, u32[]{:S(2)}) collective-permute-start(bf16[512,256]{1,0:T(8,128)(2,1)S(1)} %after.1.refs_2_), channel_id=1, source_target_pairs={{0,1},{1,0},{2,3},{3,2},{4,5},{5,4},{6,7},{7,6},{8,9},{9,8},{10,11... | collective-permute-start | bytes 786440 | tf_op jit(solution)/shard_map/ppermute | solution.py:418
  15.1 6.5 %collective-permute-start.7 = (bf16[144,256]{1,0:T(8,128)(2,1)S(1)}, bf16[144,256]{1,0:T(8,128)(2,1)S(1)}, u32[]{:S(2)}, u32[]{:S(2)}) collective-permute-start(bf16[144,256]{1,0:T(8,128)(2,1)S(1)} %collective-permute-done.2.refs_2_.refs_5_.refs_1_), channel_id=1, source_target_pairs={{0,4},{4,0},{8,12},{12,8},{16,20},{20,16},{24,28},{28,24},{1,5},{5... | collective-permute-start | bytes 221192 | tf_op jit(solution)/shard_map/ppermute | solution.py:443
  16.6 5.1 %collective-permute-start.8 = (bf16[144,256]{1,0:T(8,128)(2,1)S(1)}, bf16[144,256]{1,0:T(8,128)(2,1)S(1)}, u32[]{:S(2)}, u32[]{:S(2)}) collective-permute-start(bf16[144,256]{1,0:T(8,128)(2,1)S(1)} %collective-permute-done.3.refs_3_.refs_6_.refs_2_), channel_id=1, source_target_pairs={{0,4},{4,0},{8,12},{12,8},{16,20},{20,16},{24,28},{28,24},{1,5},{5... | collective-permute-start | bytes 221192 | tf_op jit(solution)/shard_map/ppermute | solution.py:443
  17.2 5.8 %collective-permute-start.9 = (bf16[144,256]{1,0:T(8,128)(2,1)S(1)}, bf16[144,256]{1,0:T(8,128)(2,1)S(1)}, u32[]{:S(2)}, u32[]{:S(2)}) collective-permute-start(bf16[144,256]{1,0:T(8,128)(2,1)S(1)} %collective-permute-done.4.refs_4_.refs_7_.refs_3_), channel_id=1, source_target_pairs={{0,4},{4,0},{8,12},{12,8},{16,20},{20,16},{24,28},{28,24},{1,5},{5... | collective-permute-start | bytes 221192 | tf_op jit(solution)/shard_map/ppermute | solution.py:443
  27.4 11.1 %all-to-all-start = ((f32[8,8,256]{2,1,0:T(8,128)}), f32[8,8,256]{2,1,0:T(8,128)S(1)}, u32[]{:S(2)}, u32[]{:S(2)}) async-start(f32[8,8,256]{2,1,0:T(8,128)} %heads.1), calls=%async_computation | async-start | bytes 131072 | tf_op jit(solution)/shard_map/all_to_all | solution.py:505

commit v10 on v9

--- a/solution.py
+++ b/solution.py
@@ -102,47 +102,42 @@
         digits.append([ancestor(unit * digit).astype(jnp.float32) for digit in range(1, 8) if unit * digit < n])
         unit *= 8
     last = [found.T for found in digits.pop()]
-    yield None
-
     rows_b, lanes_b = (ids.astype(jnp.float32).astype(jnp.bfloat16) for ids in (row_ids, lane_ids))
     one, zero = jnp.ones((n, n), jnp.bfloat16), jnp.zeros((n, n), jnp.bfloat16)
     identity = jnp.where(rows_b == lanes_b, one, zero)
-    products = [None] * len(sections)
-    for index in range(len(sections)):
+    pad_ids = lax.broadcasted_iota(jnp.int32, (EXTRA, 2 * n), 0)
+    state = [None] * len(sections)
+
+    def near_step(index):
+        done = None
         for digit in digits:
             factor = identity
             for found in digit:
                 row = jnp.broadcast_to(found[index : index + 1, :].astype(jnp.bfloat16), (n, n))
                 factor = jnp.where(rows_b == row, one, factor)
-            done = products[index]
-            products[index] = factor if done is None else product(done, factor).astype(jnp.bfloat16)
-    yield None
-
-    paths = []
-    for index in range(len(sections)):
+            done = factor if done is None else product(done, factor).astype(jnp.bfloat16)
+        state[index] = done
+
+    def paths_step(index):
         factor = identity
         for found in last:
             column = jnp.broadcast_to(found[:, index : index + 1], (n, n)).astype(jnp.bfloat16)
             factor = jnp.where(lanes_b == column, one, factor)
-        paths.append(product_nt(factor, products[index]).astype(jnp.bfloat16))
-    yield None
-
-    shared = []
-    for path, high, middle in zip(paths, highs, middles):
+        state[index] = product_nt(factor, state[index]).astype(jnp.bfloat16)
+
+    def shared_step(index):
+        path = state[index]
         wide_path = path.astype(jnp.float32)
-
-        def scaled(index):
-            return jnp.concatenate([wide_path * high[index : index + 1], wide_path * middle[index : index + 1]], axis=1)
-
-        left = jnp.concatenate([scaled(2), scaled(3)], axis=0).astype(jnp.bfloat16)
-        shared.append(product_nt(left, jnp.concatenate([path, path], axis=1)))
-    yield None
-
-    pad_ids = lax.broadcasted_iota(jnp.int32, (EXTRA, 2 * n), 0)
-    out = []
-    for both, row in zip(shared, rows):
-        resist, react = both[:n], both[n:]
-        base_active, base_reactive = row[0:1], row[1:2]
+        left = [
+            jnp.concatenate([wide_path * part[row : row + 1] for part in (highs[index], middles[index])], axis=1)
+            for row in (2, 3)
+        ]
+        left = jnp.concatenate(left, axis=0).astype(jnp.bfloat16)
+        state[index] = product_nt(left, jnp.concatenate([path, path], axis=1))
+
+    def matrix_step(index):
+        resist, react = state[index][:n], state[index][n:]
+        base_active, base_reactive = rows[index][0:1], rows[index][1:2]
         real_high, real_low = split(resist * base_active + react * base_reactive)
         imag_high, imag_low = split(react * base_active - resist * base_reactive)
         row_real = jnp.concatenate([base_active, base_reactive], axis=1)
@@ -154,12 +149,20 @@
             bottom = jnp.concatenate([imag_part, real_part], axis=1)
             return jnp.concatenate([top, bottom, sums_part], axis=0)
 
-        out.append(
-            jnp.concatenate(
-                [whole(real_high, imag_high, sums_high), whole(real_low, imag_low, sums_low)], axis=1
-            )
-        )
-    yield out
+        high, low = whole(real_high, imag_high, sums_high), whole(real_low, imag_low, sums_low)
+        state[index] = jnp.concatenate([high, low], axis=1)
+        return state[index]
+
+    return [near_step, paths_step, shared_step, matrix_step]
+
+
+def stagger(count, steps, between=None):
+    for turn in range(count + len(steps) - 1):
+        for depth in reversed(range(len(steps))):
+            if 0 <= turn - depth < count:
+                steps[depth](turn - depth)
+        if between is not None:
+            between()
 
 
 def swing_of(loadings, factors):
@@ -211,19 +214,24 @@
 
     n = swing_ref.shape[1]
     for start in range(0, len(sections), 8):
-        group = list(enumerate(sections))[start : start + 8]
-        steps = matrix_steps([section for _, section in group], n)
-        next(steps)
+        group = sections[start : start + 8]
+        near_step, *more, matrix_step = matrix_steps(group, n)
         if start == 0:
             pltpu.make_async_copy(piece_refs[0].at[0:width, :], factors_ref, sem).wait()
-        for slot, section in group:
-            swing_ref[slot] = swing_of(section[0:n, :], factors_ref[...])
-        *_, matrices = steps
-        for (slot, _), matrix in zip(group, matrices):
-            matrix_ref[slot] = matrix
-            out = apply_first(matrix_ref[slot], swing_ref[slot])
-            drop_ref[slot] = out[: 2 * n]
-            inject_ref[slot] = out[2 * n :]
+
+        def start_step(index):
+            near_step(index)
+            swing_ref[start + index] = swing_of(group[index][0:n, :], factors_ref[...])
+
+        def keep_step(index):
+            matrix_ref[start + index] = matrix_step(index)
+
+        def sweep_step(index):
+            out = apply_first(matrix_ref[start + index], swing_ref[start + index])
+            drop_ref[start + index] = out[: 2 * n]
+            inject_ref[start + index] = out[2 * n :]
+
+        stagger(len(group), [start_step, *more, keep_step, sweep_step])
     own_ref[...] = matrix_ref[0]
     for copy in keeps:
         copy.wait()
@@ -253,8 +261,6 @@
 
     groups = [list(range(start, min(start + 8, feeders))) for start in range(early, feeders, 8)]
     steps = [matrix_steps([sections[index] for index in group], n) for group in groups]
-    if steps:
-        next(steps[0])
     for index in range(feeders):
         row = constants(sections[index], n)[2]
         trunk_ref[place[index], 0:2, :] = wide(row[4:6], width)
@@ -297,13 +303,20 @@
 
     heads(0)
     ready = list(range(early))
-    for group, step in zip(groups, steps):
-        for matrices in step:
-            if ready:
-                middle(ready.pop(0), 1)
-        for index, matrix in zip(group, matrices):
-            of(index, 0)[...] = matrix
-            of(index, 2)[...] = apply_first(matrix, of(index, 1)[...])[: 2 * n]
+
+    def between():
+        if ready:
+            middle(ready.pop(0), 1)
+
+    for group, (*more, matrix_step) in zip(groups, steps):
+        def keep_step(index):
+            of(group[index], 0)[...] = matrix_step(index)
+
+        def sweep_step(index):
+            out = apply_first(of(group[index], 0)[...], of(group[index], 1)[...])
+            of(group[index], 2)[...] = out[: 2 * n]
+
+        stagger(len(group), [*more, keep_step, sweep_step], between)
     for index in ready + list(range(early, feeders)):
         middle(index, 1)
     heads(1)
@@ -371,10 +384,7 @@
             copies.append(pltpu.make_async_copy(out_ref.at[index, rows, :], to_ref.at[rows, :], sems.at[index, chunk]))
             copies[-1].start()
 
-    for turn in range(chunks + SWEEPS - 1):
-        for sweep in reversed(range(SWEEPS)):
-            if 0 <= turn - sweep < chunks:
-                advance(turn - sweep, sweep)
+    stagger(chunks, [functools.partial(advance, sweep=sweep) for sweep in range(SWEEPS)])
     for copy in copies:
         copy.wait()
 

time: 41.9 us -> 42.3 us (level)
  Pallas kernels: 14.4 us -> 15.2 us
    pallas_call x1, Pallas kernels: 4.47 us -> 4.9 us  [local(): pl.pallas_call(functools.partial(heads_kernel, slots, early), out_shape=j...]
  transfers between devices with their start and end apart: 11 -> 11, of which waited for: 5 -> 4; matrix products, arithmetic and copies ran while one was open for 0% -> 0% of each run, Pallas kernels for 16% -> 17%
where the time goes in v10:
time: 42.3 us; the launch traced here: 42 us
  starting transfers between devices  16.7 us (39%)
  Pallas kernels  15.2 us (36%)
  waiting for transfers between devices  9.32 us (22%)
  between operations  0.71 us (2%)
    ppermute x7, starting transfers between devices, swap(): lax.ppermute(block, 'feeder', [(i, i ^ offset) for i in range(feeders)])  9.47 us
    ppermute x7, waiting for transfers between devices, swap(): lax.ppermute(block, 'feeder', [(i, i ^ offset) for i in range(feeders)])  5.43 us
    pallas_call x1, Pallas kernels, local(): pl.pallas_call(functools.partial(heads_kernel, slots, early), out_shape=j...  4.9 us
    all_to_all x1, starting transfers between devices, local(): given = lax.all_to_all(heads, 'feeder', 0, 0, tiled=True)  4.17 us
    all_to_all x1, waiting for transfers between devices, local(): given = lax.all_to_all(heads, 'feeder', 0, 0, tiled=True)  3.88 us
    pallas_call x1, Pallas kernels, local(): pl.pallas_call(functools.partial(early_kernel, nodes), out_shape=[jax.Sha...  3.26 us
    pallas_call x1, Pallas kernels, local(): pl.pallas_call(volts_kernel, out_shape=(jax.ShapeDtypeStruct((scen, n), f...  3.15 us
    ppermute x3, starting transfers between devices, trade(): return lax.ppermute(block, 'node', [(i, i ^ offset) for i in range(nodes)])  3.1 us
  transfers between devices with their start and end apart: 11, of which 4 were waited for; matrix products, arithmetic and copies ran while one was open for 0% of the time, Pallas kernels for 17%

profile of v10, /device:TPU:0, one launch (start us, length us, event | category | flops | bytes accessed | tf_op | source)
XLA Modules:
  0.0 42.0 jit_solution(6195451093451620209)
XLA Ops:
  0.6 3.0 %collective-permute-start.1 = (bf16[512,256]{1,0:T(8,128)(2,1)}, bf16[512,256]{1,0:T(8,128)(2,1)S(1)}, u32[]{:S(2)}, u32[]{:S(2)}) collective-permute-start(bf16[512,256]{1,0:T(8,128)(2,1)} %rows_ref.1), channel_id=1, source_target_pairs={{0,2},{1,3},{2,0},{3,1},{4,6},{5,7},{6,4},{7,5},{8,10},{9,11},{10,... | collective-permute-start | bytes 786440 | tf_op jit(solution)/shard_map/ppermute | solution.py:428
  3.7 0.9 %pack.1.refs_1_.refs_4_.refs_0_ = bf16[144,256]{1,0:T(8,128)(2,1)S(1)} custom-call(f32[2]{0:T(128)} %bitcast.6, bf16[128,256]{1,0:T(8,128)(2,1)} %loadings_ref.3, s32[1,128]{1,0:T(1,128)} %bitcast.7, f32[2,128]{1,0:T(2,128)} %base_ref.1, f32[2,128]{1,0:T(2,128)} %z_ref.1), custom_call_target="tpu_custom_call" | custom-call | tf_op jit(solution)/shard_map/pack/pallas_call | solution.py:435
  4.6 2.7 %collective-permute-start.2 = (bf16[144,256]{1,0:T(8,128)(2,1)S(1)}, bf16[144,256]{1,0:T(8,128)(2,1)S(1)}, u32[]{:S(2)}, u32[]{:S(2)}) collective-permute-start(bf16[144,256]{1,0:T(8,128)(2,1)S(1)} %pack.1.refs_1_.refs_4_.refs_0_), channel_id=1, source_target_pairs={{0,16},{4,20},{8,24},{12,28},{16,0},{20,4},{24,8},{28,12},{1,17},{... | collective-permute-start | bytes 221192 | tf_op jit(solution)/shard_map/ppermute | solution.py:453
  7.2 1.6 %collective-permute-start.3 = (bf16[144,256]{1,0:T(8,128)(2,1)S(1)}, bf16[144,256]{1,0:T(8,128)(2,1)S(1)}, u32[]{:S(2)}, u32[]{:S(2)}) collective-permute-start(bf16[144,256]{1,0:T(8,128)(2,1)S(1)} %pack.1.refs_1_.refs_4_.refs_0_), channel_id=1, source_target_pairs={{0,8},{4,12},{8,0},{12,4},{16,24},{20,28},{24,16},{28,20},{1,9},{5... | collective-permute-start | bytes 221192 | tf_op jit(solution)/shard_map/ppermute | solution.py:453
  8.8 0.2 collective-permute-start.4
  9.0 1.5 %collective-permute-start.5 = (bf16[144,256]{1,0:T(8,128)(2,1)S(1)}, bf16[144,256]{1,0:T(8,128)(2,1)S(1)}, u32[]{:S(2)}, u32[]{:S(2)}) collective-permute-start(bf16[144,256]{1,0:T(8,128)(2,1)S(1)} %pack.1.refs_1_.refs_4_.refs_0_), channel_id=1, source_target_pairs={{0,4},{4,0},{8,12},{12,8},{16,20},{20,16},{24,28},{28,24},{1,5},{5... | collective-permute-start | bytes 221192 | tf_op jit(solution)/shard_map/ppermute | solution.py:453
  10.5 0.0 collective-permute-done.2.refs_2_.refs_5_.refs_1_
  10.5 0.0 collective-permute-start
  10.5 1.1 %collective-permute-done.3.refs_3_.refs_6_.refs_2_ = bf16[144,256]{1,0:T(8,128)(2,1)S(1)} collective-permute-done((bf16[144,256]{1,0:T(8,128)(2,1)S(1)}, bf16[144,256]{1,0:T(8,128)(2,1)S(1)}, u32[]{:S(2)}, u32[]{:S(2)}) %collective-permute-start.3) | collective-permute-done | bytes 73760 | tf_op jit(solution)/shard_map/ppermute | solution.py:453
  11.6 3.4 %collective-permute-done.4.refs_4_.refs_7_.refs_3_ = bf16[144,256]{1,0:T(8,128)(2,1)S(1)} collective-permute-done((bf16[144,256]{1,0:T(8,128)(2,1)S(1)}, bf16[144,256]{1,0:T(8,128)(2,1)S(1)}, u32[]{:S(2)}, u32[]{:S(2)}) %collective-permute-start.4) | collective-permute-done | bytes 73760 | tf_op jit(solution)/shard_map/ppermute | solution.py:453
  14.9 0.1 collective-permute-start.6
  15.0 0.1 pad_add_fusion.place_ref
  15.1 1.5 %collective-permute-start.7 = (bf16[144,256]{1,0:T(8,128)(2,1)S(1)}, bf16[144,256]{1,0:T(8,128)(2,1)S(1)}, u32[]{:S(2)}, u32[]{:S(2)}) collective-permute-start(bf16[144,256]{1,0:T(8,128)(2,1)S(1)} %collective-permute-done.2.refs_2_.refs_5_.refs_1_), channel_id=1, source_target_pairs={{0,4},{4,0},{8,12},{12,8},{16,20},{20,16},{24,28},{28,24},{1,5},{5... | collective-permute-start | bytes 221192 | tf_op jit(solution)/shard_map/ppermute | solution.py:453
  16.6 0.5 %collective-permute-start.8 = (bf16[144,256]{1,0:T(8,128)(2,1)S(1)}, bf16[144,256]{1,0:T(8,128)(2,1)S(1)}, u32[]{:S(2)}, u32[]{:S(2)}) collective-permute-start(bf16[144,256]{1,0:T(8,128)(2,1)S(1)} %collective-permute-done.3.refs_3_.refs_6_.refs_2_), channel_id=1, source_target_pairs={{0,4},{4,0},{8,12},{12,8},{16,20},{20,16},{24,28},{28,24},{1,5},{5... | collective-permute-start | bytes 221192 | tf_op jit(solution)/shard_map/ppermute | solution.py:453
  17.2 1.5 %collective-permute-start.9 = (bf16[144,256]{1,0:T(8,128)(2,1)S(1)}, bf16[144,256]{1,0:T(8,128)(2,1)S(1)}, u32[]{:S(2)}, u32[]{:S(2)}) collective-permute-start(bf16[144,256]{1,0:T(8,128)(2,1)S(1)} %collective-permute-done.4.refs_4_.refs_7_.refs_3_), channel_id=1, source_target_pairs={{0,4},{4,0},{8,12},{12,8},{16,20},{20,16},{24,28},{28,24},{1,5},{5... | collective-permute-start | bytes 221192 | tf_op jit(solution)/shard_map/ppermute | solution.py:453
  18.6 0.0 collective-permute-done.refs_1_
  18.7 0.0 collective-permute-done.6.refs_3_
  18.7 3.3 %early.1 = (bf16[256,256]{1,0:T(8,128)(2,1)S(1)}, bf16[272,512]{1,0:T(8,128)(2,1)S(1)}, bf16[3,512,256]{2,1,0:T(8,128)(2,1)}, bf16[5,272,512]{2,1,0:T(8,128)(2,1...) custom-call(s32[3]{0:T(128)S(1)} %pad_add_fusion.place_ref, ...), custom_call_target="tpu_custom_call" | custom-call | flops 2684354560 | bytes 3809280 | tf_op jit(solution)/shard_map/early/pallas_call | solution.py:486
  21.9 1.0 %collective-permute-done.9.refs_7_ = bf16[144,256]{1,0:T(8,128)(2,1)S(1)} collective-permute-done((bf16[144,256]{1,0:T(8,128)(2,1)S(1)}, bf16[144,256]{1,0:T(8,128)(2,1)S(1)}, u32[]{:S(2)}, u32[]{:S(2)}) %collective-permute-start.9) | collective-permute-done | bytes 73760 | tf_op jit(solution)/shard_map/ppermute | solution.py:453
  22.9 4.9 %heads.1 = f32[8,8,256]{2,1,0:T(8,128)} custom-call(s32[3]{0:T(128)S(1)} %pad_add_fusion.place_ref, bf16[256,256]{1,0:T(8,128)(2,1)S(1)} %get-tuple-element.15.factors_ref, bf16[144,256]{1,0:T(8,128)(2,1)S(1)} %pack.1.refs_1_.refs_4_.refs_0_, bf16[144,256]{1,0:T(8,128)(2,1)S(1)} %collective-permute-done.2.refs_2_.refs_5_.refs_1_, ...), custom_call_target="tpu_custom_call" | custom-call | tf_op jit(solution)/shard_map/heads/pallas_call | solution.py:501
  27.8 4.2 %all-to-all-start = ((f32[8,8,256]{2,1,0:T(8,128)}), f32[8,8,256]{2,1,0:T(8,128)S(1)}, u32[]{:S(2)}, u32[]{:S(2)}) async-start(f32[8,8,256]{2,1,0:T(8,128)} %heads.1), calls=%async_computation | async-start | bytes 131072 | tf_op jit(solution)/shard_map/all_to_all | solution.py:515
  32.0 3.0 %first.1 = (f32[8,128,256]{2,1,0:T(8,128)S(1)}, f32[8,256,256]{2,1,0:T(8,128)S(1)}) custom-call(s32[1]{0:T(128)} %bitcast.5.node_ref, bf16[272,512]{1,0:T(8,128)(2,1)S(1)} %get-tuple-element.11.matrix_ref, bf16[128,256]{1,0:T(8,128)(2,1)} %loadings_ref.3, bf16[512,256]{1,0:T(8,128)(2,1)} %rows_ref.1, bf16[3,512,256]{2,1,0:T(8,128)(2,1)} %get-tuple-element.12.kept_ref), custom_call_target="tpu_custom_call" | custom-call | flops 536870912 | bytes 3145728 | tf_op jit(solution)/shard_map/first/pallas_call | solution.py:519
  35.0 3.9 %all-to-all-done.head_ref = f32[8,8,256]{2,1,0:T(8,128)S(1)} async-done(((f32[8,8,256]{2,1,0:T(8,128)}), f32[8,8,256]{2,1,0:T(8,128)S(1)}, u32[]{:S(2)}, u32[]{:S(2)}) %all-to-all-start) | async-done | bytes 65568 | tf_op jit(solution)/shard_map/all_to_all | solution.py:515
  38.9 3.1 %volts.1 = (f32[2048,128]{1,0:T(8,128)}, f32[2048,128]{1,0:T(8,128)}) custom-call(bf16[272,512]{1,0:T(8,128)(2,1)S(1)} %get-tuple-element.11.matrix_ref, f32[8,128,256]{2,1,0:T(8,128)S(1)} %get-tuple-element.13.swing_ref, f32[8,256,256]{2,1,0:T(8,128)S(1)} %get-tuple-element.14.drop_ref, f32[8,8,256]{2,1,0:T(8,128)S(1)} %all-to-all-done.head_ref), custom_call_target="tpu_custom_call" | custom-call | tf_op jit(solution)/shard_map/volts/pallas_call | solution.py:536
  (5 shorter events, 0.0 us)
Async XLA Ops:
  0.6 14.3 %collective-permute-start.1 = (bf16[512,256]{1,0:T(8,128)(2,1)}, bf16[512,256]{1,0:T(8,128)(2,1)S(1)}, u32[]{:S(2)}, u32[]{:S(2)}) collective-permute-start(bf16[512,256]{1,0:T(8,128)(2,1)} %rows_ref.1), channel_id=1, source_target_pairs={{0,2},{1,3},{2,0},{3,1},{4,6},{5,7},{6,4},{7,5},{8,10},{9,11},{10,... | collective-permute-start | bytes 786440 | tf_op jit(solution)/shard_map/ppermute | solution.py:428
  4.6 5.9 %collective-permute-start.2 = (bf16[144,256]{1,0:T(8,128)(2,1)S(1)}, bf16[144,256]{1,0:T(8,128)(2,1)S(1)}, u32[]{:S(2)}, u32[]{:S(2)}) collective-permute-start(bf16[144,256]{1,0:T(8,128)(2,1)S(1)} %pack.1.refs_1_.refs_4_.refs_0_), channel_id=1, source_target_pairs={{0,16},{4,20},{8,24},{12,28},{16,0},{20,4},{24,8},{28,12},{1,17},{... | collective-permute-start | bytes 221192 | tf_op jit(solution)/shard_map/ppermute | solution.py:453
  7.2 4.4 %collective-permute-start.3 = (bf16[144,256]{1,0:T(8,128)(2,1)S(1)}, bf16[144,256]{1,0:T(8,128)(2,1)S(1)}, u32[]{:S(2)}, u32[]{:S(2)}) collective-permute-start(bf16[144,256]{1,0:T(8,128)(2,1)S(1)} %pack.1.refs_1_.refs_4_.refs_0_), channel_id=1, source_target_pairs={{0,8},{4,12},{8,0},{12,4},{16,24},{20,28},{24,16},{28,20},{1,9},{5... | collective-permute-start | bytes 221192 | tf_op jit(solution)/shard_map/ppermute | solution.py:453
  8.8 6.2 %collective-permute-start.4 = (bf16[144,256]{1,0:T(8,128)(2,1)S(1)}, bf16[144,256]{1,0:T(8,128)(2,1)S(1)}, u32[]{:S(2)}, u32[]{:S(2)}) collective-permute-start(bf16[144,256]{1,0:T(8,128)(2,1)S(1)} %pack.1.refs_1_.refs_4_.refs_0_), channel_id=1, source_target_pairs={{0,24},{4,28},{8,16},{12,20},{16,8},{20,12},{24,0},{28,4},{1,25},{... | collective-permute-start | bytes 221192 | tf_op jit(solution)/shard_map/ppermute | solution.py:453
  9.0 5.9 %collective-permute-start.5 = (bf16[144,256]{1,0:T(8,128)(2,1)S(1)}, bf16[144,256]{1,0:T(8,128)(2,1)S(1)}, u32[]{:S(2)}, u32[]{:S(2)}) collective-permute-start(bf16[144,256]{1,0:T(8,128)(2,1)S(1)} %pack.1.refs_1_.refs_4_.refs_0_), channel_id=1, source_target_pairs={{0,4},{4,0},{8,12},{12,8},{16,20},{20,16},{24,28},{28,24},{1,5},{5... | collective-permute-start | bytes 221192 | tf_op jit(solution)/shard_map/ppermute | solution.py:453
  10.5 8.1 %collective-permute-start = (bf16[512,256]{1,0:T(8,128)(2,1)}, bf16[512,256]{1,0:T(8,128)(2,1)S(1)}, u32[]{:S(2)}, u32[]{:S(2)}) collective-permute-start(bf16[512,256]{1,0:T(8,128)(2,1)} %rows_ref.1), channel_id=1, source_target_pairs={{0,1},{1,0},{2,3},{3,2},{4,5},{5,4},{6,7},{7,6},{8,9},{9,8},{10,11... | collective-permute-start | bytes 786440 | tf_op jit(solution)/shard_map/ppermute | solution.py:428
  14.9 3.7 %collective-permute-start.6 = (bf16[512,256]{1,0:T(8,128)(2,1)S(1)}, bf16[512,256]{1,0:T(8,128)(2,1)S(1)}, u32[]{:S(2)}, u32[]{:S(2)}) collective-permute-start(bf16[512,256]{1,0:T(8,128)(2,1)S(1)} %after.1.refs_2_), channel_id=1, source_target_pairs={{0,1},{1,0},{2,3},{3,2},{4,5},{5,4},{6,7},{7,6},{8,9},{9,8},{10,11... | collective-permute-start | bytes 786440 | tf_op jit(solution)/shard_map/ppermute | solution.py:428
  15.1 6.8 %collective-permute-start.7 = (bf16[144,256]{1,0:T(8,128)(2,1)S(1)}, bf16[144,256]{1,0:T(8,128)(2,1)S(1)}, u32[]{:S(2)}, u32[]{:S(2)}) collective-permute-start(bf16[144,256]{1,0:T(8,128)(2,1)S(1)} %collective-permute-done.2.refs_2_.refs_5_.refs_1_), channel_id=1, source_target_pairs={{0,4},{4,0},{8,12},{12,8},{16,20},{20,16},{24,28},{28,24},{1,5},{5... | collective-permute-start | bytes 221192 | tf_op jit(solution)/shard_map/ppermute | solution.py:453
  16.6 5.3 %collective-permute-start.8 = (bf16[144,256]{1,0:T(8,128)(2,1)S(1)}, bf16[144,256]{1,0:T(8,128)(2,1)S(1)}, u32[]{:S(2)}, u32[]{:S(2)}) collective-permute-start(bf16[144,256]{1,0:T(8,128)(2,1)S(1)} %collective-permute-done.3.refs_3_.refs_6_.refs_2_), channel_id=1, source_target_pairs={{0,4},{4,0},{8,12},{12,8},{16,20},{20,16},{24,28},{28,24},{1,5},{5... | collective-permute-start | bytes 221192 | tf_op jit(solution)/shard_map/ppermute | solution.py:453
  17.2 5.8 %collective-permute-start.9 = (bf16[144,256]{1,0:T(8,128)(2,1)S(1)}, bf16[144,256]{1,0:T(8,128)(2,1)S(1)}, u32[]{:S(2)}, u32[]{:S(2)}) collective-permute-start(bf16[144,256]{1,0:T(8,128)(2,1)S(1)} %collective-permute-done.4.refs_4_.refs_7_.refs_3_), channel_id=1, source_target_pairs={{0,4},{4,0},{8,12},{12,8},{16,20},{20,16},{24,28},{28,24},{1,5},{5... | collective-permute-start | bytes 221192 | tf_op jit(solution)/shard_map/ppermute | solution.py:453
  27.8 11.1 %all-to-all-start = ((f32[8,8,256]{2,1,0:T(8,128)}), f32[8,8,256]{2,1,0:T(8,128)S(1)}, u32[]{:S(2)}, u32[]{:S(2)}) async-start(f32[8,8,256]{2,1,0:T(8,128)} %heads.1), calls=%async_computation | async-start | bytes 131072 | tf_op jit(solution)/shard_map/all_to_all | solution.py:515

commit v11 on v9

--- a/solution.py
+++ b/solution.py
@@ -448,8 +448,12 @@
     every[1] = swap(packed, 1)
     slots = list(every)
     early = len(slots)
-    for offset in slots[1:-1]:
+    first_on, *others_on, last_on = slots[1:-1]
+    every[first_on + 1] = swap(every[first_on], 1)
+    for offset in others_on:
         every[offset + 1] = swap(every[offset], 1)
+    every[last_on] = after(every[last_on], every[first_on + 1], *(every[offset + 1] for offset in others_on))
+    every[last_on + 1] = swap(every[last_on], 1)
     slots = list(every)
 
     if far:

time: 41.9 us -> 44.8 us (1.069)
  starting transfers between devices: 16.7 us -> 20 us
    all_to_all x1, starting transfers between devices: 4.16 us -> 7.8 us  [local(): given = lax.all_to_all(heads, 'feeder', 0, 0, tiled=True)]
    ppermute x7, waiting for transfers between devices: 5.77 us -> 5.15 us  [swap(): lax.ppermute(block, 'feeder', [(i, i ^ offset) for i in range(feeders)])]
  transfers between devices with their start and end apart: 11 -> 11, of which waited for: 5 -> 8; matrix products, arithmetic and copies ran while one was open for 0% -> 0% of each run, Pallas kernels for 16% -> 15%
where the time goes in v11:
time: 44.8 us; the launch traced here: 44.5 us
  starting transfers between devices  20 us (45%)
  Pallas kernels  14.5 us (32%)
  waiting for transfers between devices  9.33 us (21%)
  between operations  0.67 us (1%)
    ppermute x7, starting transfers between devices, swap(): lax.ppermute(block, 'feeder', [(i, i ^ offset) for i in range(feeders)])  9.14 us
    all_to_all x1, starting transfers between devices, local(): given = lax.all_to_all(heads, 'feeder', 0, 0, tiled=True)  7.8 us
    ppermute x7, waiting for transfers between devices, swap(): lax.ppermute(block, 'feeder', [(i, i ^ offset) for i in range(feeders)])  5.15 us
    pallas_call x1, Pallas kernels, local(): pl.pallas_call(functools.partial(heads_kernel, slots, early), out_shape=j...  4.47 us
    all_to_all x1, waiting for transfers between devices, local(): given = lax.all_to_all(heads, 'feeder', 0, 0, tiled=True)  3.88 us
    pallas_call x1, Pallas kernels, local(): pl.pallas_call(volts_kernel, out_shape=(jax.ShapeDtypeStruct((scen, n), f...  3.15 us
    ppermute x3, starting transfers between devices, trade(): return lax.ppermute(block, 'node', [(i, i ^ offset) for i in range(nodes)])  3.04 us
    pallas_call x1, Pallas kernels, local(): pl.pallas_call(first_kernel, out_shape=(jax.ShapeDtypeStruct((chunks, n,...  3.02 us
  transfers between devices with their start and end apart: 11, of which 8 were waited for; matrix products, arithmetic and copies ran while one was open for 0% of the time, Pallas kernels for 15%

profile of v11, /device:TPU:0, one launch (start us, length us, event | category | flops | bytes accessed | tf_op | source)
XLA Modules:
  0.0 44.5 jit_solution(7787351256737871664)
XLA Ops:
  0.6 3.0 %collective-permute-start.1 = (bf16[512,256]{1,0:T(8,128)(2,1)}, bf16[512,256]{1,0:T(8,128)(2,1)S(1)}, u32[]{:S(2)}, u32[]{:S(2)}) collective-permute-start(bf16[512,256]{1,0:T(8,128)(2,1)} %rows_ref.1), channel_id=1, source_target_pairs={{0,2},{1,3},{2,0},{3,1},{4,6},{5,7},{6,4},{7,5},{8,10},{9,11},{10,... | collective-permute-start | bytes 786440 | tf_op jit(solution)/shard_map/ppermute | solution.py:418
  3.7 0.9 %pack.1.refs_1_.refs_4_.refs_0_ = bf16[144,256]{1,0:T(8,128)(2,1)S(1)} custom-call(f32[2]{0:T(128)} %bitcast.6, bf16[128,256]{1,0:T(8,128)(2,1)} %loadings_ref.3, s32[1,128]{1,0:T(1,128)} %bitcast.7, f32[2,128]{1,0:T(2,128)} %base_ref.1, f32[2,128]{1,0:T(2,128)} %z_ref.1), custom_call_target="tpu_custom_call" | custom-call | tf_op jit(solution)/shard_map/pack/pallas_call | solution.py:425
  4.6 2.7 %collective-permute-start.2 = (bf16[144,256]{1,0:T(8,128)(2,1)S(1)}, bf16[144,256]{1,0:T(8,128)(2,1)S(1)}, u32[]{:S(2)}, u32[]{:S(2)}) collective-permute-start(bf16[144,256]{1,0:T(8,128)(2,1)S(1)} %pack.1.refs_1_.refs_4_.refs_0_), channel_id=1, source_target_pairs={{0,16},{4,20},{8,24},{12,28},{16,0},{20,4},{24,8},{28,12},{1,17},{... | collective-permute-start | bytes 221192 | tf_op jit(solution)/shard_map/ppermute | solution.py:443
  7.2 1.6 %collective-permute-start.3 = (bf16[144,256]{1,0:T(8,128)(2,1)S(1)}, bf16[144,256]{1,0:T(8,128)(2,1)S(1)}, u32[]{:S(2)}, u32[]{:S(2)}) collective-permute-start(bf16[144,256]{1,0:T(8,128)(2,1)S(1)} %pack.1.refs_1_.refs_4_.refs_0_), channel_id=1, source_target_pairs={{0,8},{4,12},{8,0},{12,4},{16,24},{20,28},{24,16},{28,20},{1,9},{5... | collective-permute-start | bytes 221192 | tf_op jit(solution)/shard_map/ppermute | solution.py:443
  8.8 0.2 collective-permute-start.4
  9.0 1.4 %collective-permute-done.2.refs_2_.refs_5_.refs_1_ = bf16[144,256]{1,0:T(8,128)(2,1)S(1)} collective-permute-done((bf16[144,256]{1,0:T(8,128)(2,1)S(1)}, bf16[144,256]{1,0:T(8,128)(2,1)S(1)}, u32[]{:S(2)}, u32[]{:S(2)}) %collective-permute-start.2) | collective-permute-done | bytes 73760 | tf_op jit(solution)/shard_map/ppermute | solution.py:443
  10.4 1.5 %collective-permute-start.5 = (bf16[144,256]{1,0:T(8,128)(2,1)S(1)}, bf16[144,256]{1,0:T(8,128)(2,1)S(1)}, u32[]{:S(2)}, u32[]{:S(2)}) collective-permute-start(bf16[144,256]{1,0:T(8,128)(2,1)S(1)} %collective-permute-done.2.refs_2_.refs_5_.refs_1_), channel_id=1, source_target_pairs={{0,4},{4,0},{8,12},{12,8},{16,20},{20,16},{24,28},{28,24},{1,5},{5... | collective-permute-start | bytes 221192 | tf_op jit(solution)/shard_map/ppermute | solution.py:443
  11.9 1.1 %collective-permute-start.6 = (bf16[144,256]{1,0:T(8,128)(2,1)S(1)}, bf16[144,256]{1,0:T(8,128)(2,1)S(1)}, u32[]{:S(2)}, u32[]{:S(2)}) collective-permute-start(bf16[144,256]{1,0:T(8,128)(2,1)S(1)} %collective-permute-done.3.refs_3_.refs_6_.refs_2_), channel_id=1, source_target_pairs={{0,4},{4,0},{8,12},{12,8},{16,20},{20,16},{24,28},{28,24},{1,5},{5... | collective-permute-start | bytes 221192 | tf_op jit(solution)/shard_map/ppermute | solution.py:443
  13.1 0.9 %collective-permute-start.7 = (bf16[144,256]{1,0:T(8,128)(2,1)S(1)}, bf16[144,256]{1,0:T(8,128)(2,1)S(1)}, u32[]{:S(2)}, u32[]{:S(2)}) collective-permute-start(bf16[144,256]{1,0:T(8,128)(2,1)S(1)} %pack.1.refs_1_.refs_4_.refs_0_), channel_id=1, source_target_pairs={{0,4},{4,0},{8,12},{12,8},{16,20},{20,16},{24,28},{28,24},{1,5},{5... | collective-permute-start | bytes 221192 | tf_op jit(solution)/shard_map/ppermute | solution.py:443
  14.0 1.0 %collective-permute-done.4.refs_0_ = bf16[144,256]{1,0:T(8,128)(2,1)S(1)} collective-permute-done((bf16[144,256]{1,0:T(8,128)(2,1)S(1)}, bf16[144,256]{1,0:T(8,128)(2,1)S(1)}, u32[]{:S(2)}, u32[]{:S(2)}) %collective-permute-start.4) | collective-permute-done | bytes 73760 | tf_op jit(solution)/shard_map/ppermute | solution.py:443
  14.9 0.4 collective-permute-done.5.refs_1_.refs_5_
  15.3 1.1 %collective-permute-done.6.refs_2_.refs_6_ = bf16[144,256]{1,0:T(8,128)(2,1)S(1)} collective-permute-done((bf16[144,256]{1,0:T(8,128)(2,1)S(1)}, bf16[144,256]{1,0:T(8,128)(2,1)S(1)}, u32[]{:S(2)}, u32[]{:S(2)}) %collective-permute-start.6) | collective-permute-done | bytes 73760 | tf_op jit(solution)/shard_map/ppermute | solution.py:443
  16.4 1.1 %collective-permute-done.7.refs_5_.refs_8_.refs_4_ = bf16[144,256]{1,0:T(8,128)(2,1)S(1)} collective-permute-done((bf16[144,256]{1,0:T(8,128)(2,1)S(1)}, bf16[144,256]{1,0:T(8,128)(2,1)S(1)}, u32[]{:S(2)}, u32[]{:S(2)}) %collective-permute-start.7) | collective-permute-done | bytes 73760 | tf_op jit(solution)/shard_map/ppermute | solution.py:443
  17.4 0.0 collective-permute-done.1.refs_0_
  17.4 0.1 pad_add_fusion.place_ref
  17.5 1.2 %collective-permute-start.9 = (bf16[144,256]{1,0:T(8,128)(2,1)S(1)}, bf16[144,256]{1,0:T(8,128)(2,1)S(1)}, u32[]{:S(2)}, u32[]{:S(2)}) collective-permute-start(bf16[144,256]{1,0:T(8,128)(2,1)S(1)} %after.2.refs_4_.refs_7_.refs_3_), channel_id=1, source_target_pairs={{0,4},{4,0},{8,12},{12,8},{16,20},{20,16},{24,28},{28,24},{1,5},{5... | collective-permute-start | bytes 221192 | tf_op jit(solution)/shard_map/ppermute | solution.py:443
  18.7 0.3 collective-permute-done.8.refs_3_
  19.0 2.9 %early.1 = (bf16[256,256]{1,0:T(8,128)(2,1)S(1)}, bf16[272,512]{1,0:T(8,128)(2,1)S(1)}, bf16[3,512,256]{2,1,0:T(8,128)(2,1)}, bf16[5,272,512]{2,1,0:T(8,128)(2,1...) custom-call(s32[3]{0:T(128)S(1)} %pad_add_fusion.place_ref, ...), custom_call_target="tpu_custom_call" | custom-call | flops 2684354560 | bytes 3809280 | tf_op jit(solution)/shard_map/early/pallas_call | solution.py:480
  21.9 0.3 collective-permute-done.9.refs_7_
  22.2 4.5 %heads.1 = f32[8,8,256]{2,1,0:T(8,128)} custom-call(s32[3]{0:T(128)S(1)} %pad_add_fusion.place_ref, bf16[256,256]{1,0:T(8,128)(2,1)S(1)} %get-tuple-element.15.factors_ref, bf16[144,256]{1,0:T(8,128)(2,1)S(1)} %pack.1.refs_1_.refs_4_.refs_0_, bf16[144,256]{1,0:T(8,128)(2,1)S(1)} %collective-permute-done.2.refs_2_.refs_5_.refs_1_, ...), custom_call_target="tpu_custom_call" | custom-call | tf_op jit(solution)/shard_map/heads/pallas_call | solution.py:495
  26.7 7.8 %all-to-all-start = ((f32[8,8,256]{2,1,0:T(8,128)}), f32[8,8,256]{2,1,0:T(8,128)S(1)}, u32[]{:S(2)}, u32[]{:S(2)}) async-start(f32[8,8,256]{2,1,0:T(8,128)} %heads.1), calls=%async_computation | async-start | bytes 131072 | tf_op jit(solution)/shard_map/all_to_all | solution.py:509
  34.5 3.0 %first.1 = (f32[8,128,256]{2,1,0:T(8,128)S(1)}, f32[8,256,256]{2,1,0:T(8,128)S(1)}) custom-call(s32[1]{0:T(128)} %bitcast.5.node_ref, bf16[272,512]{1,0:T(8,128)(2,1)S(1)} %get-tuple-element.11.matrix_ref, bf16[128,256]{1,0:T(8,128)(2,1)} %loadings_ref.3, bf16[512,256]{1,0:T(8,128)(2,1)} %rows_ref.1, bf16[3,512,256]{2,1,0:T(8,128)(2,1)} %get-tuple-element.12.kept_ref), custom_call_target="tpu_custom_call" | custom-call | flops 536870912 | bytes 3145728 | tf_op jit(solution)/shard_map/first/pallas_call | solution.py:513
  37.5 3.9 %all-to-all-done.head_ref = f32[8,8,256]{2,1,0:T(8,128)S(1)} async-done(((f32[8,8,256]{2,1,0:T(8,128)}), f32[8,8,256]{2,1,0:T(8,128)S(1)}, u32[]{:S(2)}, u32[]{:S(2)}) %all-to-all-start) | async-done | bytes 65568 | tf_op jit(solution)/shard_map/all_to_all | solution.py:509
  41.4 3.1 %volts.1 = (f32[2048,128]{1,0:T(8,128)}, f32[2048,128]{1,0:T(8,128)}) custom-call(bf16[272,512]{1,0:T(8,128)(2,1)S(1)} %get-tuple-element.11.matrix_ref, f32[8,128,256]{2,1,0:T(8,128)S(1)} %get-tuple-element.13.swing_ref, f32[8,256,256]{2,1,0:T(8,128)S(1)} %get-tuple-element.14.drop_ref, f32[8,8,256]{2,1,0:T(8,128)S(1)} %all-to-all-done.head_ref), custom_call_target="tpu_custom_call" | custom-call | tf_op jit(solution)/shard_map/volts/pallas_call | solution.py:530
  (6 shorter events, 0.0 us)
Async XLA Ops:
  0.6 16.8 %collective-permute-start.1 = (bf16[512,256]{1,0:T(8,128)(2,1)}, bf16[512,256]{1,0:T(8,128)(2,1)S(1)}, u32[]{:S(2)}, u32[]{:S(2)}) collective-permute-start(bf16[512,256]{1,0:T(8,128)(2,1)} %rows_ref.1), channel_id=1, source_target_pairs={{0,2},{1,3},{2,0},{3,1},{4,6},{5,7},{6,4},{7,5},{8,10},{9,11},{10,... | collective-permute-start | bytes 786440 | tf_op jit(solution)/shard_map/ppermute | solution.py:418
  4.6 5.9 %collective-permute-start.2 = (bf16[144,256]{1,0:T(8,128)(2,1)S(1)}, bf16[144,256]{1,0:T(8,128)(2,1)S(1)}, u32[]{:S(2)}, u32[]{:S(2)}) collective-permute-start(bf16[144,256]{1,0:T(8,128)(2,1)S(1)} %pack.1.refs_1_.refs_4_.refs_0_), channel_id=1, source_target_pairs={{0,16},{4,20},{8,24},{12,28},{16,0},{20,4},{24,8},{28,12},{1,17},{... | collective-permute-start | bytes 221192 | tf_op jit(solution)/shard_map/ppermute | solution.py:443
  7.2 4.7 %collective-permute-start.3 = (bf16[144,256]{1,0:T(8,128)(2,1)S(1)}, bf16[144,256]{1,0:T(8,128)(2,1)S(1)}, u32[]{:S(2)}, u32[]{:S(2)}) collective-permute-start(bf16[144,256]{1,0:T(8,128)(2,1)S(1)} %pack.1.refs_1_.refs_4_.refs_0_), channel_id=1, source_target_pairs={{0,8},{4,12},{8,0},{12,4},{16,24},{20,28},{24,16},{28,20},{1,9},{5... | collective-permute-start | bytes 221192 | tf_op jit(solution)/shard_map/ppermute | solution.py:443
  8.8 6.2 %collective-permute-start.4 = (bf16[144,256]{1,0:T(8,128)(2,1)S(1)}, bf16[144,256]{1,0:T(8,128)(2,1)S(1)}, u32[]{:S(2)}, u32[]{:S(2)}) collective-permute-start(bf16[144,256]{1,0:T(8,128)(2,1)S(1)} %pack.1.refs_1_.refs_4_.refs_0_), channel_id=1, source_target_pairs={{0,24},{4,28},{8,16},{12,20},{16,8},{20,12},{24,0},{28,4},{1,25},{... | collective-permute-start | bytes 221192 | tf_op jit(solution)/shard_map/ppermute | solution.py:443
  10.4 4.9 %collective-permute-start.5 = (bf16[144,256]{1,0:T(8,128)(2,1)S(1)}, bf16[144,256]{1,0:T(8,128)(2,1)S(1)}, u32[]{:S(2)}, u32[]{:S(2)}) collective-permute-start(bf16[144,256]{1,0:T(8,128)(2,1)S(1)} %collective-permute-done.2.refs_2_.refs_5_.refs_1_), channel_id=1, source_target_pairs={{0,4},{4,0},{8,12},{12,8},{16,20},{20,16},{24,28},{28,24},{1,5},{5... | collective-permute-start | bytes 221192 | tf_op jit(solution)/shard_map/ppermute | solution.py:443
  11.9 4.4 %collective-permute-start.6 = (bf16[144,256]{1,0:T(8,128)(2,1)S(1)}, bf16[144,256]{1,0:T(8,128)(2,1)S(1)}, u32[]{:S(2)}, u32[]{:S(2)}) collective-permute-start(bf16[144,256]{1,0:T(8,128)(2,1)S(1)} %collective-permute-done.3.refs_3_.refs_6_.refs_2_), channel_id=1, source_target_pairs={{0,4},{4,0},{8,12},{12,8},{16,20},{20,16},{24,28},{28,24},{1,5},{5... | collective-permute-start | bytes 221192 | tf_op jit(solution)/shard_map/ppermute | solution.py:443
  13.1 4.4 %collective-permute-start.7 = (bf16[144,256]{1,0:T(8,128)(2,1)S(1)}, bf16[144,256]{1,0:T(8,128)(2,1)S(1)}, u32[]{:S(2)}, u32[]{:S(2)}) collective-permute-start(bf16[144,256]{1,0:T(8,128)(2,1)S(1)} %pack.1.refs_1_.refs_4_.refs_0_), channel_id=1, source_target_pairs={{0,4},{4,0},{8,12},{12,8},{16,20},{20,16},{24,28},{28,24},{1,5},{5... | collective-permute-start | bytes 221192 | tf_op jit(solution)/shard_map/ppermute | solution.py:443
  14.9 3.7 %collective-permute-start = (bf16[512,256]{1,0:T(8,128)(2,1)}, bf16[512,256]{1,0:T(8,128)(2,1)S(1)}, u32[]{:S(2)}, u32[]{:S(2)}) collective-permute-start(bf16[512,256]{1,0:T(8,128)(2,1)} %rows_ref.1), channel_id=1, source_target_pairs={{0,1},{1,0},{2,3},{3,2},{4,5},{5,4},{6,7},{7,6},{8,9},{9,8},{10,11... | collective-permute-start | bytes 786440 | tf_op jit(solution)/shard_map/ppermute | solution.py:418
  17.4 1.5 %collective-permute-start.8 = (bf16[512,256]{1,0:T(8,128)(2,1)S(1)}, bf16[512,256]{1,0:T(8,128)(2,1)S(1)}, u32[]{:S(2)}, u32[]{:S(2)}) collective-permute-start(bf16[512,256]{1,0:T(8,128)(2,1)S(1)} %after.3.refs_2_), channel_id=1, source_target_pairs={{0,1},{1,0},{2,3},{3,2},{4,5},{5,4},{6,7},{7,6},{8,9},{9,8},{10,11... | collective-permute-start | bytes 786440 | tf_op jit(solution)/shard_map/ppermute | solution.py:418
  17.5 4.7 %collective-permute-start.9 = (bf16[144,256]{1,0:T(8,128)(2,1)S(1)}, bf16[144,256]{1,0:T(8,128)(2,1)S(1)}, u32[]{:S(2)}, u32[]{:S(2)}) collective-permute-start(bf16[144,256]{1,0:T(8,128)(2,1)S(1)} %after.2.refs_4_.refs_7_.refs_3_), channel_id=1, source_target_pairs={{0,4},{4,0},{8,12},{12,8},{16,20},{20,16},{24,28},{28,24},{1,5},{5... | collective-permute-start | bytes 221192 | tf_op jit(solution)/shard_map/ppermute | solution.py:443
  26.7 14.7 %all-to-all-start = ((f32[8,8,256]{2,1,0:T(8,128)}), f32[8,8,256]{2,1,0:T(8,128)S(1)}, u32[]{:S(2)}, u32[]{:S(2)}) async-start(f32[8,8,256]{2,1,0:T(8,128)} %heads.1), calls=%async_computation | async-start | bytes 131072 | tf_op jit(solution)/shard_map/all_to_all | solution.py:509

commit v12 on v9

--- a/solution.py
+++ b/solution.py
@@ -192,6 +192,28 @@
     return jnp.concatenate([real * inverse, imag * inverse], axis=0)
 
 
+def first_sweep(sections, factors_ref, matrix_ref, swing_ref, drop_ref, inject_ref, arrived=None):
+    n = swing_ref.shape[1]
+    for start in range(0, len(sections), 8):
+        group = list(enumerate(sections))[start : start + 8]
+        steps = matrix_steps([section for _, section in group], n)
+        next(steps)
+        if start == 0 and arrived is not None:
+            arrived()
+        for slot, section in group:
+            swing_ref[slot] = swing_of(section[0:n, :], factors_ref[...])
+        *_, matrices = steps
+        for (slot, _), matrix in zip(group, matrices):
+            matrix_ref[slot] = matrix
+            out = apply_first(matrix_ref[slot], swing_ref[slot])
+            drop_ref[slot] = out[: 2 * n]
+            inject_ref[slot] = out[2 * n :]
+
+
+def between_kernel(factors_ref, *refs):
+    first_sweep(refs[:-4], factors_ref, *refs[-4:])
+
+
 def early_kernel(pieces, place_ref, *refs):
     piece_refs, sections = refs[:pieces], refs[pieces:-9]
     factors_ref, own_ref, kept_ref, matrix_ref, swing_ref, drop_ref, inject_ref, sem, keep_sems = refs[-9:]
@@ -209,38 +231,30 @@
             rows = piece_ref.at[pl.ds(pl.multiple_of(offset, width), width), :]
             pltpu.make_async_copy(rows, factors_ref, sem).start()
 
-    n = swing_ref.shape[1]
-    for start in range(0, len(sections), 8):
-        group = list(enumerate(sections))[start : start + 8]
-        steps = matrix_steps([section for _, section in group], n)
-        next(steps)
-        if start == 0:
-            pltpu.make_async_copy(piece_refs[0].at[0:width, :], factors_ref, sem).wait()
-        for slot, section in group:
-            swing_ref[slot] = swing_of(section[0:n, :], factors_ref[...])
-        *_, matrices = steps
-        for (slot, _), matrix in zip(group, matrices):
-            matrix_ref[slot] = matrix
-            out = apply_first(matrix_ref[slot], swing_ref[slot])
-            drop_ref[slot] = out[: 2 * n]
-            inject_ref[slot] = out[2 * n :]
+    def arrived():
+        pltpu.make_async_copy(piece_refs[0].at[0:width, :], factors_ref, sem).wait()
+
+    first_sweep(sections, factors_ref, matrix_ref, swing_ref, drop_ref, inject_ref, arrived)
     own_ref[...] = matrix_ref[0]
     for copy in keeps:
         copy.wait()
 
 
-def heads_kernel(slots, early, place_ref, factors_ref, *refs):
-    feeders = len(slots)
-    sections = refs[:feeders]
-    early_refs = refs[feeders : feeders + 4]
-    head_ref, matrix_ref, swing_ref, drop_ref, again_ref, flow_ref, trunk_ref = refs[feeders + 4 :]
+def heads_kernel(slots, counts, place_ref, factors_ref, *refs):
+    feeders, early = len(slots), sum(counts)
+    sections, refs = refs[:feeders], refs[feeders:]
+    done = []
+    for count in counts:
+        done += [[ref.at[index] for ref in refs[:4]] for index in range(count)]
+        refs = refs[4:]
+    head_ref, matrix_ref, swing_ref, drop_ref, again_ref, flow_ref, trunk_ref = refs
     width = factors_ref.shape[0]
     n = swing_ref.shape[1]
     place = [jnp.bitwise_xor(place_ref[2], slot) for slot in slots]
     late_refs = (matrix_ref, swing_ref, drop_ref)
 
     def of(index, which):
-        return early_refs[which].at[index] if index < early else late_refs[which].at[index - early]
+        return done[index][which] if index < early else late_refs[which].at[index - early]
 
     def flow_of(index, real, imag):
         base = constants(sections[index], n)[2].T
@@ -448,8 +462,12 @@
     every[1] = swap(packed, 1)
     slots = list(every)
     early = len(slots)
+    middle = [3] if 2 in every else []
+    for offset in middle:
+        every[offset] = swap(every[1], offset ^ 1)
     for offset in slots[1:-1]:
-        every[offset + 1] = swap(every[offset], 1)
+        if offset + 1 not in every:
+            every[offset + 1] = swap(every[offset], 1)
     slots = list(every)
 
     if far:
@@ -488,18 +506,31 @@
         cost_estimate=pl.CostEstimate(flops=early * (1 << 29), bytes_accessed=early * state_bytes, transcendentals=early * n * width),
         name="early",
     )(place, *in_hbm(pieces[0]), *pieces[1:], *(every[slot] for slot in slots[:early]))
+    counts = [early]
+    if middle:
+        counts.append(len(middle))
+        started += pl.pallas_call(
+            between_kernel,
+            out_shape=[jax.ShapeDtypeStruct(*state) for state in states(len(middle))],
+            in_specs=[VMEM] * (1 + len(middle)),
+            out_specs=[VMEM] * 4,
+            compiler_params=limit(len(middle) * state_bytes),
+            cost_estimate=pl.CostEstimate(flops=1 << 20, bytes_accessed=1 << 10, transcendentals=0),
+            name="between",
+        )(block, *(every[slot] for slot in middle))
+    late = feeders - sum(counts)
     heads = pl.pallas_call(
-        functools.partial(heads_kernel, slots, early),
+        functools.partial(heads_kernel, slots, counts),
         out_shape=jax.ShapeDtypeStruct((feeders, 8, width), f32),
-        in_specs=[SMEM] + [VMEM] * (1 + feeders + 4),
+        in_specs=[SMEM] + [VMEM] * (1 + feeders + len(started)),
         out_specs=VMEM,
-        scratch_shapes=[pltpu.VMEM(*state) for state in states(max(feeders - early, 1))[:3]]
+        scratch_shapes=[pltpu.VMEM(*state) for state in states(max(late, 1))[:3]]
         + [
             pltpu.VMEM((feeders, 2 * n, width), f32),
             pltpu.VMEM((feeders, 8, width), f32),
             pltpu.VMEM((feeders, 8, width), f32),
         ],
-        compiler_params=limit((feeders - early) * state_bytes + feeders * (2 * n + 16) * width * 4),
+        compiler_params=limit(feeders * state_bytes + feeders * (2 * n + 16) * width * 4),
         name="heads",
     )(place, block, *(every[slot] for slot in slots), *started)
     given = lax.all_to_all(heads, "feeder", 0, 0, tiled=True)

time: 41.9 us -> 41.1 us (0.981)
  waiting for transfers between devices: 9.66 us -> 8.28 us
  Pallas kernels: 14.4 us -> 15.5 us
    ppermute x7, starting transfers between devices: 9.47 us -> 7.99 us  [swap(): lax.ppermute(block, 'feeder', [(i, i ^ offset) for i in range(feeders)])]
    ppermute x7, waiting for transfers between devices: 5.77 us -> 4.39 us  [swap(): lax.ppermute(block, 'feeder', [(i, i ^ offset) for i in range(feeders)])]
    all_to_all x1, starting transfers between devices: 4.16 us -> 5.26 us  [local(): given = lax.all_to_all(heads, 'feeder', 0, 0, tiled=True)]
    pallas_call x1 -> x2, Pallas kernels: 4.47 us -> 5.48 us  [the longest x1 4.34 us: local(): pl.pallas_call(functools.partial(heads_kernel, slots, counts), out_shape=...]
  transfers between devices with their start and end apart: 11 -> 11, of which waited for: 5 -> 4; matrix products, arithmetic and copies ran while one was open for 0% -> 0% of each run, Pallas kernels for 16% -> 20%
where the time goes in v12:
time: 41.1 us; the launch traced here: 40.8 us
  starting transfers between devices  16.3 us (40%)
  Pallas kernels  15.5 us (38%)
  waiting for transfers between devices  8.28 us (20%)
  between operations  0.7 us (2%)
    ppermute x7, starting transfers between devices, swap(): lax.ppermute(block, 'feeder', [(i, i ^ offset) for i in range(feeders)])  7.99 us
    all_to_all x1, starting transfers between devices, local(): given = lax.all_to_all(heads, 'feeder', 0, 0, tiled=True)  5.26 us
    ppermute x7, waiting for transfers between devices, swap(): lax.ppermute(block, 'feeder', [(i, i ^ offset) for i in range(feeders)])  4.39 us
    pallas_call x1, Pallas kernels, local(): pl.pallas_call(functools.partial(heads_kernel, slots, counts), out_shape=...  4.34 us
    all_to_all x1, waiting for transfers between devices, local(): given = lax.all_to_all(heads, 'feeder', 0, 0, tiled=True)  3.88 us
    pallas_call x1, Pallas kernels, local(): pl.pallas_call(volts_kernel, out_shape=(jax.ShapeDtypeStruct((scen, n), f...  3.15 us
    ppermute x3, starting transfers between devices, trade(): return lax.ppermute(block, 'node', [(i, i ^ offset) for i in range(nodes)])  3.04 us
    pallas_call x1, Pallas kernels, local(): pl.pallas_call(first_kernel, out_shape=(jax.ShapeDtypeStruct((chunks, n,...  3.02 us
  transfers between devices with their start and end apart: 11, of which 4 were waited for; matrix products, arithmetic and copies ran while one was open for 0% of the time, Pallas kernels for 20%

profile of v12, /device:TPU:0, one launch (start us, length us, event | category | flops | bytes accessed | tf_op | source)
XLA Modules:
  0.0 40.8 jit_solution(9123070198945711132)
XLA Ops:
  0.6 3.0 %collective-permute-start.1 = (bf16[512,256]{1,0:T(8,128)(2,1)}, bf16[512,256]{1,0:T(8,128)(2,1)S(1)}, u32[]{:S(2)}, u32[]{:S(2)}) collective-permute-start(bf16[512,256]{1,0:T(8,128)(2,1)} %rows_ref.1), channel_id=1, source_target_pairs={{0,2},{1,3},{2,0},{3,1},{4,6},{5,7},{6,4},{7,5},{8,10},{9,11},{10,... | collective-permute-start | bytes 786440 | tf_op jit(solution)/shard_map/ppermute | solution.py:432
  3.7 0.9 %pack.1.refs_1_.refs_4_.refs_0_ = bf16[144,256]{1,0:T(8,128)(2,1)S(1)} custom-call(f32[2]{0:T(128)} %bitcast.6, bf16[128,256]{1,0:T(8,128)(2,1)} %loadings_ref.3, s32[1,128]{1,0:T(1,128)} %bitcast.7, f32[2,128]{1,0:T(2,128)} %base_ref.1, f32[2,128]{1,0:T(2,128)} %z_ref.1), custom_call_target="tpu_custom_call" | custom-call | tf_op jit(solution)/shard_map/pack/pallas_call | solution.py:439
  4.6 2.7 %collective-permute-start.2 = (bf16[144,256]{1,0:T(8,128)(2,1)S(1)}, bf16[144,256]{1,0:T(8,128)(2,1)S(1)}, u32[]{:S(2)}, u32[]{:S(2)}) collective-permute-start(bf16[144,256]{1,0:T(8,128)(2,1)S(1)} %pack.1.refs_1_.refs_4_.refs_0_), channel_id=1, source_target_pairs={{0,16},{4,20},{8,24},{12,28},{16,0},{20,4},{24,8},{28,12},{1,17},{... | collective-permute-start | bytes 221192 | tf_op jit(solution)/shard_map/ppermute | solution.py:457
  7.2 1.3 %collective-permute-start.4 = (bf16[144,256]{1,0:T(8,128)(2,1)S(1)}, bf16[144,256]{1,0:T(8,128)(2,1)S(1)}, u32[]{:S(2)}, u32[]{:S(2)}) collective-permute-start(bf16[144,256]{1,0:T(8,128)(2,1)S(1)} %pack.1.refs_1_.refs_4_.refs_0_), channel_id=1, source_target_pairs={{0,24},{4,28},{8,16},{12,20},{16,8},{20,12},{24,0},{28,4},{1,25},{... | collective-permute-start | bytes 221192 | tf_op jit(solution)/shard_map/ppermute | solution.py:457
  8.6 1.5 %collective-permute-start.5 = (bf16[144,256]{1,0:T(8,128)(2,1)S(1)}, bf16[144,256]{1,0:T(8,128)(2,1)S(1)}, u32[]{:S(2)}, u32[]{:S(2)}) collective-permute-start(bf16[144,256]{1,0:T(8,128)(2,1)S(1)} %pack.1.refs_1_.refs_4_.refs_0_), channel_id=1, source_target_pairs={{0,4},{4,0},{8,12},{12,8},{16,20},{20,16},{24,28},{28,24},{1,5},{5... | collective-permute-start | bytes 221192 | tf_op jit(solution)/shard_map/ppermute | solution.py:457
  10.1 0.2 collective-permute-start.3
  10.3 1.7 %collective-permute-done.2.refs_2_.refs_5_.refs_1_ = bf16[144,256]{1,0:T(8,128)(2,1)S(1)} collective-permute-done((bf16[144,256]{1,0:T(8,128)(2,1)S(1)}, bf16[144,256]{1,0:T(8,128)(2,1)S(1)}, u32[]{:S(2)}, u32[]{:S(2)}) %collective-permute-start.2) | collective-permute-done | bytes 73760 | tf_op jit(solution)/shard_map/ppermute | solution.py:457
  12.0 2.2 %collective-permute-done.4.refs_4_.refs_7_.refs_3_ = bf16[144,256]{1,0:T(8,128)(2,1)S(1)} collective-permute-done((bf16[144,256]{1,0:T(8,128)(2,1)S(1)}, bf16[144,256]{1,0:T(8,128)(2,1)S(1)}, u32[]{:S(2)}, u32[]{:S(2)}) %collective-permute-start.4) | collective-permute-done | bytes 73760 | tf_op jit(solution)/shard_map/ppermute | solution.py:457
  14.2 0.0 collective-permute-done.5.refs_5_.refs_8_.refs_4_
  14.2 0.5 %collective-permute-done.3.refs_3_.refs_6_.refs_2_ = bf16[144,256]{1,0:T(8,128)(2,1)S(1)} collective-permute-done((bf16[144,256]{1,0:T(8,128)(2,1)S(1)}, bf16[144,256]{1,0:T(8,128)(2,1)S(1)}, u32[]{:S(2)}, u32[]{:S(2)}) %collective-permute-start.3) | collective-permute-done | bytes 73760 | tf_op jit(solution)/shard_map/ppermute | solution.py:457
  14.7 0.0 collective-permute-start.6
  14.7 0.1 pad_add_fusion.place_ref
  14.8 0.2 collective-permute-start.7
  15.0 1.5 %collective-permute-start.8 = (bf16[144,256]{1,0:T(8,128)(2,1)S(1)}, bf16[144,256]{1,0:T(8,128)(2,1)S(1)}, u32[]{:S(2)}, u32[]{:S(2)}) collective-permute-start(bf16[144,256]{1,0:T(8,128)(2,1)S(1)} %collective-permute-done.2.refs_2_.refs_5_.refs_1_), channel_id=1, source_target_pairs={{0,4},{4,0},{8,12},{12,8},{16,20},{20,16},{24,28},{28,24},{1,5},{5... | collective-permute-start | bytes 221192 | tf_op jit(solution)/shard_map/ppermute | solution.py:457
  16.5 0.5 %collective-permute-start.9 = (bf16[144,256]{1,0:T(8,128)(2,1)S(1)}, bf16[144,256]{1,0:T(8,128)(2,1)S(1)}, u32[]{:S(2)}, u32[]{:S(2)}) collective-permute-start(bf16[144,256]{1,0:T(8,128)(2,1)S(1)} %collective-permute-done.4.refs_4_.refs_7_.refs_3_), channel_id=1, source_target_pairs={{0,4},{4,0},{8,12},{12,8},{16,20},{20,16},{24,28},{28,24},{1,5},{5... | collective-permute-start | bytes 221192 | tf_op jit(solution)/shard_map/ppermute | solution.py:457
  17.0 0.0 collective-permute-done.refs_1_
  17.0 0.0 collective-permute-done.6.refs_3_
  17.0 2.9 %early.1 = (bf16[256,256]{1,0:T(8,128)(2,1)S(1)}, bf16[272,512]{1,0:T(8,128)(2,1)S(1)}, bf16[3,512,256]{2,1,0:T(8,128)(2,1)}, bf16[5,272,512]{2,1,0:T(8,128)(2,1...) custom-call(s32[3]{0:T(128)S(1)} %pad_add_fusion.place_ref, ...), custom_call_target="tpu_custom_call" | custom-call | flops 2684354560 | bytes 3809280 | tf_op jit(solution)/shard_map/early/pallas_call | solution.py:494
  20.0 1.1 %between.1 = (bf16[1,272,512]{2,1,0:T(8,128)(2,1)S(1)}, f32[1,128,256]{2,1,0:T(8,128)S(1)}, f32[1,256,256]{2,1,0:T(8,128)S(1)}, f32[1,16,256]{2,1,0:T(8,128)S(1)}) custom-call(bf16[256,256]{1,0:T(8,128)(2,1)S(1)} %get-tuple-element.19.factors_ref, bf16[144,256]{1,0:T(8,128)(2,1)S(1)} %collective-permute-done.7.refs_0_.refs_5_), custom_call_target="tpu_custom_call" | custom-call | flops 1048576 | bytes 1024 | tf_op jit(solution)/shard_map/between/pallas_call | solution.py:512
  21.2 4.3 %heads.1 = f32[8,8,256]{2,1,0:T(8,128)} custom-call(s32[3]{0:T(128)S(1)} %pad_add_fusion.place_ref, bf16[256,256]{1,0:T(8,128)(2,1)S(1)} %get-tuple-element.19.factors_ref, bf16[144,256]{1,0:T(8,128)(2,1)S(1)} %pack.1.refs_1_.refs_4_.refs_0_, bf16[144,256]{1,0:T(8,128)(2,1)S(1)} %collective-permute-done.2.refs_2_.refs_5_.refs_1_, ...), custom_call_target="tpu_custom_call" | custom-call | tf_op jit(solution)/shard_map/heads/pallas_call | solution.py:522
  25.5 5.3 %all-to-all-start = ((f32[8,8,256]{2,1,0:T(8,128)}), f32[8,8,256]{2,1,0:T(8,128)S(1)}, u32[]{:S(2)}, u32[]{:S(2)}) async-start(f32[8,8,256]{2,1,0:T(8,128)} %heads.1), calls=%async_computation | async-start | bytes 131072 | tf_op jit(solution)/shard_map/all_to_all | solution.py:536
  30.8 3.0 %first.1 = (f32[8,128,256]{2,1,0:T(8,128)S(1)}, f32[8,256,256]{2,1,0:T(8,128)S(1)}) custom-call(s32[1]{0:T(128)} %bitcast.5.node_ref, bf16[272,512]{1,0:T(8,128)(2,1)S(1)} %get-tuple-element.15.matrix_ref, bf16[128,256]{1,0:T(8,128)(2,1)} %loadings_ref.3, bf16[512,256]{1,0:T(8,128)(2,1)} %rows_ref.1, bf16[3,512,256]{2,1,0:T(8,128)(2,1)} %get-tuple-element.16.kept_ref), custom_call_target="tpu_custom_call" | custom-call | flops 536870912 | bytes 3145728 | tf_op jit(solution)/shard_map/first/pallas_call | solution.py:540
  33.8 3.9 %all-to-all-done.head_ref = f32[8,8,256]{2,1,0:T(8,128)S(1)} async-done(((f32[8,8,256]{2,1,0:T(8,128)}), f32[8,8,256]{2,1,0:T(8,128)S(1)}, u32[]{:S(2)}, u32[]{:S(2)}) %all-to-all-start) | async-done | bytes 65568 | tf_op jit(solution)/shard_map/all_to_all | solution.py:536
  37.7 3.1 %volts.1 = (f32[2048,128]{1,0:T(8,128)}, f32[2048,128]{1,0:T(8,128)}) custom-call(bf16[272,512]{1,0:T(8,128)(2,1)S(1)} %get-tuple-element.15.matrix_ref, f32[8,128,256]{2,1,0:T(8,128)S(1)} %get-tuple-element.17.swing_ref, f32[8,256,256]{2,1,0:T(8,128)S(1)} %get-tuple-element.18.drop_ref, f32[8,8,256]{2,1,0:T(8,128)S(1)} %all-to-all-done.head_ref), custom_call_target="tpu_custom_call" | custom-call | tf_op jit(solution)/shard_map/volts/pallas_call | solution.py:557
  (6 shorter events, 0.0 us)
Async XLA Ops:
  0.6 14.0 %collective-permute-start.1 = (bf16[512,256]{1,0:T(8,128)(2,1)}, bf16[512,256]{1,0:T(8,128)(2,1)S(1)}, u32[]{:S(2)}, u32[]{:S(2)}) collective-permute-start(bf16[512,256]{1,0:T(8,128)(2,1)} %rows_ref.1), channel_id=1, source_target_pairs={{0,2},{1,3},{2,0},{3,1},{4,6},{5,7},{6,4},{7,5},{8,10},{9,11},{10,... | collective-permute-start | bytes 786440 | tf_op jit(solution)/shard_map/ppermute | solution.py:432
  4.6 7.4 %collective-permute-start.2 = (bf16[144,256]{1,0:T(8,128)(2,1)S(1)}, bf16[144,256]{1,0:T(8,128)(2,1)S(1)}, u32[]{:S(2)}, u32[]{:S(2)}) collective-permute-start(bf16[144,256]{1,0:T(8,128)(2,1)S(1)} %pack.1.refs_1_.refs_4_.refs_0_), channel_id=1, source_target_pairs={{0,16},{4,20},{8,24},{12,28},{16,0},{20,4},{24,8},{28,12},{1,17},{... | collective-permute-start | bytes 221192 | tf_op jit(solution)/shard_map/ppermute | solution.py:457
  7.2 7.0 %collective-permute-start.4 = (bf16[144,256]{1,0:T(8,128)(2,1)S(1)}, bf16[144,256]{1,0:T(8,128)(2,1)S(1)}, u32[]{:S(2)}, u32[]{:S(2)}) collective-permute-start(bf16[144,256]{1,0:T(8,128)(2,1)S(1)} %pack.1.refs_1_.refs_4_.refs_0_), channel_id=1, source_target_pairs={{0,24},{4,28},{8,16},{12,20},{16,8},{20,12},{24,0},{28,4},{1,25},{... | collective-permute-start | bytes 221192 | tf_op jit(solution)/shard_map/ppermute | solution.py:457
  8.6 5.6 %collective-permute-start.5 = (bf16[144,256]{1,0:T(8,128)(2,1)S(1)}, bf16[144,256]{1,0:T(8,128)(2,1)S(1)}, u32[]{:S(2)}, u32[]{:S(2)}) collective-permute-start(bf16[144,256]{1,0:T(8,128)(2,1)S(1)} %pack.1.refs_1_.refs_4_.refs_0_), channel_id=1, source_target_pairs={{0,4},{4,0},{8,12},{12,8},{16,20},{20,16},{24,28},{28,24},{1,5},{5... | collective-permute-start | bytes 221192 | tf_op jit(solution)/shard_map/ppermute | solution.py:457
  10.1 4.6 %collective-permute-start.3 = (bf16[144,256]{1,0:T(8,128)(2,1)S(1)}, bf16[144,256]{1,0:T(8,128)(2,1)S(1)}, u32[]{:S(2)}, u32[]{:S(2)}) collective-permute-start(bf16[144,256]{1,0:T(8,128)(2,1)S(1)} %pack.1.refs_1_.refs_4_.refs_0_), channel_id=1, source_target_pairs={{0,8},{4,12},{8,0},{12,4},{16,24},{20,28},{24,16},{28,20},{1,9},{5... | collective-permute-start | bytes 221192 | tf_op jit(solution)/shard_map/ppermute | solution.py:457
  12.0 5.0 %collective-permute-start = (bf16[512,256]{1,0:T(8,128)(2,1)}, bf16[512,256]{1,0:T(8,128)(2,1)S(1)}, u32[]{:S(2)}, u32[]{:S(2)}) collective-permute-start(bf16[512,256]{1,0:T(8,128)(2,1)} %rows_ref.1), channel_id=1, source_target_pairs={{0,1},{1,0},{2,3},{3,2},{4,5},{5,4},{6,7},{7,6},{8,9},{9,8},{10,11... | collective-permute-start | bytes 786440 | tf_op jit(solution)/shard_map/ppermute | solution.py:432
  14.7 2.4 %collective-permute-start.6 = (bf16[512,256]{1,0:T(8,128)(2,1)S(1)}, bf16[512,256]{1,0:T(8,128)(2,1)S(1)}, u32[]{:S(2)}, u32[]{:S(2)}) collective-permute-start(bf16[512,256]{1,0:T(8,128)(2,1)S(1)} %after.1.refs_2_), channel_id=1, source_target_pairs={{0,1},{1,0},{2,3},{3,2},{4,5},{5,4},{6,7},{7,6},{8,9},{9,8},{10,11... | collective-permute-start | bytes 786440 | tf_op jit(solution)/shard_map/ppermute | solution.py:432
  14.8 5.2 %collective-permute-start.7 = (bf16[144,256]{1,0:T(8,128)(2,1)S(1)}, bf16[144,256]{1,0:T(8,128)(2,1)S(1)}, u32[]{:S(2)}, u32[]{:S(2)}) collective-permute-start(bf16[144,256]{1,0:T(8,128)(2,1)S(1)} %collective-permute-done.5.refs_5_.refs_8_.refs_4_), channel_id=1, source_target_pairs={{0,8},{4,12},{8,0},{12,4},{16,24},{20,28},{24,16},{28,20},{1,9},{5... | collective-permute-start | bytes 221192 | tf_op jit(solution)/shard_map/ppermute | solution.py:457
  15.0 6.2 %collective-permute-start.8 = (bf16[144,256]{1,0:T(8,128)(2,1)S(1)}, bf16[144,256]{1,0:T(8,128)(2,1)S(1)}, u32[]{:S(2)}, u32[]{:S(2)}) collective-permute-start(bf16[144,256]{1,0:T(8,128)(2,1)S(1)} %collective-permute-done.2.refs_2_.refs_5_.refs_1_), channel_id=1, source_target_pairs={{0,4},{4,0},{8,12},{12,8},{16,20},{20,16},{24,28},{28,24},{1,5},{5... | collective-permute-start | bytes 221192 | tf_op jit(solution)/shard_map/ppermute | solution.py:457
  16.5 4.7 %collective-permute-start.9 = (bf16[144,256]{1,0:T(8,128)(2,1)S(1)}, bf16[144,256]{1,0:T(8,128)(2,1)S(1)}, u32[]{:S(2)}, u32[]{:S(2)}) collective-permute-start(bf16[144,256]{1,0:T(8,128)(2,1)S(1)} %collective-permute-done.4.refs_4_.refs_7_.refs_3_), channel_id=1, source_target_pairs={{0,4},{4,0},{8,12},{12,8},{16,20},{20,16},{24,28},{28,24},{1,5},{5... | collective-permute-start | bytes 221192 | tf_op jit(solution)/shard_map/ppermute | solution.py:457
  25.5 12.2 %all-to-all-start = ((f32[8,8,256]{2,1,0:T(8,128)}), f32[8,8,256]{2,1,0:T(8,128)S(1)}, u32[]{:S(2)}, u32[]{:S(2)}) async-start(f32[8,8,256]{2,1,0:T(8,128)} %heads.1), calls=%async_computation | async-start | bytes 131072 | tf_op jit(solution)/shard_map/all_to_all | solution.py:536

commit v13 on v12

--- a/solution.py
+++ b/solution.py
@@ -521,7 +521,7 @@
     late = feeders - sum(counts)
     heads = pl.pallas_call(
         functools.partial(heads_kernel, slots, counts),
-        out_shape=jax.ShapeDtypeStruct((feeders, 8, width), f32),
+        out_shape=pltpu.VMEM((feeders, 8, width), f32),
         in_specs=[SMEM] + [VMEM] * (1 + feeders + len(started)),
         out_specs=VMEM,
         scratch_shapes=[pltpu.VMEM(*state) for state in states(max(late, 1))[:3]]

time: 41.1 us -> 41.1 us (level)
  no operation moved by 1% of the time
where the time goes in v13:
time: 41.1 us; the launch traced here: 40.8 us
  starting transfers between devices  16.3 us (40%)
  Pallas kernels  15.5 us (38%)
  waiting for transfers between devices  8.28 us (20%)
  between operations  0.7 us (2%)
    ppermute x7, starting transfers between devices, swap(): lax.ppermute(block, 'feeder', [(i, i ^ offset) for i in range(feeders)])  7.99 us
    all_to_all x1, starting transfers between devices, local(): given = lax.all_to_all(heads, 'feeder', 0, 0, tiled=True)  5.26 us
    ppermute x7, waiting for transfers between devices, swap(): lax.ppermute(block, 'feeder', [(i, i ^ offset) for i in range(feeders)])  4.39 us
    pallas_call x1, Pallas kernels, local(): pl.pallas_call(functools.partial(heads_kernel, slots, counts), out_shape=...  4.34 us
    all_to_all x1, waiting for transfers between devices, local(): given = lax.all_to_all(heads, 'feeder', 0, 0, tiled=True)  3.88 us
    pallas_call x1, Pallas kernels, local(): pl.pallas_call(volts_kernel, out_shape=(jax.ShapeDtypeStruct((scen, n), f...  3.15 us
    ppermute x3, starting transfers between devices, trade(): return lax.ppermute(block, 'node', [(i, i ^ offset) for i in range(nodes)])  3.04 us
    pallas_call x1, Pallas kernels, local(): pl.pallas_call(first_kernel, out_shape=(jax.ShapeDtypeStruct((chunks, n,...  3.02 us
  transfers between devices with their start and end apart: 11, of which 4 were waited for; matrix products, arithmetic and copies ran while one was open for 0% of the time, Pallas kernels for 20%

profile of v13, /device:TPU:0, one launch (start us, length us, event | category | flops | bytes accessed | tf_op | source)
XLA Modules:
  0.0 40.8 jit_solution(9123070198945711132)
XLA Ops:
  0.6 3.0 %collective-permute-start.1 = (bf16[512,256]{1,0:T(8,128)(2,1)}, bf16[512,256]{1,0:T(8,128)(2,1)S(1)}, u32[]{:S(2)}, u32[]{:S(2)}) collective-permute-start(bf16[512,256]{1,0:T(8,128)(2,1)} %rows_ref.1), channel_id=1, source_target_pairs={{0,2},{1,3},{2,0},{3,1},{4,6},{5,7},{6,4},{7,5},{8,10},{9,11},{10,... | collective-permute-start | bytes 786440 | tf_op jit(solution)/shard_map/ppermute | solution.py:432
  3.7 0.9 %pack.1.refs_1_.refs_4_.refs_0_ = bf16[144,256]{1,0:T(8,128)(2,1)S(1)} custom-call(f32[2]{0:T(128)} %bitcast.6, bf16[128,256]{1,0:T(8,128)(2,1)} %loadings_ref.3, s32[1,128]{1,0:T(1,128)} %bitcast.7, f32[2,128]{1,0:T(2,128)} %base_ref.1, f32[2,128]{1,0:T(2,128)} %z_ref.1), custom_call_target="tpu_custom_call" | custom-call | tf_op jit(solution)/shard_map/pack/pallas_call | solution.py:439
  4.6 2.7 %collective-permute-start.2 = (bf16[144,256]{1,0:T(8,128)(2,1)S(1)}, bf16[144,256]{1,0:T(8,128)(2,1)S(1)}, u32[]{:S(2)}, u32[]{:S(2)}) collective-permute-start(bf16[144,256]{1,0:T(8,128)(2,1)S(1)} %pack.1.refs_1_.refs_4_.refs_0_), channel_id=1, source_target_pairs={{0,16},{4,20},{8,24},{12,28},{16,0},{20,4},{24,8},{28,12},{1,17},{... | collective-permute-start | bytes 221192 | tf_op jit(solution)/shard_map/ppermute | solution.py:457
  7.2 1.3 %collective-permute-start.4 = (bf16[144,256]{1,0:T(8,128)(2,1)S(1)}, bf16[144,256]{1,0:T(8,128)(2,1)S(1)}, u32[]{:S(2)}, u32[]{:S(2)}) collective-permute-start(bf16[144,256]{1,0:T(8,128)(2,1)S(1)} %pack.1.refs_1_.refs_4_.refs_0_), channel_id=1, source_target_pairs={{0,24},{4,28},{8,16},{12,20},{16,8},{20,12},{24,0},{28,4},{1,25},{... | collective-permute-start | bytes 221192 | tf_op jit(solution)/shard_map/ppermute | solution.py:457
  8.6 1.5 %collective-permute-start.5 = (bf16[144,256]{1,0:T(8,128)(2,1)S(1)}, bf16[144,256]{1,0:T(8,128)(2,1)S(1)}, u32[]{:S(2)}, u32[]{:S(2)}) collective-permute-start(bf16[144,256]{1,0:T(8,128)(2,1)S(1)} %pack.1.refs_1_.refs_4_.refs_0_), channel_id=1, source_target_pairs={{0,4},{4,0},{8,12},{12,8},{16,20},{20,16},{24,28},{28,24},{1,5},{5... | collective-permute-start | bytes 221192 | tf_op jit(solution)/shard_map/ppermute | solution.py:457
  10.1 0.2 collective-permute-start.3
  10.3 1.7 %collective-permute-done.2.refs_2_.refs_5_.refs_1_ = bf16[144,256]{1,0:T(8,128)(2,1)S(1)} collective-permute-done((bf16[144,256]{1,0:T(8,128)(2,1)S(1)}, bf16[144,256]{1,0:T(8,128)(2,1)S(1)}, u32[]{:S(2)}, u32[]{:S(2)}) %collective-permute-start.2) | collective-permute-done | bytes 73760 | tf_op jit(solution)/shard_map/ppermute | solution.py:457
  12.0 2.2 %collective-permute-done.4.refs_4_.refs_7_.refs_3_ = bf16[144,256]{1,0:T(8,128)(2,1)S(1)} collective-permute-done((bf16[144,256]{1,0:T(8,128)(2,1)S(1)}, bf16[144,256]{1,0:T(8,128)(2,1)S(1)}, u32[]{:S(2)}, u32[]{:S(2)}) %collective-permute-start.4) | collective-permute-done | bytes 73760 | tf_op jit(solution)/shard_map/ppermute | solution.py:457
  14.2 0.0 collective-permute-done.5.refs_5_.refs_8_.refs_4_
  14.2 0.5 %collective-permute-done.3.refs_3_.refs_6_.refs_2_ = bf16[144,256]{1,0:T(8,128)(2,1)S(1)} collective-permute-done((bf16[144,256]{1,0:T(8,128)(2,1)S(1)}, bf16[144,256]{1,0:T(8,128)(2,1)S(1)}, u32[]{:S(2)}, u32[]{:S(2)}) %collective-permute-start.3) | collective-permute-done | bytes 73760 | tf_op jit(solution)/shard_map/ppermute | solution.py:457
  14.7 0.0 collective-permute-start.6
  14.7 0.1 pad_add_fusion.place_ref
  14.8 0.2 collective-permute-start.7
  15.0 1.5 %collective-permute-start.8 = (bf16[144,256]{1,0:T(8,128)(2,1)S(1)}, bf16[144,256]{1,0:T(8,128)(2,1)S(1)}, u32[]{:S(2)}, u32[]{:S(2)}) collective-permute-start(bf16[144,256]{1,0:T(8,128)(2,1)S(1)} %collective-permute-done.2.refs_2_.refs_5_.refs_1_), channel_id=1, source_target_pairs={{0,4},{4,0},{8,12},{12,8},{16,20},{20,16},{24,28},{28,24},{1,5},{5... | collective-permute-start | bytes 221192 | tf_op jit(solution)/shard_map/ppermute | solution.py:457
  16.5 0.5 %collective-permute-start.9 = (bf16[144,256]{1,0:T(8,128)(2,1)S(1)}, bf16[144,256]{1,0:T(8,128)(2,1)S(1)}, u32[]{:S(2)}, u32[]{:S(2)}) collective-permute-start(bf16[144,256]{1,0:T(8,128)(2,1)S(1)} %collective-permute-done.4.refs_4_.refs_7_.refs_3_), channel_id=1, source_target_pairs={{0,4},{4,0},{8,12},{12,8},{16,20},{20,16},{24,28},{28,24},{1,5},{5... | collective-permute-start | bytes 221192 | tf_op jit(solution)/shard_map/ppermute | solution.py:457
  17.0 0.0 collective-permute-done.refs_1_
  17.0 0.0 collective-permute-done.6.refs_3_
  17.0 2.9 %early.1 = (bf16[256,256]{1,0:T(8,128)(2,1)S(1)}, bf16[272,512]{1,0:T(8,128)(2,1)S(1)}, bf16[3,512,256]{2,1,0:T(8,128)(2,1)}, bf16[5,272,512]{2,1,0:T(8,128)(2,1...) custom-call(s32[3]{0:T(128)S(1)} %pad_add_fusion.place_ref, ...), custom_call_target="tpu_custom_call" | custom-call | flops 2684354560 | bytes 3809280 | tf_op jit(solution)/shard_map/early/pallas_call | solution.py:494
  20.0 1.1 %between.1 = (bf16[1,272,512]{2,1,0:T(8,128)(2,1)S(1)}, f32[1,128,256]{2,1,0:T(8,128)S(1)}, f32[1,256,256]{2,1,0:T(8,128)S(1)}, f32[1,16,256]{2,1,0:T(8,128)S(1)}) custom-call(bf16[256,256]{1,0:T(8,128)(2,1)S(1)} %get-tuple-element.19.factors_ref, bf16[144,256]{1,0:T(8,128)(2,1)S(1)} %collective-permute-done.7.refs_0_.refs_5_), custom_call_target="tpu_custom_call" | custom-call | flops 1048576 | bytes 1024 | tf_op jit(solution)/shard_map/between/pallas_call | solution.py:512
  21.2 4.3 %heads.1 = f32[8,8,256]{2,1,0:T(8,128)} custom-call(s32[3]{0:T(128)S(1)} %pad_add_fusion.place_ref, bf16[256,256]{1,0:T(8,128)(2,1)S(1)} %get-tuple-element.19.factors_ref, bf16[144,256]{1,0:T(8,128)(2,1)S(1)} %pack.1.refs_1_.refs_4_.refs_0_, bf16[144,256]{1,0:T(8,128)(2,1)S(1)} %collective-permute-done.2.refs_2_.refs_5_.refs_1_, ...), custom_call_target="tpu_custom_call" | custom-call | tf_op jit(solution)/shard_map/heads/pallas_call | solution.py:522
  25.5 5.3 %all-to-all-start = ((f32[8,8,256]{2,1,0:T(8,128)}), f32[8,8,256]{2,1,0:T(8,128)S(1)}, u32[]{:S(2)}, u32[]{:S(2)}) async-start(f32[8,8,256]{2,1,0:T(8,128)} %heads.1), calls=%async_computation | async-start | bytes 131072 | tf_op jit(solution)/shard_map/all_to_all | solution.py:536
  30.8 3.0 %first.1 = (f32[8,128,256]{2,1,0:T(8,128)S(1)}, f32[8,256,256]{2,1,0:T(8,128)S(1)}) custom-call(s32[1]{0:T(128)} %bitcast.5.node_ref, bf16[272,512]{1,0:T(8,128)(2,1)S(1)} %get-tuple-element.15.matrix_ref, bf16[128,256]{1,0:T(8,128)(2,1)} %loadings_ref.3, bf16[512,256]{1,0:T(8,128)(2,1)} %rows_ref.1, bf16[3,512,256]{2,1,0:T(8,128)(2,1)} %get-tuple-element.16.kept_ref), custom_call_target="tpu_custom_call" | custom-call | flops 536870912 | bytes 3145728 | tf_op jit(solution)/shard_map/first/pallas_call | solution.py:540
  33.8 3.9 %all-to-all-done.head_ref = f32[8,8,256]{2,1,0:T(8,128)S(1)} async-done(((f32[8,8,256]{2,1,0:T(8,128)}), f32[8,8,256]{2,1,0:T(8,128)S(1)}, u32[]{:S(2)}, u32[]{:S(2)}) %all-to-all-start) | async-done | bytes 65568 | tf_op jit(solution)/shard_map/all_to_all | solution.py:536
  37.7 3.1 %volts.1 = (f32[2048,128]{1,0:T(8,128)}, f32[2048,128]{1,0:T(8,128)}) custom-call(bf16[272,512]{1,0:T(8,128)(2,1)S(1)} %get-tuple-element.15.matrix_ref, f32[8,128,256]{2,1,0:T(8,128)S(1)} %get-tuple-element.17.swing_ref, f32[8,256,256]{2,1,0:T(8,128)S(1)} %get-tuple-element.18.drop_ref, f32[8,8,256]{2,1,0:T(8,128)S(1)} %all-to-all-done.head_ref), custom_call_target="tpu_custom_call" | custom-call | tf_op jit(solution)/shard_map/volts/pallas_call | solution.py:557
  (6 shorter events, 0.0 us)
Async XLA Ops:
  0.6 14.0 %collective-permute-start.1 = (bf16[512,256]{1,0:T(8,128)(2,1)}, bf16[512,256]{1,0:T(8,128)(2,1)S(1)}, u32[]{:S(2)}, u32[]{:S(2)}) collective-permute-start(bf16[512,256]{1,0:T(8,128)(2,1)} %rows_ref.1), channel_id=1, source_target_pairs={{0,2},{1,3},{2,0},{3,1},{4,6},{5,7},{6,4},{7,5},{8,10},{9,11},{10,... | collective-permute-start | bytes 786440 | tf_op jit(solution)/shard_map/ppermute | solution.py:432
  4.6 7.4 %collective-permute-start.2 = (bf16[144,256]{1,0:T(8,128)(2,1)S(1)}, bf16[144,256]{1,0:T(8,128)(2,1)S(1)}, u32[]{:S(2)}, u32[]{:S(2)}) collective-permute-start(bf16[144,256]{1,0:T(8,128)(2,1)S(1)} %pack.1.refs_1_.refs_4_.refs_0_), channel_id=1, source_target_pairs={{0,16},{4,20},{8,24},{12,28},{16,0},{20,4},{24,8},{28,12},{1,17},{... | collective-permute-start | bytes 221192 | tf_op jit(solution)/shard_map/ppermute | solution.py:457
  7.2 7.0 %collective-permute-start.4 = (bf16[144,256]{1,0:T(8,128)(2,1)S(1)}, bf16[144,256]{1,0:T(8,128)(2,1)S(1)}, u32[]{:S(2)}, u32[]{:S(2)}) collective-permute-start(bf16[144,256]{1,0:T(8,128)(2,1)S(1)} %pack.1.refs_1_.refs_4_.refs_0_), channel_id=1, source_target_pairs={{0,24},{4,28},{8,16},{12,20},{16,8},{20,12},{24,0},{28,4},{1,25},{... | collective-permute-start | bytes 221192 | tf_op jit(solution)/shard_map/ppermute | solution.py:457
  8.6 5.6 %collective-permute-start.5 = (bf16[144,256]{1,0:T(8,128)(2,1)S(1)}, bf16[144,256]{1,0:T(8,128)(2,1)S(1)}, u32[]{:S(2)}, u32[]{:S(2)}) collective-permute-start(bf16[144,256]{1,0:T(8,128)(2,1)S(1)} %pack.1.refs_1_.refs_4_.refs_0_), channel_id=1, source_target_pairs={{0,4},{4,0},{8,12},{12,8},{16,20},{20,16},{24,28},{28,24},{1,5},{5... | collective-permute-start | bytes 221192 | tf_op jit(solution)/shard_map/ppermute | solution.py:457
  10.1 4.6 %collective-permute-start.3 = (bf16[144,256]{1,0:T(8,128)(2,1)S(1)}, bf16[144,256]{1,0:T(8,128)(2,1)S(1)}, u32[]{:S(2)}, u32[]{:S(2)}) collective-permute-start(bf16[144,256]{1,0:T(8,128)(2,1)S(1)} %pack.1.refs_1_.refs_4_.refs_0_), channel_id=1, source_target_pairs={{0,8},{4,12},{8,0},{12,4},{16,24},{20,28},{24,16},{28,20},{1,9},{5... | collective-permute-start | bytes 221192 | tf_op jit(solution)/shard_map/ppermute | solution.py:457
  12.0 5.0 %collective-permute-start = (bf16[512,256]{1,0:T(8,128)(2,1)}, bf16[512,256]{1,0:T(8,128)(2,1)S(1)}, u32[]{:S(2)}, u32[]{:S(2)}) collective-permute-start(bf16[512,256]{1,0:T(8,128)(2,1)} %rows_ref.1), channel_id=1, source_target_pairs={{0,1},{1,0},{2,3},{3,2},{4,5},{5,4},{6,7},{7,6},{8,9},{9,8},{10,11... | collective-permute-start | bytes 786440 | tf_op jit(solution)/shard_map/ppermute | solution.py:432
  14.7 2.4 %collective-permute-start.6 = (bf16[512,256]{1,0:T(8,128)(2,1)S(1)}, bf16[512,256]{1,0:T(8,128)(2,1)S(1)}, u32[]{:S(2)}, u32[]{:S(2)}) collective-permute-start(bf16[512,256]{1,0:T(8,128)(2,1)S(1)} %after.1.refs_2_), channel_id=1, source_target_pairs={{0,1},{1,0},{2,3},{3,2},{4,5},{5,4},{6,7},{7,6},{8,9},{9,8},{10,11... | collective-permute-start | bytes 786440 | tf_op jit(solution)/shard_map/ppermute | solution.py:432
  14.8 5.2 %collective-permute-start.7 = (bf16[144,256]{1,0:T(8,128)(2,1)S(1)}, bf16[144,256]{1,0:T(8,128)(2,1)S(1)}, u32[]{:S(2)}, u32[]{:S(2)}) collective-permute-start(bf16[144,256]{1,0:T(8,128)(2,1)S(1)} %collective-permute-done.5.refs_5_.refs_8_.refs_4_), channel_id=1, source_target_pairs={{0,8},{4,12},{8,0},{12,4},{16,24},{20,28},{24,16},{28,20},{1,9},{5... | collective-permute-start | bytes 221192 | tf_op jit(solution)/shard_map/ppermute | solution.py:457
  15.0 6.2 %collective-permute-start.8 = (bf16[144,256]{1,0:T(8,128)(2,1)S(1)}, bf16[144,256]{1,0:T(8,128)(2,1)S(1)}, u32[]{:S(2)}, u32[]{:S(2)}) collective-permute-start(bf16[144,256]{1,0:T(8,128)(2,1)S(1)} %collective-permute-done.2.refs_2_.refs_5_.refs_1_), channel_id=1, source_target_pairs={{0,4},{4,0},{8,12},{12,8},{16,20},{20,16},{24,28},{28,24},{1,5},{5... | collective-permute-start | bytes 221192 | tf_op jit(solution)/shard_map/ppermute | solution.py:457
  16.5 4.7 %collective-permute-start.9 = (bf16[144,256]{1,0:T(8,128)(2,1)S(1)}, bf16[144,256]{1,0:T(8,128)(2,1)S(1)}, u32[]{:S(2)}, u32[]{:S(2)}) collective-permute-start(bf16[144,256]{1,0:T(8,128)(2,1)S(1)} %collective-permute-done.4.refs_4_.refs_7_.refs_3_), channel_id=1, source_target_pairs={{0,4},{4,0},{8,12},{12,8},{16,20},{20,16},{24,28},{28,24},{1,5},{5... | collective-permute-start | bytes 221192 | tf_op jit(solution)/shard_map/ppermute | solution.py:457
  25.5 12.2 %all-to-all-start = ((f32[8,8,256]{2,1,0:T(8,128)}), f32[8,8,256]{2,1,0:T(8,128)S(1)}, u32[]{:S(2)}, u32[]{:S(2)}) async-start(f32[8,8,256]{2,1,0:T(8,128)} %heads.1), calls=%async_computation | async-start | bytes 131072 | tf_op jit(solution)/shard_map/all_to_all | solution.py:536

commit v14 on v12

--- a/solution.py
+++ b/solution.py
@@ -295,13 +295,14 @@
             real, imag = flows[g]
             head_real = head_real - (r * real - x * imag)
             head_imag = head_imag - (r * imag + x * real)
-            head_ref[g, 2 * sweep : 2 * sweep + 1, :] = head_real
-            head_ref[g, 2 * sweep + 1 : 2 * sweep + 2, :] = head_imag
+            head_ref[feeders - 1 - g, 2 * sweep : 2 * sweep + 1, :] = head_real
+            head_ref[feeders - 1 - g, 2 * sweep + 1 : 2 * sweep + 2, :] = head_imag
 
     def volts(index, sweep):
         drop = of(index, 2) if sweep == 1 else again_ref.at[index]
-        real = head_ref[place[index], 2 * sweep - 2 : 2 * sweep - 1, :] - drop[0:n, :]
-        imag = head_ref[place[index], 2 * sweep - 1 : 2 * sweep, :] - drop[n : 2 * n, :]
+        rank = feeders - 1 - place[index]
+        real = head_ref[rank, 2 * sweep - 2 : 2 * sweep - 1, :] - drop[0:n, :]
+        imag = head_ref[rank, 2 * sweep - 1 : 2 * sweep, :] - drop[n : 2 * n, :]
         return real, imag
 
     def middle(index, sweep):
@@ -365,7 +366,7 @@
                 drop_ref[chunk] = apply_first(matrix, swing)
 
 
-def volts_kernel(matrix_ref, swing_ref, drop_ref, head_ref, real_ref, imag_ref, out_ref, sems):
+def volts_kernel(share, matrix_ref, swing_ref, drop_ref, head_ref, real_ref, imag_ref, out_ref, sems):
     n = swing_ref.shape[1]
     chunks, width = swing_ref.shape[0], swing_ref.shape[2]
     matrix = matrix_ref[0 : 2 * n, :]
@@ -374,8 +375,9 @@
 
     def advance(chunk, sweep):
         drop = drop_ref[chunk] if sweep == 0 else drops[chunk]
-        real = head_ref[chunk, 2 * sweep : 2 * sweep + 1, :] - drop[:n]
-        imag = head_ref[chunk, 2 * sweep + 1 : 2 * sweep + 2, :] - drop[n:]
+        giver = head_ref.shape[0] - 1 - chunk * share
+        real = head_ref[giver, 2 * sweep : 2 * sweep + 1, :] - drop[:n]
+        imag = head_ref[giver, 2 * sweep + 1 : 2 * sweep + 2, :] - drop[n:]
         if sweep < SWEEPS - 1:
             drops[chunk] = apply(matrix, scaled_volts(swing_ref[chunk], real, imag))
             return
@@ -533,8 +535,7 @@
         compiler_params=limit(feeders * state_bytes + feeders * (2 * n + 16) * width * 4),
         name="heads",
     )(place, block, *(every[slot] for slot in slots), *started)
-    given = lax.all_to_all(heads, "feeder", 0, 0, tiled=True)
-    given = given[::share]
+    given = lax.all_to_all(heads, "feeder", 0, 0, axis_index_groups=[list(range(feeders))[::-1]], tiled=True)
 
     chunks = scen // width
     swing, drop = pl.pallas_call(
@@ -555,7 +556,7 @@
         name="first",
     )(node.reshape(1), own, *in_hbm(loadings, factors, kept))
     return pl.pallas_call(
-        volts_kernel,
+        functools.partial(volts_kernel, share),
         out_shape=(
             jax.ShapeDtypeStruct((scen, n), f32),
             jax.ShapeDtypeStruct((scen, n), f32),

time: 41.1 us -> 39.3 us (0.956)
  waiting for transfers between devices: 8.28 us -> 4.4 us
  starting transfers between devices: 16.3 us -> 18.3 us
    all_to_all x1, waiting for transfers between devices: 3.88 us -> 0.01 us  [local(): lax.all_to_all(heads, 'feeder', 0, 0, axis_index_groups=[list(range(feede...]
    all_to_all x1, starting transfers between devices: 5.26 us -> 7.29 us  [local(): lax.all_to_all(heads, 'feeder', 0, 0, axis_index_groups=[list(range(feede...]
  transfers between devices with their start and end apart: 11 -> 11, of which waited for: 4 -> 3; matrix products, arithmetic and copies ran while one was open for 0% -> 0% of each run, Pallas kernels for 20% -> 20%
where the time goes in v14:
time: 39.3 us; the launch traced here: 39 us
  starting transfers between devices  18.3 us (47%)
  Pallas kernels  15.5 us (39%)
  waiting for transfers between devices  4.4 us (11%)
  between operations  0.7 us (2%)
    ppermute x7, starting transfers between devices, swap(): lax.ppermute(block, 'feeder', [(i, i ^ offset) for i in range(feeders)])  7.99 us
    all_to_all x1, starting transfers between devices, local(): lax.all_to_all(heads, 'feeder', 0, 0, axis_index_groups=[list(range(feede...  7.29 us
    ppermute x7, waiting for transfers between devices, swap(): lax.ppermute(block, 'feeder', [(i, i ^ offset) for i in range(feeders)])  4.39 us
    pallas_call x1, Pallas kernels, local(): pl.pallas_call(functools.partial(heads_kernel, slots, counts), out_shape=...  4.33 us
    pallas_call x1, Pallas kernels, local(): pl.pallas_call(functools.partial(volts_kernel, share), out_shape=(jax.Sha...  3.15 us
    ppermute x3, starting transfers between devices, trade(): return lax.ppermute(block, 'node', [(i, i ^ offset) for i in range(nodes)])  3.04 us
    pallas_call x1, Pallas kernels, local(): pl.pallas_call(first_kernel, out_shape=(jax.ShapeDtypeStruct((chunks, n,...  3.02 us
    pallas_call x1, Pallas kernels, local(): pl.pallas_call(functools.partial(early_kernel, nodes), out_shape=[jax.Sha...  2.94 us
  transfers between devices with their start and end apart: 11, of which 3 were waited for; matrix products, arithmetic and copies ran while one was open for 0% of the time, Pallas kernels for 20%

profile of v14, /device:TPU:0, one launch (start us, length us, event | category | flops | bytes accessed | tf_op | source)
XLA Modules:
  0.0 39.0 jit_solution(10273296940055434505)
XLA Ops:
  0.6 3.0 %collective-permute-start.1 = (bf16[512,256]{1,0:T(8,128)(2,1)}, bf16[512,256]{1,0:T(8,128)(2,1)S(1)}, u32[]{:S(2)}, u32[]{:S(2)}) collective-permute-start(bf16[512,256]{1,0:T(8,128)(2,1)} %rows_ref.1), channel_id=1, source_target_pairs={{0,2},{1,3},{2,0},{3,1},{4,6},{5,7},{6,4},{7,5},{8,10},{9,11},{10,... | collective-permute-start | bytes 786440 | tf_op jit(solution)/shard_map/ppermute | solution.py:434
  3.7 0.9 %pack.1.refs_1_.refs_4_.refs_0_ = bf16[144,256]{1,0:T(8,128)(2,1)S(1)} custom-call(f32[2]{0:T(128)} %bitcast.6, bf16[128,256]{1,0:T(8,128)(2,1)} %loadings_ref.3, s32[1,128]{1,0:T(1,128)} %bitcast.7, f32[2,128]{1,0:T(2,128)} %base_ref.1, f32[2,128]{1,0:T(2,128)} %z_ref.1), custom_call_target="tpu_custom_call" | custom-call | tf_op jit(solution)/shard_map/pack/pallas_call | solution.py:441
  4.6 2.7 %collective-permute-start.2 = (bf16[144,256]{1,0:T(8,128)(2,1)S(1)}, bf16[144,256]{1,0:T(8,128)(2,1)S(1)}, u32[]{:S(2)}, u32[]{:S(2)}) collective-permute-start(bf16[144,256]{1,0:T(8,128)(2,1)S(1)} %pack.1.refs_1_.refs_4_.refs_0_), channel_id=1, source_target_pairs={{0,16},{4,20},{8,24},{12,28},{16,0},{20,4},{24,8},{28,12},{1,17},{... | collective-permute-start | bytes 221192 | tf_op jit(solution)/shard_map/ppermute | solution.py:459
  7.2 1.3 %collective-permute-start.4 = (bf16[144,256]{1,0:T(8,128)(2,1)S(1)}, bf16[144,256]{1,0:T(8,128)(2,1)S(1)}, u32[]{:S(2)}, u32[]{:S(2)}) collective-permute-start(bf16[144,256]{1,0:T(8,128)(2,1)S(1)} %pack.1.refs_1_.refs_4_.refs_0_), channel_id=1, source_target_pairs={{0,24},{4,28},{8,16},{12,20},{16,8},{20,12},{24,0},{28,4},{1,25},{... | collective-permute-start | bytes 221192 | tf_op jit(solution)/shard_map/ppermute | solution.py:459
  8.6 1.5 %collective-permute-start.5 = (bf16[144,256]{1,0:T(8,128)(2,1)S(1)}, bf16[144,256]{1,0:T(8,128)(2,1)S(1)}, u32[]{:S(2)}, u32[]{:S(2)}) collective-permute-start(bf16[144,256]{1,0:T(8,128)(2,1)S(1)} %pack.1.refs_1_.refs_4_.refs_0_), channel_id=1, source_target_pairs={{0,4},{4,0},{8,12},{12,8},{16,20},{20,16},{24,28},{28,24},{1,5},{5... | collective-permute-start | bytes 221192 | tf_op jit(solution)/shard_map/ppermute | solution.py:459
  10.1 0.2 collective-permute-start.3
  10.3 1.7 %collective-permute-done.2.refs_2_.refs_5_.refs_1_ = bf16[144,256]{1,0:T(8,128)(2,1)S(1)} collective-permute-done((bf16[144,256]{1,0:T(8,128)(2,1)S(1)}, bf16[144,256]{1,0:T(8,128)(2,1)S(1)}, u32[]{:S(2)}, u32[]{:S(2)}) %collective-permute-start.2) | collective-permute-done | bytes 73760 | tf_op jit(solution)/shard_map/ppermute | solution.py:459
  12.0 2.2 %collective-permute-done.4.refs_4_.refs_7_.refs_3_ = bf16[144,256]{1,0:T(8,128)(2,1)S(1)} collective-permute-done((bf16[144,256]{1,0:T(8,128)(2,1)S(1)}, bf16[144,256]{1,0:T(8,128)(2,1)S(1)}, u32[]{:S(2)}, u32[]{:S(2)}) %collective-permute-start.4) | collective-permute-done | bytes 73760 | tf_op jit(solution)/shard_map/ppermute | solution.py:459
  14.2 0.0 collective-permute-done.5.refs_5_.refs_8_.refs_4_
  14.2 0.5 %collective-permute-done.3.refs_3_.refs_6_.refs_2_ = bf16[144,256]{1,0:T(8,128)(2,1)S(1)} collective-permute-done((bf16[144,256]{1,0:T(8,128)(2,1)S(1)}, bf16[144,256]{1,0:T(8,128)(2,1)S(1)}, u32[]{:S(2)}, u32[]{:S(2)}) %collective-permute-start.3) | collective-permute-done | bytes 73760 | tf_op jit(solution)/shard_map/ppermute | solution.py:459
  14.7 0.0 collective-permute-start.6
  14.7 0.1 pad_add_fusion.place_ref
  14.8 0.2 collective-permute-start.7
  15.0 1.5 %collective-permute-start.8 = (bf16[144,256]{1,0:T(8,128)(2,1)S(1)}, bf16[144,256]{1,0:T(8,128)(2,1)S(1)}, u32[]{:S(2)}, u32[]{:S(2)}) collective-permute-start(bf16[144,256]{1,0:T(8,128)(2,1)S(1)} %collective-permute-done.2.refs_2_.refs_5_.refs_1_), channel_id=1, source_target_pairs={{0,4},{4,0},{8,12},{12,8},{16,20},{20,16},{24,28},{28,24},{1,5},{5... | collective-permute-start | bytes 221192 | tf_op jit(solution)/shard_map/ppermute | solution.py:459
  16.5 0.5 %collective-permute-start.9 = (bf16[144,256]{1,0:T(8,128)(2,1)S(1)}, bf16[144,256]{1,0:T(8,128)(2,1)S(1)}, u32[]{:S(2)}, u32[]{:S(2)}) collective-permute-start(bf16[144,256]{1,0:T(8,128)(2,1)S(1)} %collective-permute-done.4.refs_4_.refs_7_.refs_3_), channel_id=1, source_target_pairs={{0,4},{4,0},{8,12},{12,8},{16,20},{20,16},{24,28},{28,24},{1,5},{5... | collective-permute-start | bytes 221192 | tf_op jit(solution)/shard_map/ppermute | solution.py:459
  17.0 0.0 collective-permute-done.refs_1_
  17.0 0.0 collective-permute-done.6.refs_3_
  17.0 2.9 %early.1 = (bf16[256,256]{1,0:T(8,128)(2,1)S(1)}, bf16[272,512]{1,0:T(8,128)(2,1)S(1)}, bf16[3,512,256]{2,1,0:T(8,128)(2,1)}, bf16[5,272,512]{2,1,0:T(8,128)(2,1...) custom-call(s32[3]{0:T(128)S(1)} %pad_add_fusion.place_ref, ...), custom_call_target="tpu_custom_call" | custom-call | flops 2684354560 | bytes 3809280 | tf_op jit(solution)/shard_map/early/pallas_call | solution.py:496
  20.0 0.0 collective-permute-done.7.refs_0_.refs_5_
  20.0 1.1 %between.1 = (bf16[1,272,512]{2,1,0:T(8,128)(2,1)S(1)}, f32[1,128,256]{2,1,0:T(8,128)S(1)}, f32[1,256,256]{2,1,0:T(8,128)S(1)}, f32[1,16,256]{2,1,0:T(8,128)S(1)}) custom-call(bf16[256,256]{1,0:T(8,128)(2,1)S(1)} %get-tuple-element.19.factors_ref, bf16[144,256]{1,0:T(8,128)(2,1)S(1)} %collective-permute-done.7.refs_0_.refs_5_), custom_call_target="tpu_custom_call" | custom-call | flops 1048576 | bytes 1024 | tf_op jit(solution)/shard_map/between/pallas_call | solution.py:514
  21.2 4.3 %heads.1 = f32[8,8,256]{2,1,0:T(8,128)} custom-call(s32[3]{0:T(128)S(1)} %pad_add_fusion.place_ref, bf16[256,256]{1,0:T(8,128)(2,1)S(1)} %get-tuple-element.19.factors_ref, bf16[144,256]{1,0:T(8,128)(2,1)S(1)} %pack.1.refs_1_.refs_4_.refs_0_, bf16[144,256]{1,0:T(8,128)(2,1)S(1)} %collective-permute-done.2.refs_2_.refs_5_.refs_1_, ...), custom_call_target="tpu_custom_call" | custom-call | tf_op jit(solution)/shard_map/heads/pallas_call | solution.py:524
  25.5 7.3 %all-to-all-start = ((f32[8,8,256]{2,1,0:T(8,128)}), f32[8,8,256]{2,1,0:T(8,128)S(1)}, u32[]{:S(2)}, u32[]{:S(2)}) async-start(f32[8,8,256]{2,1,0:T(8,128)} %heads.1), calls=%async_computation | async-start | bytes 131072 | tf_op jit(solution)/shard_map/all_to_all | solution.py:538
  32.8 3.0 %first.1 = (f32[8,128,256]{2,1,0:T(8,128)S(1)}, f32[8,256,256]{2,1,0:T(8,128)S(1)}) custom-call(s32[1]{0:T(128)} %bitcast.5.node_ref, bf16[272,512]{1,0:T(8,128)(2,1)S(1)} %get-tuple-element.15.matrix_ref, bf16[128,256]{1,0:T(8,128)(2,1)} %loadings_ref.3, bf16[512,256]{1,0:T(8,128)(2,1)} %rows_ref.1, bf16[3,512,256]{2,1,0:T(8,128)(2,1)} %get-tuple-element.16.kept_ref), custom_call_target="tpu_custom_call" | custom-call | flops 536870912 | bytes 3145728 | tf_op jit(solution)/shard_map/first/pallas_call | solution.py:541
  35.8 3.2 %volts.1 = (f32[2048,128]{1,0:T(8,128)}, f32[2048,128]{1,0:T(8,128)}) custom-call(bf16[272,512]{1,0:T(8,128)(2,1)S(1)} %get-tuple-element.15.matrix_ref, f32[8,128,256]{2,1,0:T(8,128)S(1)} %get-tuple-element.17.swing_ref, f32[8,256,256]{2,1,0:T(8,128)S(1)} %get-tuple-element.18.drop_ref, f32[8,8,256]{2,1,0:T(8,128)S(1)} %all-to-all-done.head_ref), custom_call_target="tpu_custom_call" | custom-call | tf_op jit(solution)/shard_map/volts/pallas_call | solution.py:558
  (6 shorter events, 0.0 us)
Async XLA Ops:
  0.6 14.0 %collective-permute-start.1 = (bf16[512,256]{1,0:T(8,128)(2,1)}, bf16[512,256]{1,0:T(8,128)(2,1)S(1)}, u32[]{:S(2)}, u32[]{:S(2)}) collective-permute-start(bf16[512,256]{1,0:T(8,128)(2,1)} %rows_ref.1), channel_id=1, source_target_pairs={{0,2},{1,3},{2,0},{3,1},{4,6},{5,7},{6,4},{7,5},{8,10},{9,11},{10,... | collective-permute-start | bytes 786440 | tf_op jit(solution)/shard_map/ppermute | solution.py:434
  4.6 7.4 %collective-permute-start.2 = (bf16[144,256]{1,0:T(8,128)(2,1)S(1)}, bf16[144,256]{1,0:T(8,128)(2,1)S(1)}, u32[]{:S(2)}, u32[]{:S(2)}) collective-permute-start(bf16[144,256]{1,0:T(8,128)(2,1)S(1)} %pack.1.refs_1_.refs_4_.refs_0_), channel_id=1, source_target_pairs={{0,16},{4,20},{8,24},{12,28},{16,0},{20,4},{24,8},{28,12},{1,17},{... | collective-permute-start | bytes 221192 | tf_op jit(solution)/shard_map/ppermute | solution.py:459
  7.2 7.0 %collective-permute-start.4 = (bf16[144,256]{1,0:T(8,128)(2,1)S(1)}, bf16[144,256]{1,0:T(8,128)(2,1)S(1)}, u32[]{:S(2)}, u32[]{:S(2)}) collective-permute-start(bf16[144,256]{1,0:T(8,128)(2,1)S(1)} %pack.1.refs_1_.refs_4_.refs_0_), channel_id=1, source_target_pairs={{0,24},{4,28},{8,16},{12,20},{16,8},{20,12},{24,0},{28,4},{1,25},{... | collective-permute-start | bytes 221192 | tf_op jit(solution)/shard_map/ppermute | solution.py:459
  8.6 5.6 %collective-permute-start.5 = (bf16[144,256]{1,0:T(8,128)(2,1)S(1)}, bf16[144,256]{1,0:T(8,128)(2,1)S(1)}, u32[]{:S(2)}, u32[]{:S(2)}) collective-permute-start(bf16[144,256]{1,0:T(8,128)(2,1)S(1)} %pack.1.refs_1_.refs_4_.refs_0_), channel_id=1, source_target_pairs={{0,4},{4,0},{8,12},{12,8},{16,20},{20,16},{24,28},{28,24},{1,5},{5... | collective-permute-start | bytes 221192 | tf_op jit(solution)/shard_map/ppermute | solution.py:459
  10.1 4.6 %collective-permute-start.3 = (bf16[144,256]{1,0:T(8,128)(2,1)S(1)}, bf16[144,256]{1,0:T(8,128)(2,1)S(1)}, u32[]{:S(2)}, u32[]{:S(2)}) collective-permute-start(bf16[144,256]{1,0:T(8,128)(2,1)S(1)} %pack.1.refs_1_.refs_4_.refs_0_), channel_id=1, source_target_pairs={{0,8},{4,12},{8,0},{12,4},{16,24},{20,28},{24,16},{28,20},{1,9},{5... | collective-permute-start | bytes 221192 | tf_op jit(solution)/shard_map/ppermute | solution.py:459
  12.0 5.0 %collective-permute-start = (bf16[512,256]{1,0:T(8,128)(2,1)}, bf16[512,256]{1,0:T(8,128)(2,1)S(1)}, u32[]{:S(2)}, u32[]{:S(2)}) collective-permute-start(bf16[512,256]{1,0:T(8,128)(2,1)} %rows_ref.1), channel_id=1, source_target_pairs={{0,1},{1,0},{2,3},{3,2},{4,5},{5,4},{6,7},{7,6},{8,9},{9,8},{10,11... | collective-permute-start | bytes 786440 | tf_op jit(solution)/shard_map/ppermute | solution.py:434
  14.7 2.4 %collective-permute-start.6 = (bf16[512,256]{1,0:T(8,128)(2,1)S(1)}, bf16[512,256]{1,0:T(8,128)(2,1)S(1)}, u32[]{:S(2)}, u32[]{:S(2)}) collective-permute-start(bf16[512,256]{1,0:T(8,128)(2,1)S(1)} %after.1.refs_2_), channel_id=1, source_target_pairs={{0,1},{1,0},{2,3},{3,2},{4,5},{5,4},{6,7},{7,6},{8,9},{9,8},{10,11... | collective-permute-start | bytes 786440 | tf_op jit(solution)/shard_map/ppermute | solution.py:434
  14.8 5.2 %collective-permute-start.7 = (bf16[144,256]{1,0:T(8,128)(2,1)S(1)}, bf16[144,256]{1,0:T(8,128)(2,1)S(1)}, u32[]{:S(2)}, u32[]{:S(2)}) collective-permute-start(bf16[144,256]{1,0:T(8,128)(2,1)S(1)} %collective-permute-done.5.refs_5_.refs_8_.refs_4_), channel_id=1, source_target_pairs={{0,8},{4,12},{8,0},{12,4},{16,24},{20,28},{24,16},{28,20},{1,9},{5... | collective-permute-start | bytes 221192 | tf_op jit(solution)/shard_map/ppermute | solution.py:459
  15.0 6.2 %collective-permute-start.8 = (bf16[144,256]{1,0:T(8,128)(2,1)S(1)}, bf16[144,256]{1,0:T(8,128)(2,1)S(1)}, u32[]{:S(2)}, u32[]{:S(2)}) collective-permute-start(bf16[144,256]{1,0:T(8,128)(2,1)S(1)} %collective-permute-done.2.refs_2_.refs_5_.refs_1_), channel_id=1, source_target_pairs={{0,4},{4,0},{8,12},{12,8},{16,20},{20,16},{24,28},{28,24},{1,5},{5... | collective-permute-start | bytes 221192 | tf_op jit(solution)/shard_map/ppermute | solution.py:459
  16.5 4.7 %collective-permute-start.9 = (bf16[144,256]{1,0:T(8,128)(2,1)S(1)}, bf16[144,256]{1,0:T(8,128)(2,1)S(1)}, u32[]{:S(2)}, u32[]{:S(2)}) collective-permute-start(bf16[144,256]{1,0:T(8,128)(2,1)S(1)} %collective-permute-done.4.refs_4_.refs_7_.refs_3_), channel_id=1, source_target_pairs={{0,4},{4,0},{8,12},{12,8},{16,20},{20,16},{24,28},{28,24},{1,5},{5... | collective-permute-start | bytes 221192 | tf_op jit(solution)/shard_map/ppermute | solution.py:459
  25.5 10.3 %all-to-all-start = ((f32[8,8,256]{2,1,0:T(8,128)}), f32[8,8,256]{2,1,0:T(8,128)S(1)}, u32[]{:S(2)}, u32[]{:S(2)}) async-start(f32[8,8,256]{2,1,0:T(8,128)} %heads.1), calls=%async_computation | async-start | bytes 131072 | tf_op jit(solution)/shard_map/all_to_all | solution.py:538

commit v15 on v14

--- a/solution.py
+++ b/solution.py
@@ -162,6 +162,13 @@
     yield out
 
 
+def stagger(count, steps):
+    for turn in range(count + len(steps) - 1):
+        for depth in reversed(range(len(steps))):
+            if 0 <= turn - depth < count:
+                steps[depth](turn - depth)
+
+
 def swing_of(loadings, factors):
     level = product_nt(loadings, factors).astype(jnp.bfloat16).astype(jnp.float32)
     return 1.0 + 0.5 * jnp.tanh(level)
@@ -350,20 +357,22 @@
     for copy in copies:
         copy.start()
     matrix = matrix_ref[0 : 2 * n, :]
-    for copy in copies:
-        copy.wait()
+    copies[0].wait()
     loadings = loads[...]
-    together = 4 // chunks if chunks < 4 else 1
-
-    @pl.loop(0, pieces // together)
-    def _(outer):
-        for inner in range(together):
-            index = outer * together + inner
-            for part in range(chunks):
-                chunk = jnp.bitwise_xor(node_ref[0], index) * chunks + part
-                swing = swing_of(loadings, factors_ref[index, part * width : (part + 1) * width, :])
-                swing_ref[chunk] = swing
-                drop_ref[chunk] = apply_first(matrix, swing)
+
+    def place(item):
+        return jnp.bitwise_xor(node_ref[0], item // chunks) * chunks + item % chunks
+
+    def swing_step(item):
+        index, part = divmod(item, chunks)
+        if part == 0:
+            copies[1 + index].wait()
+        swing_ref[place(item)] = swing_of(loadings, factors_ref[index, part * width : (part + 1) * width, :])
+
+    def drop_step(item):
+        drop_ref[place(item)] = apply_first(matrix, swing_ref[place(item)])
+
+    stagger(pieces * chunks, [swing_step, drop_step])
 
 
 def volts_kernel(share, matrix_ref, swing_ref, drop_ref, head_ref, real_ref, imag_ref, out_ref, sems):
@@ -387,10 +396,7 @@
             copies.append(pltpu.make_async_copy(out_ref.at[index, rows, :], to_ref.at[rows, :], sems.at[index, chunk]))
             copies[-1].start()
 
-    for turn in range(chunks + SWEEPS - 1):
-        for sweep in reversed(range(SWEEPS)):
-            if 0 <= turn - sweep < chunks:
-                advance(turn - sweep, sweep)
+    stagger(chunks, [functools.partial(advance, sweep=sweep) for sweep in range(SWEEPS)])
     for copy in copies:
         copy.wait()
 

time: 39.3 us -> 39.4 us (level)
  transfers between devices with their start and end apart: 11 -> 11, of which waited for: 3 -> 3; matrix products, arithmetic and copies ran while one was open for 0% -> 0% of each run, Pallas kernels for 20% -> 21%
where the time goes in v15:
time: 39.4 us; the launch traced here: 39.1 us
  starting transfers between devices  18.3 us (46%)
  Pallas kernels  15.6 us (40%)
  waiting for transfers between devices  4.4 us (11%)
  between operations  0.7 us (2%)
    ppermute x7, starting transfers between devices, swap(): lax.ppermute(block, 'feeder', [(i, i ^ offset) for i in range(feeders)])  7.99 us
    all_to_all x1, starting transfers between devices, local(): lax.all_to_all(heads, 'feeder', 0, 0, axis_index_groups=[list(range(feede...  7.29 us
    ppermute x7, waiting for transfers between devices, swap(): lax.ppermute(block, 'feeder', [(i, i ^ offset) for i in range(feeders)])  4.39 us
    pallas_call x1, Pallas kernels, local(): pl.pallas_call(functools.partial(heads_kernel, slots, counts), out_shape=...  4.33 us
    pallas_call x1, Pallas kernels, local(): pl.pallas_call(functools.partial(volts_kernel, share), out_shape=(jax.Sha...  3.15 us
    pallas_call x1, Pallas kernels, local(): pl.pallas_call(first_kernel, out_shape=(jax.ShapeDtypeStruct((chunks, n,...  3.15 us
    ppermute x3, starting transfers between devices, trade(): return lax.ppermute(block, 'node', [(i, i ^ offset) for i in range(nodes)])  3.04 us
    pallas_call x1, Pallas kernels, local(): pl.pallas_call(functools.partial(early_kernel, nodes), out_shape=[jax.Sha...  2.94 us
  transfers between devices with their start and end apart: 11, of which 3 were waited for; matrix products, arithmetic and copies ran while one was open for 0% of the time, Pallas kernels for 21%

profile of v15, /device:TPU:0, one launch (start us, length us, event | category | flops | bytes accessed | tf_op | source)
XLA Modules:
  0.0 39.1 jit_solution(6434132662693658818)
XLA Ops:
  0.6 3.0 %collective-permute-start.1 = (bf16[512,256]{1,0:T(8,128)(2,1)}, bf16[512,256]{1,0:T(8,128)(2,1)S(1)}, u32[]{:S(2)}, u32[]{:S(2)}) collective-permute-start(bf16[512,256]{1,0:T(8,128)(2,1)} %rows_ref.1), channel_id=1, source_target_pairs={{0,2},{1,3},{2,0},{3,1},{4,6},{5,7},{6,4},{7,5},{8,10},{9,11},{10,... | collective-permute-start | bytes 786440 | tf_op jit(solution)/shard_map/ppermute | solution.py:440
  3.7 0.9 %pack.1.refs_1_.refs_4_.refs_0_ = bf16[144,256]{1,0:T(8,128)(2,1)S(1)} custom-call(f32[2]{0:T(128)} %bitcast.6, bf16[128,256]{1,0:T(8,128)(2,1)} %loadings_ref.3, s32[1,128]{1,0:T(1,128)} %bitcast.7, f32[2,128]{1,0:T(2,128)} %base_ref.1, f32[2,128]{1,0:T(2,128)} %z_ref.1), custom_call_target="tpu_custom_call" | custom-call | tf_op jit(solution)/shard_map/pack/pallas_call | solution.py:447
  4.6 2.7 %collective-permute-start.2 = (bf16[144,256]{1,0:T(8,128)(2,1)S(1)}, bf16[144,256]{1,0:T(8,128)(2,1)S(1)}, u32[]{:S(2)}, u32[]{:S(2)}) collective-permute-start(bf16[144,256]{1,0:T(8,128)(2,1)S(1)} %pack.1.refs_1_.refs_4_.refs_0_), channel_id=1, source_target_pairs={{0,16},{4,20},{8,24},{12,28},{16,0},{20,4},{24,8},{28,12},{1,17},{... | collective-permute-start | bytes 221192 | tf_op jit(solution)/shard_map/ppermute | solution.py:465
  7.2 1.3 %collective-permute-start.4 = (bf16[144,256]{1,0:T(8,128)(2,1)S(1)}, bf16[144,256]{1,0:T(8,128)(2,1)S(1)}, u32[]{:S(2)}, u32[]{:S(2)}) collective-permute-start(bf16[144,256]{1,0:T(8,128)(2,1)S(1)} %pack.1.refs_1_.refs_4_.refs_0_), channel_id=1, source_target_pairs={{0,24},{4,28},{8,16},{12,20},{16,8},{20,12},{24,0},{28,4},{1,25},{... | collective-permute-start | bytes 221192 | tf_op jit(solution)/shard_map/ppermute | solution.py:465
  8.6 1.5 %collective-permute-start.5 = (bf16[144,256]{1,0:T(8,128)(2,1)S(1)}, bf16[144,256]{1,0:T(8,128)(2,1)S(1)}, u32[]{:S(2)}, u32[]{:S(2)}) collective-permute-start(bf16[144,256]{1,0:T(8,128)(2,1)S(1)} %pack.1.refs_1_.refs_4_.refs_0_), channel_id=1, source_target_pairs={{0,4},{4,0},{8,12},{12,8},{16,20},{20,16},{24,28},{28,24},{1,5},{5... | collective-permute-start | bytes 221192 | tf_op jit(solution)/shard_map/ppermute | solution.py:465
  10.1 0.2 collective-permute-start.3
  10.3 1.7 %collective-permute-done.2.refs_2_.refs_5_.refs_1_ = bf16[144,256]{1,0:T(8,128)(2,1)S(1)} collective-permute-done((bf16[144,256]{1,0:T(8,128)(2,1)S(1)}, bf16[144,256]{1,0:T(8,128)(2,1)S(1)}, u32[]{:S(2)}, u32[]{:S(2)}) %collective-permute-start.2) | collective-permute-done | bytes 73760 | tf_op jit(solution)/shard_map/ppermute | solution.py:465
  12.0 2.2 %collective-permute-done.4.refs_4_.refs_7_.refs_3_ = bf16[144,256]{1,0:T(8,128)(2,1)S(1)} collective-permute-done((bf16[144,256]{1,0:T(8,128)(2,1)S(1)}, bf16[144,256]{1,0:T(8,128)(2,1)S(1)}, u32[]{:S(2)}, u32[]{:S(2)}) %collective-permute-start.4) | collective-permute-done | bytes 73760 | tf_op jit(solution)/shard_map/ppermute | solution.py:465
  14.2 0.0 collective-permute-done.5.refs_5_.refs_8_.refs_4_
  14.2 0.5 %collective-permute-done.3.refs_3_.refs_6_.refs_2_ = bf16[144,256]{1,0:T(8,128)(2,1)S(1)} collective-permute-done((bf16[144,256]{1,0:T(8,128)(2,1)S(1)}, bf16[144,256]{1,0:T(8,128)(2,1)S(1)}, u32[]{:S(2)}, u32[]{:S(2)}) %collective-permute-start.3) | collective-permute-done | bytes 73760 | tf_op jit(solution)/shard_map/ppermute | solution.py:465
  14.7 0.0 collective-permute-start.6
  14.7 0.1 pad_add_fusion.place_ref
  14.8 0.2 collective-permute-start.7
  15.0 1.5 %collective-permute-start.8 = (bf16[144,256]{1,0:T(8,128)(2,1)S(1)}, bf16[144,256]{1,0:T(8,128)(2,1)S(1)}, u32[]{:S(2)}, u32[]{:S(2)}) collective-permute-start(bf16[144,256]{1,0:T(8,128)(2,1)S(1)} %collective-permute-done.2.refs_2_.refs_5_.refs_1_), channel_id=1, source_target_pairs={{0,4},{4,0},{8,12},{12,8},{16,20},{20,16},{24,28},{28,24},{1,5},{5... | collective-permute-start | bytes 221192 | tf_op jit(solution)/shard_map/ppermute | solution.py:465
  16.5 0.5 %collective-permute-start.9 = (bf16[144,256]{1,0:T(8,128)(2,1)S(1)}, bf16[144,256]{1,0:T(8,128)(2,1)S(1)}, u32[]{:S(2)}, u32[]{:S(2)}) collective-permute-start(bf16[144,256]{1,0:T(8,128)(2,1)S(1)} %collective-permute-done.4.refs_4_.refs_7_.refs_3_), channel_id=1, source_target_pairs={{0,4},{4,0},{8,12},{12,8},{16,20},{20,16},{24,28},{28,24},{1,5},{5... | collective-permute-start | bytes 221192 | tf_op jit(solution)/shard_map/ppermute | solution.py:465
  17.0 0.0 collective-permute-done.refs_1_
  17.0 0.0 collective-permute-done.6.refs_3_
  17.0 2.9 %early.1 = (bf16[256,256]{1,0:T(8,128)(2,1)S(1)}, bf16[272,512]{1,0:T(8,128)(2,1)S(1)}, bf16[3,512,256]{2,1,0:T(8,128)(2,1)}, bf16[5,272,512]{2,1,0:T(8,128)(2,1...) custom-call(s32[3]{0:T(128)S(1)} %pad_add_fusion.place_ref, ...), custom_call_target="tpu_custom_call" | custom-call | flops 2684354560 | bytes 3809280 | tf_op jit(solution)/shard_map/early/pallas_call | solution.py:502
  20.0 0.0 collective-permute-done.7.refs_0_.refs_5_
  20.0 1.1 %between.1 = (bf16[1,272,512]{2,1,0:T(8,128)(2,1)S(1)}, f32[1,128,256]{2,1,0:T(8,128)S(1)}, f32[1,256,256]{2,1,0:T(8,128)S(1)}, f32[1,16,256]{2,1,0:T(8,128)S(1)}) custom-call(bf16[256,256]{1,0:T(8,128)(2,1)S(1)} %get-tuple-element.19.factors_ref, bf16[144,256]{1,0:T(8,128)(2,1)S(1)} %collective-permute-done.7.refs_0_.refs_5_), custom_call_target="tpu_custom_call" | custom-call | flops 1048576 | bytes 1024 | tf_op jit(solution)/shard_map/between/pallas_call | solution.py:520
  21.2 4.3 %heads.1 = f32[8,8,256]{2,1,0:T(8,128)} custom-call(s32[3]{0:T(128)S(1)} %pad_add_fusion.place_ref, bf16[256,256]{1,0:T(8,128)(2,1)S(1)} %get-tuple-element.19.factors_ref, bf16[144,256]{1,0:T(8,128)(2,1)S(1)} %pack.1.refs_1_.refs_4_.refs_0_, bf16[144,256]{1,0:T(8,128)(2,1)S(1)} %collective-permute-done.2.refs_2_.refs_5_.refs_1_, ...), custom_call_target="tpu_custom_call" | custom-call | tf_op jit(solution)/shard_map/heads/pallas_call | solution.py:530
  25.5 7.3 %all-to-all-start = ((f32[8,8,256]{2,1,0:T(8,128)}), f32[8,8,256]{2,1,0:T(8,128)S(1)}, u32[]{:S(2)}, u32[]{:S(2)}) async-start(f32[8,8,256]{2,1,0:T(8,128)} %heads.1), calls=%async_computation | async-start | bytes 131072 | tf_op jit(solution)/shard_map/all_to_all | solution.py:544
  32.8 3.1 %first.1 = (f32[8,128,256]{2,1,0:T(8,128)S(1)}, f32[8,256,256]{2,1,0:T(8,128)S(1)}) custom-call(s32[1]{0:T(128)} %bitcast.5.node_ref, bf16[272,512]{1,0:T(8,128)(2,1)S(1)} %get-tuple-element.15.matrix_ref, bf16[128,256]{1,0:T(8,128)(2,1)} %loadings_ref.3, bf16[512,256]{1,0:T(8,128)(2,1)} %rows_ref.1, bf16[3,512,256]{2,1,0:T(8,128)(2,1)} %get-tuple-element.16.kept_ref), custom_call_target="tpu_custom_call" | custom-call | flops 536870912 | bytes 3145728 | tf_op jit(solution)/shard_map/first/pallas_call | solution.py:547
  36.0 3.2 %volts.1 = (f32[2048,128]{1,0:T(8,128)}, f32[2048,128]{1,0:T(8,128)}) custom-call(bf16[272,512]{1,0:T(8,128)(2,1)S(1)} %get-tuple-element.15.matrix_ref, f32[8,128,256]{2,1,0:T(8,128)S(1)} %get-tuple-element.17.swing_ref, f32[8,256,256]{2,1,0:T(8,128)S(1)} %get-tuple-element.18.drop_ref, f32[8,8,256]{2,1,0:T(8,128)S(1)} %all-to-all-done.head_ref), custom_call_target="tpu_custom_call" | custom-call | tf_op jit(solution)/shard_map/volts/pallas_call | solution.py:564
  (6 shorter events, 0.0 us)
Async XLA Ops:
  0.6 14.0 %collective-permute-start.1 = (bf16[512,256]{1,0:T(8,128)(2,1)}, bf16[512,256]{1,0:T(8,128)(2,1)S(1)}, u32[]{:S(2)}, u32[]{:S(2)}) collective-permute-start(bf16[512,256]{1,0:T(8,128)(2,1)} %rows_ref.1), channel_id=1, source_target_pairs={{0,2},{1,3},{2,0},{3,1},{4,6},{5,7},{6,4},{7,5},{8,10},{9,11},{10,... | collective-permute-start | bytes 786440 | tf_op jit(solution)/shard_map/ppermute | solution.py:440
  4.6 7.4 %collective-permute-start.2 = (bf16[144,256]{1,0:T(8,128)(2,1)S(1)}, bf16[144,256]{1,0:T(8,128)(2,1)S(1)}, u32[]{:S(2)}, u32[]{:S(2)}) collective-permute-start(bf16[144,256]{1,0:T(8,128)(2,1)S(1)} %pack.1.refs_1_.refs_4_.refs_0_), channel_id=1, source_target_pairs={{0,16},{4,20},{8,24},{12,28},{16,0},{20,4},{24,8},{28,12},{1,17},{... | collective-permute-start | bytes 221192 | tf_op jit(solution)/shard_map/ppermute | solution.py:465
  7.2 7.0 %collective-permute-start.4 = (bf16[144,256]{1,0:T(8,128)(2,1)S(1)}, bf16[144,256]{1,0:T(8,128)(2,1)S(1)}, u32[]{:S(2)}, u32[]{:S(2)}) collective-permute-start(bf16[144,256]{1,0:T(8,128)(2,1)S(1)} %pack.1.refs_1_.refs_4_.refs_0_), channel_id=1, source_target_pairs={{0,24},{4,28},{8,16},{12,20},{16,8},{20,12},{24,0},{28,4},{1,25},{... | collective-permute-start | bytes 221192 | tf_op jit(solution)/shard_map/ppermute | solution.py:465
  8.6 5.6 %collective-permute-start.5 = (bf16[144,256]{1,0:T(8,128)(2,1)S(1)}, bf16[144,256]{1,0:T(8,128)(2,1)S(1)}, u32[]{:S(2)}, u32[]{:S(2)}) collective-permute-start(bf16[144,256]{1,0:T(8,128)(2,1)S(1)} %pack.1.refs_1_.refs_4_.refs_0_), channel_id=1, source_target_pairs={{0,4},{4,0},{8,12},{12,8},{16,20},{20,16},{24,28},{28,24},{1,5},{5... | collective-permute-start | bytes 221192 | tf_op jit(solution)/shard_map/ppermute | solution.py:465
  10.1 4.6 %collective-permute-start.3 = (bf16[144,256]{1,0:T(8,128)(2,1)S(1)}, bf16[144,256]{1,0:T(8,128)(2,1)S(1)}, u32[]{:S(2)}, u32[]{:S(2)}) collective-permute-start(bf16[144,256]{1,0:T(8,128)(2,1)S(1)} %pack.1.refs_1_.refs_4_.refs_0_), channel_id=1, source_target_pairs={{0,8},{4,12},{8,0},{12,4},{16,24},{20,28},{24,16},{28,20},{1,9},{5... | collective-permute-start | bytes 221192 | tf_op jit(solution)/shard_map/ppermute | solution.py:465
  12.0 5.0 %collective-permute-start = (bf16[512,256]{1,0:T(8,128)(2,1)}, bf16[512,256]{1,0:T(8,128)(2,1)S(1)}, u32[]{:S(2)}, u32[]{:S(2)}) collective-permute-start(bf16[512,256]{1,0:T(8,128)(2,1)} %rows_ref.1), channel_id=1, source_target_pairs={{0,1},{1,0},{2,3},{3,2},{4,5},{5,4},{6,7},{7,6},{8,9},{9,8},{10,11... | collective-permute-start | bytes 786440 | tf_op jit(solution)/shard_map/ppermute | solution.py:440
  14.7 2.4 %collective-permute-start.6 = (bf16[512,256]{1,0:T(8,128)(2,1)S(1)}, bf16[512,256]{1,0:T(8,128)(2,1)S(1)}, u32[]{:S(2)}, u32[]{:S(2)}) collective-permute-start(bf16[512,256]{1,0:T(8,128)(2,1)S(1)} %after.1.refs_2_), channel_id=1, source_target_pairs={{0,1},{1,0},{2,3},{3,2},{4,5},{5,4},{6,7},{7,6},{8,9},{9,8},{10,11... | collective-permute-start | bytes 786440 | tf_op jit(solution)/shard_map/ppermute | solution.py:440
  14.8 5.2 %collective-permute-start.7 = (bf16[144,256]{1,0:T(8,128)(2,1)S(1)}, bf16[144,256]{1,0:T(8,128)(2,1)S(1)}, u32[]{:S(2)}, u32[]{:S(2)}) collective-permute-start(bf16[144,256]{1,0:T(8,128)(2,1)S(1)} %collective-permute-done.5.refs_5_.refs_8_.refs_4_), channel_id=1, source_target_pairs={{0,8},{4,12},{8,0},{12,4},{16,24},{20,28},{24,16},{28,20},{1,9},{5... | collective-permute-start | bytes 221192 | tf_op jit(solution)/shard_map/ppermute | solution.py:465
  15.0 6.2 %collective-permute-start.8 = (bf16[144,256]{1,0:T(8,128)(2,1)S(1)}, bf16[144,256]{1,0:T(8,128)(2,1)S(1)}, u32[]{:S(2)}, u32[]{:S(2)}) collective-permute-start(bf16[144,256]{1,0:T(8,128)(2,1)S(1)} %collective-permute-done.2.refs_2_.refs_5_.refs_1_), channel_id=1, source_target_pairs={{0,4},{4,0},{8,12},{12,8},{16,20},{20,16},{24,28},{28,24},{1,5},{5... | collective-permute-start | bytes 221192 | tf_op jit(solution)/shard_map/ppermute | solution.py:465
  16.5 4.7 %collective-permute-start.9 = (bf16[144,256]{1,0:T(8,128)(2,1)S(1)}, bf16[144,256]{1,0:T(8,128)(2,1)S(1)}, u32[]{:S(2)}, u32[]{:S(2)}) collective-permute-start(bf16[144,256]{1,0:T(8,128)(2,1)S(1)} %collective-permute-done.4.refs_4_.refs_7_.refs_3_), channel_id=1, source_target_pairs={{0,4},{4,0},{8,12},{12,8},{16,20},{20,16},{24,28},{28,24},{1,5},{5... | collective-permute-start | bytes 221192 | tf_op jit(solution)/shard_map/ppermute | solution.py:465
  25.5 10.5 %all-to-all-start = ((f32[8,8,256]{2,1,0:T(8,128)}), f32[8,8,256]{2,1,0:T(8,128)S(1)}, u32[]{:S(2)}, u32[]{:S(2)}) async-start(f32[8,8,256]{2,1,0:T(8,128)} %heads.1), calls=%async_computation | async-start | bytes 131072 | tf_op jit(solution)/shard_map/all_to_all | solution.py:544

commit v16 on v14

--- a/solution.py
+++ b/solution.py
@@ -39,19 +39,23 @@
 
 
 def pack_kernel(
-    trunk_ref, loadings_ref, parents_ref, base_ref, z_ref, out_ref, trunk, loads, owners, rows_ref, meta_ref, sems
+    place_ref, trunk_ref, loadings_ref, parents_ref, base_ref, z_ref, factors_ref, out_ref, block_ref,
+    trunk, loads, owners, rows_ref, meta_ref, sems,
 ):
     n = loadings_ref.shape[0]
+    width = block_ref.shape[0]
+    offset = pl.multiple_of(place_ref[1], width)
     copies = [
         pltpu.make_async_copy(loadings_ref, loads, sems.at[0]),
         pltpu.make_async_copy(parents_ref, owners, sems.at[1]),
         pltpu.make_async_copy(base_ref, rows_ref.at[0], sems.at[2]),
         pltpu.make_async_copy(z_ref, rows_ref.at[1], sems.at[3]),
         pltpu.make_async_copy(trunk_ref, trunk, sems.at[4]),
+        pltpu.make_async_copy(factors_ref.at[pl.ds(offset, width), :], block_ref, sems.at[5]),
     ]
     for copy in copies:
         copy.start()
-    for copy in copies[1:]:
+    for copy in copies[1:5]:
         copy.wait()
     pair_ids = lax.broadcasted_iota(jnp.int32, (2, n), 0)
     trunk_rows = jnp.where(pair_ids == 0, trunk[0], trunk[1])
@@ -69,6 +73,7 @@
     copies[0].wait()
     out_ref[0:n, :] = loads[...]
     out_ref[n : n + EXTRA, :] = meta
+    copies[5].wait()
 
 
 def constants(section_ref, n):
@@ -227,12 +232,12 @@
         copy.start()
     for index, piece_ref in enumerate(piece_refs):
         @pl.when(piece == index)
-        def _(piece_ref=piece_ref):
-            rows = piece_ref.at[pl.ds(pl.multiple_of(offset, width), width), :]
+        def _(piece_ref=piece_ref, index=index):
+            rows = piece_ref.at[pl.ds(pl.multiple_of(offset, width), width), :] if index else piece_ref
             pltpu.make_async_copy(rows, factors_ref, sem).start()
 
     def arrived():
-        pltpu.make_async_copy(piece_refs[0].at[0:width, :], factors_ref, sem).wait()
+        pltpu.make_async_copy(piece_refs[0], factors_ref, sem).wait()
 
     first_sweep(sections, factors_ref, matrix_ref, swing_ref, drop_ref, inject_ref, arrived)
     own_ref[...] = matrix_ref[0]
@@ -438,22 +443,25 @@
     if far:
         held[far] = trade(factors, far)
 
-    packed = pl.pallas_call(
+    start = (feeder // share) * width
+    place = jnp.stack([(start // rows) ^ node, start % rows, feeder])
+
+    packed, own_rows = pl.pallas_call(
         pack_kernel,
-        out_shape=jax.ShapeDtypeStruct((n + EXTRA, rank), bf16),
-        in_specs=[HBM] * 5,
-        out_specs=VMEM,
+        out_shape=(jax.ShapeDtypeStruct((n + EXTRA, rank), bf16), jax.ShapeDtypeStruct((width, rank), bf16)),
+        in_specs=[SMEM] + [HBM] * 6,
+        out_specs=(VMEM, VMEM),
         scratch_shapes=[
             pltpu.SMEM((2,), f32),
             pltpu.VMEM((n, rank), bf16),
             pltpu.VMEM((1, n), jnp.int32),
             pltpu.VMEM((2, 2, n), f32),
             pltpu.VMEM((EXTRA, rank), f32),
-            pltpu.SemaphoreType.DMA((5,)),
+            pltpu.SemaphoreType.DMA((6,)),
         ],
         compiler_params=limit(2 * (n + EXTRA) * rank * 2),
         name="pack",
-    )(*in_hbm(trunk_z.reshape(2), loadings, parents.reshape(1, n), load_base, lateral_z))
+    )(place, *in_hbm(trunk_z.reshape(2), loadings, parents.reshape(1, n), load_base, lateral_z, factors))
 
     def swap(block, offset):
         return lax.ppermute(block, "feeder", [(i, i ^ offset) for i in range(feeders)])
@@ -481,9 +489,6 @@
         step //= 2
     pieces = [held[offset] for offset in range(nodes)]
 
-    start = (feeder // share) * width
-    place = jnp.stack([(start // rows) ^ node, start % rows, feeder])
-
     def states(count):
         return [
             ((count, *matrix_shape), bf16),
@@ -501,13 +506,13 @@
             pltpu.HBM((nodes - 1, rows, rank), bf16),
         ]
         + [jax.ShapeDtypeStruct(*state) for state in states(early)],
-        in_specs=[SMEM, HBM] + [ANY] * (nodes - 1) + [VMEM] * early,
+        in_specs=[SMEM, VMEM] + [ANY] * (nodes - 1) + [VMEM] * early,
         out_specs=[VMEM, VMEM, HBM] + [VMEM] * 4,
         scratch_shapes=[pltpu.SemaphoreType.DMA, pltpu.SemaphoreType.DMA((nodes - 1,))],
         compiler_params=limit(early * state_bytes),
         cost_estimate=pl.CostEstimate(flops=early * (1 << 29), bytes_accessed=early * state_bytes, transcendentals=early * n * width),
         name="early",
-    )(place, *in_hbm(pieces[0]), *pieces[1:], *(every[slot] for slot in slots[:early]))
+    )(place, own_rows, *pieces[1:], *(every[slot] for slot in slots[:early]))
     counts = [early]
     if middle:
         counts.append(len(middle))

time: 39.3 us -> 39.9 us (1.015)
  Pallas kernels: 15.5 us -> 15.9 us
    pallas_call x1, Pallas kernels: 0.89 us -> 1.58 us  [local(): pl.pallas_call(pack_kernel, out_shape=(jax.ShapeDtypeStruct((n + EXTRA, r...]
  transfers between devices with their start and end apart: 11 -> 11, of which waited for: 3 -> 3; matrix products, arithmetic and copies ran while one was open for 0% -> 0% of each run, Pallas kernels for 20% -> 21%
where the time goes in v16:
time: 39.9 us; the launch traced here: 39.6 us
  starting transfers between devices  18.3 us (46%)
  Pallas kernels  15.9 us (40%)
  waiting for transfers between devices  4.74 us (12%)
  between operations  0.71 us (2%)
    ppermute x7, starting transfers between devices, swap(): lax.ppermute(block, 'feeder', [(i, i ^ offset) for i in range(feeders)])  8.11 us
    all_to_all x1, starting transfers between devices, local(): lax.all_to_all(heads, 'feeder', 0, 0, axis_index_groups=[list(range(feede...  7.06 us
    ppermute x7, waiting for transfers between devices, swap(): lax.ppermute(block, 'feeder', [(i, i ^ offset) for i in range(feeders)])  4.73 us
    pallas_call x1, Pallas kernels, local(): pl.pallas_call(functools.partial(heads_kernel, slots, counts), out_shape=...  4.35 us
    pallas_call x1, Pallas kernels, local(): pl.pallas_call(functools.partial(volts_kernel, share), out_shape=(jax.Sha...  3.15 us
    ppermute x3, starting transfers between devices, trade(): return lax.ppermute(block, 'node', [(i, i ^ offset) for i in range(nodes)])  3.1 us
    pallas_call x1, Pallas kernels, local(): pl.pallas_call(first_kernel, out_shape=(jax.ShapeDtypeStruct((chunks, n,...  3.02 us
    pallas_call x1, Pallas kernels, local(): pl.pallas_call(functools.partial(early_kernel, nodes), out_shape=[jax.Sha...  2.61 us
  transfers between devices with their start and end apart: 11, of which 3 were waited for; matrix products, arithmetic and copies ran while one was open for 0% of the time, Pallas kernels for 21%

profile of v16, /device:TPU:0, one launch (start us, length us, event | category | flops | bytes accessed | tf_op | source)
XLA Modules:
  0.0 39.6 jit_solution(17398274585624735292)
XLA Ops:
  0.6 3.0 %collective-permute-start.1 = (bf16[512,256]{1,0:T(8,128)(2,1)}, bf16[512,256]{1,0:T(8,128)(2,1)S(1)}, u32[]{:S(2)}, u32[]{:S(2)}) collective-permute-start(bf16[512,256]{1,0:T(8,128)(2,1)} %rows_ref.1), channel_id=1, source_target_pairs={{0,2},{1,3},{2,0},{3,1},{4,6},{5,7},{6,4},{7,5},{8,10},{9,11},{10,... | collective-permute-start | bytes 786440 | tf_op jit(solution)/shard_map/ppermute | solution.py:439
  3.7 0.1 pad_add_fusion.place_ref
  3.7 1.6 %pack.1 = (bf16[144,256]{1,0:T(8,128)(2,1)S(1)}, bf16[256,256]{1,0:T(8,128)(2,1)S(1)}) custom-call(s32[3]{0:T(128)S(1)} %pad_add_fusion.place_ref, f32[2]{0:T(128)} %bitcast.6, bf16[128,256]{1,0:T(8,128)(2,1)} %loadings_ref.3, s32[1,128]{1,0:T(1,128)} %bitcast.7, f32[2,128]{1,0:T(2,128)} %base_ref.1, f32[2,128]{1,0:T(2,128)} %z_ref.1, bf16[512,256]{1,0:T(8,128)(2,1)} %rows_ref.1), custom_call_target="tpu_custom_call" | custom-call | tf_op jit(solution)/shard_map/pack/pallas_call | solution.py:449
  5.3 2.7 %collective-permute-start.2 = (bf16[144,256]{1,0:T(8,128)(2,1)S(1)}, bf16[144,256]{1,0:T(8,128)(2,1)S(1)}, u32[]{:S(2)}, u32[]{:S(2)}) collective-permute-start(bf16[144,256]{1,0:T(8,128)(2,1)S(1)} %get-tuple-element.18.refs_1_.refs_4_.refs_0_), channel_id=1, source_target_pairs={{0,16},{4,20},{8,24},{12,28},{16,0},{20,4},{24,8},{28,12},{1,17},{... | collective-permute-start | bytes 221192 | tf_op jit(solution)/shard_map/ppermute | solution.py:467
  8.0 1.6 %collective-permute-start.3 = (bf16[144,256]{1,0:T(8,128)(2,1)S(1)}, bf16[144,256]{1,0:T(8,128)(2,1)S(1)}, u32[]{:S(2)}, u32[]{:S(2)}) collective-permute-start(bf16[144,256]{1,0:T(8,128)(2,1)S(1)} %get-tuple-element.18.refs_1_.refs_4_.refs_0_), channel_id=1, source_target_pairs={{0,8},{4,12},{8,0},{12,4},{16,24},{20,28},{24,16},{28,20},{1,9},{5... | collective-permute-start | bytes 221192 | tf_op jit(solution)/shard_map/ppermute | solution.py:467
  9.6 0.2 collective-permute-start.4
  9.8 1.5 %collective-permute-start.5 = (bf16[144,256]{1,0:T(8,128)(2,1)S(1)}, bf16[144,256]{1,0:T(8,128)(2,1)S(1)}, u32[]{:S(2)}, u32[]{:S(2)}) collective-permute-start(bf16[144,256]{1,0:T(8,128)(2,1)S(1)} %get-tuple-element.18.refs_1_.refs_4_.refs_0_), channel_id=1, source_target_pairs={{0,4},{4,0},{8,12},{12,8},{16,20},{20,16},{24,28},{28,24},{1,5},{5... | collective-permute-start | bytes 221192 | tf_op jit(solution)/shard_map/ppermute | solution.py:467
  11.3 0.0 collective-permute-done.2.refs_2_.refs_5_.refs_1_
  11.3 1.1 %collective-permute-done.3.refs_3_.refs_6_.refs_2_ = bf16[144,256]{1,0:T(8,128)(2,1)S(1)} collective-permute-done((bf16[144,256]{1,0:T(8,128)(2,1)S(1)}, bf16[144,256]{1,0:T(8,128)(2,1)S(1)}, u32[]{:S(2)}, u32[]{:S(2)}) %collective-permute-start.3) | collective-permute-done | bytes 73760 | tf_op jit(solution)/shard_map/ppermute | solution.py:467
  12.3 3.4 %collective-permute-done.4.refs_4_.refs_7_.refs_3_ = bf16[144,256]{1,0:T(8,128)(2,1)S(1)} collective-permute-done((bf16[144,256]{1,0:T(8,128)(2,1)S(1)}, bf16[144,256]{1,0:T(8,128)(2,1)S(1)}, u32[]{:S(2)}, u32[]{:S(2)}) %collective-permute-start.4) | collective-permute-done | bytes 73760 | tf_op jit(solution)/shard_map/ppermute | solution.py:467
  15.7 0.0 collective-permute-done.5.refs_5_.refs_8_.refs_4_
  15.7 0.0 collective-permute-done.1.refs_0_
  15.7 0.1 collective-permute-start.6
  15.8 0.1 collective-permute-start.7
  15.9 1.6 %collective-permute-start.8 = (bf16[144,256]{1,0:T(8,128)(2,1)S(1)}, bf16[144,256]{1,0:T(8,128)(2,1)S(1)}, u32[]{:S(2)}, u32[]{:S(2)}) collective-permute-start(bf16[144,256]{1,0:T(8,128)(2,1)S(1)} %collective-permute-done.2.refs_2_.refs_5_.refs_1_), channel_id=1, source_target_pairs={{0,4},{4,0},{8,12},{12,8},{16,20},{20,16},{24,28},{28,24},{1,5},{5... | collective-permute-start | bytes 221192 | tf_op jit(solution)/shard_map/ppermute | solution.py:467
  17.4 0.5 %collective-permute-start.9 = (bf16[144,256]{1,0:T(8,128)(2,1)S(1)}, bf16[144,256]{1,0:T(8,128)(2,1)S(1)}, u32[]{:S(2)}, u32[]{:S(2)}) collective-permute-start(bf16[144,256]{1,0:T(8,128)(2,1)S(1)} %collective-permute-done.4.refs_4_.refs_7_.refs_3_), channel_id=1, source_target_pairs={{0,4},{4,0},{8,12},{12,8},{16,20},{20,16},{24,28},{28,24},{1,5},{5... | collective-permute-start | bytes 221192 | tf_op jit(solution)/shard_map/ppermute | solution.py:467
  18.0 0.0 collective-permute-done.refs_1_
  18.0 2.6 %early.1 = (bf16[256,256]{1,0:T(8,128)(2,1)S(1)}, bf16[272,512]{1,0:T(8,128)(2,1)S(1)}, bf16[3,512,256]{2,1,0:T(8,128)(2,1)}, bf16[5,272,512]{2,1,0:T(8,128)(2,1...) custom-call(s32[3]{0:T(128)S(1)} %pad_add_fusion.place_ref, ...), custom_call_target="tpu_custom_call" | custom-call | flops 2684354560 | bytes 3809280 | tf_op jit(solution)/shard_map/early/pallas_call | solution.py:501
  20.6 1.1 %between.1 = (bf16[1,272,512]{2,1,0:T(8,128)(2,1)S(1)}, f32[1,128,256]{2,1,0:T(8,128)S(1)}, f32[1,256,256]{2,1,0:T(8,128)S(1)}, f32[1,16,256]{2,1,0:T(8,128)S(1)}) custom-call(bf16[256,256]{1,0:T(8,128)(2,1)S(1)} %get-tuple-element.23.factors_ref, bf16[144,256]{1,0:T(8,128)(2,1)S(1)} %collective-permute-done.7.refs_0_.refs_5_), custom_call_target="tpu_custom_call" | custom-call | flops 1048576 | bytes 1024 | tf_op jit(solution)/shard_map/between/pallas_call | solution.py:519
  21.8 0.3 collective-permute-done.9.refs_7_
  22.0 4.3 %heads.1 = f32[8,8,256]{2,1,0:T(8,128)} custom-call(s32[3]{0:T(128)S(1)} %pad_add_fusion.place_ref, bf16[256,256]{1,0:T(8,128)(2,1)S(1)} %get-tuple-element.23.factors_ref, bf16[144,256]{1,0:T(8,128)(2,1)S(1)} %get-tuple-element.18.refs_1_.refs_4_.refs_0_, bf16[144,256]{1,0:T(8,128)(2,1)S(1)} %collective-permute-done.2.refs_2_.refs_5_.refs_1_, ...), custom_call_target="tpu_custom_call" | custom-call | tf_op jit(solution)/shard_map/heads/pallas_call | solution.py:529
  26.4 7.1 %all-to-all-start = ((f32[8,8,256]{2,1,0:T(8,128)}), f32[8,8,256]{2,1,0:T(8,128)S(1)}, u32[]{:S(2)}, u32[]{:S(2)}) async-start(f32[8,8,256]{2,1,0:T(8,128)} %heads.1), calls=%async_computation | async-start | bytes 131072 | tf_op jit(solution)/shard_map/all_to_all | solution.py:543
  33.5 3.0 %first.1 = (f32[8,128,256]{2,1,0:T(8,128)S(1)}, f32[8,256,256]{2,1,0:T(8,128)S(1)}) custom-call(s32[1]{0:T(128)} %bitcast.5.node_ref, bf16[272,512]{1,0:T(8,128)(2,1)S(1)} %get-tuple-element.19.matrix_ref, bf16[128,256]{1,0:T(8,128)(2,1)} %loadings_ref.3, bf16[512,256]{1,0:T(8,128)(2,1)} %rows_ref.1, bf16[3,512,256]{2,1,0:T(8,128)(2,1)} %get-tuple-element.20.kept_ref), custom_call_target="tpu_custom_call" | custom-call | flops 536870912 | bytes 3145728 | tf_op jit(solution)/shard_map/first/pallas_call | solution.py:546
  36.5 3.2 %volts.1 = (f32[2048,128]{1,0:T(8,128)}, f32[2048,128]{1,0:T(8,128)}) custom-call(bf16[272,512]{1,0:T(8,128)(2,1)S(1)} %get-tuple-element.19.matrix_ref, f32[8,128,256]{2,1,0:T(8,128)S(1)} %get-tuple-element.21.swing_ref, f32[8,256,256]{2,1,0:T(8,128)S(1)} %get-tuple-element.22.drop_ref, f32[8,8,256]{2,1,0:T(8,128)S(1)} %all-to-all-done.head_ref), custom_call_target="tpu_custom_call" | custom-call | tf_op jit(solution)/shard_map/volts/pallas_call | solution.py:563
  (6 shorter events, 0.0 us)
Async XLA Ops:
  0.6 15.1 %collective-permute-start.1 = (bf16[512,256]{1,0:T(8,128)(2,1)}, bf16[512,256]{1,0:T(8,128)(2,1)S(1)}, u32[]{:S(2)}, u32[]{:S(2)}) collective-permute-start(bf16[512,256]{1,0:T(8,128)(2,1)} %rows_ref.1), channel_id=1, source_target_pairs={{0,2},{1,3},{2,0},{3,1},{4,6},{5,7},{6,4},{7,5},{8,10},{9,11},{10,... | collective-permute-start | bytes 786440 | tf_op jit(solution)/shard_map/ppermute | solution.py:439
  5.3 5.9 %collective-permute-start.2 = (bf16[144,256]{1,0:T(8,128)(2,1)S(1)}, bf16[144,256]{1,0:T(8,128)(2,1)S(1)}, u32[]{:S(2)}, u32[]{:S(2)}) collective-permute-start(bf16[144,256]{1,0:T(8,128)(2,1)S(1)} %get-tuple-element.18.refs_1_.refs_4_.refs_0_), channel_id=1, source_target_pairs={{0,16},{4,20},{8,24},{12,28},{16,0},{20,4},{24,8},{28,12},{1,17},{... | collective-permute-start | bytes 221192 | tf_op jit(solution)/shard_map/ppermute | solution.py:467
  8.0 4.4 %collective-permute-start.3 = (bf16[144,256]{1,0:T(8,128)(2,1)S(1)}, bf16[144,256]{1,0:T(8,128)(2,1)S(1)}, u32[]{:S(2)}, u32[]{:S(2)}) collective-permute-start(bf16[144,256]{1,0:T(8,128)(2,1)S(1)} %get-tuple-element.18.refs_1_.refs_4_.refs_0_), channel_id=1, source_target_pairs={{0,8},{4,12},{8,0},{12,4},{16,24},{20,28},{24,16},{28,20},{1,9},{5... | collective-permute-start | bytes 221192 | tf_op jit(solution)/shard_map/ppermute | solution.py:467
  9.6 6.2 %collective-permute-start.4 = (bf16[144,256]{1,0:T(8,128)(2,1)S(1)}, bf16[144,256]{1,0:T(8,128)(2,1)S(1)}, u32[]{:S(2)}, u32[]{:S(2)}) collective-permute-start(bf16[144,256]{1,0:T(8,128)(2,1)S(1)} %get-tuple-element.18.refs_1_.refs_4_.refs_0_), channel_id=1, source_target_pairs={{0,24},{4,28},{8,16},{12,20},{16,8},{20,12},{24,0},{28,4},{1,25},{... | collective-permute-start | bytes 221192 | tf_op jit(solution)/shard_map/ppermute | solution.py:467
  9.8 5.9 %collective-permute-start.5 = (bf16[144,256]{1,0:T(8,128)(2,1)S(1)}, bf16[144,256]{1,0:T(8,128)(2,1)S(1)}, u32[]{:S(2)}, u32[]{:S(2)}) collective-permute-start(bf16[144,256]{1,0:T(8,128)(2,1)S(1)} %get-tuple-element.18.refs_1_.refs_4_.refs_0_), channel_id=1, source_target_pairs={{0,4},{4,0},{8,12},{12,8},{16,20},{20,16},{24,28},{28,24},{1,5},{5... | collective-permute-start | bytes 221192 | tf_op jit(solution)/shard_map/ppermute | solution.py:467
  11.3 6.7 %collective-permute-start = (bf16[512,256]{1,0:T(8,128)(2,1)}, bf16[512,256]{1,0:T(8,128)(2,1)S(1)}, u32[]{:S(2)}, u32[]{:S(2)}) collective-permute-start(bf16[512,256]{1,0:T(8,128)(2,1)} %rows_ref.1), channel_id=1, source_target_pairs={{0,1},{1,0},{2,3},{3,2},{4,5},{5,4},{6,7},{7,6},{8,9},{9,8},{10,11... | collective-permute-start | bytes 786440 | tf_op jit(solution)/shard_map/ppermute | solution.py:439
  15.7 2.3 %collective-permute-start.6 = (bf16[512,256]{1,0:T(8,128)(2,1)S(1)}, bf16[512,256]{1,0:T(8,128)(2,1)S(1)}, u32[]{:S(2)}, u32[]{:S(2)}) collective-permute-start(bf16[512,256]{1,0:T(8,128)(2,1)S(1)} %after.1.refs_2_), channel_id=1, source_target_pairs={{0,1},{1,0},{2,3},{3,2},{4,5},{5,4},{6,7},{7,6},{8,9},{9,8},{10,11... | collective-permute-start | bytes 786440 | tf_op jit(solution)/shard_map/ppermute | solution.py:439
  15.8 4.8 %collective-permute-start.7 = (bf16[144,256]{1,0:T(8,128)(2,1)S(1)}, bf16[144,256]{1,0:T(8,128)(2,1)S(1)}, u32[]{:S(2)}, u32[]{:S(2)}) collective-permute-start(bf16[144,256]{1,0:T(8,128)(2,1)S(1)} %collective-permute-done.5.refs_5_.refs_8_.refs_4_), channel_id=1, source_target_pairs={{0,8},{4,12},{8,0},{12,4},{16,24},{20,28},{24,16},{28,20},{1,9},{5... | collective-permute-start | bytes 221192 | tf_op jit(solution)/shard_map/ppermute | solution.py:467
  15.9 5.9 %collective-permute-start.8 = (bf16[144,256]{1,0:T(8,128)(2,1)S(1)}, bf16[144,256]{1,0:T(8,128)(2,1)S(1)}, u32[]{:S(2)}, u32[]{:S(2)}) collective-permute-start(bf16[144,256]{1,0:T(8,128)(2,1)S(1)} %collective-permute-done.2.refs_2_.refs_5_.refs_1_), channel_id=1, source_target_pairs={{0,4},{4,0},{8,12},{12,8},{16,20},{20,16},{24,28},{28,24},{1,5},{5... | collective-permute-start | bytes 221192 | tf_op jit(solution)/shard_map/ppermute | solution.py:467
  17.4 4.6 %collective-permute-start.9 = (bf16[144,256]{1,0:T(8,128)(2,1)S(1)}, bf16[144,256]{1,0:T(8,128)(2,1)S(1)}, u32[]{:S(2)}, u32[]{:S(2)}) collective-permute-start(bf16[144,256]{1,0:T(8,128)(2,1)S(1)} %collective-permute-done.4.refs_4_.refs_7_.refs_3_), channel_id=1, source_target_pairs={{0,4},{4,0},{8,12},{12,8},{16,20},{20,16},{24,28},{28,24},{1,5},{5... | collective-permute-start | bytes 221192 | tf_op jit(solution)/shard_map/ppermute | solution.py:467
  26.4 10.1 %all-to-all-start = ((f32[8,8,256]{2,1,0:T(8,128)}), f32[8,8,256]{2,1,0:T(8,128)S(1)}, u32[]{:S(2)}, u32[]{:S(2)}) async-start(f32[8,8,256]{2,1,0:T(8,128)} %heads.1), calls=%async_computation | async-start | bytes 131072 | tf_op jit(solution)/shard_map/all_to_all | solution.py:543
